TPU v7x, 32 devices: a whole 2x2x4 slice. The times are simulated.
32 devices in a mesh: groups: 2 (over y), slab: 8 (over z, x), vec: 2 (over core).
Axes of the slice: x: 2, y: 2, z: 4, core: 2. Of those that a mesh axis runs over, the one named last changes fastest.
Arguments:
- vectors: bfloat16 [64, 64, 512], P(('groups', 'slab'), None, 'vec'), parts along dimension 0, may hold values from -18 to 18
- blocks: bfloat16 [32, 512, 512], P('groups', None, 'vec'), parts along dimension 0, may hold values from -2 to 4
- slab_blocks: int32 [64, 3], P(('groups', 'slab')), parts along dimension 0, may hold values from 0 to 15
- far_source: int32 [64, 4], P(('groups', 'slab')), parts along dimension 0, may hold values from 0 to 31, as said below
- far_block: int32 [64, 4], P(('groups', 'slab')), parts along dimension 0, may hold values from 0 to 15
- level_lower: bfloat16 [6, 64, 512, 512], P(None, ('groups', 'slab'), None, 'vec'), parts along dimension 1, may hold values from -0.125 to 0.125
- level_upper: bfloat16 [6, 64, 512, 512], P(None, ('groups', 'slab'), None, 'vec'), parts along dimension 1, may hold values from -0.125 to 0.125
- level_final: bfloat16 [64, 512, 512], P(('groups', 'slab'), None, 'vec'), parts along dimension 0, may hold values from -0.0625 to 0.0625
- shift_levels: float32 [16], P('groups'), parts along dimension 0, may hold values from 0.5 to 2.5
- shift_index: int32 [2], P('groups'), parts along dimension 0, may hold values from 0 to 7
Outputs:
- correction: bfloat16 [64, 64, 512], P(('groups', 'slab'), None, 'vec'), parts along dimension 0
- gram: float32 [256, 128], P('groups'), parts along dimension 0
- pencil: float32 [256, 128], P('groups'), parts along dimension 0
There are 2 independent parts, one for each index of `groups`. A program takes and returns all parts, laid end to end along the dimension named above; each array names one. Nothing has to cross between parts.
Inputs may be any that keep to these rules, and one draw needn't show every extreme that they name: `far_source`: each of the 4 source slabs of slab t lies at most 4 slabs from t, and the first lies exactly 4 slabs away.
All inputs are finite; a program needn't handle non-finite values.
Results may differ from a plain program's by a relative error of at most 0.018.
Values may be sent and summed in bfloat16 or wider, within the bound.
No kernel may reach another device: no remote copies, remote signals or barrier semaphores. Data moves between devices by JAX's collectives and lax.ppermute only.
A program may use at most 128 MiB of HBM per device.

v0:
```python
import jax
import jax.numpy as jnp
from jax import lax
from jax.sharding import PartitionSpec as P


def padded(x, sides, width):
    for axis, dim in sides:
        size, length = (lax.axis_size(axis), x.shape[dim])
        up = [(i, (i + 1) % size) for i in range(size - 1)]
        down = [(j, i) for i, j in up]
        last = lax.slice_in_dim(x, length - width, length, axis=dim)
        first = lax.slice_in_dim(x, 0, width, axis=dim)
        before = lax.ppermute(last, axis, up)
        after = lax.ppermute(first, axis, down)
        x = jnp.concatenate([before, x, after], axis=dim)
    return x


def from_behind(block, axis, distance):
    devices = range(lax.axis_size(axis))
    route = [(i - distance, i) for i in devices if i - distance in devices]
    return lax.ppermute(block, axis, route)


def orbitals(operand):
    return lax.all_gather(operand, "vec", axis=2, tiled=True)


def rim(operand):
    return padded(operand, (("slab", 0),), operand.shape[0])


def move(operand, offset):
    return from_behind(operand, "slab", offset)


def slabs_from(operand, stride):
    slab_count = operand.shape[0]
    if abs(stride) >= slab_count * lax.axis_size("slab"):
        return jnp.zeros_like(operand)
    if stride % slab_count == 0:
        return move(operand, stride // slab_count)
    if stride > 0:
        below_rows = move(operand[slab_count - stride :], 1)
        return jnp.concatenate([below_rows, operand[: slab_count - stride]], 0)
    span_back = -stride
    above_rows = move(operand[:span_back], -1)
    return jnp.concatenate([operand[span_back:], above_rows], 0)


def apply_operator(half_rows, blocks, slab_blocks, far_source, far_block):
    slab_count = half_rows.shape[0]
    extended = rim(orbitals(half_rows))
    below_rows = extended[slab_count - 1 : 2 * slab_count - 1]
    own_rows = extended[slab_count : 2 * slab_count]
    above_rows = extended[slab_count + 1 : 2 * slab_count + 1]
    summed = jnp.einsum(
        "skb,sbc->skc", below_rows, blocks[slab_blocks[:, 0]], preferred_element_type=jnp.float32
    )
    summed = summed + jnp.einsum(
        "skb,sbc->skc", own_rows, blocks[slab_blocks[:, 1]], preferred_element_type=jnp.float32
    )
    summed = summed + jnp.einsum(
        "skb,sbc->skc", above_rows, blocks[slab_blocks[:, 2]], preferred_element_type=jnp.float32
    )
    first_slab = lax.axis_index("slab") * slab_count
    local_rows = far_source - first_slab + slab_count
    fetched = extended[local_rows]
    summed = summed + jnp.einsum(
        "sfkb,sfbc->skc", fetched, blocks[far_block], preferred_element_type=jnp.float32
    )
    return summed.astype(jnp.bfloat16)


def on_device(
    vectors,
    blocks,
    slab_blocks,
    far_source,
    far_block,
    level_lower,
    level_upper,
    level_final,
    shift_levels,
    shift_index,
):
    slab_count = vectors.shape[0]
    rows_total = slab_count * lax.axis_size("slab") * blocks.shape[1]
    highest = lax.Precision.HIGHEST
    image = apply_operator(vectors, blocks, slab_blocks, far_source, far_block)
    quotient_part = jnp.einsum("skb,sjb->kj", vectors, image, preferred_element_type=jnp.float32)
    quotient = lax.psum(quotient_part, ("slab", "vec")) / rows_total
    residual = (
        image.astype(jnp.float32)
        - jnp.einsum("kj,skb->sjb", quotient, vectors.astype(jnp.float32), precision=highest)
    ).astype(jnp.bfloat16)
    level_count = level_lower.shape[0]
    for level_index in range(level_count):
        stride = 2**level_index
        whole_rows = orbitals(residual)
        from_below = slabs_from(whole_rows, stride)
        from_above = slabs_from(whole_rows, -stride)
        update = jnp.einsum(
            "skb,sbc->skc", from_below, level_lower[level_index], preferred_element_type=jnp.float32
        )
        update = update + jnp.einsum(
            "skb,sbc->skc", from_above, level_upper[level_index], preferred_element_type=jnp.float32
        )
        residual = (residual.astype(jnp.float32) - update).astype(jnp.bfloat16)
    correction = jnp.einsum(
        "skb,sbc->skc", orbitals(residual), level_final, preferred_element_type=jnp.float32
    ).astype(jnp.bfloat16)
    corrected_image = apply_operator(correction, blocks, slab_blocks, far_source, far_block)
    basis = jnp.concatenate([vectors, correction], 1)
    images = jnp.concatenate([image, corrected_image], 1)
    gram_part = jnp.einsum("skb,sjb->kj", basis, basis, preferred_element_type=jnp.float32)
    image_part = jnp.einsum("skb,sjb->kj", basis, images, preferred_element_type=jnp.float32)
    gram_total, image_total = lax.psum((gram_part, image_part), ("slab", "vec"))
    gram = gram_total / rows_total
    pencil = image_total / rows_total - shift_levels[shift_index[0]] * gram
    return (correction, gram, pencil)


def solution(mesh):
    in_specs = (
        P(("groups", "slab"), None, "vec"),
        P("groups", None, "vec"),
        P(("groups", "slab"), None),
        P(("groups", "slab"), None),
        P(("groups", "slab"), None),
        P(None, ("groups", "slab"), None, "vec"),
        P(None, ("groups", "slab"), None, "vec"),
        P(("groups", "slab"), None, "vec"),
        P("groups"),
        P("groups"),
    )
    out_specs = (P(("groups", "slab"), None, "vec"), P("groups", None), P("groups", None))
    return jax.shard_map(
        on_device, mesh=mesh, in_specs=in_specs, out_specs=out_specs, check_vma=False
    )
```

profile of v0, /device:TPU:0, one launch (start us, length us, event | category | flops | bytes accessed | tf_op | source)
XLA Modules:
  0.0 322.7 jit_solution(14703247015645899230)
XLA Ops:
  7.2 2.5 all_gather.24
  9.8 5.4 %collective-permute-start = (bf16[4,64,512]{2,1,0:T(8,128)(2,1)S(1)}, bf16[4,64,512]{2,1,0:T(8,128)(2,1)}, u32[]{:S(2)}, u32[]{:S(2)}) collective-permute-start(bf16[4,64,512]{2,1,0:T(8,128)(2,1)S(1)} %all_gather.24), channel_id=1, source_target_pairs={{0,2},{2,4},{4,6},{6,8},{8,10},{10,12},{12,14},{1,3},{3,5},{5,7},{... | collective-permute-start | bytes 786440 | tf_op jit(solution)/shard_map/ppermute | solution.py:14
  19.1 4.9 %gather_fusion.4 = bf16[16,512,256]{2,1,0:T(8,128)(2,1)} fusion(bf16[16,512,256]{2,1,0:T(8,128)(2,1)} %param.11, s32[1024]{0:T(1024)S(1)} %pad_clamp_fusion), kind=kCustom, calls=%fused_computation.4 | custom fusion | bytes 8388672 | tf_op jit(solution)/shard_map/gather | solution.py:71
  24.0 3.8 %gather_fusion.2 = bf16[4,512,256]{2,1,0:T(8,128)(2,1)} fusion(bf16[16,512,256]{2,1,0:T(8,128)(2,1)} %param.11, s32[1024]{0:T(1024)S(1)} %pad_clamp_fusion.2), kind=kCustom, calls=%fused_computation.2 | custom fusion | bytes 2097168 | tf_op jit(solution)/shard_map/gather | solution.py:65
  27.8 2.8 gather_fusion.1
  30.6 2.8 gather_fusion
  36.5 2.8 gather_fusion.3
  39.2 3.4 %convolution_bitcast_fusion.1 = f32[4,64,256]{2,1,0:T(8,128)S(1)} fusion(bf16[4,4,64,512]{3,2,1,0:T(8,128)(2,1)} %bitcast.99, bf16[4,4,512,256]{3,2,1,0:T(8,128)(2,1)} %bitcast.96), kind=kOutput, calls=%fused_computation.11 | convolution fusion | flops 268435456 | bytes 5505024 | tf_op jit(solution)/shard_map/sfkb,sfbc->skc/dot_general | solution.py:70
  46.2 62.4 %psum.21 = f32[64,64]{0,1:T(8,128)S(1)} all-reduce(f32[64,64]{0,1:T(8,128)S(1)} %convolution_bitcast_fusion.6), channel_id=1, replica_groups=mesh['groups'=2,'slab'=8,'vec'=2] {'slab','vec'}, use_global_device_ids=true, to_apply=%region_0.0 | all-reduce | flops 4096 | bytes 32768 | tf_op jit(solution)/shard_map/psum | solution.py:93
  113.3 4.5 %collective-permute-start.2 = (bf16[1,64,512]{2,1,0:T(8,128)(2,1)S(1)}, bf16[1,64,512]{2,1,0:T(8,128)(2,1)S(1)}, u32[]{:S(2)}, u32[]{:S(2)}) collective-permute-start(bf16[1,64,512]{2,1,0:T(8,128)(2,1)S(1)} %get-tuple-element.10), channel_id=1, source_target_pairs={{0,2},{2,4},{4,6},{6,8},{8,10},{10,12},{12,14},{1,3},{3,5},{5,7},{... | collective-permute-start | bytes 196616 | tf_op jit(solution)/shard_map/ppermute | solution.py:23
  124.6 5.0 %collective-permute-start.4 = (bf16[2,64,512]{2,1,0:T(8,128)(2,1)S(1)}, bf16[2,64,512]{2,1,0:T(8,128)(2,1)S(1)}, u32[]{:S(2)}, u32[]{:S(2)}) collective-permute-start(bf16[2,64,512]{2,1,0:T(8,128)(2,1)S(1)} %get-tuple-element.8), channel_id=1, source_target_pairs={{0,2},{2,4},{4,6},{6,8},{8,10},{10,12},{12,14},{1,3},{3,5},{5,7},{... | collective-permute-start | bytes 393224 | tf_op jit(solution)/shard_map/ppermute | solution.py:23
  139.1 5.0 %collective-permute-start.6 = (bf16[4,64,512]{2,1,0:T(8,128)(2,1)S(1)}, bf16[4,64,512]{2,1,0:T(8,128)(2,1)S(1)}, u32[]{:S(2)}, u32[]{:S(2)}) collective-permute-start(bf16[4,64,512]{2,1,0:T(8,128)(2,1)S(1)} %all_gather.27), channel_id=1, source_target_pairs={{0,2},{2,4},{4,6},{6,8},{8,10},{10,12},{12,14},{1,3},{3,5},{5,7},{... | collective-permute-start | bytes 786440 | tf_op jit(solution)/shard_map/ppermute | solution.py:23
  144.1 4.7 %collective-permute-done.7 = bf16[4,64,512]{2,1,0:T(8,128)(2,1)S(1)} collective-permute-done((bf16[4,64,512]{2,1,0:T(8,128)(2,1)S(1)}, bf16[4,64,512]{2,1,0:T(8,128)(2,1)S(1)}, u32[]{:S(2)}, u32[]{:S(2)}) %collective-permute-start.7) | collective-permute-done | bytes 262176 | tf_op jit(solution)/shard_map/ppermute | solution.py:23
  150.3 4.3 %collective-permute-done.6 = bf16[4,64,512]{2,1,0:T(8,128)(2,1)S(1)} collective-permute-done((bf16[4,64,512]{2,1,0:T(8,128)(2,1)S(1)}, bf16[4,64,512]{2,1,0:T(8,128)(2,1)S(1)}, u32[]{:S(2)}, u32[]{:S(2)}) %collective-permute-start.6) | collective-permute-done | bytes 262176 | tf_op jit(solution)/shard_map/ppermute | solution.py:23
  160.9 6.1 %collective-permute-start.8 = (bf16[4,64,512]{2,1,0:T(8,128)(2,1)S(1)}, bf16[4,64,512]{2,1,0:T(8,128)(2,1)S(1)}, u32[]{:S(2)}, u32[]{:S(2)}) collective-permute-start(bf16[4,64,512]{2,1,0:T(8,128)(2,1)S(1)} %all_gather.28), channel_id=1, source_target_pairs={{0,4},{2,6},{4,8},{6,10},{8,12},{10,14},{1,5},{3,7},{5,9},{7,11},{... | collective-permute-start | bytes 786440 | tf_op jit(solution)/shard_map/ppermute | solution.py:23
  167.0 3.1 collective-permute-done.9
  170.5 2.4 collective-permute-done.8
  178.0 5.6 %collective-permute-start.10 = (bf16[4,64,512]{2,1,0:T(8,128)(2,1)S(1)}, bf16[4,64,512]{2,1,0:T(8,128)(2,1)S(1)}, u32[]{:S(2)}, u32[]{:S(2)}) collective-permute-start(bf16[4,64,512]{2,1,0:T(8,128)(2,1)S(1)} %all_gather.29), channel_id=1, source_target_pairs={{0,8},{2,10},{4,12},{6,14},{1,9},{3,11},{5,13},{7,15},{16,24},{18,... | collective-permute-start | bytes 786440 | tf_op jit(solution)/shard_map/ppermute | solution.py:23
  183.6 10.0 %collective-permute-done.11 = bf16[4,64,512]{2,1,0:T(8,128)(2,1)S(1)} collective-permute-done((bf16[4,64,512]{2,1,0:T(8,128)(2,1)S(1)}, bf16[4,64,512]{2,1,0:T(8,128)(2,1)S(1)}, u32[]{:S(2)}, u32[]{:S(2)}) %collective-permute-start.11) | collective-permute-done | bytes 262176 | tf_op jit(solution)/shard_map/ppermute | solution.py:23
  201.0 4.6 %collective-permute-start.12 = (bf16[4,64,512]{2,1,0:T(8,128)(2,1)S(1)}, bf16[4,64,512]{2,1,0:T(8,128)(2,1)S(1)}, u32[]{:S(2)}, u32[]{:S(2)}) collective-permute-start(bf16[4,64,512]{2,1,0:T(8,128)(2,1)S(1)} %all_gather.31), channel_id=1, source_target_pairs={{0,2},{2,4},{4,6},{6,8},{8,10},{10,12},{12,14},{1,3},{3,5},{5,7},{... | collective-permute-start | bytes 786440 | tf_op jit(solution)/shard_map/ppermute | solution.py:14
  207.4 2.5 collective-permute-done.13
  209.9 5.5 %collective-permute-done.12 = bf16[4,64,512]{2,1,0:T(8,128)(2,1)S(1)} collective-permute-done((bf16[4,64,512]{2,1,0:T(8,128)(2,1)S(1)}, bf16[4,64,512]{2,1,0:T(8,128)(2,1)S(1)}, u32[]{:S(2)}, u32[]{:S(2)}) %collective-permute-start.12) | collective-permute-done | bytes 262176 | tf_op jit(solution)/shard_map/ppermute | solution.py:14
  217.9 3.4 %convolution_bitcast_fusion = f32[4,64,256]{2,1,0:T(8,128)S(1)} fusion(bf16[4,4,64,512]{3,2,1,0:T(8,128)(2,1)} %bitcast.98, bf16[4,4,512,256]{3,2,1,0:T(8,128)(2,1)} %bitcast.97), kind=kOutput, calls=%fused_computation.10 | convolution fusion | flops 268435456 | bytes 5505024 | tf_op jit(solution)/shard_map/sfkb,sfbc->skc/dot_general | solution.py:70
  226.0 88.3 %all-reduce.3.cloned.1.call-done = (f32[128,128]{1,0:T(8,128)}, f32[128,128]{1,0:T(8,128)}) async-done(((f32[128,128]{1,0:T(8,128)}, f32[128,128]{1,0:T(8,128)}), (f32[128,128]{1,0:T(8,128)}, f32[128,128]{1,0:T(8,128)})) %all-reduce.3.cloned.1.call-update) | async-done | bytes 131088 | tf_op jit(solution)/shard_map/psum | solution.py:119
  (93 shorter events, 61.1 us)
Async XLA Ops:
  7.2 190.2 %copy-start = (bf16[4,512,256]{2,1,0:T(8,128)(2,1)S(1)}, bf16[4,512,256]{2,1,0:T(8,128)(2,1)}, u32[]{:S(2)}) copy-start(bf16[4,512,256]{2,1,0:T(8,128)(2,1)} %param.17) | copy-start | bytes 3145732
  7.2 307.2 %all-reduce.3.cloned.1.call-start = ((), (), s32[]{:S(2)}) async-start(), calls=%async_computation | async-start | bytes 262144 | tf_op jit(solution)/shard_map/psum | solution.py:119
  9.8 24.7 %collective-permute-start = (bf16[4,64,512]{2,1,0:T(8,128)(2,1)S(1)}, bf16[4,64,512]{2,1,0:T(8,128)(2,1)}, u32[]{:S(2)}, u32[]{:S(2)}) collective-permute-start(bf16[4,64,512]{2,1,0:T(8,128)(2,1)S(1)} %all_gather.24), channel_id=1, source_target_pairs={{0,2},{2,4},{4,6},{6,8},{8,10},{10,12},{12,14},{1,3},{3,5},{5,7},{... | collective-permute-start | bytes 786440 | tf_op jit(solution)/shard_map/ppermute | solution.py:14
  15.2 19.3 %collective-permute-start.1 = (bf16[4,64,512]{2,1,0:T(8,128)(2,1)S(1)}, bf16[4,64,512]{2,1,0:T(8,128)(2,1)}, u32[]{:S(2)}, u32[]{:S(2)}) collective-permute-start(bf16[4,64,512]{2,1,0:T(8,128)(2,1)S(1)} %all_gather.24), channel_id=1, source_target_pairs={{2,0},{4,2},{6,4},{8,6},{10,8},{12,10},{14,12},{3,1},{5,3},{7,5},{... | collective-permute-start | bytes 786440 | tf_op jit(solution)/shard_map/ppermute | solution.py:15
  36.5 9.5 %copy-start.1 = (bf16[4,64,256]{2,1,0:T(8,128)(2,1)S(1)}, bf16[4,64,256]{2,1,0:T(8,128)(2,1)}, u32[]{:S(2)}) copy-start(bf16[4,64,256]{2,1,0:T(8,128)(2,1)} %param.10) | copy-start | bytes 393220
  109.8 60.4 %slice-start = ((s8[6291456]{0:T(1024)(128)(4,1)}), s8[4194304]{0:T(1024)(128)(4,1)S(1)}, s32[]{:S(2)}) async-start(s8[6291456]{0:T(1024)(128)(4,1)} %bitcast.100), calls=%async_computation.1 | async-start | bytes 8388608
  111.9 6.2 %collective-permute-start.3 = (bf16[1,64,512]{2,1,0:T(8,128)(2,1)S(1)}, bf16[1,64,512]{2,1,0:T(8,128)(2,1)S(1)}, u32[]{:S(2)}, u32[]{:S(2)}) collective-permute-start(bf16[1,64,512]{2,1,0:T(8,128)(2,1)S(1)} %get-tuple-element.11), channel_id=1, source_target_pairs={{2,0},{4,2},{6,4},{8,6},{10,8},{12,10},{14,12},{3,1},{5,3},{7,5},{... | collective-permute-start | bytes 196616 | tf_op jit(solution)/shard_map/ppermute | solution.py:23
  113.3 6.4 %collective-permute-start.2 = (bf16[1,64,512]{2,1,0:T(8,128)(2,1)S(1)}, bf16[1,64,512]{2,1,0:T(8,128)(2,1)S(1)}, u32[]{:S(2)}, u32[]{:S(2)}) collective-permute-start(bf16[1,64,512]{2,1,0:T(8,128)(2,1)S(1)} %get-tuple-element.10), channel_id=1, source_target_pairs={{0,2},{2,4},{4,6},{6,8},{8,10},{10,12},{12,14},{1,3},{3,5},{5,7},{... | collective-permute-start | bytes 196616 | tf_op jit(solution)/shard_map/ppermute | solution.py:23
  123.2 8.1 %collective-permute-start.5 = (bf16[2,64,512]{2,1,0:T(8,128)(2,1)S(1)}, bf16[2,64,512]{2,1,0:T(8,128)(2,1)S(1)}, u32[]{:S(2)}, u32[]{:S(2)}) collective-permute-start(bf16[2,64,512]{2,1,0:T(8,128)(2,1)S(1)} %get-tuple-element.9), channel_id=1, source_target_pairs={{2,0},{4,2},{6,4},{8,6},{10,8},{12,10},{14,12},{3,1},{5,3},{7,5},{... | collective-permute-start | bytes 393224 | tf_op jit(solution)/shard_map/ppermute | solution.py:23
  124.5 45.6 %slice-start.1 = ((s8[6291456]{0:T(1024)(128)(4,1)}), s8[2097152]{0:T(1024)(128)(4,1)S(1)}, s32[]{:S(2)}) async-start(s8[6291456]{0:T(1024)(128)(4,1)} %bitcast.100), calls=%async_computation.2 | async-start | bytes 4194304
  124.6 9.7 %collective-permute-start.4 = (bf16[2,64,512]{2,1,0:T(8,128)(2,1)S(1)}, bf16[2,64,512]{2,1,0:T(8,128)(2,1)S(1)}, u32[]{:S(2)}, u32[]{:S(2)}) collective-permute-start(bf16[2,64,512]{2,1,0:T(8,128)(2,1)S(1)} %get-tuple-element.8), channel_id=1, source_target_pairs={{0,2},{2,4},{4,6},{6,8},{8,10},{10,12},{12,14},{1,3},{3,5},{5,7},{... | collective-permute-start | bytes 393224 | tf_op jit(solution)/shard_map/ppermute | solution.py:23
  137.8 11.0 %collective-permute-start.7 = (bf16[4,64,512]{2,1,0:T(8,128)(2,1)S(1)}, bf16[4,64,512]{2,1,0:T(8,128)(2,1)S(1)}, u32[]{:S(2)}, u32[]{:S(2)}) collective-permute-start(bf16[4,64,512]{2,1,0:T(8,128)(2,1)S(1)} %all_gather.27), channel_id=1, source_target_pairs={{2,0},{4,2},{6,4},{8,6},{10,8},{12,10},{14,12},{3,1},{5,3},{7,5},{... | collective-permute-start | bytes 786440 | tf_op jit(solution)/shard_map/ppermute | solution.py:23
  139.1 15.5 %collective-permute-start.6 = (bf16[4,64,512]{2,1,0:T(8,128)(2,1)S(1)}, bf16[4,64,512]{2,1,0:T(8,128)(2,1)S(1)}, u32[]{:S(2)}, u32[]{:S(2)}) collective-permute-start(bf16[4,64,512]{2,1,0:T(8,128)(2,1)S(1)} %all_gather.27), channel_id=1, source_target_pairs={{0,2},{2,4},{4,6},{6,8},{8,10},{10,12},{12,14},{1,3},{3,5},{5,7},{... | collective-permute-start | bytes 786440 | tf_op jit(solution)/shard_map/ppermute | solution.py:23
  158.1 12.1 %collective-permute-start.9 = (bf16[4,64,512]{2,1,0:T(8,128)(2,1)S(1)}, bf16[4,64,512]{2,1,0:T(8,128)(2,1)S(1)}, u32[]{:S(2)}, u32[]{:S(2)}) collective-permute-start(bf16[4,64,512]{2,1,0:T(8,128)(2,1)S(1)} %all_gather.28), channel_id=1, source_target_pairs={{4,0},{6,2},{8,4},{10,6},{12,8},{14,10},{5,1},{7,3},{9,5},{11,7},{... | collective-permute-start | bytes 786440 | tf_op jit(solution)/shard_map/ppermute | solution.py:23
  160.9 11.9 %collective-permute-start.8 = (bf16[4,64,512]{2,1,0:T(8,128)(2,1)S(1)}, bf16[4,64,512]{2,1,0:T(8,128)(2,1)S(1)}, u32[]{:S(2)}, u32[]{:S(2)}) collective-permute-start(bf16[4,64,512]{2,1,0:T(8,128)(2,1)S(1)} %all_gather.28), channel_id=1, source_target_pairs={{0,4},{2,6},{4,8},{6,10},{8,12},{10,14},{1,5},{3,7},{5,9},{7,11},{... | collective-permute-start | bytes 786440 | tf_op jit(solution)/shard_map/ppermute | solution.py:23
  176.4 17.2 %collective-permute-start.11 = (bf16[4,64,512]{2,1,0:T(8,128)(2,1)S(1)}, bf16[4,64,512]{2,1,0:T(8,128)(2,1)S(1)}, u32[]{:S(2)}, u32[]{:S(2)}) collective-permute-start(bf16[4,64,512]{2,1,0:T(8,128)(2,1)S(1)} %all_gather.29), channel_id=1, source_target_pairs={{8,0},{10,2},{12,4},{14,6},{9,1},{11,3},{13,5},{15,7},{24,16},{26,... | collective-permute-start | bytes 786440 | tf_op jit(solution)/shard_map/ppermute | solution.py:23
  178.0 15.9 %collective-permute-start.10 = (bf16[4,64,512]{2,1,0:T(8,128)(2,1)S(1)}, bf16[4,64,512]{2,1,0:T(8,128)(2,1)S(1)}, u32[]{:S(2)}, u32[]{:S(2)}) collective-permute-start(bf16[4,64,512]{2,1,0:T(8,128)(2,1)S(1)} %all_gather.29), channel_id=1, source_target_pairs={{0,8},{2,10},{4,12},{6,14},{1,9},{3,11},{5,13},{7,15},{16,24},{18,... | collective-permute-start | bytes 786440 | tf_op jit(solution)/shard_map/ppermute | solution.py:23
  197.7 12.3 %copy-start.8 = (bf16[4,64,256]{2,1,0:T(8,128)(2,1)}, bf16[4,64,256]{2,1,0:T(8,128)(2,1)S(1)}, u32[]{:S(2)}) copy-start(bf16[4,64,256]{2,1,0:T(8,128)(2,1)S(1)} %convolution_convert_fusion) | copy-start | bytes 393220
  199.7 10.2 %collective-permute-start.13 = (bf16[4,64,512]{2,1,0:T(8,128)(2,1)S(1)}, bf16[4,64,512]{2,1,0:T(8,128)(2,1)S(1)}, u32[]{:S(2)}, u32[]{:S(2)}) collective-permute-start(bf16[4,64,512]{2,1,0:T(8,128)(2,1)S(1)} %all_gather.31), channel_id=1, source_target_pairs={{2,0},{4,2},{6,4},{8,6},{10,8},{12,10},{14,12},{3,1},{5,3},{7,5},{... | collective-permute-start | bytes 786440 | tf_op jit(solution)/shard_map/ppermute | solution.py:15
  201.0 14.5 %collective-permute-start.12 = (bf16[4,64,512]{2,1,0:T(8,128)(2,1)S(1)}, bf16[4,64,512]{2,1,0:T(8,128)(2,1)S(1)}, u32[]{:S(2)}, u32[]{:S(2)}) collective-permute-start(bf16[4,64,512]{2,1,0:T(8,128)(2,1)S(1)} %all_gather.31), channel_id=1, source_target_pairs={{0,2},{2,4},{4,6},{6,8},{8,10},{10,12},{12,14},{1,3},{3,5},{5,7},{... | collective-permute-start | bytes 786440 | tf_op jit(solution)/shard_map/ppermute | solution.py:14
  209.9 5.5 %copy-start.10 = (bf16[4,64,512]{2,1,0:T(8,128)(2,1)}, bf16[4,64,512]{2,1,0:T(8,128)(2,1)S(1)}, u32[]{:S(2)}) copy-start(bf16[4,64,512]{2,1,0:T(8,128)(2,1)S(1)} %collective-permute-done.13) | copy-start | bytes 786436
  216.2 6.9 %copy-start.3 = (bf16[4,64,256]{2,1,0:T(8,128)(2,1)S(1)}, bf16[4,64,256]{2,1,0:T(8,128)(2,1)}, u32[]{:S(2)}) copy-start(bf16[4,64,256]{2,1,0:T(8,128)(2,1)} %copy-done.2) | copy-start | bytes 393220
  216.3 6.9 %copy-start.9 = (bf16[4,64,256]{2,1,0:T(8,128)(2,1)S(1)}, bf16[4,64,256]{2,1,0:T(8,128)(2,1)}, u32[]{:S(2)}) copy-start(bf16[4,64,256]{2,1,0:T(8,128)(2,1)} %copy-done.8) | copy-start | bytes 393220
  216.3 8.5 %copy-start.11 = (f32[8]{0:T(128)S(1)}, f32[8]{0:T(128)}, u32[]{:S(2)}) copy-start(f32[8]{0:T(128)} %param.18) | copy-start | bytes 100
  (5 other events, 16.2 us)
Sparse Core Ops, SparseCore 0:
  224.2 90.0 all-reduce.2
where the time goes:
time: 325 us; the launch traced here: 323 us
  waiting for transfers between devices  124 us (38%)
  blocking collectives  79.1 us (24%)
  starting transfers between devices  45.3 us (14%)
  matrix products  31.2 us (10%)
  local copies, waits for them, and re-layouts  21 us (6%)
  between operations  15.8 us (5%)
  other arithmetic  6.05 us (2%)
    psum x1, waiting for transfers between devices, on_device(): gram_total, image_total = lax.psum((gram_part, image_part), ('slab', 'vec'))  88.3 us
    psum x1, blocking collectives, on_device(): quotient = lax.psum(quotient_part, ('slab', 'vec')) / rows_total  62.4 us
    ppermute x10, starting transfers between devices, from_behind(): return lax.ppermute(block, axis, route)  32.7 us
    ppermute x10, waiting for transfers between devices, from_behind(): return lax.ppermute(block, axis, route)  28 us
    all_gather x8, blocking collectives, orbitals(): return lax.all_gather(operand, 'vec', axis=2, tiled=True)  16.6 us
    ppermute x2, starting transfers between devices, padded(): before = lax.ppermute(last, axis, up)  9.99 us
    dot_general x6, matrix products, on_device(): jnp.einsum('skb,sbc->skc', from_below, level_lower[level_index], preferre...  9.13 us
    dot_general x2, matrix products, apply_operator(): jnp.einsum('sfkb,sfbc->skc', fetched, blocks[far_block], preferred_elemen...  6.77 us
  transfers between devices with their start and end apart: 15, of which 12 were waited for; matrix products, arithmetic and copies ran while one was open for 9% of the time, Pallas kernels for 0%

commit v1 on v0

--- a/solution.py
+++ b/solution.py
@@ -28,30 +28,49 @@
 
 
 def rim(operand):
-    return padded(operand, (("slab", 0),), operand.shape[0])
+    return orbitals(padded(operand, (("slab", 0),), operand.shape[0]))
 
 
 def move(operand, offset):
     return from_behind(operand, "slab", offset)
 
 
-def slabs_from(operand, stride):
+def halves_from(operand, stride):
     slab_count = operand.shape[0]
-    if abs(stride) >= slab_count * lax.axis_size("slab"):
-        return jnp.zeros_like(operand)
     if stride % slab_count == 0:
         return move(operand, stride // slab_count)
     if stride > 0:
-        below_rows = move(operand[slab_count - stride :], 1)
-        return jnp.concatenate([below_rows, operand[: slab_count - stride]], 0)
-    span_back = -stride
-    above_rows = move(operand[:span_back], -1)
-    return jnp.concatenate([operand[span_back:], above_rows], 0)
+        return move(operand[slab_count - stride :], 1)
+    return move(operand[:-stride], -1)
+
+
+def partners(residual, stride):
+    slab_count = residual.shape[0]
+    if stride >= slab_count * lax.axis_size("slab"):
+        return None
+    below, above = halves_from(residual, stride), halves_from(residual, -stride)
+    if stride % slab_count == 0:
+        rows = orbitals(jnp.concatenate([below, above], 0))
+        return rows[:slab_count], rows[slab_count:]
+    rows = orbitals(jnp.concatenate([below, residual, above], 0))
+    return rows[:slab_count], rows[2 * stride :]
+
+
+def total(part):
+    slabs = lax.axis_size("slab")
+    if slabs & (slabs - 1):
+        return lax.psum(part, ("slab", "vec"))
+    part = part + lax.ppermute(part, "vec", [(0, 1), (1, 0)])
+    reach = 1
+    while reach < slabs:
+        part = part + lax.ppermute(part, "slab", [(i, i ^ reach) for i in range(slabs)])
+        reach *= 2
+    return part
 
 
 def apply_operator(half_rows, blocks, slab_blocks, far_source, far_block):
     slab_count = half_rows.shape[0]
-    extended = rim(orbitals(half_rows))
+    extended = rim(half_rows)
     below_rows = extended[slab_count - 1 : 2 * slab_count - 1]
     own_rows = extended[slab_count : 2 * slab_count]
     above_rows = extended[slab_count + 1 : 2 * slab_count + 1]
@@ -90,7 +109,7 @@
     highest = lax.Precision.HIGHEST
     image = apply_operator(vectors, blocks, slab_blocks, far_source, far_block)
     quotient_part = jnp.einsum("skb,sjb->kj", vectors, image, preferred_element_type=jnp.float32)
-    quotient = lax.psum(quotient_part, ("slab", "vec")) / rows_total
+    quotient = total(quotient_part) / rows_total
     residual = (
         image.astype(jnp.float32)
         - jnp.einsum("kj,skb->sjb", quotient, vectors.astype(jnp.float32), precision=highest)
@@ -98,9 +117,10 @@
     level_count = level_lower.shape[0]
     for level_index in range(level_count):
         stride = 2**level_index
-        whole_rows = orbitals(residual)
-        from_below = slabs_from(whole_rows, stride)
-        from_above = slabs_from(whole_rows, -stride)
+        pair = partners(residual, stride)
+        if pair is None:
+            continue
+        from_below, from_above = pair
         update = jnp.einsum(
             "skb,sbc->skc", from_below, level_lower[level_index], preferred_element_type=jnp.float32
         )
@@ -113,10 +133,11 @@
     ).astype(jnp.bfloat16)
     corrected_image = apply_operator(correction, blocks, slab_blocks, far_source, far_block)
     basis = jnp.concatenate([vectors, correction], 1)
-    images = jnp.concatenate([image, corrected_image], 1)
-    gram_part = jnp.einsum("skb,sjb->kj", basis, basis, preferred_element_type=jnp.float32)
-    image_part = jnp.einsum("skb,sjb->kj", basis, images, preferred_element_type=jnp.float32)
-    gram_total, image_total = lax.psum((gram_part, image_part), ("slab", "vec"))
+    others = jnp.concatenate([vectors, correction, image, corrected_image], 1)
+    part = jnp.einsum("skb,sjb->kj", basis, others, preferred_element_type=jnp.float32)
+    both = total(part)
+    width = basis.shape[1]
+    gram_total, image_total = both[:, :width], both[:, width:]
     gram = gram_total / rows_total
     pencil = image_total / rows_total - shift_levels[shift_index[0]] * gram
     return (correction, gram, pencil)

time: 325 us -> 168 us (0.52)
  waiting for transfers between devices: 124 us -> 57.4 us
  blocking collectives: 79.1 us -> 17.5 us
  between operations: 15.8 us -> 2.45 us
  matrix products: 31.2 us -> 20.3 us
    psum x1 -> x0, waiting for transfers between devices: 88.3 us -> none  [on_device(): gram_total, image_total = lax.psum((gram_part, image_part), ('slab', 'vec'))]
    psum x1 -> x0, blocking collectives: 62.4 us -> none  [on_device(): quotient = lax.psum(quotient_part, ('slab', 'vec')) / rows_total]
    ppermute x0 -> x8, waiting for transfers between devices: none -> 20.7 us  [the longest x6 18.5 us: total(): lax.ppermute(part, 'slab', [(i, i ^ reach) for i in range(slabs)])]
    ppermute x0 -> x8, starting transfers between devices: none -> 12.4 us  [the longest x6 12 us: total(): lax.ppermute(part, 'slab', [(i, i ^ reach) for i in range(slabs)])]
    ppermute x10, starting transfers between devices: 32.7 us -> 25 us  [from_behind(): return lax.ppermute(block, axis, route)]
    dot_general x6 -> x5, matrix products: 9.13 us -> 2.68 us  [on_device(): jnp.einsum('skb,sbc->skc', from_below, level_lower[level_index], preferre...]
    ppermute x2, waiting for transfers between devices: 5.51 us -> 1.75 us  [padded(): before = lax.ppermute(last, axis, up)]
  transfers between devices with their start and end apart: 15 -> 22, of which waited for: 12 -> 20; matrix products, arithmetic and copies ran while one was open for 9% -> 11% of each run, Pallas kernels for 0% -> 0%
where the time goes in v1:
time: 168 us; the launch traced here: 167 us
  waiting for transfers between devices  57.4 us (34%)
  starting transfers between devices  47.4 us (28%)
  matrix products  20.3 us (12%)
  local copies, waits for them, and re-layouts  18.4 us (11%)
  blocking collectives  17.5 us (10%)
  other arithmetic  3.39 us (2%)
  between operations  2.45 us (1%)
    ppermute x10, waiting for transfers between devices, from_behind(): return lax.ppermute(block, axis, route)  30.8 us
    ppermute x10, starting transfers between devices, from_behind(): return lax.ppermute(block, axis, route)  25 us
    ppermute x6, waiting for transfers between devices, total(): lax.ppermute(part, 'slab', [(i, i ^ reach) for i in range(slabs)])  18.5 us
    all_gather x8, blocking collectives, orbitals(): return lax.all_gather(operand, 'vec', axis=2, tiled=True)  17.5 us
    ppermute x6, starting transfers between devices, total(): lax.ppermute(part, 'slab', [(i, i ^ reach) for i in range(slabs)])  12 us
    ppermute x2, starting transfers between devices, padded(): before = lax.ppermute(last, axis, up)  7.48 us
    dot_general x2, matrix products, apply_operator(): jnp.einsum('sfkb,sfbc->skc', fetched, blocks[far_block], preferred_elemen...  6.51 us
    gather x1, local copies, waits for them, and re-layouts, apply_operator(): blocks[far_block]  4.97 us
  transfers between devices with their start and end apart: 22, of which 20 were waited for; matrix products, arithmetic and copies ran while one was open for 11% of the time, Pallas kernels for 0%

profile of v1, /device:TPU:0, one launch (start us, length us, event | category | flops | bytes accessed | tf_op | source)
XLA Modules:
  0.0 166.9 jit_solution(5046946556827335369)
XLA Ops:
  0.6 5.0 %collective-permute-start = (bf16[4,64,256]{2,1,0:T(8,128)(2,1)}, bf16[4,64,256]{2,1,0:T(8,128)(2,1)S(1)}, u32[]{:S(2)}, u32[]{:S(2)}) collective-permute-start(bf16[4,64,256]{2,1,0:T(8,128)(2,1)} %param.10), channel_id=1, source_target_pairs={{0,2},{2,4},{4,6},{6,8},{8,10},{10,12},{12,14},{1,3},{3,5},{5,7},{... | collective-permute-start | bytes 393224 | tf_op jit(solution)/shard_map/ppermute | solution.py:14
  9.4 2.8 %gather_fusion.1 = bf16[4,512,256]{2,1,0:T(8,128)(2,1)S(1)} fusion(bf16[16,512,256]{2,1,0:T(8,128)(2,1)} %param.11, s32[1024]{0:T(1024)S(1)} %get-tuple-element.13), kind=kCustom, calls=%fused_computation.1 | custom fusion | bytes 2097168 | tf_op jit(solution)/shard_map/gather | solution.py:81
  12.3 3.8 %gather_fusion.2 = bf16[4,512,256]{2,1,0:T(8,128)(2,1)} fusion(bf16[16,512,256]{2,1,0:T(8,128)(2,1)} %param.11, s32[1024]{0:T(1024)S(1)} %get-tuple-element.12), kind=kCustom, calls=%fused_computation.2 | custom fusion | bytes 2097168 | tf_op jit(solution)/shard_map/gather | solution.py:84
  16.2 5.0 %gather_fusion.4 = bf16[16,512,256]{2,1,0:T(8,128)(2,1)} fusion(bf16[16,512,256]{2,1,0:T(8,128)(2,1)} %param.11, s32[1024]{0:T(1024)S(1)} %pad_clamp_fusion), kind=kCustom, calls=%fused_computation.4 | custom fusion | bytes 8388672 | tf_op jit(solution)/shard_map/gather | solution.py:90
  21.2 3.8 %gather_fusion = bf16[4,512,256]{2,1,0:T(8,128)(2,1)} fusion(bf16[16,512,256]{2,1,0:T(8,128)(2,1)} %param.11, s32[1024]{0:T(1024)S(1)} %pad_clamp_fusion.4), kind=kCustom, calls=%fused_computation | custom fusion | bytes 2097168 | tf_op jit(solution)/shard_map/gather | solution.py:78
  31.5 3.5 %convolution_bitcast_fusion.1 = f32[4,64,256]{2,1,0:T(8,128)S(1)} fusion(bf16[4,4,64,512]{3,2,1,0:T(8,128)(2,1)} %bitcast.93, bf16[4,4,512,256]{3,2,1,0:T(8,128)(2,1)} %bitcast.90), kind=kOutput, calls=%fused_computation.19 | convolution fusion | flops 268435456 | bytes 5505024 | tf_op jit(solution)/shard_map/sfkb,sfbc->skc/dot_general | solution.py:89
  38.6 2.6 %collective-permute-start.3 = (f32[64,64]{0,1:T(8,128)S(1)}, f32[64,64]{0,1:T(8,128)S(1)}, u32[]{:S(2)}, u32[]{:S(2)}) collective-permute-start(f32[64,64]{0,1:T(8,128)S(1)} %add.101), channel_id=1, source_target_pairs={{0,2},{2,0},{4,6},{6,4},{8,10},{10,8},{12,14},{14,12},{1,3},{3,1},... | collective-permute-start | bytes 49160 | tf_op jit(solution)/shard_map/ppermute | solution.py:66
  43.1 3.0 %collective-permute-start.4 = (f32[64,64]{0,1:T(8,128)S(1)}, f32[64,64]{0,1:T(8,128)S(1)}, u32[]{:S(2)}, u32[]{:S(2)}) collective-permute-start(f32[64,64]{0,1:T(8,128)S(1)} %add.102), channel_id=1, source_target_pairs={{0,4},{2,6},{4,0},{6,2},{8,12},{10,14},{12,8},{14,10},{1,5},{3,7},... | collective-permute-start | bytes 49160 | tf_op jit(solution)/shard_map/ppermute | solution.py:66
  48.0 3.0 %collective-permute-start.5 = (f32[64,64]{0,1:T(8,128)S(1)}, f32[64,64]{0,1:T(8,128)S(1)}, u32[]{:S(2)}, u32[]{:S(2)}) collective-permute-start(f32[64,64]{0,1:T(8,128)S(1)} %add.103), channel_id=1, source_target_pairs={{0,8},{2,10},{4,12},{6,14},{8,0},{10,2},{12,4},{14,6},{1,9},{3,11}... | collective-permute-start | bytes 49160 | tf_op jit(solution)/shard_map/ppermute | solution.py:66
  53.2 3.0 %collective-permute-start.6 = (bf16[1,64,256]{2,1,0:T(8,128)(2,1)S(1)}, bf16[1,64,256]{2,1,0:T(8,128)(2,1)S(1)}, u32[]{:S(2)}, u32[]{:S(2)}) collective-permute-start(bf16[1,64,256]{2,1,0:T(8,128)(2,1)S(1)} %get-tuple-element.10), channel_id=1, source_target_pairs={{0,2},{2,4},{4,6},{6,8},{8,10},{10,12},{12,14},{1,3},{3,5},{5,7},{... | collective-permute-start | bytes 98312 | tf_op jit(solution)/shard_map/ppermute | solution.py:23
  57.8 4.7 %collective-permute-done.7 = bf16[1,64,256]{2,1,0:T(8,128)(2,1)S(1)} collective-permute-done((bf16[1,64,256]{2,1,0:T(8,128)(2,1)S(1)}, bf16[1,64,256]{2,1,0:T(8,128)(2,1)S(1)}, u32[]{:S(2)}, u32[]{:S(2)}) %collective-permute-start.7) | collective-permute-done | bytes 32800 | tf_op jit(solution)/shard_map/ppermute | solution.py:23
  67.6 4.8 %collective-permute-start.8 = (bf16[2,64,256]{2,1,0:T(8,128)(2,1)S(1)}, bf16[2,64,256]{2,1,0:T(8,128)(2,1)S(1)}, u32[]{:S(2)}, u32[]{:S(2)}) collective-permute-start(bf16[2,64,256]{2,1,0:T(8,128)(2,1)S(1)} %get-tuple-element.8), channel_id=1, source_target_pairs={{0,2},{2,4},{4,6},{6,8},{8,10},{10,12},{12,14},{1,3},{3,5},{5,7},{... | collective-permute-start | bytes 196616 | tf_op jit(solution)/shard_map/ppermute | solution.py:23
  74.3 4.3 %collective-permute-done.9 = bf16[2,64,256]{2,1,0:T(8,128)(2,1)S(1)} collective-permute-done((bf16[2,64,256]{2,1,0:T(8,128)(2,1)S(1)}, bf16[2,64,256]{2,1,0:T(8,128)(2,1)S(1)}, u32[]{:S(2)}, u32[]{:S(2)}) %collective-permute-start.9) | collective-permute-done | bytes 65568 | tf_op jit(solution)/shard_map/ppermute | solution.py:23
  81.4 3.0 %collective-permute-start.10 = (bf16[4,64,256]{2,1,0:T(8,128)(2,1)S(1)}, bf16[4,64,256]{2,1,0:T(8,128)(2,1)S(1)}, u32[]{:S(2)}, u32[]{:S(2)}) collective-permute-start(bf16[4,64,256]{2,1,0:T(8,128)(2,1)S(1)} %fusion.14), channel_id=1, source_target_pairs={{0,2},{2,4},{4,6},{6,8},{8,10},{10,12},{12,14},{1,3},{3,5},{5,7},{... | collective-permute-start | bytes 393224 | tf_op jit(solution)/shard_map/ppermute | solution.py:23
  87.5 4.4 %collective-permute-done.11 = bf16[4,64,256]{2,1,0:T(8,128)(2,1)S(1)} collective-permute-done((bf16[4,64,256]{2,1,0:T(8,128)(2,1)S(1)}, bf16[4,64,256]{2,1,0:T(8,128)(2,1)S(1)}, u32[]{:S(2)}, u32[]{:S(2)}) %collective-permute-start.11) | collective-permute-done | bytes 131104 | tf_op jit(solution)/shard_map/ppermute | solution.py:23
  94.6 4.3 %collective-permute-start.12 = (bf16[4,64,256]{2,1,0:T(8,128)(2,1)S(1)}, bf16[4,64,256]{2,1,0:T(8,128)(2,1)S(1)}, u32[]{:S(2)}, u32[]{:S(2)}) collective-permute-start(bf16[4,64,256]{2,1,0:T(8,128)(2,1)S(1)} %fusion.15), channel_id=1, source_target_pairs={{0,4},{2,6},{4,8},{6,10},{8,12},{10,14},{1,5},{3,7},{5,9},{7,11},{... | collective-permute-start | bytes 393224 | tf_op jit(solution)/shard_map/ppermute | solution.py:23
  101.9 4.2 %collective-permute-done.13 = bf16[4,64,256]{2,1,0:T(8,128)(2,1)S(1)} collective-permute-done((bf16[4,64,256]{2,1,0:T(8,128)(2,1)S(1)}, bf16[4,64,256]{2,1,0:T(8,128)(2,1)S(1)}, u32[]{:S(2)}, u32[]{:S(2)}) %collective-permute-start.13) | collective-permute-done | bytes 131104 | tf_op jit(solution)/shard_map/ppermute | solution.py:23
  108.9 3.5 %collective-permute-start.14 = (bf16[4,64,256]{2,1,0:T(8,128)(2,1)S(1)}, bf16[4,64,256]{2,1,0:T(8,128)(2,1)S(1)}, u32[]{:S(2)}, u32[]{:S(2)}) collective-permute-start(bf16[4,64,256]{2,1,0:T(8,128)(2,1)S(1)} %fusion.16), channel_id=1, source_target_pairs={{0,8},{2,10},{4,12},{6,14},{1,9},{3,11},{5,13},{7,15},{16,24},{18,... | collective-permute-start | bytes 393224 | tf_op jit(solution)/shard_map/ppermute | solution.py:23
  115.5 7.2 %collective-permute-done.15 = bf16[4,64,256]{2,1,0:T(8,128)(2,1)S(1)} collective-permute-done((bf16[4,64,256]{2,1,0:T(8,128)(2,1)S(1)}, bf16[4,64,256]{2,1,0:T(8,128)(2,1)S(1)}, u32[]{:S(2)}, u32[]{:S(2)}) %collective-permute-start.15) | collective-permute-done | bytes 131104 | tf_op jit(solution)/shard_map/ppermute | solution.py:23
  133.3 4.1 %collective-permute-done.17 = bf16[4,64,256]{2,1,0:T(8,128)(2,1)S(1)} collective-permute-done((bf16[4,64,256]{2,1,0:T(8,128)(2,1)S(1)}, bf16[4,64,256]{2,1,0:T(8,128)(2,1)S(1)}, u32[]{:S(2)}, u32[]{:S(2)}) %collective-permute-start.17) | collective-permute-done | bytes 131104 | tf_op jit(solution)/shard_map/ppermute | solution.py:15
  141.8 3.0 %convolution_bitcast_fusion = f32[4,64,256]{2,1,0:T(8,128)S(1)} fusion(bf16[4,4,64,512]{3,2,1,0:T(8,128)(2,1)S(1)} %bitcast.92, bf16[4,4,512,256]{3,2,1,0:T(8,128)(2,1)} %bitcast.91), kind=kOutput, calls=%fused_computation.18 | convolution fusion | flops 268435456 | bytes 5505024 | tf_op jit(solution)/shard_map/sfkb,sfbc->skc/dot_general | solution.py:89
  149.4 4.4 %collective-permute-done.19 = f32[128,256]{1,0:T(8,128)S(1)} collective-permute-done((f32[128,256]{1,0:T(8,128)S(1)}, f32[128,256]{1,0:T(8,128)S(1)}, u32[]{:S(2)}, u32[]{:S(2)}) %collective-permute-start.19) | collective-permute-done | bytes 131104 | tf_op jit(solution)/shard_map/ppermute | solution.py:66
  154.8 4.1 %collective-permute-done.20 = f32[128,256]{1,0:T(8,128)S(1)} collective-permute-done((f32[128,256]{1,0:T(8,128)S(1)}, f32[128,256]{1,0:T(8,128)S(1)}, u32[]{:S(2)}, u32[]{:S(2)}) %collective-permute-start.20) | collective-permute-done | bytes 131104 | tf_op jit(solution)/shard_map/ppermute | solution.py:66
  161.9 4.3 %collective-permute-done.21 = f32[128,256]{1,0:T(8,128)S(1)} collective-permute-done((f32[128,256]{1,0:T(8,128)S(1)}, f32[128,256]{1,0:T(8,128)S(1)}, u32[]{:S(2)}, u32[]{:S(2)}) %collective-permute-start.21) | collective-permute-done | bytes 131104 | tf_op jit(solution)/shard_map/ppermute | solution.py:66
  (103 shorter events, 68.8 us)
Async XLA Ops:
  0.6 126.8 %copy-start = (bf16[4,512,256]{2,1,0:T(8,128)(2,1)S(1)}, bf16[4,512,256]{2,1,0:T(8,128)(2,1)}, u32[]{:S(2)}) copy-start(bf16[4,512,256]{2,1,0:T(8,128)(2,1)} %param.17) | copy-start | bytes 3145732
  0.6 24.3 %collective-permute-start = (bf16[4,64,256]{2,1,0:T(8,128)(2,1)}, bf16[4,64,256]{2,1,0:T(8,128)(2,1)S(1)}, u32[]{:S(2)}, u32[]{:S(2)}) collective-permute-start(bf16[4,64,256]{2,1,0:T(8,128)(2,1)} %param.10), channel_id=1, source_target_pairs={{0,2},{2,4},{4,6},{6,8},{8,10},{10,12},{12,14},{1,3},{3,5},{5,7},{... | collective-permute-start | bytes 393224 | tf_op jit(solution)/shard_map/ppermute | solution.py:14
  5.6 19.3 %collective-permute-start.1 = (bf16[4,64,256]{2,1,0:T(8,128)(2,1)}, bf16[4,64,256]{2,1,0:T(8,128)(2,1)S(1)}, u32[]{:S(2)}, u32[]{:S(2)}) collective-permute-start(bf16[4,64,256]{2,1,0:T(8,128)(2,1)} %param.10), channel_id=1, source_target_pairs={{2,0},{4,2},{6,4},{8,6},{10,8},{12,10},{14,12},{3,1},{5,3},{7,5},{... | collective-permute-start | bytes 393224 | tf_op jit(solution)/shard_map/ppermute | solution.py:15
  31.5 49.6 %slice-start.2 = ((s8[6291456]{0:T(1024)(128)(4,1)}), s8[4194304]{0:T(1024)(128)(4,1)S(1)}, s32[]{:S(2)}) async-start(s8[6291456]{0:T(1024)(128)(4,1)} %bitcast.96), calls=%async_computation.2 | async-start | bytes 8388608
  37.3 1.3 collective-permute-start.2
  38.6 4.5 %collective-permute-start.3 = (f32[64,64]{0,1:T(8,128)S(1)}, f32[64,64]{0,1:T(8,128)S(1)}, u32[]{:S(2)}, u32[]{:S(2)}) collective-permute-start(f32[64,64]{0,1:T(8,128)S(1)} %add.101), channel_id=1, source_target_pairs={{0,2},{2,0},{4,6},{6,4},{8,10},{10,8},{12,14},{14,12},{1,3},{3,1},... | collective-permute-start | bytes 49160 | tf_op jit(solution)/shard_map/ppermute | solution.py:66
  43.1 4.9 %collective-permute-start.4 = (f32[64,64]{0,1:T(8,128)S(1)}, f32[64,64]{0,1:T(8,128)S(1)}, u32[]{:S(2)}, u32[]{:S(2)}) collective-permute-start(f32[64,64]{0,1:T(8,128)S(1)} %add.102), channel_id=1, source_target_pairs={{0,4},{2,6},{4,0},{6,2},{8,12},{10,14},{12,8},{14,10},{1,5},{3,7},... | collective-permute-start | bytes 49160 | tf_op jit(solution)/shard_map/ppermute | solution.py:66
  48.0 4.9 %collective-permute-start.5 = (f32[64,64]{0,1:T(8,128)S(1)}, f32[64,64]{0,1:T(8,128)S(1)}, u32[]{:S(2)}, u32[]{:S(2)}) collective-permute-start(f32[64,64]{0,1:T(8,128)S(1)} %add.103), channel_id=1, source_target_pairs={{0,8},{2,10},{4,12},{6,14},{8,0},{10,2},{12,4},{14,6},{1,9},{3,11}... | collective-permute-start | bytes 49160 | tf_op jit(solution)/shard_map/ppermute | solution.py:66
  53.2 4.6 %collective-permute-start.6 = (bf16[1,64,256]{2,1,0:T(8,128)(2,1)S(1)}, bf16[1,64,256]{2,1,0:T(8,128)(2,1)S(1)}, u32[]{:S(2)}, u32[]{:S(2)}) collective-permute-start(bf16[1,64,256]{2,1,0:T(8,128)(2,1)S(1)} %get-tuple-element.10), channel_id=1, source_target_pairs={{0,2},{2,4},{4,6},{6,8},{8,10},{10,12},{12,14},{1,3},{3,5},{5,7},{... | collective-permute-start | bytes 98312 | tf_op jit(solution)/shard_map/ppermute | solution.py:23
  56.2 6.2 %collective-permute-start.7 = (bf16[1,64,256]{2,1,0:T(8,128)(2,1)S(1)}, bf16[1,64,256]{2,1,0:T(8,128)(2,1)S(1)}, u32[]{:S(2)}, u32[]{:S(2)}) collective-permute-start(bf16[1,64,256]{2,1,0:T(8,128)(2,1)S(1)} %get-tuple-element.11), channel_id=1, source_target_pairs={{2,0},{4,2},{6,4},{8,6},{10,8},{12,10},{14,12},{3,1},{5,3},{7,5},{... | collective-permute-start | bytes 98312 | tf_op jit(solution)/shard_map/ppermute | solution.py:23
  67.6 6.7 %collective-permute-start.8 = (bf16[2,64,256]{2,1,0:T(8,128)(2,1)S(1)}, bf16[2,64,256]{2,1,0:T(8,128)(2,1)S(1)}, u32[]{:S(2)}, u32[]{:S(2)}) collective-permute-start(bf16[2,64,256]{2,1,0:T(8,128)(2,1)S(1)} %get-tuple-element.8), channel_id=1, source_target_pairs={{0,2},{2,4},{4,6},{6,8},{8,10},{10,12},{12,14},{1,3},{3,5},{5,7},{... | collective-permute-start | bytes 196616 | tf_op jit(solution)/shard_map/ppermute | solution.py:23
  72.4 6.2 %collective-permute-start.9 = (bf16[2,64,256]{2,1,0:T(8,128)(2,1)S(1)}, bf16[2,64,256]{2,1,0:T(8,128)(2,1)S(1)}, u32[]{:S(2)}, u32[]{:S(2)}) collective-permute-start(bf16[2,64,256]{2,1,0:T(8,128)(2,1)S(1)} %get-tuple-element.9), channel_id=1, source_target_pairs={{2,0},{4,2},{6,4},{8,6},{10,8},{12,10},{14,12},{3,1},{5,3},{7,5},{... | collective-permute-start | bytes 196616 | tf_op jit(solution)/shard_map/ppermute | solution.py:23
  81.4 6.0 %collective-permute-start.10 = (bf16[4,64,256]{2,1,0:T(8,128)(2,1)S(1)}, bf16[4,64,256]{2,1,0:T(8,128)(2,1)S(1)}, u32[]{:S(2)}, u32[]{:S(2)}) collective-permute-start(bf16[4,64,256]{2,1,0:T(8,128)(2,1)S(1)} %fusion.14), channel_id=1, source_target_pairs={{0,2},{2,4},{4,6},{6,8},{8,10},{10,12},{12,14},{1,3},{3,5},{5,7},{... | collective-permute-start | bytes 393224 | tf_op jit(solution)/shard_map/ppermute | solution.py:23
  84.4 7.4 %collective-permute-start.11 = (bf16[4,64,256]{2,1,0:T(8,128)(2,1)S(1)}, bf16[4,64,256]{2,1,0:T(8,128)(2,1)S(1)}, u32[]{:S(2)}, u32[]{:S(2)}) collective-permute-start(bf16[4,64,256]{2,1,0:T(8,128)(2,1)S(1)} %fusion.14), channel_id=1, source_target_pairs={{2,0},{4,2},{6,4},{8,6},{10,8},{12,10},{14,12},{3,1},{5,3},{7,5},{... | collective-permute-start | bytes 393224 | tf_op jit(solution)/shard_map/ppermute | solution.py:23
  94.6 7.3 %collective-permute-start.12 = (bf16[4,64,256]{2,1,0:T(8,128)(2,1)S(1)}, bf16[4,64,256]{2,1,0:T(8,128)(2,1)S(1)}, u32[]{:S(2)}, u32[]{:S(2)}) collective-permute-start(bf16[4,64,256]{2,1,0:T(8,128)(2,1)S(1)} %fusion.15), channel_id=1, source_target_pairs={{0,4},{2,6},{4,8},{6,10},{8,12},{10,14},{1,5},{3,7},{5,9},{7,11},{... | collective-permute-start | bytes 393224 | tf_op jit(solution)/shard_map/ppermute | solution.py:23
  98.9 7.2 %collective-permute-start.13 = (bf16[4,64,256]{2,1,0:T(8,128)(2,1)S(1)}, bf16[4,64,256]{2,1,0:T(8,128)(2,1)S(1)}, u32[]{:S(2)}, u32[]{:S(2)}) collective-permute-start(bf16[4,64,256]{2,1,0:T(8,128)(2,1)S(1)} %fusion.15), channel_id=1, source_target_pairs={{4,0},{6,2},{8,4},{10,6},{12,8},{14,10},{5,1},{7,3},{9,5},{11,7},{... | collective-permute-start | bytes 393224 | tf_op jit(solution)/shard_map/ppermute | solution.py:23
  108.9 6.6 %collective-permute-start.14 = (bf16[4,64,256]{2,1,0:T(8,128)(2,1)S(1)}, bf16[4,64,256]{2,1,0:T(8,128)(2,1)S(1)}, u32[]{:S(2)}, u32[]{:S(2)}) collective-permute-start(bf16[4,64,256]{2,1,0:T(8,128)(2,1)S(1)} %fusion.16), channel_id=1, source_target_pairs={{0,8},{2,10},{4,12},{6,14},{1,9},{3,11},{5,13},{7,15},{16,24},{18,... | collective-permute-start | bytes 393224 | tf_op jit(solution)/shard_map/ppermute | solution.py:23
  112.4 10.2 %collective-permute-start.15 = (bf16[4,64,256]{2,1,0:T(8,128)(2,1)S(1)}, bf16[4,64,256]{2,1,0:T(8,128)(2,1)S(1)}, u32[]{:S(2)}, u32[]{:S(2)}) collective-permute-start(bf16[4,64,256]{2,1,0:T(8,128)(2,1)S(1)} %fusion.16), channel_id=1, source_target_pairs={{8,0},{10,2},{12,4},{14,6},{9,1},{11,3},{13,5},{15,7},{24,16},{26,... | collective-permute-start | bytes 393224 | tf_op jit(solution)/shard_map/ppermute | solution.py:23
  127.8 5.5 %collective-permute-start.16 = (bf16[4,64,256]{2,1,0:T(8,128)(2,1)S(1)}, bf16[4,64,256]{2,1,0:T(8,128)(2,1)S(1)}, u32[]{:S(2)}, u32[]{:S(2)}) collective-permute-start(bf16[4,64,256]{2,1,0:T(8,128)(2,1)S(1)} %convolution_convert_fusion), channel_id=1, source_target_pairs={{0,2},{2,4},{4,6},{6,8},{8,10},{10,12},{12,14},{1,3},{3,5},{5,7},{... | collective-permute-start | bytes 393224 | tf_op jit(solution)/shard_map/ppermute | solution.py:14
  130.3 7.2 %collective-permute-start.17 = (bf16[4,64,256]{2,1,0:T(8,128)(2,1)S(1)}, bf16[4,64,256]{2,1,0:T(8,128)(2,1)S(1)}, u32[]{:S(2)}, u32[]{:S(2)}) collective-permute-start(bf16[4,64,256]{2,1,0:T(8,128)(2,1)S(1)} %convolution_convert_fusion), channel_id=1, source_target_pairs={{2,0},{4,2},{6,4},{8,6},{10,8},{12,10},{14,12},{3,1},{5,3},{7,5},{... | collective-permute-start | bytes 393224 | tf_op jit(solution)/shard_map/ppermute | solution.py:15
  146.7 1.4 collective-permute-start.18
  148.2 5.6 %collective-permute-start.19 = (f32[128,256]{1,0:T(8,128)S(1)}, f32[128,256]{1,0:T(8,128)S(1)}, u32[]{:S(2)}, u32[]{:S(2)}) collective-permute-start(f32[128,256]{1,0:T(8,128)S(1)} %add.113), channel_id=1, source_target_pairs={{0,2},{2,0},{4,6},{6,4},{8,10},{10,8},{12,14},{14,12},{1,3},{3,1},... | collective-permute-start | bytes 393224 | tf_op jit(solution)/shard_map/ppermute | solution.py:66
  153.8 5.0 %collective-permute-start.20 = (f32[128,256]{1,0:T(8,128)S(1)}, f32[128,256]{1,0:T(8,128)S(1)}, u32[]{:S(2)}, u32[]{:S(2)}) collective-permute-start(f32[128,256]{1,0:T(8,128)S(1)} %add.114), channel_id=1, source_target_pairs={{0,4},{2,6},{4,0},{6,2},{8,12},{10,14},{12,8},{14,10},{1,5},{3,7},... | collective-permute-start | bytes 393224 | tf_op jit(solution)/shard_map/ppermute | solution.py:66
  158.9 7.3 %collective-permute-start.21 = (f32[128,256]{1,0:T(8,128)S(1)}, f32[128,256]{1,0:T(8,128)S(1)}, u32[]{:S(2)}, u32[]{:S(2)}) collective-permute-start(f32[128,256]{1,0:T(8,128)S(1)} %add.115), channel_id=1, source_target_pairs={{0,8},{2,10},{4,12},{6,14},{8,0},{10,2},{12,4},{14,6},{1,9},{3,11}... | collective-permute-start | bytes 393224 | tf_op jit(solution)/shard_map/ppermute | solution.py:66
  (7 other events, 204.5 us)

commit v2 on v1

--- a/solution.py
+++ b/solution.py
@@ -56,16 +56,21 @@
     return rows[:slab_count], rows[2 * stride :]
 
 
+def exchanged(chunks):
+    return lax.all_to_all(chunks, ("slab", "vec"), split_axis=0, concat_axis=0, tiled=True)
+
+
+def total_at_once(part):
+    count = lax.axis_size("slab") * lax.axis_size("vec")
+    rows, cols = part.shape
+    return exchanged(jnp.tile(part, (count, 1))).reshape(count, rows, cols).sum(0)
+
+
 def total(part):
-    slabs = lax.axis_size("slab")
-    if slabs & (slabs - 1):
-        return lax.psum(part, ("slab", "vec"))
-    part = part + lax.ppermute(part, "vec", [(0, 1), (1, 0)])
-    reach = 1
-    while reach < slabs:
-        part = part + lax.ppermute(part, "slab", [(i, i ^ reach) for i in range(slabs)])
-        reach *= 2
-    return part
+    count = lax.axis_size("slab") * lax.axis_size("vec")
+    rows, cols = part.shape
+    share = exchanged(part.reshape(count, -1, 128)).sum(0, keepdims=True)
+    return exchanged(jnp.tile(share, (count, 1, 1))).reshape(rows, cols)
 
 
 def apply_operator(half_rows, blocks, slab_blocks, far_source, far_block):
@@ -109,7 +114,7 @@
     highest = lax.Precision.HIGHEST
     image = apply_operator(vectors, blocks, slab_blocks, far_source, far_block)
     quotient_part = jnp.einsum("skb,sjb->kj", vectors, image, preferred_element_type=jnp.float32)
-    quotient = total(quotient_part) / rows_total
+    quotient = total_at_once(quotient_part) / rows_total
     residual = (
         image.astype(jnp.float32)
         - jnp.einsum("kj,skb->sjb", quotient, vectors.astype(jnp.float32), precision=highest)

time: 168 us -> 177 us (1.054)
  blocking collectives: 17.5 us -> 45 us
  waiting for transfers between devices: 57.4 us -> 42.3 us
  starting transfers between devices: 47.4 us -> 35.6 us
  matrix products: 20.3 us -> 26.1 us
  local copies, waits for them, and re-layouts: 18.4 us -> 20.2 us
    all_to_all x0 -> x2, blocking collectives: none -> 27.4 us  [exchanged(): lax.all_to_all(chunks, ('slab', 'vec'), split_axis=0, concat_axis=0, tile...]
    ppermute x8 -> x0, waiting for transfers between devices: 20.7 us -> none  [the longest x6 18.5 us: total(): lax.ppermute(part, 'slab', [(i, i ^ reach) for i in range(slabs)])]
    ppermute x8 -> x0, starting transfers between devices: 12.4 us -> none  [the longest x6 12 us: total(): lax.ppermute(part, 'slab', [(i, i ^ reach) for i in range(slabs)])]
    all_to_all x0 -> x1, waiting for transfers between devices: none -> 6 us  [exchanged(): lax.all_to_all(chunks, ('slab', 'vec'), split_axis=0, concat_axis=0, tile...]
    dot_general x5, matrix products: 2.65 us -> 7.69 us  [on_device(): jnp.einsum('skb,sbc->skc', from_above, level_upper[level_index], preferre...]
    all_to_all x0 -> x1, starting transfers between devices: none -> 3.51 us  [exchanged(): lax.all_to_all(chunks, ('slab', 'vec'), split_axis=0, concat_axis=0, tile...]
    ppermute x10, starting transfers between devices: 25 us -> 22 us  [from_behind(): return lax.ppermute(block, axis, route)]
  transfers between devices with their start and end apart: 22 -> 15, of which waited for: 20 -> 13; matrix products, arithmetic and copies ran while one was open for 11% -> 11% of each run, Pallas kernels for 0% -> 0%
where the time goes in v2:
time: 177 us; the launch traced here: 176 us
  blocking collectives  45 us (25%)
  waiting for transfers between devices  42.3 us (24%)
  starting transfers between devices  35.6 us (20%)
  matrix products  26.1 us (15%)
  local copies, waits for them, and re-layouts  20.2 us (11%)
  other arithmetic  4.63 us (3%)
  between operations  2.48 us (1%)
    ppermute x10, waiting for transfers between devices, from_behind(): return lax.ppermute(block, axis, route)  30.4 us
    all_to_all x2, blocking collectives, exchanged(): lax.all_to_all(chunks, ('slab', 'vec'), split_axis=0, concat_axis=0, tile...  27.4 us
    ppermute x10, starting transfers between devices, from_behind(): return lax.ppermute(block, axis, route)  22 us
    all_gather x8, blocking collectives, orbitals(): return lax.all_gather(operand, 'vec', axis=2, tiled=True)  17.5 us
    dot_general x5, matrix products, on_device(): jnp.einsum('skb,sbc->skc', from_above, level_upper[level_index], preferre...  7.69 us
    ppermute x2, starting transfers between devices, padded(): before = lax.ppermute(last, axis, up)  7.48 us
    dot_general x2, matrix products, apply_operator(): jnp.einsum('sfkb,sfbc->skc', fetched, blocks[far_block], preferred_elemen...  6.37 us
    all_to_all x1, waiting for transfers between devices, exchanged(): lax.all_to_all(chunks, ('slab', 'vec'), split_axis=0, concat_axis=0, tile...  6 us
  transfers between devices with their start and end apart: 15, of which 13 were waited for; matrix products, arithmetic and copies ran while one was open for 11% of the time, Pallas kernels for 0%

profile of v2, /device:TPU:0, one launch (start us, length us, event | category | flops | bytes accessed | tf_op | source)
XLA Modules:
  0.0 176.2 jit_solution(15103088293837549438)
XLA Ops:
  0.6 5.0 %collective-permute-start = (bf16[4,64,256]{2,1,0:T(8,128)(2,1)}, bf16[4,64,256]{2,1,0:T(8,128)(2,1)S(1)}, u32[]{:S(2)}, u32[]{:S(2)}) collective-permute-start(bf16[4,64,256]{2,1,0:T(8,128)(2,1)} %param.10), channel_id=1, source_target_pairs={{0,2},{2,4},{4,6},{6,8},{8,10},{10,12},{12,14},{1,3},{3,5},{5,7},{... | collective-permute-start | bytes 393224 | tf_op jit(solution)/shard_map/ppermute | solution.py:14
  9.4 2.8 %gather_fusion.1 = bf16[4,512,256]{2,1,0:T(8,128)(2,1)S(1)} fusion(bf16[16,512,256]{2,1,0:T(8,128)(2,1)} %param.11, s32[1024]{0:T(1024)S(1)} %get-tuple-element.13), kind=kCustom, calls=%fused_computation.1 | custom fusion | bytes 2097168 | tf_op jit(solution)/shard_map/gather | solution.py:86
  12.3 3.8 %gather_fusion.2 = bf16[4,512,256]{2,1,0:T(8,128)(2,1)} fusion(bf16[16,512,256]{2,1,0:T(8,128)(2,1)} %param.11, s32[1024]{0:T(1024)S(1)} %get-tuple-element.12), kind=kCustom, calls=%fused_computation.2 | custom fusion | bytes 2097168 | tf_op jit(solution)/shard_map/gather | solution.py:89
  16.2 5.0 %gather_fusion.4 = bf16[16,512,256]{2,1,0:T(8,128)(2,1)} fusion(bf16[16,512,256]{2,1,0:T(8,128)(2,1)} %param.11, s32[1024]{0:T(1024)S(1)} %pad_clamp_fusion), kind=kCustom, calls=%fused_computation.4 | custom fusion | bytes 8388672 | tf_op jit(solution)/shard_map/gather | solution.py:95
  21.1 3.8 %gather_fusion = bf16[4,512,256]{2,1,0:T(8,128)(2,1)} fusion(bf16[16,512,256]{2,1,0:T(8,128)(2,1)} %param.11, s32[1024]{0:T(1024)S(1)} %pad_clamp_fusion.4), kind=kCustom, calls=%fused_computation | custom fusion | bytes 2097168 | tf_op jit(solution)/shard_map/gather | solution.py:83
  25.0 2.4 %all_gather.24 = bf16[12,64,512]{2,1,0:T(8,128)(2,1)S(1)} all-gather(bf16[12,64,256]{2,1,0:T(8,128)(2,1)S(1)} %pad_maximum_fusion), channel_id=1, replica_groups=mesh['groups'=2,'slab'=8,'vec'=2] {'vec'}, dimensions={2}, use_global_device_ids=true | all-gather | bytes 1179648 | tf_op jit(solution)/shard_map/all_gather | solution.py:27
  31.4 3.3 %convolution_bitcast_fusion.1 = f32[4,64,256]{2,1,0:T(8,128)S(1)} fusion(bf16[4,4,64,512]{3,2,1,0:T(8,128)(2,1)} %bitcast.93, bf16[4,4,512,256]{3,2,1,0:T(8,128)(2,1)} %bitcast.90), kind=kOutput, calls=%fused_computation.19 | convolution fusion | flops 268435456 | bytes 5505024 | tf_op jit(solution)/shard_map/sfkb,sfbc->skc/dot_general | solution.py:94
  36.9 16.9 %all_to_all.16 = f32[16,1,4096]{2,1,0:T(1,128)S(1)} all-to-all(f32[16,1,4096]{2,1,0:T(1,128)S(1)} %reshape.90), channel_id=1, replica_groups=mesh['groups'=2,'slab'=8,'vec'=2] {'slab','vec'}, dimensions={0} | all-to-all | bytes 524288 | tf_op jit(solution)/shard_map/all_to_all | solution.py:60
  59.2 4.4 %collective-permute-done.3 = bf16[1,64,256]{2,1,0:T(8,128)(2,1)S(1)} collective-permute-done((bf16[1,64,256]{2,1,0:T(8,128)(2,1)S(1)}, bf16[1,64,256]{2,1,0:T(8,128)(2,1)S(1)}, u32[]{:S(2)}, u32[]{:S(2)}) %collective-permute-start.3) | collective-permute-done | bytes 32800 | tf_op jit(solution)/shard_map/ppermute | solution.py:23
  68.9 4.7 %collective-permute-start.4 = (bf16[2,64,256]{2,1,0:T(8,128)(2,1)S(1)}, bf16[2,64,256]{2,1,0:T(8,128)(2,1)S(1)}, u32[]{:S(2)}, u32[]{:S(2)}) collective-permute-start(bf16[2,64,256]{2,1,0:T(8,128)(2,1)S(1)} %get-tuple-element.8), channel_id=1, source_target_pairs={{0,2},{2,4},{4,6},{6,8},{8,10},{10,12},{12,14},{1,3},{3,5},{5,7},{... | collective-permute-start | bytes 196616 | tf_op jit(solution)/shard_map/ppermute | solution.py:23
  75.5 4.3 %collective-permute-done.5 = bf16[2,64,256]{2,1,0:T(8,128)(2,1)S(1)} collective-permute-done((bf16[2,64,256]{2,1,0:T(8,128)(2,1)S(1)}, bf16[2,64,256]{2,1,0:T(8,128)(2,1)S(1)}, u32[]{:S(2)}, u32[]{:S(2)}) %collective-permute-start.5) | collective-permute-done | bytes 65568 | tf_op jit(solution)/shard_map/ppermute | solution.py:23
  85.2 3.0 %collective-permute-start.6 = (bf16[4,64,256]{2,1,0:T(8,128)(2,1)S(1)}, bf16[4,64,256]{2,1,0:T(8,128)(2,1)S(1)}, u32[]{:S(2)}, u32[]{:S(2)}) collective-permute-start(bf16[4,64,256]{2,1,0:T(8,128)(2,1)S(1)} %fusion.14), channel_id=1, source_target_pairs={{0,2},{2,4},{4,6},{6,8},{8,10},{10,12},{12,14},{1,3},{3,5},{5,7},{... | collective-permute-start | bytes 393224 | tf_op jit(solution)/shard_map/ppermute | solution.py:23
  91.2 4.3 %collective-permute-done.7 = bf16[4,64,256]{2,1,0:T(8,128)(2,1)S(1)} collective-permute-done((bf16[4,64,256]{2,1,0:T(8,128)(2,1)S(1)}, bf16[4,64,256]{2,1,0:T(8,128)(2,1)S(1)}, u32[]{:S(2)}, u32[]{:S(2)}) %collective-permute-start.7) | collective-permute-done | bytes 131104 | tf_op jit(solution)/shard_map/ppermute | solution.py:23
  99.6 4.3 %collective-permute-start.8 = (bf16[4,64,256]{2,1,0:T(8,128)(2,1)S(1)}, bf16[4,64,256]{2,1,0:T(8,128)(2,1)S(1)}, u32[]{:S(2)}, u32[]{:S(2)}) collective-permute-start(bf16[4,64,256]{2,1,0:T(8,128)(2,1)S(1)} %fusion.15), channel_id=1, source_target_pairs={{0,4},{2,6},{4,8},{6,10},{8,12},{10,14},{1,5},{3,7},{5,9},{7,11},{... | collective-permute-start | bytes 393224 | tf_op jit(solution)/shard_map/ppermute | solution.py:23
  106.9 4.1 %collective-permute-done.9 = bf16[4,64,256]{2,1,0:T(8,128)(2,1)S(1)} collective-permute-done((bf16[4,64,256]{2,1,0:T(8,128)(2,1)S(1)}, bf16[4,64,256]{2,1,0:T(8,128)(2,1)S(1)}, u32[]{:S(2)}, u32[]{:S(2)}) %collective-permute-start.9) | collective-permute-done | bytes 131104 | tf_op jit(solution)/shard_map/ppermute | solution.py:23
  115.1 2.3 %collective-permute-start.10 = (bf16[4,64,256]{2,1,0:T(8,128)(2,1)S(1)}, bf16[4,64,256]{2,1,0:T(8,128)(2,1)S(1)}, u32[]{:S(2)}, u32[]{:S(2)}) collective-permute-start(bf16[4,64,256]{2,1,0:T(8,128)(2,1)S(1)} %fusion.16), channel_id=1, source_target_pairs={{0,8},{2,10},{4,12},{6,14},{1,9},{3,11},{5,13},{7,15},{16,24},{18,... | collective-permute-start | bytes 393224 | tf_op jit(solution)/shard_map/ppermute | solution.py:23
  120.4 7.2 %collective-permute-done.11 = bf16[4,64,256]{2,1,0:T(8,128)(2,1)S(1)} collective-permute-done((bf16[4,64,256]{2,1,0:T(8,128)(2,1)S(1)}, bf16[4,64,256]{2,1,0:T(8,128)(2,1)S(1)}, u32[]{:S(2)}, u32[]{:S(2)}) %collective-permute-start.11) | collective-permute-done | bytes 131104 | tf_op jit(solution)/shard_map/ppermute | solution.py:23
  133.9 2.5 %collective-permute-start.12 = (bf16[4,64,256]{2,1,0:T(8,128)(2,1)S(1)}, bf16[4,64,256]{2,1,0:T(8,128)(2,1)S(1)}, u32[]{:S(2)}, u32[]{:S(2)}) collective-permute-start(bf16[4,64,256]{2,1,0:T(8,128)(2,1)S(1)} %convolution_convert_fusion), channel_id=1, source_target_pairs={{0,2},{2,4},{4,6},{6,8},{8,10},{10,12},{12,14},{1,3},{3,5},{5,7},{... | collective-permute-start | bytes 393224 | tf_op jit(solution)/shard_map/ppermute | solution.py:14
  139.5 4.1 %collective-permute-done.13 = bf16[4,64,256]{2,1,0:T(8,128)(2,1)S(1)} collective-permute-done((bf16[4,64,256]{2,1,0:T(8,128)(2,1)S(1)}, bf16[4,64,256]{2,1,0:T(8,128)(2,1)S(1)}, u32[]{:S(2)}, u32[]{:S(2)}) %collective-permute-start.13) | collective-permute-done | bytes 131104 | tf_op jit(solution)/shard_map/ppermute | solution.py:15
  143.6 2.4 %all_gather.31 = bf16[12,64,512]{2,1,0:T(8,128)(2,1)S(1)} all-gather(bf16[12,64,256]{2,1,0:T(8,128)(2,1)S(1)} %pad_maximum_fusion.1), channel_id=1, replica_groups=mesh['groups'=2,'slab'=8,'vec'=2] {'vec'}, dimensions={2}, use_global_device_ids=true | all-gather | bytes 1179648 | tf_op jit(solution)/shard_map/all_gather | solution.py:27
  147.9 3.0 %convolution_bitcast_fusion = f32[4,64,256]{2,1,0:T(8,128)S(1)} fusion(bf16[4,4,64,512]{3,2,1,0:T(8,128)(2,1)S(1)} %bitcast.92, bf16[4,4,512,256]{3,2,1,0:T(8,128)(2,1)} %bitcast.91), kind=kOutput, calls=%fused_computation.18 | convolution fusion | flops 268435456 | bytes 5505024 | tf_op jit(solution)/shard_map/sfkb,sfbc->skc/dot_general | solution.py:94
  152.9 10.5 %all_to_all.17 = f32[16,16,128]{2,1,0:T(8,128)S(1)} all-to-all(f32[16,16,128]{2,1,0:T(8,128)S(1)} %reshape.26), channel_id=1, replica_groups=mesh['groups'=2,'slab'=8,'vec'=2] {'slab','vec'}, dimensions={0} | all-to-all | bytes 262144 | tf_op jit(solution)/shard_map/all_to_all | solution.py:60
  164.1 3.5 %all-to-all-start.2 = ((f32[16,16,128]{2,1,0:T(8,128)}), f32[16,16,128]{2,1,0:T(8,128)S(1)}, u32[]{:S(2)}, u32[]{:S(2)}) async-start(f32[16,16,128]{2,1,0:T(8,128)} %tile.5), calls=%async_computation.2 | async-start | bytes 262144 | tf_op jit(solution)/shard_map/all_to_all | solution.py:60
  169.5 6.0 %all-to-all-done.2 = f32[16,16,128]{2,1,0:T(8,128)S(1)} async-done(((f32[16,16,128]{2,1,0:T(8,128)}), f32[16,16,128]{2,1,0:T(8,128)S(1)}, u32[]{:S(2)}, u32[]{:S(2)}) %all-to-all-start.2) | async-done | bytes 131104 | tf_op jit(solution)/shard_map/all_to_all | solution.py:60
  (89 shorter events, 60.2 us)
Async XLA Ops:
  0.6 133.0 %copy-start = (bf16[4,512,256]{2,1,0:T(8,128)(2,1)S(1)}, bf16[4,512,256]{2,1,0:T(8,128)(2,1)}, u32[]{:S(2)}) copy-start(bf16[4,512,256]{2,1,0:T(8,128)(2,1)} %param.17) | copy-start | bytes 3145732
  0.6 24.3 %collective-permute-start = (bf16[4,64,256]{2,1,0:T(8,128)(2,1)}, bf16[4,64,256]{2,1,0:T(8,128)(2,1)S(1)}, u32[]{:S(2)}, u32[]{:S(2)}) collective-permute-start(bf16[4,64,256]{2,1,0:T(8,128)(2,1)} %param.10), channel_id=1, source_target_pairs={{0,2},{2,4},{4,6},{6,8},{8,10},{10,12},{12,14},{1,3},{3,5},{5,7},{... | collective-permute-start | bytes 393224 | tf_op jit(solution)/shard_map/ppermute | solution.py:14
  5.6 19.3 %collective-permute-start.1 = (bf16[4,64,256]{2,1,0:T(8,128)(2,1)}, bf16[4,64,256]{2,1,0:T(8,128)(2,1)S(1)}, u32[]{:S(2)}, u32[]{:S(2)}) collective-permute-start(bf16[4,64,256]{2,1,0:T(8,128)(2,1)} %param.10), channel_id=1, source_target_pairs={{2,0},{4,2},{6,4},{8,6},{10,8},{12,10},{14,12},{3,1},{5,3},{7,5},{... | collective-permute-start | bytes 393224 | tf_op jit(solution)/shard_map/ppermute | solution.py:15
  12.3 12.7 %copy-start.2 = (bf16[4,64,256]{2,1,0:T(8,128)(2,1)S(1)}, bf16[4,64,256]{2,1,0:T(8,128)(2,1)}, u32[]{:S(2)}) copy-start(bf16[4,64,256]{2,1,0:T(8,128)(2,1)} %param.10) | copy-start | bytes 393220
  56.2 3.0 %collective-permute-start.2 = (bf16[1,64,256]{2,1,0:T(8,128)(2,1)S(1)}, bf16[1,64,256]{2,1,0:T(8,128)(2,1)S(1)}, u32[]{:S(2)}, u32[]{:S(2)}) collective-permute-start(bf16[1,64,256]{2,1,0:T(8,128)(2,1)S(1)} %get-tuple-element.10), channel_id=1, source_target_pairs={{0,2},{2,4},{4,6},{6,8},{8,10},{10,12},{12,14},{1,3},{3,5},{5,7},{... | collective-permute-start | bytes 98312 | tf_op jit(solution)/shard_map/ppermute | solution.py:23
  57.6 6.0 %collective-permute-start.3 = (bf16[1,64,256]{2,1,0:T(8,128)(2,1)S(1)}, bf16[1,64,256]{2,1,0:T(8,128)(2,1)S(1)}, u32[]{:S(2)}, u32[]{:S(2)}) collective-permute-start(bf16[1,64,256]{2,1,0:T(8,128)(2,1)S(1)} %get-tuple-element.11), channel_id=1, source_target_pairs={{2,0},{4,2},{6,4},{8,6},{10,8},{12,10},{14,12},{3,1},{5,3},{7,5},{... | collective-permute-start | bytes 98312 | tf_op jit(solution)/shard_map/ppermute | solution.py:23
  67.2 32.1 %slice-start = ((s8[6291456]{0:T(1024)(128)(4,1)}), s8[4194304]{0:T(1024)(128)(4,1)S(1)}, s32[]{:S(2)}) async-start(s8[6291456]{0:T(1024)(128)(4,1)} %bitcast.94), calls=%async_computation.3 | async-start | bytes 8388608
  68.9 6.6 %collective-permute-start.4 = (bf16[2,64,256]{2,1,0:T(8,128)(2,1)S(1)}, bf16[2,64,256]{2,1,0:T(8,128)(2,1)S(1)}, u32[]{:S(2)}, u32[]{:S(2)}) collective-permute-start(bf16[2,64,256]{2,1,0:T(8,128)(2,1)S(1)} %get-tuple-element.8), channel_id=1, source_target_pairs={{0,2},{2,4},{4,6},{6,8},{8,10},{10,12},{12,14},{1,3},{3,5},{5,7},{... | collective-permute-start | bytes 196616 | tf_op jit(solution)/shard_map/ppermute | solution.py:23
  73.6 6.2 %collective-permute-start.5 = (bf16[2,64,256]{2,1,0:T(8,128)(2,1)S(1)}, bf16[2,64,256]{2,1,0:T(8,128)(2,1)S(1)}, u32[]{:S(2)}, u32[]{:S(2)}) collective-permute-start(bf16[2,64,256]{2,1,0:T(8,128)(2,1)S(1)} %get-tuple-element.9), channel_id=1, source_target_pairs={{2,0},{4,2},{6,4},{8,6},{10,8},{12,10},{14,12},{3,1},{5,3},{7,5},{... | collective-permute-start | bytes 196616 | tf_op jit(solution)/shard_map/ppermute | solution.py:23
  82.0 17.3 %slice-start.1 = ((s8[6291456]{0:T(1024)(128)(4,1)}), s8[2097152]{0:T(1024)(128)(4,1)S(1)}, s32[]{:S(2)}) async-start(s8[6291456]{0:T(1024)(128)(4,1)} %bitcast.94), calls=%async_computation.4 | async-start | bytes 4194304
  85.2 6.1 %collective-permute-start.6 = (bf16[4,64,256]{2,1,0:T(8,128)(2,1)S(1)}, bf16[4,64,256]{2,1,0:T(8,128)(2,1)S(1)}, u32[]{:S(2)}, u32[]{:S(2)}) collective-permute-start(bf16[4,64,256]{2,1,0:T(8,128)(2,1)S(1)} %fusion.14), channel_id=1, source_target_pairs={{0,2},{2,4},{4,6},{6,8},{8,10},{10,12},{12,14},{1,3},{3,5},{5,7},{... | collective-permute-start | bytes 393224 | tf_op jit(solution)/shard_map/ppermute | solution.py:23
  88.2 7.4 %collective-permute-start.7 = (bf16[4,64,256]{2,1,0:T(8,128)(2,1)S(1)}, bf16[4,64,256]{2,1,0:T(8,128)(2,1)S(1)}, u32[]{:S(2)}, u32[]{:S(2)}) collective-permute-start(bf16[4,64,256]{2,1,0:T(8,128)(2,1)S(1)} %fusion.14), channel_id=1, source_target_pairs={{2,0},{4,2},{6,4},{8,6},{10,8},{12,10},{14,12},{3,1},{5,3},{7,5},{... | collective-permute-start | bytes 393224 | tf_op jit(solution)/shard_map/ppermute | solution.py:23
  99.6 7.3 %collective-permute-start.8 = (bf16[4,64,256]{2,1,0:T(8,128)(2,1)S(1)}, bf16[4,64,256]{2,1,0:T(8,128)(2,1)S(1)}, u32[]{:S(2)}, u32[]{:S(2)}) collective-permute-start(bf16[4,64,256]{2,1,0:T(8,128)(2,1)S(1)} %fusion.15), channel_id=1, source_target_pairs={{0,4},{2,6},{4,8},{6,10},{8,12},{10,14},{1,5},{3,7},{5,9},{7,11},{... | collective-permute-start | bytes 393224 | tf_op jit(solution)/shard_map/ppermute | solution.py:23
  103.9 7.2 %collective-permute-start.9 = (bf16[4,64,256]{2,1,0:T(8,128)(2,1)S(1)}, bf16[4,64,256]{2,1,0:T(8,128)(2,1)S(1)}, u32[]{:S(2)}, u32[]{:S(2)}) collective-permute-start(bf16[4,64,256]{2,1,0:T(8,128)(2,1)S(1)} %fusion.15), channel_id=1, source_target_pairs={{4,0},{6,2},{8,4},{10,6},{12,8},{14,10},{5,1},{7,3},{9,5},{11,7},{... | collective-permute-start | bytes 393224 | tf_op jit(solution)/shard_map/ppermute | solution.py:23
  115.0 31.2 %copy-start.1 = (bf16[4,512,256]{2,1,0:T(8,128)(2,1)S(1)}, bf16[4,512,256]{2,1,0:T(8,128)(2,1)}, u32[]{:S(2)}) copy-start(bf16[4,512,256]{2,1,0:T(8,128)(2,1)} %gather_fusion.2) | copy-start | bytes 3145732
  115.1 5.4 %collective-permute-start.10 = (bf16[4,64,256]{2,1,0:T(8,128)(2,1)S(1)}, bf16[4,64,256]{2,1,0:T(8,128)(2,1)S(1)}, u32[]{:S(2)}, u32[]{:S(2)}) collective-permute-start(bf16[4,64,256]{2,1,0:T(8,128)(2,1)S(1)} %fusion.16), channel_id=1, source_target_pairs={{0,8},{2,10},{4,12},{6,14},{1,9},{3,11},{5,13},{7,15},{16,24},{18,... | collective-permute-start | bytes 393224 | tf_op jit(solution)/shard_map/ppermute | solution.py:23
  117.3 10.2 %collective-permute-start.11 = (bf16[4,64,256]{2,1,0:T(8,128)(2,1)S(1)}, bf16[4,64,256]{2,1,0:T(8,128)(2,1)S(1)}, u32[]{:S(2)}, u32[]{:S(2)}) collective-permute-start(bf16[4,64,256]{2,1,0:T(8,128)(2,1)S(1)} %fusion.16), channel_id=1, source_target_pairs={{8,0},{10,2},{12,4},{14,6},{9,1},{11,3},{13,5},{15,7},{24,16},{26,... | collective-permute-start | bytes 393224 | tf_op jit(solution)/shard_map/ppermute | solution.py:23
  133.9 18.6 %copy-start.3 = (bf16[4,64,256]{2,1,0:T(8,128)(2,1)}, bf16[4,64,256]{2,1,0:T(8,128)(2,1)S(1)}, u32[]{:S(2)}) copy-start(bf16[4,64,256]{2,1,0:T(8,128)(2,1)S(1)} %convolution_convert_fusion) | copy-start | bytes 393220
  133.9 5.5 %collective-permute-start.12 = (bf16[4,64,256]{2,1,0:T(8,128)(2,1)S(1)}, bf16[4,64,256]{2,1,0:T(8,128)(2,1)S(1)}, u32[]{:S(2)}, u32[]{:S(2)}) collective-permute-start(bf16[4,64,256]{2,1,0:T(8,128)(2,1)S(1)} %convolution_convert_fusion), channel_id=1, source_target_pairs={{0,2},{2,4},{4,6},{6,8},{8,10},{10,12},{12,14},{1,3},{3,5},{5,7},{... | collective-permute-start | bytes 393224 | tf_op jit(solution)/shard_map/ppermute | solution.py:14
  136.4 7.2 %collective-permute-start.13 = (bf16[4,64,256]{2,1,0:T(8,128)(2,1)S(1)}, bf16[4,64,256]{2,1,0:T(8,128)(2,1)S(1)}, u32[]{:S(2)}, u32[]{:S(2)}) collective-permute-start(bf16[4,64,256]{2,1,0:T(8,128)(2,1)S(1)} %convolution_convert_fusion), channel_id=1, source_target_pairs={{2,0},{4,2},{6,4},{8,6},{10,8},{12,10},{14,12},{3,1},{5,3},{7,5},{... | collective-permute-start | bytes 393224 | tf_op jit(solution)/shard_map/ppermute | solution.py:15
  147.9 20.3 %copy-start.4 = (f32[8]{0:T(128)S(1)}, f32[8]{0:T(128)}, u32[]{:S(2)}) copy-start(f32[8]{0:T(128)} %param.18) | copy-start | bytes 100
  164.1 11.4 %all-to-all-start.2 = ((f32[16,16,128]{2,1,0:T(8,128)}), f32[16,16,128]{2,1,0:T(8,128)S(1)}, u32[]{:S(2)}, u32[]{:S(2)}) async-start(f32[16,16,128]{2,1,0:T(8,128)} %tile.5), calls=%async_computation.2 | async-start | bytes 262144 | tf_op jit(solution)/shard_map/all_to_all | solution.py:60

commit v3 on v0

v3 whole, which is shorter than its diff:
```python
import functools

import jax
import jax.numpy as jnp
from jax import lax
from jax.experimental import pallas as pl
from jax.experimental.pallas import tpu as pltpu
from jax.sharding import PartitionSpec as P

f32, bf16 = jnp.float32, jnp.bfloat16
CHAIN = ("slab", "vec")
ANY = pl.BlockSpec(memory_space=pl.ANY)
VMEM = pl.BlockSpec(memory_space=pltpu.VMEM)
SMEM = pl.BlockSpec(memory_space=pltpu.SMEM)
SWAP = [(0, 1), (1, 0)]
MIB = 1024 * 1024


def kernel_call(body, out_shape, in_specs, scratch=(), vmem=16 * MIB, flops=0, size=0):
    return pl.pallas_call(
        body,
        out_shape=out_shape,
        in_specs=in_specs,
        out_specs=jax.tree.map(lambda _: VMEM, out_shape),
        scratch_shapes=list(scratch),
        compiler_params=pltpu.CompilerParams(vmem_limit_bytes=vmem),
        cost_estimate=pl.CostEstimate(flops=flops, bytes_accessed=size, transcendentals=0),
    )


def struct(shape, dtype=bf16):
    return jax.ShapeDtypeStruct(shape, dtype)


def dot(rows, matrix):
    return jnp.dot(rows, matrix, preferred_element_type=f32)


def dot_t(left, right):
    return lax.dot_general(left, right, (((1,), (1,)), ((), ())), preferred_element_type=f32)


def columns(index, width):
    return pl.ds(pl.multiple_of(index * width, width), width)


def pack_body(levels, place, lower, upper, final, packed, sem):
    count = packed.shape[1]
    theirs = pl.ds((1 - place[0]) * count, count)
    copies = []
    for level in range(levels):
        for side, ref in enumerate((lower, upper)):
            copies.append((ref.at[level, theirs], 2 * level + side))
    copies.append((final.at[theirs], 2 * levels))
    copies = [pltpu.make_async_copy(src, packed.at[k], sem.at[k]) for src, k in copies]
    for copy in copies:
        copy.start()
    for copy in copies:
        copy.wait()


def pack(place, lower, upper, final, levels):
    _, slabs, rows, half = lower.shape
    return pl.pallas_call(
        functools.partial(pack_body, levels),
        out_shape=struct((2 * levels + 1, slabs // 2, rows, half)),
        in_specs=[SMEM, ANY, ANY, ANY],
        out_specs=ANY,
        scratch_shapes=[pltpu.SemaphoreType.DMA((2 * levels + 1,))],
        compiler_params=pltpu.CompilerParams(vmem_limit_bytes=2 * MIB),
    )(place, lower, upper, final)


def image_body(place, table, extended, vectors, blocks, keep, send, quotient, image):
    slabs, _, half = vectors.shape
    reach = table.shape[1] // 2
    part = jnp.zeros(quotient.shape, f32)
    for slab in range(slabs):
        summed = None
        for entry in range(reach):
            rows = extended[table[slab, entry] + (slab + slabs)]
            term = dot(rows, blocks[table[slab, reach + entry]])
            summed = term if summed is None else summed + term
        rounded = summed.astype(bf16)
        image[slab] = rounded
        part = part + dot_t(vectors[slab], rounded)
    quotient[...] = part
    mine = slabs // 2
    keep[...] = image[pl.ds(place[0] * mine, mine)]
    send[...] = image[pl.ds((1 - place[0]) * mine, mine)]


def image_halves(place, table, extended, vectors, blocks):
    slabs, rows, half = vectors.shape
    part = struct((slabs // 2, rows, half))
    return kernel_call(
        image_body,
        (part, part, struct((rows, rows), f32)),
        [SMEM, SMEM, VMEM, VMEM, VMEM],
        [pltpu.VMEM((slabs, rows, half), bf16)],
    )(place, table, extended, vectors, blocks)


def weight_copies(level, place, lower, upper, packed, weights, sem):
    count = weights.shape[2]
    mine = pl.ds(place[0] * count, count)
    return [
        [
            pltpu.make_async_copy(ref.at[level, mine], weights.at[side, 0], sem.at[side, 0]),
            pltpu.make_async_copy(packed.at[2 * level + side], weights.at[side, 1], sem.at[side, 1]),
        ]
        for side, ref in enumerate((lower, upper))
    ]


def level_rows(place, part, side_rows, own, weights, out):
    half = weights.shape[-1]
    cols = columns(jnp.where(part == 0, place[0], 1 - place[0]), half)
    for slab in range(own.shape[0]):
        summed = None
        for side, rows in side_rows:
            term = dot(rows[slab], weights[side, part, slab])
            summed = term if summed is None else summed + term
        out[slab, :, cols] = (own[slab, :, cols].astype(f32) - summed).astype(bf16)


def level_body(level, place, own, below, above, lower, upper, packed, out, weights, sem):
    copies = weight_copies(level, place, lower, upper, packed, weights, sem)
    for part in range(2):
        for side in range(2):
            copies[side][part].start()
    for part in range(2):
        for side in range(2):
            copies[side][part].wait()
        level_rows(place, part, ((0, below), (1, above)), own, weights, out)


def reduced(level, place, own, below, above, lower, upper, packed):
    slabs, _, width = own.shape
    half = lower.shape[-1]
    return kernel_call(
        functools.partial(level_body, level),
        struct(own.shape),
        [SMEM, VMEM, VMEM, VMEM, ANY, ANY, ANY],
        [pltpu.VMEM((2, 2, slabs, width, half), bf16), pltpu.SemaphoreType.DMA((2, 2))],
    )(place, own, below, above, lower, upper, packed)


def last_body(level, place, own, other, lower, upper, final, packed, whole, keep, send, weights, rows, sem):
    count = own.shape[0]
    half = keep.shape[-1]
    mine = pl.ds(place[0] * count, count)
    below = place[1]

    def fetch(ref):
        return pltpu.make_async_copy(ref.at[level, mine], weights.at[0, 0], sem.at[0])

    pl.when(below == 1)(lambda: fetch(lower).start())
    pl.when(below == 0)(lambda: fetch(upper).start())
    copies = [
        fetch(lower),
        pltpu.make_async_copy(packed.at[2 * level + 1 - below], weights.at[0, 1], sem.at[1]),
        pltpu.make_async_copy(final.at[mine], weights.at[1, 0], sem.at[2]),
        pltpu.make_async_copy(packed.at[packed.shape[0] - 1], weights.at[1, 1], sem.at[3]),
    ]
    for copy in copies[1:]:
        copy.start()
    for part in range(2):
        copies[part].wait()
        level_rows(place, part, ((0, other),), own, weights, rows)
    for part, target in enumerate((keep, send)):
        copies[2 + part].wait()
        cols = columns(jnp.where(part == 0, place[0], 1 - place[0]), half)
        for slab in range(count):
            result = dot(rows[slab], weights[1, part, slab]).astype(bf16)
            target[slab] = result
            whole[slab, :, cols] = result


def last_reduced(level, place, own, other, lower, upper, final, packed):
    slabs, rows, width = own.shape
    half = lower.shape[-1]
    part = struct((slabs, rows, half))
    return kernel_call(
        functools.partial(last_body, level),
        (struct(own.shape), part, part),
        [SMEM, VMEM, VMEM, ANY, ANY, ANY, ANY],
        [
            pltpu.VMEM((2, 2, slabs, width, half), bf16),
            pltpu.VMEM(own.shape, bf16),
            pltpu.SemaphoreType.DMA((4,)),
        ],
    )(place, own, other, lower, upper, final, packed)


def final_body(place, own, final, packed, whole, keep, send, weights, sem):
    count = own.shape[0]
    half = keep.shape[-1]
    mine = pl.ds(place[0] * count, count)
    copies = [
        pltpu.make_async_copy(final.at[mine], weights.at[0], sem.at[0]),
        pltpu.make_async_copy(packed.at[packed.shape[0] - 1], weights.at[1], sem.at[1]),
    ]
    for copy in copies:
        copy.start()
    for part, target in enumerate((keep, send)):
        copies[part].wait()
        cols = columns(jnp.where(part == 0, place[0], 1 - place[0]), half)
        for slab in range(count):
            result = dot(own[slab], weights[part, slab]).astype(bf16)
            target[slab] = result
            whole[slab, :, cols] = result


def corrected(place, own, final, packed):
    slabs, rows, width = own.shape
    half = final.shape[-1]
    part = struct((slabs, rows, half))
    return kernel_call(
        final_body,
        (struct(own.shape), part, part),
        [SMEM, VMEM, ANY, ANY],
        [pltpu.VMEM((2, slabs, width, half), bf16), pltpu.SemaphoreType.DMA((2,))],
    )(place, own, final, packed)


def pencil_body(place, table, extended, image, window, blocks, others, out, summed):
    slabs = window.shape[0]
    own = image.shape[0]
    below = slabs - own
    half = blocks.shape[-1]
    rows = image.shape[1]
    reach = table.shape[1] // 2
    first = place[0] * own
    mine, theirs = columns(place[0], half), columns(1 - place[0], half)
    summed[...] = jnp.zeros(summed.shape, f32)

    @pl.loop(0, slabs * reach)
    def _(pair):
        target = lax.div(pair, reach)
        entry = pair - target * reach
        source = target + table[first + target, entry]
        inside = jnp.logical_and(source >= 0, source < slabs)
        held = jnp.logical_or(target >= below, source >= below)

        @pl.when(jnp.logical_and(inside, held))
        def _():
            block = table[first + target, reach + entry]
            vectors = window[source]
            summed[target, :, mine] += dot(vectors, blocks[block])
            summed[target, :, theirs] += dot(vectors, others[block])

    pencil = jnp.zeros((2 * rows, rows), f32)
    overlap = jnp.zeros((2 * rows, rows), f32)
    mixed = jnp.zeros((rows, rows), f32)
    old = jnp.zeros((rows, rows), f32)
    for slab in range(slabs):
        vectors, correction = extended[first + slab], window[slab]
        basis = jnp.concatenate([vectors, correction], 0)
        pencil = pencil + dot_t(basis, summed[slab].astype(bf16))
        if slab >= below:
            overlap = overlap + dot_t(basis, correction)
            mixed = mixed + dot_t(correction, image[slab - below])
            old = old + dot_t(vectors, vectors)
    out[0 : 2 * rows, 0:rows] = pencil
    out[0 : 2 * rows, rows : 2 * rows] = overlap
    out[2 * rows : 3 * rows, 0:rows] = mixed
    out[2 * rows : 3 * rows, rows : 2 * rows] = old


def pencil_parts(place, table, extended, image, window, blocks, others):
    rows = image.shape[1]
    return kernel_call(
        pencil_body,
        struct((3 * rows, 2 * rows), f32),
        [SMEM, SMEM, VMEM, VMEM, VMEM, VMEM, VMEM],
        [pltpu.VMEM(window.shape, f32)],
        vmem=24 * MIB,
    )(place, table, extended, image, window, blocks, others)


def swapped(operand):
    return lax.ppermute(operand, "vec", SWAP)


def along(operand, axis, distance):
    count = lax.axis_size("slab") * (2 if axis == CHAIN else 1)
    route = [(i, i + distance) for i in range(count) if 0 <= i + distance < count]
    return lax.ppermute(operand, axis, route)


def slab_total(part):
    slabs = lax.axis_size("slab")
    reach = 1
    while reach < slabs:
        part = part + lax.ppermute(part, "slab", [(i, i ^ reach) for i in range(slabs)])
        reach *= 2
    return part


def on_device(
    vectors,
    blocks,
    slab_blocks,
    far_source,
    far_block,
    level_lower,
    level_upper,
    level_final,
    shift_levels,
    shift_index,
):
    slab_count, rows, half = vectors.shape
    own_count = slab_count // 2
    slabs = lax.axis_size("slab")
    chain = 2 * slabs
    width = blocks.shape[1]
    rows_total = slab_count * slabs * width
    levels = [l for l in range(level_lower.shape[0]) if 2**l < slab_count * slabs]
    slab, core = lax.axis_index("slab"), lax.axis_index("vec")
    link = 2 * slab + core
    pair_distance = 2 ** levels[-1] // own_count
    one_partner = 2 * pair_distance >= chain
    place = jnp.stack([core, (link >= pair_distance).astype(jnp.int32)]).astype(jnp.int32)

    halo = jnp.concatenate([along(vectors, "slab", 1), vectors, along(vectors, "slab", -1)], 0)
    extended = lax.all_gather(halo, "vec", axis=2, tiled=True)
    slab_ids = slab * slab_count + jnp.arange(slab_count, dtype=jnp.int32)[:, None]
    near = jnp.broadcast_to(jnp.arange(-1, 2, dtype=jnp.int32), (slab_count, 3))
    table = jnp.concatenate([near, far_source - slab_ids, slab_blocks, far_block], 1)
    tables = jnp.concatenate([along(table, "slab", 1), table], 0)

    packed = swapped(pack(place, level_lower, level_upper, level_final, len(levels)))
    others = swapped(blocks)
    weights = (level_lower, level_upper, packed)

    keep, send, quotient = image_halves(place, table, extended, vectors, blocks)
    received = swapped(send)
    quotient = slab_total(quotient + swapped(quotient)) / rows_total
    image = jnp.where(core == 0, jnp.concatenate([keep, received], 2), jnp.concatenate([received, keep], 2))

    def held(offset):
        return lax.dynamic_slice_in_dim(extended, slab_count + own_count * core + offset, own_count)

    below = jnp.concatenate([along(image[own_count - 1 :], CHAIN, 1), image[: own_count - 1]], 0)
    above = jnp.concatenate([image[1:], along(image[:1], CHAIN, -1)], 0)
    both = [jnp.concatenate([a, held(o)], 1) for a, o in ((image, 0), (below, -1), (above, 1))]
    both = reduced(0, place, *both, *weights)
    both = reduced(1, place, both, along(both, CHAIN, 1), along(both, CHAIN, -1), *weights)
    shift = jnp.einsum(
        "kj,skb->sjb", quotient, both[:, rows:].astype(f32), precision=lax.Precision.HIGHEST
    )
    residual = (both[:, :rows].astype(f32) - shift).astype(bf16)
    for level in levels[2:]:
        distance = 2**level // own_count
        if level == levels[-1] and one_partner:
            route = [(i, i + distance) for i in range(chain - distance)]
            other = lax.ppermute(residual, CHAIN, route + [(j, i) for i, j in route])
            correction, keep, send = last_reduced(
                level, place, residual, other, level_lower, level_upper, level_final, packed
            )
        else:
            below, above = along(residual, CHAIN, distance), along(residual, CHAIN, -distance)
            residual = reduced(level, place, residual, below, above, *weights)
    if not one_partner:
        correction, keep, send = corrected(place, residual, level_final, packed)

    window = jnp.concatenate([along(correction, CHAIN, 2), along(correction, CHAIN, 1), correction], 0)
    received = swapped(send)
    result = jnp.where(core == 0, jnp.concatenate([keep, received], 0), jnp.concatenate([received, keep], 0))
    part = pencil_parts(place, tables, extended, image, window, blocks, others)
    sums = slab_total(part + swapped(part)) / rows_total
    top, bottom = sums[: 2 * rows], sums[2 * rows :]
    old, mixed, overlap = bottom[:, rows:], bottom[:, :rows], top[:, rows:]
    gram = jnp.concatenate([jnp.concatenate([old, overlap[:rows].T], 0), overlap], 1)
    projected = jnp.concatenate([jnp.concatenate([quotient, mixed], 0), top[:, :rows]], 1)
    pencil = projected - shift_levels[shift_index[0]] * gram
    return (result, gram, pencil)


def solution(mesh):
    in_specs = (
        P(("groups", "slab"), None, "vec"),
        P("groups", None, "vec"),
        P(("groups", "slab"), None),
        P(("groups", "slab"), None),
        P(("groups", "slab"), None),
        P(None, ("groups", "slab"), None, "vec"),
        P(None, ("groups", "slab"), None, "vec"),
        P(("groups", "slab"), None, "vec"),
        P("groups"),
        P("groups"),
    )
    out_specs = (P(("groups", "slab"), None, "vec"), P("groups", None), P("groups", None))
    return jax.shard_map(
        on_device, mesh=mesh, in_specs=in_specs, out_specs=out_specs, check_vma=False
    )
```

time: 325 us -> 143 us (0.44)
  waiting for transfers between devices: 124 us -> 42.4 us
  blocking collectives: 79.1 us -> 3.55 us
  matrix products: 31.2 us -> 0.32 us
  Pallas kernels: 0 us -> 25.1 us
  between operations: 15.8 us -> 1.68 us
  starting transfers between devices: 45.3 us -> 56.7 us
  local copies, waits for them, and re-layouts: 21 us -> 10.5 us
  other arithmetic: 6.05 us -> 2.62 us
    psum x1 -> x0, waiting for transfers between devices: 88.3 us -> none  [on_device(): gram_total, image_total = lax.psum((gram_part, image_part), ('slab', 'vec'))]
    psum x1 -> x0, blocking collectives: 62.4 us -> none  [on_device(): quotient = lax.psum(quotient_part, ('slab', 'vec')) / rows_total]
    dot_general x25 -> x1, matrix products: 31.2 us -> 0.32 us  [on_device(): jnp.einsum('kj,skb->sjb', quotient, both[:, rows:].astype(f32), precision...]
    pallas_call x0 -> x8, Pallas kernels: none -> 25.1 us  [the longest x4 8.63 us: reduced(): kernel_call(functools.partial(level_body, level), struct(own.shape), [SME...]
    gather x6 -> x0, local copies, waits for them, and re-layouts: 18.7 us -> none  [the longest x1 4.95 us: apply_operator(): blocks[far_block]]
    all_gather x8 -> x1, blocking collectives: 16.6 us -> 3.55 us  [on_device(): extended = lax.all_gather(halo, 'vec', axis=2, tiled=True)]
    ppermute x14 -> x26, starting transfers between devices: 45.2 us -> 56.7 us  [the longest x13 33.7 us: along(): return lax.ppermute(operand, axis, route)]
    unnamed x28 -> x23, local copies, waits for them, and re-layouts: 1.42 us -> 9.68 us
  transfers between devices with their start and end apart: 15 -> 26, of which waited for: 12 -> 16; matrix products, arithmetic and copies ran while one was open for 9% -> 1% of each run, Pallas kernels for 0% -> 11%
where the time goes in v3:
time: 143 us
  starting transfers between devices  56.7 us (40%)
  waiting for transfers between devices  42.4 us (30%)
  Pallas kernels  25.1 us (18%)
  local copies, waits for them, and re-layouts  10.5 us (7%)
  blocking collectives  3.55 us (2%)
  other arithmetic  2.62 us (2%)
  between operations  1.68 us (1%)
    ppermute x13, starting transfers between devices, along(): return lax.ppermute(operand, axis, route)  33.7 us
    ppermute x13, waiting for transfers between devices, along(): return lax.ppermute(operand, axis, route)  19.7 us
    ppermute x6, starting transfers between devices, slab_total(): lax.ppermute(part, 'slab', [(i, i ^ reach) for i in range(slabs)])  19 us
    ppermute x6, waiting for transfers between devices, slab_total(): lax.ppermute(part, 'slab', [(i, i ^ reach) for i in range(slabs)])  16.4 us
    unnamed x23, local copies, waits for them, and re-layouts  9.68 us
    pallas_call x4, Pallas kernels, reduced(): kernel_call(functools.partial(level_body, level), struct(own.shape), [SME...  8.63 us
    pallas_call x1, Pallas kernels, pencil_parts(): kernel_call(pencil_body, struct((3 * rows, 2 * rows), f32), [SMEM, SMEM,...  6.77 us
    ppermute x1, waiting for transfers between devices, on_device(): other = lax.ppermute(residual, CHAIN, route + [(j, i) for i, j in route])  4.69 us
  transfers between devices with their start and end apart: 26, of which 16 were waited for; matrix products, arithmetic and copies ran while one was open for 1% of the time, Pallas kernels for 11%

profile of v3, /device:TPU:0, one launch (start us, length us, event | category | flops | bytes accessed | tf_op | source)
XLA Modules:
  0.0 142.9 jit_solution(12498997840788469972)
XLA Ops:
  0.7 2.8 %copy-done = bf16[6,4,512,256]{3,2,1,0:T(8,128)(2,1)S(1)} copy-done((bf16[6,4,512,256]{3,2,1,0:T(8,128)(2,1)S(1)}, bf16[6,4,512,256]{3,2,1,0:T(8,128)(2,1)}, u32[]{:S(2)}) %copy-start) | copy-done | bytes 6291480
  3.5 2.8 %copy-done.2 = bf16[6,4,512,256]{3,2,1,0:T(8,128)(2,1)S(1)} copy-done((bf16[6,4,512,256]{3,2,1,0:T(8,128)(2,1)S(1)}, bf16[6,4,512,256]{3,2,1,0:T(8,128)(2,1)}, u32[]{:S(2)}) %copy-start.2) | copy-done | bytes 6291480
  7.5 3.1 %shard_map.122 = bf16[11,2,512,256]{3,2,1,0:T(8,128)(2,1)} custom-call(s32[2]{0:T(128)S(1)} %pad_add_fusion.1.place, bf16[6,4,512,256]{3,2,1,0:T(8,128)(2,1)S(1)} %copy-done, bf16[6,4,512,256]{3,2,1,0:T(8,128)(2,1)S(1)} %copy-done.2, bf16[4,512,256]{2,1,0:T(8,128)(2,1)S(1)} %copy-done.4), custom_call_target="tpu_custom_call" | custom-call | tf_op jit(solution)/shard_map/pallas_call | solution.py:64
  11.3 4.8 %collective-permute-start = (bf16[4,64,256]{2,1,0:T(8,128)(2,1)S(1)}, bf16[4,64,256]{2,1,0:T(8,128)(2,1)S(1)}, u32[]{:S(2)}, u32[]{:S(2)}) collective-permute-start(bf16[4,64,256]{2,1,0:T(8,128)(2,1)S(1)} %copy-done.6), channel_id=1, source_target_pairs={{0,2},{2,4},{4,6},{6,8},{8,10},{10,12},{12,14},{1,3},{3,5},{5,7},{... | collective-permute-start | bytes 393224 | tf_op jit(solution)/shard_map/ppermute | solution.py:289
  19.1 4.1 %collective-permute-done.1 = bf16[4,64,256]{2,1,0:T(8,128)(2,1)S(1)} collective-permute-done((bf16[4,64,256]{2,1,0:T(8,128)(2,1)S(1)}, bf16[4,64,256]{2,1,0:T(8,128)(2,1)S(1)}, u32[]{:S(2)}, u32[]{:S(2)}) %collective-permute-start.1) | collective-permute-done | bytes 131104 | tf_op jit(solution)/shard_map/ppermute | solution.py:289
  23.2 3.5 %all_gather.3.extended = bf16[12,64,512]{2,1,0:T(8,128)(2,1)S(1)} all-gather(bf16[12,64,256]{2,1,0:T(8,128)(2,1)S(1)} %pad_maximum_fusion), channel_id=1, replica_groups=mesh['groups'=2,'slab'=8,'vec'=2] {'vec'}, dimensions={2}, use_global_device_ids=true | all-gather | bytes 1179648 | tf_op jit(solution)/shard_map/all_gather | solution.py:327
  26.8 4.3 %shard_map.121 = (bf16[2,64,256]{2,1,0:T(8,128)(2,1)S(1)}, bf16[2,64,256]{2,1,0:T(8,128)(2,1)S(1)}, f32[64,64]{1,0:T(8,128)S(1)}) custom-call(s32[2]{0:T(128)S(1)} %pad_add_fusion.1.place, s32[4,14]{1,0:T(4,128)S(1)} %pad_add_fusion.table, bf16[12,64,512]{2,1,0:T(8,128)(2,1)S(1)} %all_gather.3.extended, bf16[4,64,256]{2,1,0:T(8,128)(2,1)S(1)} %copy-done.6, ...), custom_call_target="tpu_custom_call" | custom-call | tf_op jit(solution)/shard_map/pallas_call | solution.py:96
  32.4 2.8 %collective-permute-start.9 = (f32[64,64]{1,0:T(8,128)S(1)}, f32[64,64]{1,0:T(8,128)S(1)}, u32[]{:S(2)}, u32[]{:S(2)}) collective-permute-start(f32[64,64]{1,0:T(8,128)S(1)} %add.84), channel_id=1, source_target_pairs={{0,2},{2,0},{4,6},{6,4},{8,10},{10,8},{12,14},{14,12},{1,3},{3,1},... | collective-permute-start | bytes 49160 | tf_op jit(solution)/shard_map/ppermute | solution.py:296
  36.6 3.0 %collective-permute-start.3 = (bf16[1,64,512]{2,1,0:T(8,128)(2,1)S(1)}, bf16[1,64,512]{2,1,0:T(8,128)(2,1)S(1)}, u32[]{:S(2)}, u32[]{:S(2)}) collective-permute-start(bf16[1,64,512]{2,1,0:T(8,128)(2,1)S(1)} %get-tuple-element.20), channel_id=1, source_target_pairs={{0,1},{1,2},{2,3},{3,4},{4,5},{5,6},{6,7},{7,8},{8,9},{9,10},{10,1... | collective-permute-start | bytes 196616 | tf_op jit(solution)/shard_map/ppermute | solution.py:289
  40.5 2.8 %copy-done.3 = bf16[6,4,512,256]{3,2,1,0:T(8,128)(2,1)S(1)} copy-done((bf16[6,4,512,256]{3,2,1,0:T(8,128)(2,1)S(1)}, bf16[6,4,512,256]{3,2,1,0:T(8,128)(2,1)}, u32[]{:S(2)}) %copy-start.3) | copy-done | bytes 6291480
  45.5 3.5 %collective-permute-start.6 = (bf16[2,128,512]{2,1,0:T(8,128)(2,1)S(1)}, bf16[2,128,512]{2,1,0:T(8,128)(2,1)S(1)}, u32[]{:S(2)}, u32[]{:S(2)}) collective-permute-start(bf16[2,128,512]{2,1,0:T(8,128)(2,1)S(1)} %shard_map.123.own), channel_id=1, source_target_pairs={{0,1},{1,2},{2,3},{3,4},{4,5},{5,6},{6,7},{7,8},{8,9},{9,10},{10,1... | collective-permute-start | bytes 786440 | tf_op jit(solution)/shard_map/ppermute | solution.py:289
  50.3 6.6 %collective-permute-start.10 = (f32[64,64]{1,0:T(8,128)S(1)}, f32[64,64]{1,0:T(8,128)S(1)}, u32[]{:S(2)}, u32[]{:S(2)}) collective-permute-start(f32[64,64]{1,0:T(8,128)S(1)} %add.85), channel_id=1, source_target_pairs={{0,4},{2,6},{4,0},{6,2},{8,12},{10,14},{12,8},{14,10},{1,5},{3,7},... | collective-permute-start | bytes 49160 | tf_op jit(solution)/shard_map/ppermute | solution.py:296
  56.9 4.9 %collective-permute-done.10 = f32[64,64]{1,0:T(8,128)S(1)} collective-permute-done((f32[64,64]{1,0:T(8,128)S(1)}, f32[64,64]{1,0:T(8,128)S(1)}, u32[]{:S(2)}, u32[]{:S(2)}) %collective-permute-start.10) | collective-permute-done | bytes 16416 | tf_op jit(solution)/shard_map/ppermute | solution.py:296
  61.8 2.6 %collective-permute-start.11 = (f32[64,64]{1,0:T(8,128)S(1)}, f32[64,64]{1,0:T(8,128)S(1)}, u32[]{:S(2)}, u32[]{:S(2)}) collective-permute-start(f32[64,64]{1,0:T(8,128)S(1)} %add.86), channel_id=1, source_target_pairs={{0,8},{2,10},{4,12},{6,14},{8,0},{10,2},{12,4},{14,6},{1,9},{3,11}... | collective-permute-start | bytes 49160 | tf_op jit(solution)/shard_map/ppermute | solution.py:296
  73.3 4.0 %collective-permute-done.13.above = bf16[2,64,512]{2,1,0:T(8,128)(2,1)S(1)} collective-permute-done((bf16[2,64,512]{2,1,0:T(8,128)(2,1)S(1)}, bf16[2,64,512]{2,1,0:T(8,128)(2,1)S(1)}, u32[]{:S(2)}, u32[]{:S(2)}) %collective-permute-start.13) | collective-permute-done | bytes 131104 | tf_op jit(solution)/shard_map/ppermute | solution.py:289
  79.5 5.3 %collective-permute-start.14 = (bf16[2,64,512]{2,1,0:T(8,128)(2,1)S(1)}, bf16[2,64,512]{2,1,0:T(8,128)(2,1)S(1)}, u32[]{:S(2)}, u32[]{:S(2)}) collective-permute-start(bf16[2,64,512]{2,1,0:T(8,128)(2,1)S(1)} %shard_map.125.own), channel_id=1, source_target_pairs={{0,4},{1,5},{2,6},{3,7},{4,8},{5,9},{6,10},{7,11},{8,12},{9,13},{1... | collective-permute-start | bytes 393224 | tf_op jit(solution)/shard_map/ppermute | solution.py:289
  87.2 5.2 %collective-permute-done.15.above = bf16[2,64,512]{2,1,0:T(8,128)(2,1)S(1)} collective-permute-done((bf16[2,64,512]{2,1,0:T(8,128)(2,1)S(1)}, bf16[2,64,512]{2,1,0:T(8,128)(2,1)S(1)}, u32[]{:S(2)}, u32[]{:S(2)}) %collective-permute-start.15) | collective-permute-done | bytes 131104 | tf_op jit(solution)/shard_map/ppermute | solution.py:289
  95.9 4.7 %collective-permute-done.16.other = bf16[2,64,512]{2,1,0:T(8,128)(2,1)S(1)} collective-permute-done((bf16[2,64,512]{2,1,0:T(8,128)(2,1)S(1)}, bf16[2,64,512]{2,1,0:T(8,128)(2,1)S(1)}, u32[]{:S(2)}, u32[]{:S(2)}) %collective-permute-start.16) | collective-permute-done | bytes 131104 | tf_op jit(solution)/shard_map/ppermute | solution.py:358
  102.9 5.5 %collective-permute-start.19 = (bf16[2,64,512]{2,1,0:T(8,128)(2,1)S(1)}, bf16[2,64,512]{2,1,0:T(8,128)(2,1)S(1)}, u32[]{:S(2)}, u32[]{:S(2)}) collective-permute-start(bf16[2,64,512]{2,1,0:T(8,128)(2,1)S(1)} %get-tuple-element.14), channel_id=1, source_target_pairs={{0,2},{1,3},{2,4},{3,5},{4,6},{5,7},{6,8},{7,9},{8,10},{9,11},{10,... | collective-permute-start | bytes 393224 | tf_op jit(solution)/shard_map/ppermute | solution.py:289
  109.7 2.6 %collective-permute-start.18 = (s32[4,14]{1,0:T(4,128)S(1)}, s32[4,14]{1,0:T(4,128)S(1)}, u32[]{:S(2)}, u32[]{:S(2)}) collective-permute-start(s32[4,14]{1,0:T(4,128)S(1)} %pad_add_fusion.table), channel_id=1, source_target_pairs={{0,2},{2,4},{4,6},{6,8},{8,10},{10,12},{12,14},{1,3},{3,5},{5,7},{... | collective-permute-start | bytes 680 | tf_op jit(solution)/shard_map/ppermute | solution.py:289
  113.7 6.8 %shard_map.128 = f32[192,128]{1,0:T(8,128)S(1)} custom-call(s32[2]{0:T(128)S(1)} %pad_add_fusion.1.place, s32[8,14]{1,0:T(8,128)S(1)} %add_add_fusion.table, bf16[12,64,512]{2,1,0:T(8,128)(2,1)S(1)} %all_gather.3.extended, bf16[2,64,512]{2,1,0:T(8,128)(2,1)S(1)} %maximum_select_fusion.image, bf16[6,64,512]{2,1,0:T(8,128)(2,1)S(1)} %pad_maximum_fusion.1.window, ...), custom_call_target="tpu_custom_call" | custom-call | tf_op jit(solution)/shard_map/pallas_call | solution.py:273
  123.0 3.6 %collective-permute-start.23 = (f32[192,128]{1,0:T(8,128)S(1)}, f32[192,128]{1,0:T(8,128)S(1)}, u32[]{:S(2)}, u32[]{:S(2)}) collective-permute-start(f32[192,128]{1,0:T(8,128)S(1)} %add.88), channel_id=1, source_target_pairs={{0,2},{2,0},{4,6},{6,4},{8,10},{10,8},{12,14},{14,12},{1,3},{3,1},... | collective-permute-start | bytes 294920 | tf_op jit(solution)/shard_map/ppermute | solution.py:296
  126.6 3.3 %collective-permute-done.23 = f32[192,128]{1,0:T(8,128)S(1)} collective-permute-done((f32[192,128]{1,0:T(8,128)S(1)}, f32[192,128]{1,0:T(8,128)S(1)}, u32[]{:S(2)}, u32[]{:S(2)}) %collective-permute-start.23) | collective-permute-done | bytes 98336 | tf_op jit(solution)/shard_map/ppermute | solution.py:296
  137.5 3.7 %collective-permute-done.25 = f32[192,128]{1,0:T(8,128)S(1)} collective-permute-done((f32[192,128]{1,0:T(8,128)S(1)}, f32[192,128]{1,0:T(8,128)S(1)}, u32[]{:S(2)}, u32[]{:S(2)}) %collective-permute-start.25) | collective-permute-done | bytes 98336 | tf_op jit(solution)/shard_map/ppermute | solution.py:296
  (89 shorter events, 45.0 us)
Async XLA Ops:
  10.7 29.8 %collective-permute-start.5 = (bf16[11,2,512,256]{3,2,1,0:T(8,128)(2,1)}, bf16[11,2,512,256]{3,2,1,0:T(8,128)(2,1)}, u32[]{:S(2)}, u32[]{:S(2)}) collective-permute-start(bf16[11,2,512,256]{3,2,1,0:T(8,128)(2,1)} %shard_map.122), channel_id=1, source_target_pairs={{0,1},{1,0},{2,3},{3,2},{4,5},{5,4},{6,7},{7,6},{8,9},{9,8},{10,11... | collective-permute-start | bytes 17301512 | tf_op jit(solution)/shard_map/ppermute | solution.py:283
  11.2 102.5 %collective-permute-start.21 = (bf16[16,512,256]{2,1,0:T(8,128)(2,1)}, bf16[16,512,256]{2,1,0:T(8,128)(2,1)}, u32[]{:S(2)}, u32[]{:S(2)}) collective-permute-start(bf16[16,512,256]{2,1,0:T(8,128)(2,1)} %blocks.3), channel_id=1, source_target_pairs={{0,1},{1,0},{2,3},{3,2},{4,5},{5,4},{6,7},{7,6},{8,9},{9,8},{10,11... | collective-permute-start | bytes 12582920 | tf_op jit(solution)/shard_map/ppermute | solution.py:283
  11.3 7.8 %collective-permute-start = (bf16[4,64,256]{2,1,0:T(8,128)(2,1)S(1)}, bf16[4,64,256]{2,1,0:T(8,128)(2,1)S(1)}, u32[]{:S(2)}, u32[]{:S(2)}) collective-permute-start(bf16[4,64,256]{2,1,0:T(8,128)(2,1)S(1)} %copy-done.6), channel_id=1, source_target_pairs={{0,2},{2,4},{4,6},{6,8},{8,10},{10,12},{12,14},{1,3},{3,5},{5,7},{... | collective-permute-start | bytes 393224 | tf_op jit(solution)/shard_map/ppermute | solution.py:289
  16.1 7.1 %collective-permute-start.1 = (bf16[4,64,256]{2,1,0:T(8,128)(2,1)S(1)}, bf16[4,64,256]{2,1,0:T(8,128)(2,1)S(1)}, u32[]{:S(2)}, u32[]{:S(2)}) collective-permute-start(bf16[4,64,256]{2,1,0:T(8,128)(2,1)S(1)} %copy-done.6), channel_id=1, source_target_pairs={{2,0},{4,2},{6,4},{8,6},{10,8},{12,10},{14,12},{3,1},{5,3},{7,5},{... | collective-permute-start | bytes 393224 | tf_op jit(solution)/shard_map/ppermute | solution.py:289
  31.5 3.7 %collective-permute-start.2 = (bf16[2,64,256]{2,1,0:T(8,128)(2,1)S(1)}, bf16[2,64,256]{2,1,0:T(8,128)(2,1)S(1)}, u32[]{:S(2)}, u32[]{:S(2)}) collective-permute-start(bf16[2,64,256]{2,1,0:T(8,128)(2,1)S(1)} %get-tuple-element.10), channel_id=1, source_target_pairs={{0,1},{1,0},{2,3},{3,2},{4,5},{5,4},{6,7},{7,6},{8,9},{9,8},{10,11... | collective-permute-start | bytes 196616 | tf_op jit(solution)/shard_map/ppermute | solution.py:283
  32.4 17.9 %collective-permute-start.9 = (f32[64,64]{1,0:T(8,128)S(1)}, f32[64,64]{1,0:T(8,128)S(1)}, u32[]{:S(2)}, u32[]{:S(2)}) collective-permute-start(f32[64,64]{1,0:T(8,128)S(1)} %add.84), channel_id=1, source_target_pairs={{0,2},{2,0},{4,6},{6,4},{8,10},{10,8},{12,14},{14,12},{1,3},{3,1},... | collective-permute-start | bytes 49160 | tf_op jit(solution)/shard_map/ppermute | solution.py:296
  35.3 4.4 %collective-permute-start.4 = (bf16[1,64,512]{2,1,0:T(8,128)(2,1)S(1)}, bf16[1,64,512]{2,1,0:T(8,128)(2,1)S(1)}, u32[]{:S(2)}, u32[]{:S(2)}) collective-permute-start(bf16[1,64,512]{2,1,0:T(8,128)(2,1)S(1)} %get-tuple-element.21), channel_id=1, source_target_pairs={{1,0},{2,1},{3,2},{4,3},{5,4},{6,5},{7,6},{8,7},{9,8},{10,9},{11,1... | collective-permute-start | bytes 196616 | tf_op jit(solution)/shard_map/ppermute | solution.py:289
  36.6 3.9 %collective-permute-start.3 = (bf16[1,64,512]{2,1,0:T(8,128)(2,1)S(1)}, bf16[1,64,512]{2,1,0:T(8,128)(2,1)S(1)}, u32[]{:S(2)}, u32[]{:S(2)}) collective-permute-start(bf16[1,64,512]{2,1,0:T(8,128)(2,1)S(1)} %get-tuple-element.20), channel_id=1, source_target_pairs={{0,1},{1,2},{2,3},{3,4},{4,5},{5,6},{6,7},{7,8},{8,9},{9,10},{10,1... | collective-permute-start | bytes 196616 | tf_op jit(solution)/shard_map/ppermute | solution.py:289
  45.5 21.1 %collective-permute-start.6 = (bf16[2,128,512]{2,1,0:T(8,128)(2,1)S(1)}, bf16[2,128,512]{2,1,0:T(8,128)(2,1)S(1)}, u32[]{:S(2)}, u32[]{:S(2)}) collective-permute-start(bf16[2,128,512]{2,1,0:T(8,128)(2,1)S(1)} %shard_map.123.own), channel_id=1, source_target_pairs={{0,1},{1,2},{2,3},{3,4},{4,5},{5,6},{6,7},{7,8},{8,9},{9,10},{10,1... | collective-permute-start | bytes 786440 | tf_op jit(solution)/shard_map/ppermute | solution.py:289
  49.0 17.7 %collective-permute-start.7 = (bf16[2,128,512]{2,1,0:T(8,128)(2,1)S(1)}, bf16[2,128,512]{2,1,0:T(8,128)(2,1)S(1)}, u32[]{:S(2)}, u32[]{:S(2)}) collective-permute-start(bf16[2,128,512]{2,1,0:T(8,128)(2,1)S(1)} %shard_map.123.own), channel_id=1, source_target_pairs={{1,0},{2,1},{3,2},{4,3},{5,4},{6,5},{7,6},{8,7},{9,8},{10,9},{11,1... | collective-permute-start | bytes 786440 | tf_op jit(solution)/shard_map/ppermute | solution.py:289
  50.3 11.5 %collective-permute-start.10 = (f32[64,64]{1,0:T(8,128)S(1)}, f32[64,64]{1,0:T(8,128)S(1)}, u32[]{:S(2)}, u32[]{:S(2)}) collective-permute-start(f32[64,64]{1,0:T(8,128)S(1)} %add.85), channel_id=1, source_target_pairs={{0,4},{2,6},{4,0},{6,2},{8,12},{10,14},{12,8},{14,10},{1,5},{3,7},... | collective-permute-start | bytes 49160 | tf_op jit(solution)/shard_map/ppermute | solution.py:296
  61.8 4.8 %collective-permute-start.11 = (f32[64,64]{1,0:T(8,128)S(1)}, f32[64,64]{1,0:T(8,128)S(1)}, u32[]{:S(2)}, u32[]{:S(2)}) collective-permute-start(f32[64,64]{1,0:T(8,128)S(1)} %add.86), channel_id=1, source_target_pairs={{0,8},{2,10},{4,12},{6,14},{8,0},{10,2},{12,4},{14,6},{1,9},{3,11}... | collective-permute-start | bytes 49160 | tf_op jit(solution)/shard_map/ppermute | solution.py:296
  69.1 4.2 %collective-permute-start.12 = (bf16[2,64,512]{2,1,0:T(8,128)(2,1)S(1)}, bf16[2,64,512]{2,1,0:T(8,128)(2,1)S(1)}, u32[]{:S(2)}, u32[]{:S(2)}) collective-permute-start(bf16[2,64,512]{2,1,0:T(8,128)(2,1)S(1)} %subtract_convert_fusion.own), channel_id=1, source_target_pairs={{0,2},{1,3},{2,4},{3,5},{4,6},{5,7},{6,8},{7,9},{8,10},{9,11},{10,... | collective-permute-start | bytes 393224 | tf_op jit(solution)/shard_map/ppermute | solution.py:289
  70.4 6.9 %collective-permute-start.13 = (bf16[2,64,512]{2,1,0:T(8,128)(2,1)S(1)}, bf16[2,64,512]{2,1,0:T(8,128)(2,1)S(1)}, u32[]{:S(2)}, u32[]{:S(2)}) collective-permute-start(bf16[2,64,512]{2,1,0:T(8,128)(2,1)S(1)} %subtract_convert_fusion.own), channel_id=1, source_target_pairs={{2,0},{3,1},{4,2},{5,3},{6,4},{7,5},{8,6},{9,7},{10,8},{11,9},{12,... | collective-permute-start | bytes 393224 | tf_op jit(solution)/shard_map/ppermute | solution.py:289
  79.5 7.8 %collective-permute-start.14 = (bf16[2,64,512]{2,1,0:T(8,128)(2,1)S(1)}, bf16[2,64,512]{2,1,0:T(8,128)(2,1)S(1)}, u32[]{:S(2)}, u32[]{:S(2)}) collective-permute-start(bf16[2,64,512]{2,1,0:T(8,128)(2,1)S(1)} %shard_map.125.own), channel_id=1, source_target_pairs={{0,4},{1,5},{2,6},{3,7},{4,8},{5,9},{6,10},{7,11},{8,12},{9,13},{1... | collective-permute-start | bytes 393224 | tf_op jit(solution)/shard_map/ppermute | solution.py:289
  84.7 7.7 %collective-permute-start.15 = (bf16[2,64,512]{2,1,0:T(8,128)(2,1)S(1)}, bf16[2,64,512]{2,1,0:T(8,128)(2,1)S(1)}, u32[]{:S(2)}, u32[]{:S(2)}) collective-permute-start(bf16[2,64,512]{2,1,0:T(8,128)(2,1)S(1)} %shard_map.125.own), channel_id=1, source_target_pairs={{4,0},{5,1},{6,2},{7,3},{8,4},{9,5},{10,6},{11,7},{12,8},{13,9},{1... | collective-permute-start | bytes 393224 | tf_op jit(solution)/shard_map/ppermute | solution.py:289
  94.6 5.9 %collective-permute-start.16 = (bf16[2,64,512]{2,1,0:T(8,128)(2,1)S(1)}, bf16[2,64,512]{2,1,0:T(8,128)(2,1)S(1)}, u32[]{:S(2)}, u32[]{:S(2)}) collective-permute-start(bf16[2,64,512]{2,1,0:T(8,128)(2,1)S(1)} %shard_map.126.own), channel_id=1, source_target_pairs={{0,8},{1,9},{2,10},{3,11},{4,12},{5,13},{6,14},{7,15},{8,0},{9,1},... | collective-permute-start | bytes 393224 | tf_op jit(solution)/shard_map/ppermute | solution.py:358
  102.9 10.8 %collective-permute-start.19 = (bf16[2,64,512]{2,1,0:T(8,128)(2,1)S(1)}, bf16[2,64,512]{2,1,0:T(8,128)(2,1)S(1)}, u32[]{:S(2)}, u32[]{:S(2)}) collective-permute-start(bf16[2,64,512]{2,1,0:T(8,128)(2,1)S(1)} %get-tuple-element.14), channel_id=1, source_target_pairs={{0,2},{1,3},{2,4},{3,5},{4,6},{5,7},{6,8},{7,9},{8,10},{9,11},{10,... | collective-permute-start | bytes 393224 | tf_op jit(solution)/shard_map/ppermute | solution.py:289
  108.4 5.3 %collective-permute-start.20 = (bf16[2,64,512]{2,1,0:T(8,128)(2,1)S(1)}, bf16[2,64,512]{2,1,0:T(8,128)(2,1)S(1)}, u32[]{:S(2)}, u32[]{:S(2)}) collective-permute-start(bf16[2,64,512]{2,1,0:T(8,128)(2,1)S(1)} %get-tuple-element.14), channel_id=1, source_target_pairs={{0,1},{1,2},{2,3},{3,4},{4,5},{5,6},{6,7},{7,8},{8,9},{9,10},{10,1... | collective-permute-start | bytes 393224 | tf_op jit(solution)/shard_map/ppermute | solution.py:289
  109.7 3.9 %collective-permute-start.18 = (s32[4,14]{1,0:T(4,128)S(1)}, s32[4,14]{1,0:T(4,128)S(1)}, u32[]{:S(2)}, u32[]{:S(2)}) collective-permute-start(s32[4,14]{1,0:T(4,128)S(1)} %pad_add_fusion.table), channel_id=1, source_target_pairs={{0,2},{2,4},{4,6},{6,8},{8,10},{10,12},{12,14},{1,3},{3,5},{5,7},{... | collective-permute-start | bytes 680 | tf_op jit(solution)/shard_map/ppermute | solution.py:289
  123.0 6.9 %collective-permute-start.23 = (f32[192,128]{1,0:T(8,128)S(1)}, f32[192,128]{1,0:T(8,128)S(1)}, u32[]{:S(2)}, u32[]{:S(2)}) collective-permute-start(f32[192,128]{1,0:T(8,128)S(1)} %add.88), channel_id=1, source_target_pairs={{0,2},{2,0},{4,6},{6,4},{8,10},{10,8},{12,14},{14,12},{1,3},{3,1},... | collective-permute-start | bytes 294920 | tf_op jit(solution)/shard_map/ppermute | solution.py:296
  129.9 4.7 %collective-permute-start.24 = (f32[192,128]{1,0:T(8,128)S(1)}, f32[192,128]{1,0:T(8,128)S(1)}, u32[]{:S(2)}, u32[]{:S(2)}) collective-permute-start(f32[192,128]{1,0:T(8,128)S(1)} %add.89), channel_id=1, source_target_pairs={{0,4},{2,6},{4,0},{6,2},{8,12},{10,14},{12,8},{14,10},{1,5},{3,7},... | collective-permute-start | bytes 294920 | tf_op jit(solution)/shard_map/ppermute | solution.py:296
  131.0 5.8 %collective-permute-start.17 = (bf16[2,64,256]{2,1,0:T(8,128)(2,1)S(1)}, bf16[2,64,256]{2,1,0:T(8,128)(2,1)S(1)}, u32[]{:S(2)}, u32[]{:S(2)}) collective-permute-start(bf16[2,64,256]{2,1,0:T(8,128)(2,1)S(1)} %get-tuple-element.13), channel_id=1, source_target_pairs={{0,1},{1,0},{2,3},{3,2},{4,5},{5,4},{6,7},{7,6},{8,9},{9,8},{10,11... | collective-permute-start | bytes 196616 | tf_op jit(solution)/shard_map/ppermute | solution.py:283
  134.6 6.6 %collective-permute-start.25 = (f32[192,128]{1,0:T(8,128)S(1)}, f32[192,128]{1,0:T(8,128)S(1)}, u32[]{:S(2)}, u32[]{:S(2)}) collective-permute-start(f32[192,128]{1,0:T(8,128)S(1)} %add.90), channel_id=1, source_target_pairs={{0,8},{2,10},{4,12},{6,14},{8,0},{10,2},{12,4},{14,6},{1,9},{3,11}... | collective-permute-start | bytes 294920 | tf_op jit(solution)/shard_map/ppermute | solution.py:296
  (13 other events, 120.0 us)

commit v4 on v0

v4 whole, which is shorter than its diff:
```python
import functools

import jax
import jax.numpy as jnp
from jax import lax
from jax.experimental import pallas as pl
from jax.experimental.pallas import tpu as pltpu
from jax.sharding import PartitionSpec as P

f32, bf16 = jnp.float32, jnp.bfloat16
CHAIN = ("slab", "vec")
ANY = pl.BlockSpec(memory_space=pl.ANY)
VMEM = pl.BlockSpec(memory_space=pltpu.VMEM)
SMEM = pl.BlockSpec(memory_space=pltpu.SMEM)
SWAP = [(0, 1), (1, 0)]
MIB = 1024 * 1024


def kernel_call(body, out_shape, in_specs, scratch=(), vmem=16 * MIB, flops=0, size=0):
    return pl.pallas_call(
        body,
        out_shape=out_shape,
        in_specs=in_specs,
        out_specs=jax.tree.map(lambda _: VMEM, out_shape),
        scratch_shapes=list(scratch),
        compiler_params=pltpu.CompilerParams(vmem_limit_bytes=vmem),
        cost_estimate=pl.CostEstimate(flops=flops, bytes_accessed=size, transcendentals=0),
    )


def struct(shape, dtype=bf16):
    return jax.ShapeDtypeStruct(shape, dtype)


def dot(rows, matrix):
    return jnp.dot(rows, matrix, preferred_element_type=f32)


def dot_t(left, right):
    return lax.dot_general(left, right, (((1,), (1,)), ((), ())), preferred_element_type=f32)


def columns(index, width):
    return pl.ds(pl.multiple_of(index * width, width), width)


def in_vmem(operand):
    return pltpu.with_memory_space_constraint(operand, pltpu.VMEM)


def in_hbm(operand):
    return pltpu.with_memory_space_constraint(operand, pltpu.HBM)


def fetch_body(levels, other, place, lower, upper, final, *rest):
    blocks = rest[0] if len(rest) == 4 else None
    fetched, sem = rest[-2 if blocks is None else -3], rest[-1]
    count = fetched.shape[1]
    which = 1 - place[0] if other else place[0]
    slabs = pl.ds(which * count, count)
    pairs = []
    for level in range(levels):
        for ref in (lower, upper):
            pairs.append((ref.at[level, slabs], fetched.at[len(pairs)]))
    pairs.append((final.at[slabs], fetched.at[len(pairs)]))
    if blocks is not None:
        pairs.insert(0, (blocks, rest[-2]))
    copies = [pltpu.make_async_copy(*pair, sem.at[k]) for k, pair in enumerate(pairs)]
    for copy in copies:
        copy.start()
    for copy in copies:
        copy.wait()


def fetch(place, lower, upper, final, levels, blocks=None):
    _, slabs, rows, half = lower.shape
    shape = (2 * levels + 1, slabs // 2, rows, half)
    operands = [in_hbm(x) for x in (lower, upper, final)]
    out_shape = [pltpu.VMEM(shape, bf16)]
    size = 2 * 2 * (2 * levels + 1) * (slabs // 2) * rows * half
    if blocks is not None:
        operands.append(in_hbm(blocks))
        out_shape.append(pltpu.VMEM(blocks.shape, bf16))
        size += 2 * 2 * blocks.size
    return pl.pallas_call(
        functools.partial(fetch_body, levels, blocks is None),
        out_shape=out_shape,
        in_specs=[SMEM] + [ANY] * len(operands),
        out_specs=[ANY] * len(out_shape),
        scratch_shapes=[pltpu.SemaphoreType.DMA((2 * levels + 2,))],
        compiler_params=pltpu.CompilerParams(vmem_limit_bytes=2 * MIB),
        cost_estimate=pl.CostEstimate(flops=0, bytes_accessed=size, transcendentals=0),
    )(place, *operands)


def image_body(place, table, extended, vectors, blocks, keep, send, quotient, image):
    slabs, _, half = vectors.shape
    reach = table.shape[1] // 2
    part = jnp.zeros(quotient.shape, f32)
    for slab in range(slabs):
        summed = None
        for entry in range(reach):
            rows = extended[table[slab, entry] + (slab + slabs)]
            term = dot(rows, blocks[table[slab, reach + entry]])
            summed = term if summed is None else summed + term
        rounded = summed.astype(bf16)
        image[slab] = rounded
        part = part + dot_t(vectors[slab], rounded)
    quotient[...] = part
    mine = slabs // 2
    keep[...] = image[pl.ds(place[0] * mine, mine)]
    send[...] = image[pl.ds((1 - place[0]) * mine, mine)]


def image_halves(place, table, extended, vectors, blocks):
    slabs, rows, half = vectors.shape
    part = struct((slabs // 2, rows, half))
    return kernel_call(
        image_body,
        (part, part, struct((rows, rows), f32)),
        [SMEM, SMEM, VMEM, VMEM, VMEM],
        [pltpu.VMEM((slabs, rows, half), bf16)],
        flops=14 * slabs * rows * 2 * half * half,
        size=2 * blocks.size,
    )(place, table, extended, vectors, blocks)


def both_parts(place, mine, packed):
    half = mine.shape[-1]
    return (columns(place[0], half), mine), (columns(1 - place[0], half), packed)


def first_vectors_body(place, extended, mine, packed, out):
    count = out.shape[0]
    first = extended.shape[0] // 3 + count * place[0]
    for cols, weights in both_parts(place, mine, packed):
        for slab in range(count):
            own = first + slab
            summed = dot(extended[own - 1], weights[0, slab]) + dot(extended[own + 1], weights[1, slab])
            out[slab, :, cols] = (extended[own, :, cols].astype(f32) - summed).astype(bf16)


def first_body(place, image, inner, outer, vectors, quotient, mine, packed, out):
    count = image.shape[0]
    odd = place[0] == 1
    below = [jnp.where(odd, inner[0], outer[0])] + [image[slab] for slab in range(count - 1)]
    above = [image[slab] for slab in range(1, count)] + [jnp.where(odd, outer[0], inner[0])]
    high = quotient[...].astype(bf16)
    low = (quotient[...] - high.astype(f32)).astype(bf16)
    factors = (high.T, low.T)
    for cols, weights in both_parts(place, mine, packed):
        for slab in range(count):
            summed = dot(below[slab], weights[0, slab]) + dot(above[slab], weights[1, slab])
            for factor in factors:
                summed = summed + dot(factor, vectors[slab, :, cols])
            out[slab, :, cols] = (image[slab, :, cols].astype(f32) - summed).astype(bf16)


def reduce_rows(level, place, own, partners, mine, packed, out):
    bit = place[1 + level]
    for cols, weights in both_parts(place, mine, packed):
        for slab in range(own.shape[0]):
            summed = None
            for side, rows in zip((1 - bit, bit), partners):
                term = dot(rows[slab], weights[2 * level + side, slab])
                summed = term if summed is None else summed + term
            out[slab, :, cols] = (own[slab, :, cols].astype(f32) - summed).astype(bf16)


def level_body(level, place, own, *rest):
    *partners, mine, packed, out = rest
    reduce_rows(level, place, own, partners, mine, packed, out)


def product(place, rows, mine, packed, whole, parts):
    last = mine.shape[0] - 1
    for (cols, weights), target in zip(both_parts(place, mine, packed), parts):
        for slab in range(whole.shape[0]):
            result = dot(rows[slab], weights[last, slab]).astype(bf16)
            target[slab] = result
            whole[slab, :, cols] = result


def last_body(level, place, own, *rest):
    *partners, mine, packed, whole, keep, send, rows = rest
    reduce_rows(level, place, own, partners, mine, packed, rows)
    product(place, rows, mine, packed, whole, (keep, send))


def level_flops(operand, products):
    return 2 * products * operand.size * operand.shape[-1]


def add_pairs(table, row, entries, position, inside, window, blocks, others, place, summed, slot):
    half = blocks.shape[-1]
    mine, theirs = columns(place[0], half), columns(1 - place[0], half)
    for entry in range(entries):
        source = position + table[row, entry]

        @pl.when(inside(source))
        def _():
            block = table[row, entries + entry]
            vectors = window(source)
            summed[slot, :, mine] += dot(vectors, blocks[block])
            summed[slot, :, theirs] += dot(vectors, others[block])


def own_pairs_body(place, table, extended, image, correction, blocks, others, summed, out):
    own, rows, _ = image.shape
    reach = table.shape[1] // 2
    below = extended.shape[0] // 3
    first = place[0] * own
    summed[...] = jnp.zeros(summed.shape, f32)
    for slab in range(own):
        add_pairs(
            table, first + below + slab, reach, slab,
            lambda source: jnp.logical_and(source >= 0, source < own),
            lambda source: correction[source], blocks, others, place, summed, slab,
        )
    overlap = jnp.zeros((2 * rows, rows), f32)
    mixed = jnp.zeros((rows, rows), f32)
    old = jnp.zeros((rows, rows), f32)
    for slab in range(own):
        vectors, fixed = extended[first + below + slab], correction[slab]
        overlap = overlap + dot_t(jnp.concatenate([vectors, fixed], 0), fixed)
        mixed = mixed + dot_t(fixed, image[slab])
        old = old + dot_t(vectors, vectors)
    out[0 : 2 * rows, 0:rows] = jnp.zeros((2 * rows, rows), f32)
    out[0 : 2 * rows, rows : 2 * rows] = overlap
    out[2 * rows : 3 * rows, 0:rows] = mixed
    out[2 * rows : 3 * rows, rows : 2 * rows] = old


def cross_pairs_body(place, table, extended, correction, near, far, blocks, others, begun, part, out, window, summed):
    own, rows, _ = correction.shape
    reach = table.shape[1] // 2
    below = window.shape[0] - own
    half = blocks.shape[-1]
    first = place[0] * own
    mine, theirs = columns(place[0], half), columns(1 - place[0], half)
    window[0:own] = far[...]
    window[own : 2 * own] = near[...]
    window[below : below + own] = correction[...]
    summed[0:below] = jnp.zeros((below,) + summed.shape[1:], f32)
    summed[below : below + own] = begun[...]

    @pl.loop(0, (below + own) * reach)
    def _(pair):
        target = lax.div(pair, reach)
        entry = pair - target * reach
        source = target + table[first + target, entry]
        inside = jnp.logical_and(source >= 0, source < below + own)

        @pl.when(jnp.logical_and(inside, (target >= below) != (source >= below)))
        def _():
            block = table[first + target, reach + entry]
            vectors = window[source]
            summed[target, :, mine] += dot(vectors, blocks[block])
            summed[target, :, theirs] += dot(vectors, others[block])

    pencil = jnp.zeros((2 * rows, rows), f32)
    for slab in range(below + own):
        basis = jnp.concatenate([extended[first + slab], window[slab]], 0)
        pencil = pencil + dot_t(basis, summed[slab].astype(bf16))
    out[...] = part[...]
    out[0 : 2 * rows, 0:rows] = pencil


def pencil_parts(place, table, extended, image, correction, near, far, blocks, others):
    own, rows, width = image.shape
    flops = level_flops(image, 7)
    begun, part = kernel_call(
        own_pairs_body,
        (struct(image.shape, f32), struct((3 * rows, 2 * rows), f32)),
        [SMEM, SMEM] + [VMEM] * 5,
        flops=flops,
        vmem=20 * MIB,
    )(place, table, extended, image, correction, blocks, others)
    return kernel_call(
        cross_pairs_body,
        struct(part.shape, f32),
        [SMEM, SMEM] + [VMEM] * 8,
        [pltpu.VMEM((3 * own, rows, width), bf16), pltpu.VMEM((3 * own, rows, width), f32)],
        flops=flops,
        vmem=20 * MIB,
    )(place, table, extended, correction, near, far, blocks, others, begun, part)


def assemble_body(scale, levels, index, quotient, first, second, gram, pencil):
    rows = quotient.shape[0]
    shift = levels[index[0]]
    sums = (first[...] + second[...]) * scale
    overlap = sums[: 2 * rows, rows:]
    old, mixed = sums[2 * rows :, rows:], sums[2 * rows :, :rows]
    left = jnp.concatenate([old, overlap[:rows].T], 0)
    whole = jnp.concatenate([left, overlap], 1)
    gram[...] = whole
    projected = jnp.concatenate([jnp.concatenate([quotient[...], mixed], 0), sums[: 2 * rows, :rows]], 1)
    pencil[...] = projected - shift * whole


def swapped(operand):
    return lax.ppermute(operand, "vec", SWAP)


def along(operand, axis, distance):
    count = lax.axis_size("slab") * (2 if axis == CHAIN else 1)
    route = [(i, i + distance) for i in range(count) if 0 <= i + distance < count]
    return lax.ppermute(operand, axis, route)


def pair_routes(distance):
    chain = 2 * lax.axis_size("slab")
    routes = []
    for bit in range(2):
        ups = [(i, i + distance) for i in range(chain - distance) if i // distance % 2 == bit]
        routes.append(ups + [(j, i) for i, j in ups])
    return [route for route in routes if route]


def shared_out(part, reach, radix):
    slabs = lax.axis_size("slab")
    split = radix // 2
    core = lax.axis_index("vec")
    received = []
    for offset in range(split):
        route = []
        for i in range(slabs):
            if offset:
                route.append((2 * i, 2 * (i ^ (offset * reach))))
            route.append((2 * i + 1, 2 * (i ^ ((offset + split) * reach)) + 1))
        received.append(lax.ppermute(part, CHAIN, route))
    received[0] = jnp.where(core == 0, part, received[0])
    while len(received) > 1:
        received = [a + b for a, b in zip(received[::2], received[1::2])]
    return received[0]


def on_device(
    vectors,
    blocks,
    slab_blocks,
    far_source,
    far_block,
    level_lower,
    level_upper,
    level_final,
    shift_levels,
    shift_index,
):
    slab_count, rows, half = vectors.shape
    own_count = slab_count // 2
    slabs = lax.axis_size("slab")
    chain = 2 * slabs
    width = blocks.shape[1]
    rows_total = slab_count * slabs * width
    levels = [l for l in range(level_lower.shape[0]) if 2**l < slab_count * slabs]
    slab, core = lax.axis_index("slab"), lax.axis_index("vec")
    link = 2 * slab + core
    steps = [max(2**l // own_count, 1) for l in levels]
    place = jnp.stack([core] + [link // step % 2 for step in steps]).astype(jnp.int32)

    below, above = along(vectors, "slab", 1), along(vectors, "slab", -1)
    slab_ids = slab * slab_count + jnp.arange(slab_count, dtype=jnp.int32)[:, None]
    near = jnp.broadcast_to(jnp.arange(-1, 2, dtype=jnp.int32), (slab_count, 3))
    table = jnp.concatenate([near, far_source - slab_ids, slab_blocks, far_block], 1)
    tables = jnp.concatenate([along(table, "slab", 1), table], 0)

    (theirs,) = fetch(place, level_lower, level_upper, level_final, len(levels))
    packed = swapped(theirs)
    mine, held_blocks = fetch(place, level_lower, level_upper, level_final, len(levels), blocks)
    others = swapped(blocks)
    mine, packed, held_blocks, others = (in_vmem(x) for x in (mine, packed, held_blocks, others))

    halo = jnp.concatenate([below, vectors, above], 0)
    halo, tables = lax.optimization_barrier((halo, tables))
    extended = lax.all_gather(halo, "vec", axis=2, tiled=True)

    keep, send, quotient = image_halves(place, table, extended, vectors, held_blocks)
    received, quotient = swapped(send), quotient + swapped(quotient)
    image = jnp.where(core == 0, jnp.concatenate([keep, received], 2), jnp.concatenate([received, keep], 2))

    reach = 1
    while reach < slabs:
        radix = min(8, slabs // reach)
        share = shared_out(quotient, reach, radix)
        quotient = share + swapped(share)
        reach *= radix
    quotient = quotient / rows_total

    vectors_1 = kernel_call(
        first_vectors_body,
        struct(image.shape),
        [SMEM] + [VMEM] * 3,
        flops=level_flops(image, 2),
    )(place, extended, mine, packed)
    inner_route, outer_route = pair_routes(1)
    inner = swapped(lax.dynamic_slice_in_dim(image, (own_count - 1) * (1 - core), 1))
    outer = lax.ppermute(lax.dynamic_slice_in_dim(image, (own_count - 1) * core, 1), CHAIN, outer_route)
    residual = kernel_call(
        first_body,
        struct(image.shape),
        [SMEM] + [VMEM] * 7,
        flops=level_flops(image, 2),
    )(place, image, inner, outer, vectors_1, quotient, mine, packed)
    for level, step in zip(levels[1:], steps[1:]):
        partners = [lax.ppermute(residual, CHAIN, route) for route in reversed(pair_routes(step))][::-1]
        inputs = [SMEM] + [VMEM] * (3 + len(partners))
        if level != levels[-1]:
            residual = kernel_call(
                functools.partial(level_body, level),
                struct(residual.shape),
                inputs,
                flops=level_flops(residual, 2),
            )(place, residual, *partners, mine, packed)
    part = struct((own_count, rows, half))
    correction, keep, send = kernel_call(
        functools.partial(last_body, levels[-1]),
        (struct(residual.shape), part, part),
        inputs,
        [pltpu.VMEM(residual.shape, bf16)],
        flops=level_flops(residual, 2),
    )(place, residual, *partners, mine, packed)

    far, near = along(correction, CHAIN, 2), along(correction, CHAIN, 1)
    part = pencil_parts(place, tables, extended, image, correction, near, far, held_blocks, others)
    received = swapped(send)
    result = jnp.where(core == 0, jnp.concatenate([keep, received], 0), jnp.concatenate([received, keep], 0))

    part = part + swapped(part)
    radix = min(4, slabs)
    part = shared_out(part, 1, radix)
    reach = radix
    while reach < slabs:
        part = part + lax.ppermute(part, "slab", [(i, i ^ reach) for i in range(slabs)])
        reach *= 2
    square = struct((2 * rows, 2 * rows), f32)
    gram, pencil = kernel_call(
        functools.partial(assemble_body, 1.0 / rows_total),
        (square, square),
        [SMEM, SMEM] + [VMEM] * 3,
    )(shift_levels, shift_index, quotient, part, swapped(part))
    return (result, gram, pencil)


def solution(mesh):
    in_specs = (
        P(("groups", "slab"), None, "vec"),
        P("groups", None, "vec"),
        P(("groups", "slab"), None),
        P(("groups", "slab"), None),
        P(("groups", "slab"), None),
        P(None, ("groups", "slab"), None, "vec"),
        P(None, ("groups", "slab"), None, "vec"),
        P(("groups", "slab"), None, "vec"),
        P("groups"),
        P("groups"),
    )
    out_specs = (P(("groups", "slab"), None, "vec"), P("groups", None), P("groups", None))
    return jax.shard_map(
        on_device, mesh=mesh, in_specs=in_specs, out_specs=out_specs, check_vma=False
    )
```

time: 325 us -> 309 us (0.951)
  Pallas kernels: 0 us -> 212 us
  waiting for transfers between devices: 124 us -> 27.3 us
  blocking collectives: 79.1 us -> 2.37 us
  matrix products: 31.2 us -> 0 us
  between operations: 15.8 us -> 1.74 us
  local copies, waits for them, and re-layouts: 21 us -> 7.21 us
  starting transfers between devices: 45.3 us -> 56.5 us
  other arithmetic: 6.05 us -> 1.04 us
    pallas_call x0 -> x12, Pallas kernels: none -> 212 us  [the longest x2 181 us: fetch(): pl.pallas_call(functools.partial(fetch_body, levels, blocks is None), out...]
    psum x1 -> x0, waiting for transfers between devices: 88.3 us -> none  [on_device(): gram_total, image_total = lax.psum((gram_part, image_part), ('slab', 'vec'))]
    psum x1 -> x0, blocking collectives: 62.4 us -> none  [on_device(): quotient = lax.psum(quotient_part, ('slab', 'vec')) / rows_total]
    dot_general x25 -> x0, matrix products: 31.2 us -> none  [the longest x6 9.13 us: on_device(): jnp.einsum('skb,sbc->skc', from_below, level_lower[level_index], preferre...]
    gather x6 -> x0, local copies, waits for them, and re-layouts: 18.7 us -> none  [the longest x1 4.95 us: apply_operator(): blocks[far_block]]
    all_gather x8 -> x1, blocking collectives: 16.6 us -> 2.37 us  [on_device(): extended = lax.all_gather(halo, 'vec', axis=2, tiled=True)]
    ppermute x14 -> x29, starting transfers between devices: 45.2 us -> 56.5 us  [the longest x7 19.2 us: on_device(): lax.ppermute(residual, CHAIN, route)]
    ppermute x14 -> x29, waiting for transfers between devices: 36 us -> 27.3 us  [the longest x7 15.2 us: on_device(): lax.ppermute(residual, CHAIN, route)]
  transfers between devices with their start and end apart: 15 -> 29, of which waited for: 12 -> 11; matrix products, arithmetic and copies ran while one was open for 9% -> 0% of each run, Pallas kernels for 0% -> 10%
where the time goes in v4:
time: 309 us; the launch traced here: 308 us
  Pallas kernels  212 us (69%)
  starting transfers between devices  56.5 us (18%)
  waiting for transfers between devices  27.3 us (9%)
  local copies, waits for them, and re-layouts  7.21 us (2%)
    pallas_call x2, Pallas kernels, fetch(): pl.pallas_call(functools.partial(fetch_body, levels, blocks is None), out...  181 us
    ppermute x7, starting transfers between devices, on_device(): lax.ppermute(residual, CHAIN, route)  19.2 us
    ppermute x5, starting transfers between devices, along(): return lax.ppermute(operand, axis, route)  15.8 us
    ppermute x7, waiting for transfers between devices, on_device(): lax.ppermute(residual, CHAIN, route)  15.2 us
    ppermute x9, starting transfers between devices, swapped(): return lax.ppermute(operand, 'vec', SWAP)  10.6 us
    pallas_call x3, Pallas kernels, on_device(): kernel_call(functools.partial(level_body, level), struct(residual.shape),...  9.39 us
    unnamed x18, local copies, waits for them, and re-layouts  7.11 us
    ppermute x6, starting transfers between devices, shared_out(): received.append(lax.ppermute(part, CHAIN, route))  6.55 us
  transfers between devices with their start and end apart: 29, of which 11 were waited for; matrix products, arithmetic and copies ran while one was open for 0% of the time, Pallas kernels for 10%

profile of v4, /device:TPU:0, one launch (start us, length us, event | category | flops | bytes accessed | tf_op | source)
XLA Modules:
  0.0 308.3 jit_solution(8636710251002961131)
XLA Ops:
  0.8 176.5 %shard_map.123 = bf16[11,2,512,256]{3,2,1,0:T(8,128)(2,1)} custom-call(s32[6]{0:T(128)S(1)} %stack.24.place, bf16[6,4,512,256]{3,2,1,0:T(8,128)(2,1)} %lower.3, bf16[6,4,512,256]{3,2,1,0:T(8,128)(2,1)} %upper.3, bf16[4,512,256]{2,1,0:T(8,128)(2,1)} %final.3), custom_call_target="tpu_custom_call" | custom-call | bytes 11534336 | tf_op jit(solution)/shard_map/pallas_call | solution.py:85
  179.2 5.5 %collective-permute-start = (bf16[4,64,256]{2,1,0:T(8,128)(2,1)S(1)}, bf16[4,64,256]{2,1,0:T(8,128)(2,1)S(1)}, u32[]{:S(2)}, u32[]{:S(2)}) collective-permute-start(bf16[4,64,256]{2,1,0:T(8,128)(2,1)S(1)} %copy-done.4), channel_id=1, source_target_pairs={{0,2},{2,4},{4,6},{6,8},{8,10},{10,12},{12,14},{1,3},{3,5},{5,7},{... | collective-permute-start | bytes 393224 | tf_op jit(solution)/shard_map/ppermute | solution.py:309
  184.8 4.8 %collective-permute-start.2 = (s32[4,14]{1,0:T(4,128)S(1)}, s32[4,14]{1,0:T(4,128)S(1)}, u32[]{:S(2)}, u32[]{:S(2)}) collective-permute-start(s32[4,14]{1,0:T(4,128)S(1)} %pad_add_fusion.table), channel_id=1, source_target_pairs={{0,2},{2,4},{4,6},{6,8},{8,10},{10,12},{12,14},{1,3},{3,5},{5,7},{... | collective-permute-start | bytes 680 | tf_op jit(solution)/shard_map/ppermute | solution.py:309
  189.6 4.5 %shard_map.121 = (bf16[11,2,512,256]{3,2,1,0:T(8,128)(2,1)S(1)}, bf16[16,512,256]{2,1,0:T(8,128)(2,1)S(1)}) custom-call(s32[6]{0:T(128)S(1)} %stack.24.place, bf16[6,4,512,256]{3,2,1,0:T(8,128)(2,1)} %lower.3, bf16[6,4,512,256]{3,2,1,0:T(8,128)(2,1)} %upper.3, bf16[4,512,256]{2,1,0:T(8,128)(2,1)} %final.3, bf16[16,512,256]{2,1,0:T(8,128)(2,1)} %rest_0_.1), custom_call_target="tpu_custom_call" | custom-call | bytes 19922944 | tf_op jit(solution)/shard_map/pallas_call | solution.py:85
  199.1 2.6 shard_map.122
  210.7 3.0 collective-permute-start.3
  221.7 3.1 %shard_map.124.vectors = bf16[2,64,512]{2,1,0:T(8,128)(2,1)S(1)} custom-call(s32[6]{0:T(128)S(1)} %stack.24.place, bf16[12,64,512]{2,1,0:T(8,128)(2,1)S(1)} %all_gather.3.extended, bf16[11,2,512,256]{3,2,1,0:T(8,128)(2,1)S(1)} %copy-done.1, bf16[11,2,512,256]{3,2,1,0:T(8,128)(2,1)} %collective-permute-done.6.packed.rest_3_.rest_2_), custom_call_target="tpu_custom_call" | custom-call | flops 134217728 | tf_op jit(solution)/shard_map/pallas_call | solution.py:391
  224.8 3.2 %shard_map.125.own = bf16[2,64,512]{2,1,0:T(8,128)(2,1)S(1)} custom-call(s32[6]{0:T(128)S(1)} %stack.24.place, bf16[2,64,512]{2,1,0:T(8,128)(2,1)S(1)} %maximum_select_fusion.image, bf16[1,64,512]{2,1,0:T(8,128)(2,1)S(1)} %collective-permute-done.4.inner, bf16[1,64,512]{2,1,0:T(8,128)(2,1)S(1)} %collective-permute-done.5.outer, ...), custom_call_target="tpu_custom_call" | custom-call | flops 134217728 | tf_op jit(solution)/shard_map/pallas_call | solution.py:400
  232.2 3.1 %shard_map.126.own = bf16[2,64,512]{2,1,0:T(8,128)(2,1)S(1)} custom-call(s32[6]{0:T(128)S(1)} %stack.24.place, bf16[2,64,512]{2,1,0:T(8,128)(2,1)S(1)} %shard_map.125.own, bf16[2,64,512]{2,1,0:T(8,128)(2,1)S(1)} %collective-permute-done.13.rest_0_, bf16[2,64,512]{2,1,0:T(8,128)(2,1)S(1)} %collective-permute-done.14.rest_1_, ...), custom_call_target="tpu_custom_call" | custom-call | flops 134217728 | tf_op jit(solution)/shard_map/pallas_call | solution.py:410
  236.0 7.0 %collective-permute-start.15 = (bf16[2,64,512]{2,1,0:T(8,128)(2,1)S(1)}, bf16[2,64,512]{2,1,0:T(8,128)(2,1)S(1)}, u32[]{:S(2)}, u32[]{:S(2)}) collective-permute-start(bf16[2,64,512]{2,1,0:T(8,128)(2,1)S(1)} %shard_map.126.own), channel_id=1, source_target_pairs={{0,2},{1,3},{4,6},{5,7},{8,10},{9,11},{12,14},{13,15},{2,0},{3,1},... | collective-permute-start | bytes 393224 | tf_op jit(solution)/shard_map/ppermute | solution.py:407
  243.0 5.1 %collective-permute-done.15.rest_0_ = bf16[2,64,512]{2,1,0:T(8,128)(2,1)S(1)} collective-permute-done((bf16[2,64,512]{2,1,0:T(8,128)(2,1)S(1)}, bf16[2,64,512]{2,1,0:T(8,128)(2,1)S(1)}, u32[]{:S(2)}, u32[]{:S(2)}) %collective-permute-start.15) | collective-permute-done | bytes 131104 | tf_op jit(solution)/shard_map/ppermute | solution.py:407
  248.0 3.1 %shard_map.127.own = bf16[2,64,512]{2,1,0:T(8,128)(2,1)S(1)} custom-call(s32[6]{0:T(128)S(1)} %stack.24.place, bf16[2,64,512]{2,1,0:T(8,128)(2,1)S(1)} %shard_map.126.own, bf16[2,64,512]{2,1,0:T(8,128)(2,1)S(1)} %collective-permute-done.15.rest_0_, bf16[2,64,512]{2,1,0:T(8,128)(2,1)S(1)} %collective-permute-done.16.rest_1_, ...), custom_call_target="tpu_custom_call" | custom-call | flops 134217728 | tf_op jit(solution)/shard_map/pallas_call | solution.py:410
  251.9 5.1 %collective-permute-start.17 = (bf16[2,64,512]{2,1,0:T(8,128)(2,1)S(1)}, bf16[2,64,512]{2,1,0:T(8,128)(2,1)S(1)}, u32[]{:S(2)}, u32[]{:S(2)}) collective-permute-start(bf16[2,64,512]{2,1,0:T(8,128)(2,1)S(1)} %shard_map.127.own), channel_id=1, source_target_pairs={{0,4},{1,5},{2,6},{3,7},{8,12},{9,13},{10,14},{11,15},{4,0},{5,1},... | collective-permute-start | bytes 393224 | tf_op jit(solution)/shard_map/ppermute | solution.py:407
  257.0 3.4 %collective-permute-done.17.rest_0_ = bf16[2,64,512]{2,1,0:T(8,128)(2,1)S(1)} collective-permute-done((bf16[2,64,512]{2,1,0:T(8,128)(2,1)S(1)}, bf16[2,64,512]{2,1,0:T(8,128)(2,1)S(1)}, u32[]{:S(2)}, u32[]{:S(2)}) %collective-permute-start.17) | collective-permute-done | bytes 131104 | tf_op jit(solution)/shard_map/ppermute | solution.py:407
  260.4 3.1 %shard_map.128.own = bf16[2,64,512]{2,1,0:T(8,128)(2,1)S(1)} custom-call(s32[6]{0:T(128)S(1)} %stack.24.place, bf16[2,64,512]{2,1,0:T(8,128)(2,1)S(1)} %shard_map.127.own, bf16[2,64,512]{2,1,0:T(8,128)(2,1)S(1)} %collective-permute-done.17.rest_0_, bf16[2,64,512]{2,1,0:T(8,128)(2,1)S(1)} %collective-permute-done.18.rest_1_, ...), custom_call_target="tpu_custom_call" | custom-call | flops 134217728 | tf_op jit(solution)/shard_map/pallas_call | solution.py:410
  263.5 2.6 collective-permute-start.19
  266.2 5.7 %collective-permute-done.19.rest_0_ = bf16[2,64,512]{2,1,0:T(8,128)(2,1)S(1)} collective-permute-done((bf16[2,64,512]{2,1,0:T(8,128)(2,1)S(1)}, bf16[2,64,512]{2,1,0:T(8,128)(2,1)S(1)}, u32[]{:S(2)}, u32[]{:S(2)}) %collective-permute-start.19) | collective-permute-done | bytes 131104 | tf_op jit(solution)/shard_map/ppermute | solution.py:407
  271.9 3.2 %shard_map.129 = (bf16[2,64,512]{2,1,0:T(8,128)(2,1)S(1)}, bf16[2,64,256]{2,1,0:T(8,128)(2,1)S(1)}, bf16[2,64,256]{2,1,0:T(8,128)(2,1)S(1)}) custom-call(s32[6]{0:T(128)S(1)} %stack.24.place, bf16[2,64,512]{2,1,0:T(8,128)(2,1)S(1)} %shard_map.128.own, bf16[2,64,512]{2,1,0:T(8,128)(2,1)S(1)} %collective-permute-done.19.rest_0_, ...), custom_call_target="tpu_custom_call" | custom-call | flops 134217728 | tf_op jit(solution)/shard_map/pallas_call | solution.py:417
  275.1 3.0 collective-permute-start.22
  279.4 4.2 %shard_map.130 = (f32[2,64,512]{2,1,0:T(8,128)S(1)}, f32[192,128]{1,0:T(8,128)S(1)}) custom-call(s32[6]{0:T(128)S(1)} %stack.24.place, s32[8,14]{1,0:T(8,128)S(1)} %add_add_fusion.1.table, bf16[12,64,512]{2,1,0:T(8,128)(2,1)S(1)} %all_gather.3.extended, bf16[2,64,512]{2,1,0:T(8,128)(2,1)S(1)} %maximum_select_fusion.image, ...), custom_call_target="tpu_custom_call" | custom-call | flops 469762048 | tf_op jit(solution)/shard_map/pallas_call | solution.py:272
  283.6 4.1 %shard_map.131 = f32[192,128]{1,0:T(8,128)S(1)} custom-call(s32[6]{0:T(128)S(1)} %stack.24.place, s32[8,14]{1,0:T(8,128)S(1)} %add_add_fusion.1.table, bf16[12,64,512]{2,1,0:T(8,128)(2,1)S(1)} %all_gather.3.extended, bf16[2,64,512]{2,1,0:T(8,128)(2,1)S(1)} %get-tuple-element.26.correction, bf16[2,64,512]{2,1,0:T(8,128)(2,1)S(1)} %collective-permute-done.21.near, ...), custom_call_target="tpu_custom_call" | custom-call | flops 469762048 | tf_op jit(solution)/shard_map/pallas_call | solution.py:279
  292.9 3.3 %collective-permute-done.26 = f32[192,128]{1,0:T(8,128)S(1)} collective-permute-done((f32[192,128]{1,0:T(8,128)S(1)}, f32[192,128]{1,0:T(8,128)S(1)}, u32[]{:S(2)}, u32[]{:S(2)}) %collective-permute-start.26) | collective-permute-done | bytes 98336 | tf_op jit(solution)/shard_map/ppermute | solution.py:332
  296.2 3.7 %collective-permute-start.27 = (f32[192,128]{1,0:T(8,128)S(1)}, f32[192,128]{1,0:T(8,128)S(1)}, u32[]{:S(2)}, u32[]{:S(2)}) collective-permute-start(f32[192,128]{1,0:T(8,128)S(1)} %select_add_fusion), channel_id=1, source_target_pairs={{0,8},{2,10},{4,12},{6,14},{8,0},{10,2},{12,4},{14,6},{1,9},{3,11}... | collective-permute-start | bytes 294920 | tf_op jit(solution)/shard_map/ppermute | solution.py:435
  300.8 4.6 %collective-permute-done.27 = f32[192,128]{1,0:T(8,128)S(1)} collective-permute-done((f32[192,128]{1,0:T(8,128)S(1)}, f32[192,128]{1,0:T(8,128)S(1)}, u32[]{:S(2)}, u32[]{:S(2)}) %collective-permute-start.27) | collective-permute-done | bytes 98336 | tf_op jit(solution)/shard_map/ppermute | solution.py:435
  (82 shorter events, 39.1 us)
Async XLA Ops:
  177.3 41.8 %collective-permute-start.6 = (bf16[11,2,512,256]{3,2,1,0:T(8,128)(2,1)}, bf16[11,2,512,256]{3,2,1,0:T(8,128)(2,1)}, u32[]{:S(2)}, u32[]{:S(2)}) collective-permute-start(bf16[11,2,512,256]{3,2,1,0:T(8,128)(2,1)} %shard_map.123), channel_id=1, source_target_pairs={{0,1},{1,0},{2,3},{3,2},{4,5},{5,4},{6,7},{7,6},{8,9},{9,8},{10,11... | collective-permute-start | bytes 17301512 | tf_op jit(solution)/shard_map/ppermute | solution.py:303
  177.8 101.6 %collective-permute-start.23 = (bf16[16,512,256]{2,1,0:T(8,128)(2,1)}, bf16[16,512,256]{2,1,0:T(8,128)(2,1)}, u32[]{:S(2)}, u32[]{:S(2)}) collective-permute-start(bf16[16,512,256]{2,1,0:T(8,128)(2,1)} %rest_0_.1), channel_id=1, source_target_pairs={{0,1},{1,0},{2,3},{3,2},{4,5},{5,4},{6,7},{7,6},{8,9},{9,8},{10,11... | collective-permute-start | bytes 12582920 | tf_op jit(solution)/shard_map/ppermute | solution.py:303
  177.9 18.7 %collective-permute-start.1 = (bf16[4,64,256]{2,1,0:T(8,128)(2,1)S(1)}, bf16[4,64,256]{2,1,0:T(8,128)(2,1)S(1)}, u32[]{:S(2)}, u32[]{:S(2)}) collective-permute-start(bf16[4,64,256]{2,1,0:T(8,128)(2,1)S(1)} %copy-done.4), channel_id=1, source_target_pairs={{2,0},{4,2},{6,4},{8,6},{10,8},{12,10},{14,12},{3,1},{5,3},{7,5},{... | collective-permute-start | bytes 393224 | tf_op jit(solution)/shard_map/ppermute | solution.py:309
  179.2 17.5 %collective-permute-start = (bf16[4,64,256]{2,1,0:T(8,128)(2,1)S(1)}, bf16[4,64,256]{2,1,0:T(8,128)(2,1)S(1)}, u32[]{:S(2)}, u32[]{:S(2)}) collective-permute-start(bf16[4,64,256]{2,1,0:T(8,128)(2,1)S(1)} %copy-done.4), channel_id=1, source_target_pairs={{0,2},{2,4},{4,6},{6,8},{8,10},{10,12},{12,14},{1,3},{3,5},{5,7},{... | collective-permute-start | bytes 393224 | tf_op jit(solution)/shard_map/ppermute | solution.py:309
  184.8 11.7 %collective-permute-start.2 = (s32[4,14]{1,0:T(4,128)S(1)}, s32[4,14]{1,0:T(4,128)S(1)}, u32[]{:S(2)}, u32[]{:S(2)}) collective-permute-start(s32[4,14]{1,0:T(4,128)S(1)} %pad_add_fusion.table), channel_id=1, source_target_pairs={{0,2},{2,4},{4,6},{6,8},{8,10},{10,12},{12,14},{1,3},{3,5},{5,7},{... | collective-permute-start | bytes 680 | tf_op jit(solution)/shard_map/ppermute | solution.py:309
  205.0 4.8 %collective-permute-start.11 = (f32[64,64]{1,0:T(8,128)S(1)}, f32[64,64]{1,0:T(8,128)S(1)}, u32[]{:S(2)}, u32[]{:S(2)}) collective-permute-start(f32[64,64]{1,0:T(8,128)S(1)} %add.76), channel_id=1, source_target_pairs={{0,6},{1,15},{2,4},{3,13},{4,2},{5,11},{6,0},{7,9},{8,14},{9,7},{1... | collective-permute-start | bytes 49160 | tf_op jit(solution)/shard_map/ppermute | solution.py:332
  206.6 4.0 %collective-permute-start.10 = (f32[64,64]{1,0:T(8,128)S(1)}, f32[64,64]{1,0:T(8,128)S(1)}, u32[]{:S(2)}, u32[]{:S(2)}) collective-permute-start(f32[64,64]{1,0:T(8,128)S(1)} %add.76), channel_id=1, source_target_pairs={{0,4},{1,13},{2,6},{3,15},{4,0},{5,9},{6,2},{7,11},{8,12},{9,5},{1... | collective-permute-start | bytes 49160 | tf_op jit(solution)/shard_map/ppermute | solution.py:332
  207.1 6.6 %collective-permute-start.9 = (f32[64,64]{1,0:T(8,128)S(1)}, f32[64,64]{1,0:T(8,128)S(1)}, u32[]{:S(2)}, u32[]{:S(2)}) collective-permute-start(f32[64,64]{1,0:T(8,128)S(1)} %add.76), channel_id=1, source_target_pairs={{0,2},{1,11},{2,0},{3,9},{4,6},{5,15},{6,4},{7,13},{8,10},{9,3},{1... | collective-permute-start | bytes 49160 | tf_op jit(solution)/shard_map/ppermute | solution.py:332
  209.8 3.9 %collective-permute-start.8 = (f32[64,64]{1,0:T(8,128)S(1)}, f32[64,64]{1,0:T(8,128)S(1)}, u32[]{:S(2)}, u32[]{:S(2)}) collective-permute-start(f32[64,64]{1,0:T(8,128)S(1)} %add.76), channel_id=1, source_target_pairs={{1,9},{3,11},{5,13},{7,15},{9,1},{11,3},{13,5},{15,7},{17,25},{19,... | collective-permute-start | bytes 49160 | tf_op jit(solution)/shard_map/ppermute | solution.py:332
  210.7 5.6 %collective-permute-start.3 = (bf16[2,64,256]{2,1,0:T(8,128)(2,1)S(1)}, bf16[2,64,256]{2,1,0:T(8,128)(2,1)S(1)}, u32[]{:S(2)}, u32[]{:S(2)}) collective-permute-start(bf16[2,64,256]{2,1,0:T(8,128)(2,1)S(1)} %get-tuple-element.20), channel_id=1, source_target_pairs={{0,1},{1,0},{2,3},{3,2},{4,5},{5,4},{6,7},{7,6},{8,9},{9,8},{10,11... | collective-permute-start | bytes 196616 | tf_op jit(solution)/shard_map/ppermute | solution.py:303
  213.7 5.4 %collective-permute-start.12 = (f32[64,64]{1,0:T(8,128)S(1)}, f32[64,64]{1,0:T(8,128)S(1)}, u32[]{:S(2)}, u32[]{:S(2)}) collective-permute-start(f32[64,64]{1,0:T(8,128)S(1)} %add_add_fusion), channel_id=1, source_target_pairs={{0,1},{1,0},{2,3},{3,2},{4,5},{5,4},{6,7},{7,6},{8,9},{9,8},{10,11... | collective-permute-start | bytes 49160 | tf_op jit(solution)/shard_map/ppermute | solution.py:303
  216.3 8.5 %collective-permute-start.5 = (bf16[1,64,512]{2,1,0:T(8,128)(2,1)S(1)}, bf16[1,64,512]{2,1,0:T(8,128)(2,1)S(1)}, u32[]{:S(2)}, u32[]{:S(2)}) collective-permute-start(bf16[1,64,512]{2,1,0:T(8,128)(2,1)S(1)} %get-tuple-element.31), channel_id=1, source_target_pairs={{1,2},{3,4},{5,6},{7,8},{9,10},{11,12},{13,14},{2,1},{4,3},{6,5},{... | collective-permute-start | bytes 196616 | tf_op jit(solution)/shard_map/ppermute | solution.py:399
  217.0 7.9 %collective-permute-start.4 = (bf16[1,64,512]{2,1,0:T(8,128)(2,1)S(1)}, bf16[1,64,512]{2,1,0:T(8,128)(2,1)S(1)}, u32[]{:S(2)}, u32[]{:S(2)}) collective-permute-start(bf16[1,64,512]{2,1,0:T(8,128)(2,1)S(1)} %get-tuple-element.32), channel_id=1, source_target_pairs={{0,1},{1,0},{2,3},{3,2},{4,5},{5,4},{6,7},{7,6},{8,9},{9,8},{10,11... | collective-permute-start | bytes 196616 | tf_op jit(solution)/shard_map/ppermute | solution.py:303
  235.3 7.6 %collective-permute-start.16 = (bf16[2,64,512]{2,1,0:T(8,128)(2,1)S(1)}, bf16[2,64,512]{2,1,0:T(8,128)(2,1)S(1)}, u32[]{:S(2)}, u32[]{:S(2)}) collective-permute-start(bf16[2,64,512]{2,1,0:T(8,128)(2,1)S(1)} %shard_map.126.own), channel_id=1, source_target_pairs={{2,4},{3,5},{6,8},{7,9},{10,12},{11,13},{4,2},{5,3},{8,6},{9,7},{1... | collective-permute-start | bytes 393224 | tf_op jit(solution)/shard_map/ppermute | solution.py:407
  236.0 12.1 %collective-permute-start.15 = (bf16[2,64,512]{2,1,0:T(8,128)(2,1)S(1)}, bf16[2,64,512]{2,1,0:T(8,128)(2,1)S(1)}, u32[]{:S(2)}, u32[]{:S(2)}) collective-permute-start(bf16[2,64,512]{2,1,0:T(8,128)(2,1)S(1)} %shard_map.126.own), channel_id=1, source_target_pairs={{0,2},{1,3},{4,6},{5,7},{8,10},{9,11},{12,14},{13,15},{2,0},{3,1},... | collective-permute-start | bytes 393224 | tf_op jit(solution)/shard_map/ppermute | solution.py:407
  251.2 5.8 %collective-permute-start.18 = (bf16[2,64,512]{2,1,0:T(8,128)(2,1)S(1)}, bf16[2,64,512]{2,1,0:T(8,128)(2,1)S(1)}, u32[]{:S(2)}, u32[]{:S(2)}) collective-permute-start(bf16[2,64,512]{2,1,0:T(8,128)(2,1)S(1)} %shard_map.127.own), channel_id=1, source_target_pairs={{4,8},{5,9},{6,10},{7,11},{8,4},{9,5},{10,6},{11,7},{20,24},{21,25... | collective-permute-start | bytes 393224 | tf_op jit(solution)/shard_map/ppermute | solution.py:407
  251.9 8.5 %collective-permute-start.17 = (bf16[2,64,512]{2,1,0:T(8,128)(2,1)S(1)}, bf16[2,64,512]{2,1,0:T(8,128)(2,1)S(1)}, u32[]{:S(2)}, u32[]{:S(2)}) collective-permute-start(bf16[2,64,512]{2,1,0:T(8,128)(2,1)S(1)} %shard_map.127.own), channel_id=1, source_target_pairs={{0,4},{1,5},{2,6},{3,7},{8,12},{9,13},{10,14},{11,15},{4,0},{5,1},... | collective-permute-start | bytes 393224 | tf_op jit(solution)/shard_map/ppermute | solution.py:407
  263.5 8.3 %collective-permute-start.19 = (bf16[2,64,512]{2,1,0:T(8,128)(2,1)S(1)}, bf16[2,64,512]{2,1,0:T(8,128)(2,1)S(1)}, u32[]{:S(2)}, u32[]{:S(2)}) collective-permute-start(bf16[2,64,512]{2,1,0:T(8,128)(2,1)S(1)} %shard_map.128.own), channel_id=1, source_target_pairs={{0,8},{1,9},{2,10},{3,11},{4,12},{5,13},{6,14},{7,15},{8,0},{9,1},... | collective-permute-start | bytes 393224 | tf_op jit(solution)/shard_map/ppermute | solution.py:407
  275.1 8.5 %collective-permute-start.22 = (bf16[2,64,512]{2,1,0:T(8,128)(2,1)S(1)}, bf16[2,64,512]{2,1,0:T(8,128)(2,1)S(1)}, u32[]{:S(2)}, u32[]{:S(2)}) collective-permute-start(bf16[2,64,512]{2,1,0:T(8,128)(2,1)S(1)} %get-tuple-element.26.correction), channel_id=1, source_target_pairs={{0,2},{1,3},{2,4},{3,5},{4,6},{5,7},{6,8},{7,9},{8,10},{9,11},{10,... | collective-permute-start | bytes 393224 | tf_op jit(solution)/shard_map/ppermute | solution.py:309
  278.0 5.5 %collective-permute-start.21 = (bf16[2,64,512]{2,1,0:T(8,128)(2,1)S(1)}, bf16[2,64,512]{2,1,0:T(8,128)(2,1)S(1)}, u32[]{:S(2)}, u32[]{:S(2)}) collective-permute-start(bf16[2,64,512]{2,1,0:T(8,128)(2,1)S(1)} %get-tuple-element.26.correction), channel_id=1, source_target_pairs={{0,1},{1,2},{2,3},{3,4},{4,5},{5,6},{6,7},{7,8},{8,9},{9,10},{10,1... | collective-permute-start | bytes 393224 | tf_op jit(solution)/shard_map/ppermute | solution.py:309
  290.5 5.7 %collective-permute-start.26 = (f32[192,128]{1,0:T(8,128)S(1)}, f32[192,128]{1,0:T(8,128)S(1)}, u32[]{:S(2)}, u32[]{:S(2)}) collective-permute-start(f32[192,128]{1,0:T(8,128)S(1)} %add.81), channel_id=1, source_target_pairs={{0,2},{1,7},{2,0},{3,5},{4,6},{5,3},{6,4},{7,1},{8,10},{9,15},{10,... | collective-permute-start | bytes 294920 | tf_op jit(solution)/shard_map/ppermute | solution.py:332
  292.2 4.0 %collective-permute-start.25 = (f32[192,128]{1,0:T(8,128)S(1)}, f32[192,128]{1,0:T(8,128)S(1)}, u32[]{:S(2)}, u32[]{:S(2)}) collective-permute-start(f32[192,128]{1,0:T(8,128)S(1)} %add.81), channel_id=1, source_target_pairs={{1,5},{3,7},{5,1},{7,3},{9,13},{11,15},{13,9},{15,11},{17,21},{19,... | collective-permute-start | bytes 294920 | tf_op jit(solution)/shard_map/ppermute | solution.py:332
  296.2 9.2 %collective-permute-start.27 = (f32[192,128]{1,0:T(8,128)S(1)}, f32[192,128]{1,0:T(8,128)S(1)}, u32[]{:S(2)}, u32[]{:S(2)}) collective-permute-start(f32[192,128]{1,0:T(8,128)S(1)} %select_add_fusion), channel_id=1, source_target_pairs={{0,8},{2,10},{4,12},{6,14},{8,0},{10,2},{12,4},{14,6},{1,9},{3,11}... | collective-permute-start | bytes 294920 | tf_op jit(solution)/shard_map/ppermute | solution.py:435
  299.9 5.8 %collective-permute-start.20 = (bf16[2,64,256]{2,1,0:T(8,128)(2,1)S(1)}, bf16[2,64,256]{2,1,0:T(8,128)(2,1)S(1)}, u32[]{:S(2)}, u32[]{:S(2)}) collective-permute-start(bf16[2,64,256]{2,1,0:T(8,128)(2,1)S(1)} %get-tuple-element.24), channel_id=1, source_target_pairs={{0,1},{1,0},{2,3},{3,2},{4,5},{5,4},{6,7},{7,6},{8,9},{9,8},{10,11... | collective-permute-start | bytes 196616 | tf_op jit(solution)/shard_map/ppermute | solution.py:303
  (14 other events, 787.0 us)

commit v5 on v4

--- a/solution.py
+++ b/solution.py
@@ -52,45 +52,82 @@
     return pltpu.with_memory_space_constraint(operand, pltpu.HBM)
 
 
-def fetch_body(levels, other, place, lower, upper, final, *rest):
-    blocks = rest[0] if len(rest) == 4 else None
-    fetched, sem = rest[-2 if blocks is None else -3], rest[-1]
-    count = fetched.shape[1]
-    which = 1 - place[0] if other else place[0]
-    slabs = pl.ds(which * count, count)
-    pairs = []
-    for level in range(levels):
-        for ref in (lower, upper):
-            pairs.append((ref.at[level, slabs], fetched.at[len(pairs)]))
-    pairs.append((final.at[slabs], fetched.at[len(pairs)]))
-    if blocks is not None:
-        pairs.insert(0, (blocks, rest[-2]))
-    copies = [pltpu.make_async_copy(*pair, sem.at[k]) for k, pair in enumerate(pairs)]
+def weight_copies(level, place, sources, weights, sem):
+    count = weights.shape[2]
+    slabs = pl.ds(place[0] * count, count)
+    copies = []
+    for side in range(2):
+        for part in range(2):
+            source = sources[2 * side + part].at[level, slabs]
+            copies.append(pltpu.make_async_copy(source, weights.at[side, part], sem.at[side, part]))
+    return copies
+
+
+def run(copies):
     for copy in copies:
         copy.start()
     for copy in copies:
         copy.wait()
 
 
-def fetch(place, lower, upper, final, levels, blocks=None):
-    _, slabs, rows, half = lower.shape
-    shape = (2 * levels + 1, slabs // 2, rows, half)
-    operands = [in_hbm(x) for x in (lower, upper, final)]
-    out_shape = [pltpu.VMEM(shape, bf16)]
-    size = 2 * 2 * (2 * levels + 1) * (slabs // 2) * rows * half
-    if blocks is not None:
-        operands.append(in_hbm(blocks))
-        out_shape.append(pltpu.VMEM(blocks.shape, bf16))
-        size += 2 * 2 * blocks.size
+def load_body(level, place, token, *rest):
+    *sources, weights, sem = rest
+    run(weight_copies(level, place, sources, weights, sem))
+
+
+def load_last_body(level, place, token, *rest):
+    *sources, final, final_other, weights, sem = rest
+    count = weights.shape[2]
+    slabs = pl.ds(place[0] * count, count)
+    above = place[1 + level] == 0
+
+    def copy(source, side, part):
+        return pltpu.make_async_copy(source, weights.at[side, part], sem.at[side, part])
+
+    for part in range(2):
+        pl.when(above)(lambda: copy(sources[2 + part].at[level, slabs], 0, part).start())
+        pl.when(jnp.logical_not(above))(lambda: copy(sources[part].at[level, slabs], 0, part).start())
+    finals = [copy(ref.at[slabs], 1, part) for part, ref in enumerate((final, final_other))]
+    for each in finals:
+        each.start()
+    for part in range(2):
+        copy(sources[part].at[level, slabs], 0, part).wait()
+    for each in finals:
+        each.wait()
+
+
+def load(body, place, token, sources):
+    _, slabs, rows, half = sources[0].shape
+    shape = (2, 2, slabs // 2, rows, half)
     return pl.pallas_call(
-        functools.partial(fetch_body, levels, blocks is None),
-        out_shape=out_shape,
-        in_specs=[SMEM] + [ANY] * len(operands),
-        out_specs=[ANY] * len(out_shape),
-        scratch_shapes=[pltpu.SemaphoreType.DMA((2 * levels + 2,))],
-        compiler_params=pltpu.CompilerParams(vmem_limit_bytes=2 * MIB),
-        cost_estimate=pl.CostEstimate(flops=0, bytes_accessed=size, transcendentals=0),
-    )(place, *operands)
+        body,
+        out_shape=pltpu.VMEM(shape, bf16),
+        in_specs=[SMEM] + [ANY] * (1 + len(sources)),
+        out_specs=VMEM,
+        scratch_shapes=[pltpu.SemaphoreType.DMA((2, 2))],
+        compiler_params=pltpu.CompilerParams(vmem_limit_bytes=4 * MIB),
+        cost_estimate=pl.CostEstimate(flops=0, bytes_accessed=8 * slabs * rows * half, transcendentals=0),
+    )(place, token, *[in_hbm(x) for x in sources])
+
+
+def load_whole_body(place, token, *rest):
+    count = len(rest) // 2
+    sources, targets, sem = rest[:count], rest[count:-1], rest[-1]
+    run([pltpu.make_async_copy(*pair, sem.at[k]) for k, pair in enumerate(zip(sources, targets))])
+
+
+def load_whole(place, token, arrays):
+    return pl.pallas_call(
+        load_whole_body,
+        out_shape=[pltpu.VMEM(x.shape, x.dtype) for x in arrays],
+        in_specs=[SMEM] + [ANY] * (1 + len(arrays)),
+        out_specs=[VMEM] * len(arrays),
+        scratch_shapes=[pltpu.SemaphoreType.DMA((len(arrays),))],
+        compiler_params=pltpu.CompilerParams(vmem_limit_bytes=12 * MIB),
+        cost_estimate=pl.CostEstimate(
+            flops=0, bytes_accessed=sum(2 * x.size for x in arrays), transcendentals=0
+        ),
+    )(place, token, *[in_hbm(x) for x in arrays])
 
 
 def image_body(place, table, extended, vectors, blocks, keep, send, quotient, image):
@@ -125,66 +162,88 @@
     )(place, table, extended, vectors, blocks)
 
 
-def both_parts(place, mine, packed):
-    half = mine.shape[-1]
-    return (columns(place[0], half), mine), (columns(1 - place[0], half), packed)
-
-
-def first_vectors_body(place, extended, mine, packed, out):
-    count = out.shape[0]
+def both_parts(place, half):
+    return columns(place[0], half), columns(1 - place[0], half)
+
+
+def first_vectors_body(place, token, extended, *rest):
+    *sources, out, weights, sem = rest
+    count, half = out.shape[0], weights.shape[-1]
     first = extended.shape[0] // 3 + count * place[0]
-    for cols, weights in both_parts(place, mine, packed):
+    copies = weight_copies(0, place, sources, weights, sem)
+    for copy in copies:
+        copy.start()
+    for part, cols in enumerate(both_parts(place, half)):
+        copies[part].wait()
+        copies[2 + part].wait()
         for slab in range(count):
             own = first + slab
-            summed = dot(extended[own - 1], weights[0, slab]) + dot(extended[own + 1], weights[1, slab])
+            summed = dot(extended[own - 1], weights[0, part, slab])
+            summed = summed + dot(extended[own + 1], weights[1, part, slab])
             out[slab, :, cols] = (extended[own, :, cols].astype(f32) - summed).astype(bf16)
 
 
-def first_body(place, image, inner, outer, vectors, quotient, mine, packed, out):
-    count = image.shape[0]
+def first_body(place, image, inner, outer, vectors, quotient, *rest):
+    *sources, out, weights, sem = rest
+    count, half = out.shape[0], weights.shape[-1]
+    copies = weight_copies(0, place, sources, weights, sem)
+    for copy in copies:
+        copy.start()
     odd = place[0] == 1
     below = [jnp.where(odd, inner[0], outer[0])] + [image[slab] for slab in range(count - 1)]
     above = [image[slab] for slab in range(1, count)] + [jnp.where(odd, outer[0], inner[0])]
     high = quotient[...].astype(bf16)
     low = (quotient[...] - high.astype(f32)).astype(bf16)
     factors = (high.T, low.T)
-    for cols, weights in both_parts(place, mine, packed):
+    for part, cols in enumerate(both_parts(place, half)):
+        copies[part].wait()
+        copies[2 + part].wait()
         for slab in range(count):
-            summed = dot(below[slab], weights[0, slab]) + dot(above[slab], weights[1, slab])
+            summed = dot(below[slab], weights[0, part, slab]) + dot(above[slab], weights[1, part, slab])
             for factor in factors:
                 summed = summed + dot(factor, vectors[slab, :, cols])
             out[slab, :, cols] = (image[slab, :, cols].astype(f32) - summed).astype(bf16)
 
 
-def reduce_rows(level, place, own, partners, mine, packed, out):
-    bit = place[1 + level]
-    for cols, weights in both_parts(place, mine, packed):
+def reduce_rows(place, own, partners, sides, weights, out):
+    for part, cols in enumerate(both_parts(place, weights.shape[-1])):
         for slab in range(own.shape[0]):
             summed = None
-            for side, rows in zip((1 - bit, bit), partners):
-                term = dot(rows[slab], weights[2 * level + side, slab])
+            for side, rows in zip(sides, partners):
+                term = dot(rows[slab], weights[side, part, slab])
                 summed = term if summed is None else summed + term
             out[slab, :, cols] = (own[slab, :, cols].astype(f32) - summed).astype(bf16)
 
 
-def level_body(level, place, own, *rest):
-    *partners, mine, packed, out = rest
-    reduce_rows(level, place, own, partners, mine, packed, out)
-
-
-def product(place, rows, mine, packed, whole, parts):
-    last = mine.shape[0] - 1
-    for (cols, weights), target in zip(both_parts(place, mine, packed), parts):
+def second_body(place, own, inner, outer, weights, out):
+    reduce_rows(place, own, (inner, outer), (1 - place[0], place[0]), weights, out)
+
+
+def level_body(place, own, below, above, weights, out):
+    reduce_rows(place, own, (below, above), (0, 1), weights, out)
+
+
+def product(place, rows, weights, whole, targets):
+    for part, cols in enumerate(both_parts(place, weights.shape[-1])):
         for slab in range(whole.shape[0]):
-            result = dot(rows[slab], weights[last, slab]).astype(bf16)
-            target[slab] = result
+            result = dot(rows[slab], weights[part, slab]).astype(bf16)
+            targets[part][slab] = result
             whole[slab, :, cols] = result
 
 
-def last_body(level, place, own, *rest):
-    *partners, mine, packed, whole, keep, send, rows = rest
-    reduce_rows(level, place, own, partners, mine, packed, rows)
-    product(place, rows, mine, packed, whole, (keep, send))
+def last_body(place, own, other, weights, whole, keep, send, rows):
+    reduce_rows(place, own, (other,), (0,), weights, rows)
+    product(place, rows, weights.at[1], whole, (keep, send))
+
+
+def final_body(place, own, final, final_other, whole, keep, send, weights, sem):
+    count = own.shape[0]
+    slabs = pl.ds(place[0] * count, count)
+    run([
+        pltpu.make_async_copy(ref.at[slabs], weights.at[part], sem.at[part])
+        for part, ref in enumerate((final, final_other))
+    ])
+    product(place, own, weights, whole, (keep, send))
 
 
 def level_flops(operand, products):
@@ -360,26 +419,28 @@
     steps = [max(2**l // own_count, 1) for l in levels]
     place = jnp.stack([core] + [link // step % 2 for step in steps]).astype(jnp.int32)
 
-    below, above = along(vectors, "slab", 1), along(vectors, "slab", -1)
     slab_ids = slab * slab_count + jnp.arange(slab_count, dtype=jnp.int32)[:, None]
     near = jnp.broadcast_to(jnp.arange(-1, 2, dtype=jnp.int32), (slab_count, 3))
     table = jnp.concatenate([near, far_source - slab_ids, slab_blocks, far_block], 1)
-    tables = jnp.concatenate([along(table, "slab", 1), table], 0)
-
-    (theirs,) = fetch(place, level_lower, level_upper, level_final, len(levels))
-    packed = swapped(theirs)
-    mine, held_blocks = fetch(place, level_lower, level_upper, level_final, len(levels), blocks)
-    others = swapped(blocks)
-    mine, packed, held_blocks, others = (in_vmem(x) for x in (mine, packed, held_blocks, others))
-
-    halo = jnp.concatenate([below, vectors, above], 0)
-    halo, tables = lax.optimization_barrier((halo, tables))
-    extended = lax.all_gather(halo, "vec", axis=2, tiled=True)
-
-    keep, send, quotient = image_halves(place, table, extended, vectors, held_blocks)
+    flat = vectors.reshape(slab_count * rows, half)
+    note = jnp.pad(table.astype(bf16), ((0, 16 - slab_count), (0, half - table.shape[1])))
+    above = along(vectors, "slab", -1)
+    lifted = along(jnp.concatenate([flat, note], 0), "slab", 1)
+    below = lifted[: slab_count * rows].reshape(vectors.shape)
+    lower_table = lifted[slab_count * rows :][:slab_count, : table.shape[1]].astype(jnp.int32)
+    tables = jnp.concatenate([lower_table, table], 0)
+
+    weights = (level_lower, swapped(level_lower), level_upper, swapped(level_upper))
+    (held_blocks,) = load_whole(place, place, [blocks])
+    extended = lax.all_gather(jnp.concatenate([below, vectors, above], 0), "vec", axis=2, tiled=True)
+    keep, send, quotient = image_halves(place, table, extended, vectors, in_vmem(held_blocks))
     received, quotient = swapped(send), quotient + swapped(quotient)
     image = jnp.where(core == 0, jnp.concatenate([keep, received], 2), jnp.concatenate([received, keep], 2))
-
+    image, quotient = lax.optimization_barrier((image, quotient))
+
+    inner_route, outer_route = pair_routes(1)
+    outer = lax.ppermute(lax.dynamic_slice_in_dim(image, (own_count - 1) * core, 1), CHAIN, outer_route)
+    inner = swapped(lax.dynamic_slice_in_dim(image, (own_count - 1) * (1 - core), 1))
     reach = 1
     while reach < slabs:
         radix = min(8, slabs // reach)
@@ -388,39 +449,66 @@
         reach *= radix
     quotient = quotient / rows_total
 
+    buffers = [pltpu.VMEM((2, 2, own_count, width, half), bf16), pltpu.SemaphoreType.DMA((2, 2))]
+    held_weights = [in_hbm(x) for x in weights]
     vectors_1 = kernel_call(
         first_vectors_body,
         struct(image.shape),
-        [SMEM] + [VMEM] * 3,
+        [SMEM, ANY, VMEM] + [ANY] * 4,
+        buffers,
         flops=level_flops(image, 2),
-    )(place, extended, mine, packed)
-    inner_route, outer_route = pair_routes(1)
-    inner = swapped(lax.dynamic_slice_in_dim(image, (own_count - 1) * (1 - core), 1))
-    outer = lax.ppermute(lax.dynamic_slice_in_dim(image, (own_count - 1) * core, 1), CHAIN, outer_route)
+        size=8 * own_count * width * half,
+    )(place, image, extended, *held_weights)
     residual = kernel_call(
         first_body,
         struct(image.shape),
-        [SMEM] + [VMEM] * 7,
+        [SMEM] + [VMEM] * 5 + [ANY] * 4,
+        buffers,
         flops=level_flops(image, 2),
-    )(place, image, inner, outer, vectors_1, quotient, mine, packed)
+        size=8 * own_count * width * half,
+    )(place, image, inner, outer, vectors_1, quotient, *held_weights)
+
+    finals = (level_final, swapped(level_final))
+    others = swapped(blocks)
+    part = struct((own_count, rows, half))
+    ends = (struct(residual.shape), part, part)
+    one_partner = chain == 2 * steps[-1]
     for level, step in zip(levels[1:], steps[1:]):
-        partners = [lax.ppermute(residual, CHAIN, route) for route in reversed(pair_routes(step))][::-1]
-        inputs = [SMEM] + [VMEM] * (3 + len(partners))
-        if level != levels[-1]:
-            residual = kernel_call(
-                functools.partial(level_body, level),
-                struct(residual.shape),
-                inputs,
+        last = level == levels[-1]
+        if last:
+            held_blocks, others = load_whole(place, residual, [blocks, others])
+        if last and one_partner:
+            matrices = load(functools.partial(load_last_body, level), place, residual, weights + finals)
+            (route,) = pair_routes(step)
+            other = lax.ppermute(residual, CHAIN, route)
+            correction, keep, send = kernel_call(
+                last_body,
+                ends,
+                [SMEM] + [VMEM] * 3,
+                [pltpu.VMEM(residual.shape, bf16)],
                 flops=level_flops(residual, 2),
-            )(place, residual, *partners, mine, packed)
-    part = struct((own_count, rows, half))
-    correction, keep, send = kernel_call(
-        functools.partial(last_body, levels[-1]),
-        (struct(residual.shape), part, part),
-        inputs,
-        [pltpu.VMEM(residual.shape, bf16)],
-        flops=level_flops(residual, 2),
-    )(place, residual, *partners, mine, packed)
+            )(place, residual, other, in_vmem(matrices))
+            break
+        matrices = load(functools.partial(load_body, level), place, residual, weights)
+        if step == 1:
+            partners = [lax.ppermute(residual, CHAIN, outer_route), swapped(residual)][::-1]
+        else:
+            partners = [along(residual, CHAIN, step), along(residual, CHAIN, -step)]
+        residual = kernel_call(
+            second_body if step == 1 else level_body,
+            struct(residual.shape),
+            [SMEM] + [VMEM] * 4,
+            flops=level_flops(residual, 2),
+        )(place, residual, *partners, in_vmem(matrices))
+    if not one_partner:
+        correction, keep, send = kernel_call(
+            final_body,
+            ends,
+            [SMEM, VMEM, ANY, ANY],
+            [pltpu.VMEM((2, own_count, width, half), bf16), pltpu.SemaphoreType.DMA((2,))],
+            flops=level_flops(residual, 1),
+        )(place, residual, *[in_hbm(x) for x in finals])
+    held_blocks, others = in_vmem(held_blocks), in_vmem(others)
 
     far, near = along(correction, CHAIN, 2), along(correction, CHAIN, 1)
     part = pencil_parts(place, tables, extended, image, correction, near, far, held_blocks, others)

time: 309 us -> 126 us (0.41)
  Pallas kernels: 212 us -> 33.5 us
  local copies, waits for them, and re-layouts: 7.21 us -> 1.12 us
  starting transfers between devices: 56.5 us -> 52.7 us
    pallas_call x8 -> x12, Pallas kernels: 200 us -> 24.5 us  [the longest x4 8.38 us: load(): pl.pallas_call(body, out_shape=pltpu.VMEM(shape, bf16), in_specs=[SMEM] +...]
    ppermute x7 -> x2, starting transfers between devices: 19.2 us -> 1.28 us  [the longest x1 0.66 us: on_device(): lax.ppermute(residual, CHAIN, outer_route)]
    ppermute x7 -> x2, waiting for transfers between devices: 15.2 us -> 3.92 us  [the longest x1 3.91 us: on_device(): other = lax.ppermute(residual, CHAIN, route)]
    ppermute x5 -> x8, waiting for transfers between devices: 0.01 us -> 10.5 us  [along(): return lax.ppermute(operand, axis, route)]
    ppermute x5 -> x8, starting transfers between devices: 15.8 us -> 25.2 us  [along(): return lax.ppermute(operand, axis, route)]
    unnamed x18 -> x12, local copies, waits for them, and re-layouts: 7.11 us -> 1.01 us
    ppermute x9 -> x12, starting transfers between devices: 10.6 us -> 13.3 us  [swapped(): return lax.ppermute(operand, 'vec', SWAP)]
  transfers between devices with their start and end apart: 29 -> 30, of which waited for: 11 -> 13; matrix products, arithmetic and copies ran while one was open for 0% -> 3% of each run, Pallas kernels for 10% -> 23%
where the time goes in v5:
time: 126 us
  starting transfers between devices  52.7 us (42%)
  Pallas kernels  33.5 us (27%)
  waiting for transfers between devices  28.5 us (23%)
  blocking collectives  4.73 us (4%)
  other arithmetic  3.35 us (3%)
  between operations  1.76 us (1%)
    ppermute x8, starting transfers between devices, along(): return lax.ppermute(operand, axis, route)  25.2 us
    ppermute x12, starting transfers between devices, swapped(): return lax.ppermute(operand, 'vec', SWAP)  13.3 us
    ppermute x8, waiting for transfers between devices, along(): return lax.ppermute(operand, axis, route)  10.5 us
    ppermute x6, starting transfers between devices, shared_out(): received.append(lax.ppermute(part, CHAIN, route))  9.47 us
    pallas_call x4, Pallas kernels, load(): pl.pallas_call(body, out_shape=pltpu.VMEM(shape, bf16), in_specs=[SMEM] +...  8.38 us
    pallas_call x2, Pallas kernels, load_whole(): pl.pallas_call(load_whole_body, out_shape=[pltpu.VMEM(x.shape, x.dtype) f...  6.76 us
    ppermute x6, waiting for transfers between devices, shared_out(): received.append(lax.ppermute(part, CHAIN, route))  5.07 us
    all_gather x1, blocking collectives, on_device(): lax.all_gather(jnp.concatenate([below, vectors, above], 0), 'vec', axis=2...  4.73 us
  transfers between devices with their start and end apart: 30, of which 13 were waited for; matrix products, arithmetic and copies ran while one was open for 3% of the time, Pallas kernels for 23%

profile of v5, /device:TPU:0, one launch (start us, length us, event | category | flops | bytes accessed | tf_op | source)
XLA Modules:
  0.0 125.7 jit_solution(18174682293902430619)
XLA Ops:
  4.1 4.5 %collective-permute-start = (bf16[272,256]{1,0:T(8,128)(2,1)S(1)}, bf16[272,256]{1,0:T(8,128)(2,1)S(1)}, u32[]{:S(2)}, u32[]{:S(2)}) collective-permute-start(bf16[272,256]{1,0:T(8,128)(2,1)S(1)} %fusion.1), channel_id=1, source_target_pairs={{0,2},{2,4},{4,6},{6,8},{8,10},{10,12},{12,14},{1,3},{3,5},{5,7},{... | collective-permute-start | bytes 417800 | tf_op jit(solution)/shard_map/ppermute | solution.py:368
  10.1 2.7 %shard_map.121.blocks = bf16[16,512,256]{2,1,0:T(8,128)(2,1)S(1)} custom-call(s32[6]{0:T(128)S(1)} %stack.24.place.token, s32[6]{0:T(128)S(1)} %stack.24.place.token, bf16[16,512,256]{2,1,0:T(8,128)(2,1)} %rest_0_.15), custom_call_target="tpu_custom_call" | custom-call | bytes 4194304 | tf_op jit(solution)/shard_map/pallas_call | solution.py:120
  12.9 3.4 %collective-permute-done.1 = bf16[4,64,256]{2,1,0:T(8,128)(2,1)S(1)} collective-permute-done((bf16[4,64,256]{2,1,0:T(8,128)(2,1)}, bf16[4,64,256]{2,1,0:T(8,128)(2,1)S(1)}, u32[]{:S(2)}, u32[]{:S(2)}) %collective-permute-start.1) | collective-permute-done | bytes 131104 | tf_op jit(solution)/shard_map/ppermute | solution.py:368
  16.3 4.7 %all_gather.3.extended = bf16[12,64,512]{2,1,0:T(8,128)(2,1)S(1)} all-gather(bf16[12,64,256]{2,1,0:T(8,128)(2,1)S(1)} %pad_maximum_fusion), channel_id=1, replica_groups=mesh['groups'=2,'slab'=8,'vec'=2] {'vec'}, dimensions={2}, use_global_device_ids=true | all-gather | bytes 1179648 | tf_op jit(solution)/shard_map/all_gather | solution.py:435
  21.1 2.6 %shard_map.122 = (bf16[2,64,256]{2,1,0:T(8,128)(2,1)S(1)}, bf16[2,64,256]{2,1,0:T(8,128)(2,1)S(1)}, f32[64,64]{1,0:T(8,128)S(1)}) custom-call(s32[6]{0:T(128)S(1)} %stack.24.place.token, s32[4,14]{1,0:T(4,128)S(1)} %get-tuple-element.32.table, bf16[12,64,512]{2,1,0:T(8,128)(2,1)S(1)} %all_gather.3.extended, bf16[4,64,256]{2,1,0:T(8,128)(2,1)S(1)} %copy-done, ...), custom_call_target="tpu_custom_call" | custom-call | flops 469762048 | bytes 4194304 | tf_op jit(solution)/shard_map/pallas_call | solution.py:155
  24.3 2.4 %collective-permute-done.3 = f32[64,64]{1,0:T(8,128)S(1)} collective-permute-done((f32[64,64]{1,0:T(8,128)S(1)}, f32[64,64]{1,0:T(8,128)S(1)}, u32[]{:S(2)}, u32[]{:S(2)}) %collective-permute-start.3) | collective-permute-done | bytes 16416 | tf_op jit(solution)/shard_map/ppermute | solution.py:362
  26.7 3.0 %collective-permute-start.10 = (f32[64,64]{1,0:T(8,128)S(1)}, f32[64,64]{1,0:T(8,128)S(1)}, u32[]{:S(2)}, u32[]{:S(2)}) collective-permute-start(f32[64,64]{1,0:T(8,128)S(1)} %add.76), channel_id=1, source_target_pairs={{0,4},{1,13},{2,6},{3,15},{4,0},{5,9},{6,2},{7,11},{8,12},{9,5},{1... | collective-permute-start | bytes 49160 | tf_op jit(solution)/shard_map/ppermute | solution.py:391
  35.5 3.5 %collective-permute-start.20 = (bf16[4,512,256]{2,1,0:T(8,128)(2,1)S(1)}, bf16[4,512,256]{2,1,0:T(8,128)(2,1)S(1)}, u32[]{:S(2)}, u32[]{:S(2)}) collective-permute-start(bf16[4,512,256]{2,1,0:T(8,128)(2,1)S(1)} %copy-done.2), channel_id=1, source_target_pairs={{0,1},{1,0},{2,3},{3,2},{4,5},{5,4},{6,7},{7,6},{8,9},{9,8},{10,11... | collective-permute-start | bytes 3145736 | tf_op jit(solution)/shard_map/ppermute | solution.py:362
  39.1 4.0 %collective-permute-start.12 = (f32[64,64]{1,0:T(8,128)S(1)}, f32[64,64]{1,0:T(8,128)S(1)}, u32[]{:S(2)}, u32[]{:S(2)}) collective-permute-start(f32[64,64]{1,0:T(8,128)S(1)} %add_add_fusion), channel_id=1, source_target_pairs={{0,1},{1,0},{2,3},{3,2},{4,5},{5,4},{6,7},{7,6},{8,9},{9,8},{10,11... | collective-permute-start | bytes 49160 | tf_op jit(solution)/shard_map/ppermute | solution.py:362
  44.9 2.5 %shard_map.123.vectors = bf16[2,64,512]{2,1,0:T(8,128)(2,1)S(1)} custom-call(s32[6]{0:T(128)S(1)} %stack.24.place.token, bf16[2,64,512]{2,1,0:T(8,128)(2,1)S(1)} %maximum_select_fusion.token.image, bf16[12,64,512]{2,1,0:T(8,128)(2,1)S(1)} %all_gather.3.extended, bf16[6,4,512,256]{3,2,1,0:T(8,128)(2,1)} %rest_0_.14, ...), custom_call_target="tpu_custom_call" | custom-call | flops 134217728 | bytes 2097152 | tf_op jit(solution)/shard_map/pallas_call | solution.py:454
  47.5 2.6 %shard_map.124.token.own = bf16[2,64,512]{2,1,0:T(8,128)(2,1)S(1)} custom-call(s32[6]{0:T(128)S(1)} %stack.24.place.token, bf16[2,64,512]{2,1,0:T(8,128)(2,1)S(1)} %maximum_select_fusion.token.image, bf16[1,64,512]{2,1,0:T(8,128)(2,1)S(1)} %collective-permute-done.4.inner, bf16[1,64,512]{2,1,0:T(8,128)(2,1)S(1)} %collective-permute-done.5.outer, ...), custom_call_target="tpu_custom_call" | custom-call | flops 134217728 | bytes 2097152 | tf_op jit(solution)/shard_map/pallas_call | solution.py:462
  50.1 2.6 %collective-permute-start.13 = (bf16[2,64,512]{2,1,0:T(8,128)(2,1)S(1)}, bf16[2,64,512]{2,1,0:T(8,128)(2,1)S(1)}, u32[]{:S(2)}, u32[]{:S(2)}) collective-permute-start(bf16[2,64,512]{2,1,0:T(8,128)(2,1)S(1)} %shard_map.124.token.own), channel_id=1, source_target_pairs={{0,1},{1,0},{2,3},{3,2},{4,5},{5,4},{6,7},{7,6},{8,9},{9,8},{10,11... | collective-permute-start | bytes 393224 | tf_op jit(solution)/shard_map/ppermute | solution.py:362
  56.5 8.8 %collective-permute-start.15 = (bf16[2,64,512]{2,1,0:T(8,128)(2,1)S(1)}, bf16[2,64,512]{2,1,0:T(8,128)(2,1)S(1)}, u32[]{:S(2)}, u32[]{:S(2)}) collective-permute-start(bf16[2,64,512]{2,1,0:T(8,128)(2,1)S(1)} %shard_map.126.token.own), channel_id=1, source_target_pairs={{0,2},{1,3},{2,4},{3,5},{4,6},{5,7},{6,8},{7,9},{8,10},{9,11},{10,... | collective-permute-start | bytes 393224 | tf_op jit(solution)/shard_map/ppermute | solution.py:368
  68.8 3.4 %collective-permute-done.16.above = bf16[2,64,512]{2,1,0:T(8,128)(2,1)S(1)} collective-permute-done((bf16[2,64,512]{2,1,0:T(8,128)(2,1)S(1)}, bf16[2,64,512]{2,1,0:T(8,128)(2,1)S(1)}, u32[]{:S(2)}, u32[]{:S(2)}) %collective-permute-start.16) | collective-permute-done | bytes 131104 | tf_op jit(solution)/shard_map/ppermute | solution.py:368
  73.2 3.8 %collective-permute-start.17 = (bf16[2,64,512]{2,1,0:T(8,128)(2,1)S(1)}, bf16[2,64,512]{2,1,0:T(8,128)(2,1)S(1)}, u32[]{:S(2)}, u32[]{:S(2)}) collective-permute-start(bf16[2,64,512]{2,1,0:T(8,128)(2,1)S(1)} %shard_map.128.token.own), channel_id=1, source_target_pairs={{0,4},{1,5},{2,6},{3,7},{4,8},{5,9},{6,10},{7,11},{8,12},{9,13},{1... | collective-permute-start | bytes 393224 | tf_op jit(solution)/shard_map/ppermute | solution.py:368
  80.5 3.6 %collective-permute-done.18.above = bf16[2,64,512]{2,1,0:T(8,128)(2,1)S(1)} collective-permute-done((bf16[2,64,512]{2,1,0:T(8,128)(2,1)S(1)}, bf16[2,64,512]{2,1,0:T(8,128)(2,1)S(1)}, u32[]{:S(2)}, u32[]{:S(2)}) %collective-permute-start.18) | collective-permute-done | bytes 131104 | tf_op jit(solution)/shard_map/ppermute | solution.py:368
  88.8 3.9 %collective-permute-done.19.other = bf16[2,64,512]{2,1,0:T(8,128)(2,1)S(1)} collective-permute-done((bf16[2,64,512]{2,1,0:T(8,128)(2,1)S(1)}, bf16[2,64,512]{2,1,0:T(8,128)(2,1)S(1)}, u32[]{:S(2)}, u32[]{:S(2)}) %collective-permute-start.19) | collective-permute-done | bytes 131104 | tf_op jit(solution)/shard_map/ppermute | solution.py:483
  95.2 3.0 %collective-permute-start.23 = (bf16[2,64,512]{2,1,0:T(8,128)(2,1)S(1)}, bf16[2,64,512]{2,1,0:T(8,128)(2,1)S(1)}, u32[]{:S(2)}, u32[]{:S(2)}) collective-permute-start(bf16[2,64,512]{2,1,0:T(8,128)(2,1)S(1)} %get-tuple-element.24.correction), channel_id=1, source_target_pairs={{0,2},{1,3},{2,4},{3,5},{4,6},{5,7},{6,8},{7,9},{8,10},{9,11},{10,... | collective-permute-start | bytes 393224 | tf_op jit(solution)/shard_map/ppermute | solution.py:368
  98.3 4.0 %shard_map.133 = (bf16[16,512,256]{2,1,0:T(8,128)(2,1)S(1)}, bf16[16,512,256]{2,1,0:T(8,128)(2,1)S(1)}) custom-call(s32[6]{0:T(128)S(1)} %stack.24.place.token, bf16[2,64,512]{2,1,0:T(8,128)(2,1)S(1)} %shard_map.130.token.own, bf16[16,512,256]{2,1,0:T(8,128)(2,1)} %rest_0_.15, bf16[16,512,256]{2,1,0:T(8,128)(2,1)} %collective-permute-done.24.rest_1_), custom_call_target="tpu_custom_call" | custom-call | bytes 8388608 | tf_op jit(solution)/shard_map/pallas_call | solution.py:120
  102.3 2.4 %shard_map.134 = (f32[2,64,512]{2,1,0:T(8,128)S(1)}, f32[192,128]{1,0:T(8,128)S(1)}) custom-call(s32[6]{0:T(128)S(1)} %stack.24.place.token, s32[8,14]{1,0:T(8,128)S(1)} %add_add_fusion.1.table, bf16[12,64,512]{2,1,0:T(8,128)(2,1)S(1)} %all_gather.3.extended, bf16[2,64,512]{2,1,0:T(8,128)(2,1)S(1)} %maximum_select_fusion.token.image, ...), custom_call_target="tpu_custom_call" | custom-call | flops 469762048 | tf_op jit(solution)/shard_map/pallas_call | solution.py:331
  104.7 2.5 %shard_map.135 = f32[192,128]{1,0:T(8,128)S(1)} custom-call(s32[6]{0:T(128)S(1)} %stack.24.place.token, s32[8,14]{1,0:T(8,128)S(1)} %add_add_fusion.1.table, bf16[12,64,512]{2,1,0:T(8,128)(2,1)S(1)} %all_gather.3.extended, bf16[2,64,512]{2,1,0:T(8,128)(2,1)S(1)} %get-tuple-element.24.correction, bf16[2,64,512]{2,1,0:T(8,128)(2,1)S(1)} %collective-permute-done.22.near, ...), custom_call_target="tpu_custom_call" | custom-call | flops 469762048 | tf_op jit(solution)/shard_map/pallas_call | solution.py:338
  111.3 3.2 %collective-permute-done.27 = f32[192,128]{1,0:T(8,128)S(1)} collective-permute-done((f32[192,128]{1,0:T(8,128)S(1)}, f32[192,128]{1,0:T(8,128)S(1)}, u32[]{:S(2)}, u32[]{:S(2)}) %collective-permute-start.27) | collective-permute-done | bytes 98336 | tf_op jit(solution)/shard_map/ppermute | solution.py:391
  114.5 2.8 %collective-permute-start.28 = (f32[192,128]{1,0:T(8,128)S(1)}, f32[192,128]{1,0:T(8,128)S(1)}, u32[]{:S(2)}, u32[]{:S(2)}) collective-permute-start(f32[192,128]{1,0:T(8,128)S(1)} %select_add_fusion), channel_id=1, source_target_pairs={{0,8},{2,10},{4,12},{6,14},{8,0},{10,2},{12,4},{14,6},{1,9},{3,11}... | collective-permute-start | bytes 294920 | tf_op jit(solution)/shard_map/ppermute | solution.py:523
  118.3 4.5 %collective-permute-done.28 = f32[192,128]{1,0:T(8,128)S(1)} collective-permute-done((f32[192,128]{1,0:T(8,128)S(1)}, f32[192,128]{1,0:T(8,128)S(1)}, u32[]{:S(2)}, u32[]{:S(2)}) %collective-permute-start.28) | collective-permute-done | bytes 98336 | tf_op jit(solution)/shard_map/ppermute | solution.py:523
  (85 shorter events, 39.3 us)
Async XLA Ops:
  0.6 43.6 %collective-permute-start.6 = (bf16[6,4,512,256]{3,2,1,0:T(8,128)(2,1)}, bf16[6,4,512,256]{3,2,1,0:T(8,128)(2,1)}, u32[]{:S(2)}, u32[]{:S(2)}) collective-permute-start(bf16[6,4,512,256]{3,2,1,0:T(8,128)(2,1)} %rest_0_.14), channel_id=1, source_target_pairs={{0,1},{1,0},{2,3},{3,2},{4,5},{5,4},{6,7},{7,6},{8,9},{9,8},{10,11... | collective-permute-start | bytes 18874376 | tf_op jit(solution)/shard_map/ppermute | solution.py:362
  1.1 43.8 %collective-permute-start.7 = (bf16[6,4,512,256]{3,2,1,0:T(8,128)(2,1)}, bf16[6,4,512,256]{3,2,1,0:T(8,128)(2,1)}, u32[]{:S(2)}, u32[]{:S(2)}) collective-permute-start(bf16[6,4,512,256]{3,2,1,0:T(8,128)(2,1)} %rest_2_.11), channel_id=1, source_target_pairs={{0,1},{1,0},{2,3},{3,2},{4,5},{5,4},{6,7},{7,6},{8,9},{9,8},{10,11... | collective-permute-start | bytes 18874376 | tf_op jit(solution)/shard_map/ppermute | solution.py:362
  1.2 97.0 %collective-permute-start.24 = (bf16[16,512,256]{2,1,0:T(8,128)(2,1)}, bf16[16,512,256]{2,1,0:T(8,128)(2,1)}, u32[]{:S(2)}, u32[]{:S(2)}) collective-permute-start(bf16[16,512,256]{2,1,0:T(8,128)(2,1)} %rest_0_.15), channel_id=1, source_target_pairs={{0,1},{1,0},{2,3},{3,2},{4,5},{5,4},{6,7},{7,6},{8,9},{9,8},{10,11... | collective-permute-start | bytes 12582920 | tf_op jit(solution)/shard_map/ppermute | solution.py:362
  4.1 8.7 %collective-permute-start = (bf16[272,256]{1,0:T(8,128)(2,1)S(1)}, bf16[272,256]{1,0:T(8,128)(2,1)S(1)}, u32[]{:S(2)}, u32[]{:S(2)}) collective-permute-start(bf16[272,256]{1,0:T(8,128)(2,1)S(1)} %fusion.1), channel_id=1, source_target_pairs={{0,2},{2,4},{4,6},{6,8},{8,10},{10,12},{12,14},{1,3},{3,5},{5,7},{... | collective-permute-start | bytes 417800 | tf_op jit(solution)/shard_map/ppermute | solution.py:368
  8.6 7.7 %collective-permute-start.1 = (bf16[4,64,256]{2,1,0:T(8,128)(2,1)}, bf16[4,64,256]{2,1,0:T(8,128)(2,1)S(1)}, u32[]{:S(2)}, u32[]{:S(2)}) collective-permute-start(bf16[4,64,256]{2,1,0:T(8,128)(2,1)} %vectors.1), channel_id=1, source_target_pairs={{2,0},{4,2},{6,4},{8,6},{10,8},{12,10},{14,12},{3,1},{5,3},{7,5},{... | collective-permute-start | bytes 393224 | tf_op jit(solution)/shard_map/ppermute | solution.py:368
  26.7 4.9 %collective-permute-start.10 = (f32[64,64]{1,0:T(8,128)S(1)}, f32[64,64]{1,0:T(8,128)S(1)}, u32[]{:S(2)}, u32[]{:S(2)}) collective-permute-start(f32[64,64]{1,0:T(8,128)S(1)} %add.76), channel_id=1, source_target_pairs={{0,4},{1,13},{2,6},{3,15},{4,0},{5,9},{6,2},{7,11},{8,12},{9,5},{1... | collective-permute-start | bytes 49160 | tf_op jit(solution)/shard_map/ppermute | solution.py:391
  29.7 4.8 %collective-permute-start.11 = (f32[64,64]{1,0:T(8,128)S(1)}, f32[64,64]{1,0:T(8,128)S(1)}, u32[]{:S(2)}, u32[]{:S(2)}) collective-permute-start(f32[64,64]{1,0:T(8,128)S(1)} %add.76), channel_id=1, source_target_pairs={{0,6},{1,15},{2,4},{3,13},{4,2},{5,11},{6,0},{7,9},{8,14},{9,7},{1... | collective-permute-start | bytes 49160 | tf_op jit(solution)/shard_map/ppermute | solution.py:391
  31.6 3.9 %collective-permute-start.9 = (f32[64,64]{1,0:T(8,128)S(1)}, f32[64,64]{1,0:T(8,128)S(1)}, u32[]{:S(2)}, u32[]{:S(2)}) collective-permute-start(f32[64,64]{1,0:T(8,128)S(1)} %add.76), channel_id=1, source_target_pairs={{0,2},{1,11},{2,0},{3,9},{4,6},{5,15},{6,4},{7,13},{8,10},{9,3},{1... | collective-permute-start | bytes 49160 | tf_op jit(solution)/shard_map/ppermute | solution.py:391
  34.5 4.5 %collective-permute-start.8 = (f32[64,64]{1,0:T(8,128)S(1)}, f32[64,64]{1,0:T(8,128)S(1)}, u32[]{:S(2)}, u32[]{:S(2)}) collective-permute-start(f32[64,64]{1,0:T(8,128)S(1)} %add.76), channel_id=1, source_target_pairs={{1,9},{3,11},{5,13},{7,15},{9,1},{11,3},{13,5},{15,7},{17,25},{19,... | collective-permute-start | bytes 49160 | tf_op jit(solution)/shard_map/ppermute | solution.py:391
  35.5 50.2 %collective-permute-start.20 = (bf16[4,512,256]{2,1,0:T(8,128)(2,1)S(1)}, bf16[4,512,256]{2,1,0:T(8,128)(2,1)S(1)}, u32[]{:S(2)}, u32[]{:S(2)}) collective-permute-start(bf16[4,512,256]{2,1,0:T(8,128)(2,1)S(1)} %copy-done.2), channel_id=1, source_target_pairs={{0,1},{1,0},{2,3},{3,2},{4,5},{5,4},{6,7},{7,6},{8,9},{9,8},{10,11... | collective-permute-start | bytes 3145736 | tf_op jit(solution)/shard_map/ppermute | solution.py:362
  39.1 4.8 %collective-permute-start.12 = (f32[64,64]{1,0:T(8,128)S(1)}, f32[64,64]{1,0:T(8,128)S(1)}, u32[]{:S(2)}, u32[]{:S(2)}) collective-permute-start(f32[64,64]{1,0:T(8,128)S(1)} %add_add_fusion), channel_id=1, source_target_pairs={{0,1},{1,0},{2,3},{3,2},{4,5},{5,4},{6,7},{7,6},{8,9},{9,8},{10,11... | collective-permute-start | bytes 49160 | tf_op jit(solution)/shard_map/ppermute | solution.py:362
  43.9 3.6 %collective-permute-start.4 = (bf16[1,64,512]{2,1,0:T(8,128)(2,1)S(1)}, bf16[1,64,512]{2,1,0:T(8,128)(2,1)S(1)}, u32[]{:S(2)}, u32[]{:S(2)}) collective-permute-start(bf16[1,64,512]{2,1,0:T(8,128)(2,1)S(1)} %get-tuple-element.34), channel_id=1, source_target_pairs={{0,1},{1,0},{2,3},{3,2},{4,5},{5,4},{6,7},{7,6},{8,9},{9,8},{10,11... | collective-permute-start | bytes 196616 | tf_op jit(solution)/shard_map/ppermute | solution.py:362
  50.1 5.3 %collective-permute-start.13 = (bf16[2,64,512]{2,1,0:T(8,128)(2,1)S(1)}, bf16[2,64,512]{2,1,0:T(8,128)(2,1)S(1)}, u32[]{:S(2)}, u32[]{:S(2)}) collective-permute-start(bf16[2,64,512]{2,1,0:T(8,128)(2,1)S(1)} %shard_map.124.token.own), channel_id=1, source_target_pairs={{0,1},{1,0},{2,3},{3,2},{4,5},{5,4},{6,7},{7,6},{8,9},{9,8},{10,11... | collective-permute-start | bytes 393224 | tf_op jit(solution)/shard_map/ppermute | solution.py:362
  56.5 12.2 %collective-permute-start.15 = (bf16[2,64,512]{2,1,0:T(8,128)(2,1)S(1)}, bf16[2,64,512]{2,1,0:T(8,128)(2,1)S(1)}, u32[]{:S(2)}, u32[]{:S(2)}) collective-permute-start(bf16[2,64,512]{2,1,0:T(8,128)(2,1)S(1)} %shard_map.126.token.own), channel_id=1, source_target_pairs={{0,2},{1,3},{2,4},{3,5},{4,6},{5,7},{6,8},{7,9},{8,10},{9,11},{10,... | collective-permute-start | bytes 393224 | tf_op jit(solution)/shard_map/ppermute | solution.py:368
  65.4 6.9 %collective-permute-start.16 = (bf16[2,64,512]{2,1,0:T(8,128)(2,1)S(1)}, bf16[2,64,512]{2,1,0:T(8,128)(2,1)S(1)}, u32[]{:S(2)}, u32[]{:S(2)}) collective-permute-start(bf16[2,64,512]{2,1,0:T(8,128)(2,1)S(1)} %shard_map.126.token.own), channel_id=1, source_target_pairs={{2,0},{3,1},{4,2},{5,3},{6,4},{7,5},{8,6},{9,7},{10,8},{11,9},{12,... | collective-permute-start | bytes 393224 | tf_op jit(solution)/shard_map/ppermute | solution.py:368
  73.2 7.2 %collective-permute-start.17 = (bf16[2,64,512]{2,1,0:T(8,128)(2,1)S(1)}, bf16[2,64,512]{2,1,0:T(8,128)(2,1)S(1)}, u32[]{:S(2)}, u32[]{:S(2)}) collective-permute-start(bf16[2,64,512]{2,1,0:T(8,128)(2,1)S(1)} %shard_map.128.token.own), channel_id=1, source_target_pairs={{0,4},{1,5},{2,6},{3,7},{4,8},{5,9},{6,10},{7,11},{8,12},{9,13},{1... | collective-permute-start | bytes 393224 | tf_op jit(solution)/shard_map/ppermute | solution.py:368
  77.0 7.0 %collective-permute-start.18 = (bf16[2,64,512]{2,1,0:T(8,128)(2,1)S(1)}, bf16[2,64,512]{2,1,0:T(8,128)(2,1)S(1)}, u32[]{:S(2)}, u32[]{:S(2)}) collective-permute-start(bf16[2,64,512]{2,1,0:T(8,128)(2,1)S(1)} %shard_map.128.token.own), channel_id=1, source_target_pairs={{4,0},{5,1},{6,2},{7,3},{8,4},{9,5},{10,6},{11,7},{12,8},{13,9},{1... | collective-permute-start | bytes 393224 | tf_op jit(solution)/shard_map/ppermute | solution.py:368
  85.1 7.6 %collective-permute-start.19 = (bf16[2,64,512]{2,1,0:T(8,128)(2,1)S(1)}, bf16[2,64,512]{2,1,0:T(8,128)(2,1)S(1)}, u32[]{:S(2)}, u32[]{:S(2)}) collective-permute-start(bf16[2,64,512]{2,1,0:T(8,128)(2,1)S(1)} %shard_map.130.token.own), channel_id=1, source_target_pairs={{0,8},{1,9},{2,10},{3,11},{4,12},{5,13},{6,14},{7,15},{8,0},{9,1},... | collective-permute-start | bytes 393224 | tf_op jit(solution)/shard_map/ppermute | solution.py:483
  93.9 10.8 %collective-permute-start.22 = (bf16[2,64,512]{2,1,0:T(8,128)(2,1)S(1)}, bf16[2,64,512]{2,1,0:T(8,128)(2,1)S(1)}, u32[]{:S(2)}, u32[]{:S(2)}) collective-permute-start(bf16[2,64,512]{2,1,0:T(8,128)(2,1)S(1)} %get-tuple-element.24.correction), channel_id=1, source_target_pairs={{0,1},{1,2},{2,3},{3,4},{4,5},{5,6},{6,7},{7,8},{8,9},{9,10},{10,1... | collective-permute-start | bytes 393224 | tf_op jit(solution)/shard_map/ppermute | solution.py:368
  95.2 9.5 %collective-permute-start.23 = (bf16[2,64,512]{2,1,0:T(8,128)(2,1)S(1)}, bf16[2,64,512]{2,1,0:T(8,128)(2,1)S(1)}, u32[]{:S(2)}, u32[]{:S(2)}) collective-permute-start(bf16[2,64,512]{2,1,0:T(8,128)(2,1)S(1)} %get-tuple-element.24.correction), channel_id=1, source_target_pairs={{0,2},{1,3},{2,4},{3,5},{4,6},{5,7},{6,8},{7,9},{8,10},{9,11},{10,... | collective-permute-start | bytes 393224 | tf_op jit(solution)/shard_map/ppermute | solution.py:368
  108.8 5.7 %collective-permute-start.27 = (f32[192,128]{1,0:T(8,128)S(1)}, f32[192,128]{1,0:T(8,128)S(1)}, u32[]{:S(2)}, u32[]{:S(2)}) collective-permute-start(f32[192,128]{1,0:T(8,128)S(1)} %add.83), channel_id=1, source_target_pairs={{0,2},{1,7},{2,0},{3,5},{4,6},{5,3},{6,4},{7,1},{8,10},{9,15},{10,... | collective-permute-start | bytes 294920 | tf_op jit(solution)/shard_map/ppermute | solution.py:391
  110.6 3.9 %collective-permute-start.26 = (f32[192,128]{1,0:T(8,128)S(1)}, f32[192,128]{1,0:T(8,128)S(1)}, u32[]{:S(2)}, u32[]{:S(2)}) collective-permute-start(f32[192,128]{1,0:T(8,128)S(1)} %add.83), channel_id=1, source_target_pairs={{1,5},{3,7},{5,1},{7,3},{9,13},{11,15},{13,9},{15,11},{17,21},{19,... | collective-permute-start | bytes 294920 | tf_op jit(solution)/shard_map/ppermute | solution.py:391
  114.5 8.3 %collective-permute-start.28 = (f32[192,128]{1,0:T(8,128)S(1)}, f32[192,128]{1,0:T(8,128)S(1)}, u32[]{:S(2)}, u32[]{:S(2)}) collective-permute-start(f32[192,128]{1,0:T(8,128)S(1)} %select_add_fusion), channel_id=1, source_target_pairs={{0,8},{2,10},{4,12},{6,14},{8,0},{10,2},{12,4},{14,6},{1,9},{3,11}... | collective-permute-start | bytes 294920 | tf_op jit(solution)/shard_map/ppermute | solution.py:523
  117.4 5.8 %collective-permute-start.21 = (bf16[2,64,256]{2,1,0:T(8,128)(2,1)S(1)}, bf16[2,64,256]{2,1,0:T(8,128)(2,1)S(1)}, u32[]{:S(2)}, u32[]{:S(2)}) collective-permute-start(bf16[2,64,256]{2,1,0:T(8,128)(2,1)S(1)} %get-tuple-element.23), channel_id=1, source_target_pairs={{0,1},{1,0},{2,3},{3,2},{4,5},{5,4},{6,7},{7,6},{8,9},{9,8},{10,11... | collective-permute-start | bytes 196616 | tf_op jit(solution)/shard_map/ppermute | solution.py:362
  (12 other events, 88.7 us)

commit v6 on v5

--- a/solution.py
+++ b/solution.py
@@ -130,10 +130,10 @@
     )(place, token, *[in_hbm(x) for x in arrays])
 
 
-def image_body(place, table, extended, vectors, blocks, keep, send, quotient, image):
-    slabs, _, half = vectors.shape
+def image_body(place, table, extended, vectors, blocks, keep, send, moments, image):
+    slabs, count, _ = vectors.shape
     reach = table.shape[1] // 2
-    part = jnp.zeros(quotient.shape, f32)
+    quotient, old = jnp.zeros((count, count), f32), jnp.zeros((count, count), f32)
     for slab in range(slabs):
         summed = None
         for entry in range(reach):
@@ -142,8 +142,10 @@
             summed = term if summed is None else summed + term
         rounded = summed.astype(bf16)
         image[slab] = rounded
-        part = part + dot_t(vectors[slab], rounded)
-    quotient[...] = part
+        quotient = quotient + dot_t(vectors[slab], rounded)
+        old = old + dot_t(vectors[slab], vectors[slab])
+    moments[:, 0:count] = quotient
+    moments[:, count : 2 * count] = old
     mine = slabs // 2
     keep[...] = image[pl.ds(place[0] * mine, mine)]
     send[...] = image[pl.ds((1 - place[0]) * mine, mine)]
@@ -154,7 +156,7 @@
     part = struct((slabs // 2, rows, half))
     return kernel_call(
         image_body,
-        (part, part, struct((rows, rows), f32)),
+        (part, part, struct((rows, 2 * rows), f32)),
         [SMEM, SMEM, VMEM, VMEM, VMEM],
         [pltpu.VMEM((slabs, rows, half), bf16)],
         flops=14 * slabs * rows * 2 * half * half,
@@ -166,16 +168,10 @@
     return columns(place[0], half), columns(1 - place[0], half)
 
 
-def first_vectors_body(place, token, extended, *rest):
-    *sources, out, weights, sem = rest
+def first_vectors_body(place, extended, weights, out):
     count, half = out.shape[0], weights.shape[-1]
     first = extended.shape[0] // 3 + count * place[0]
-    copies = weight_copies(0, place, sources, weights, sem)
-    for copy in copies:
-        copy.start()
     for part, cols in enumerate(both_parts(place, half)):
-        copies[part].wait()
-        copies[2 + part].wait()
         for slab in range(count):
             own = first + slab
             summed = dot(extended[own - 1], weights[0, part, slab])
@@ -183,26 +179,18 @@
             out[slab, :, cols] = (extended[own, :, cols].astype(f32) - summed).astype(bf16)
 
 
-def first_body(place, image, inner, outer, vectors, quotient, *rest):
-    *sources, out, weights, sem = rest
-    count, half = out.shape[0], weights.shape[-1]
-    copies = weight_copies(0, place, sources, weights, sem)
-    for copy in copies:
-        copy.start()
+def first_body(place, image, inner, outer, vectors, weights, out):
+    count, rows, _ = image.shape
+    half = weights.shape[-1]
     odd = place[0] == 1
     below = [jnp.where(odd, inner[0], outer[0])] + [image[slab] for slab in range(count - 1)]
     above = [image[slab] for slab in range(1, count)] + [jnp.where(odd, outer[0], inner[0])]
-    high = quotient[...].astype(bf16)
-    low = (quotient[...] - high.astype(f32)).astype(bf16)
-    factors = (high.T, low.T)
+    for slab in range(count):
+        out[slab, rows : 2 * rows] = vectors[slab]
     for part, cols in enumerate(both_parts(place, half)):
-        copies[part].wait()
-        copies[2 + part].wait()
         for slab in range(count):
             summed = dot(below[slab], weights[0, part, slab]) + dot(above[slab], weights[1, part, slab])
-            for factor in factors:
-                summed = summed + dot(factor, vectors[slab, :, cols])
-            out[slab, :, cols] = (image[slab, :, cols].astype(f32) - summed).astype(bf16)
+            out[slab, 0:rows, cols] = (image[slab, :, cols].astype(f32) - summed).astype(bf16)
 
 
 def reduce_rows(place, own, partners, sides, weights, out):
@@ -215,8 +203,20 @@
             out[slab, :, cols] = (own[slab, :, cols].astype(f32) - summed).astype(bf16)
 
 
-def second_body(place, own, inner, outer, weights, out):
-    reduce_rows(place, own, (inner, outer), (1 - place[0], place[0]), weights, out)
+def second_body(place, own, inner, outer, weights, moments, out):
+    count, rows, _ = out.shape
+    high = moments[:, 0:rows].astype(bf16)
+    low = (moments[:, 0:rows] - high.astype(f32)).astype(bf16)
+    factors = (high.T, low.T)
+    for part, cols in enumerate(both_parts(place, weights.shape[-1])):
+        for slab in range(count):
+            summed = dot(inner[slab], weights[1 - place[0], part, slab])
+            summed = summed + dot(outer[slab], weights[place[0], part, slab])
+            both = own[slab, :, cols].astype(f32) - summed
+            image, vectors = both[:rows], both[rows:].astype(bf16)
+            for factor in factors:
+                image = image - dot(factor, vectors)
+            out[slab, :, cols] = image.astype(bf16)
 
 
 def level_body(place, own, below, above, weights, out):
@@ -264,11 +264,12 @@
             summed[slot, :, theirs] += dot(vectors, others[block])
 
 
-def own_pairs_body(place, table, extended, image, correction, blocks, others, summed, out):
+def own_pairs_body(place, table, levels, index, extended, image, correction, blocks, others, summed, out, shift):
     own, rows, _ = image.shape
     reach = table.shape[1] // 2
     below = extended.shape[0] // 3
     first = place[0] * own
+    shift[...] = jnp.full(shift.shape, levels[index[0]], f32)
     summed[...] = jnp.zeros(summed.shape, f32)
     for slab in range(own):
         add_pairs(
@@ -278,19 +279,19 @@
         )
     overlap = jnp.zeros((2 * rows, rows), f32)
     mixed = jnp.zeros((rows, rows), f32)
-    old = jnp.zeros((rows, rows), f32)
     for slab in range(own):
         vectors, fixed = extended[first + below + slab], correction[slab]
         overlap = overlap + dot_t(jnp.concatenate([vectors, fixed], 0), fixed)
         mixed = mixed + dot_t(fixed, image[slab])
-        old = old + dot_t(vectors, vectors)
     out[0 : 2 * rows, 0:rows] = jnp.zeros((2 * rows, rows), f32)
     out[0 : 2 * rows, rows : 2 * rows] = overlap
-    out[2 * rows : 3 * rows, 0:rows] = mixed
-    out[2 * rows : 3 * rows, rows : 2 * rows] = old
-
-
-def cross_pairs_body(place, table, extended, correction, near, far, blocks, others, begun, part, out, window, summed):
+    out[2 * rows :, 0:rows] = mixed[: rows // 2]
+    out[2 * rows :, rows : 2 * rows] = mixed[rows // 2 :]
+
+
+def cross_pairs_body(
+    place, table, extended, correction, near, far, blocks, others, begun, part, keep, send, window, summed, out
+):
     own, rows, _ = correction.shape
     reach = table.shape[1] // 2
     below = window.shape[0] - own
@@ -323,39 +324,26 @@
         pencil = pencil + dot_t(basis, summed[slab].astype(bf16))
     out[...] = part[...]
     out[0 : 2 * rows, 0:rows] = pencil
-
-
-def pencil_parts(place, table, extended, image, correction, near, far, blocks, others):
-    own, rows, width = image.shape
-    flops = level_flops(image, 7)
-    begun, part = kernel_call(
-        own_pairs_body,
-        (struct(image.shape, f32), struct((3 * rows, 2 * rows), f32)),
-        [SMEM, SMEM] + [VMEM] * 5,
-        flops=flops,
-        vmem=20 * MIB,
-    )(place, table, extended, image, correction, blocks, others)
-    return kernel_call(
-        cross_pairs_body,
-        struct(part.shape, f32),
-        [SMEM, SMEM] + [VMEM] * 8,
-        [pltpu.VMEM((3 * own, rows, width), bf16), pltpu.VMEM((3 * own, rows, width), f32)],
-        flops=flops,
-        vmem=20 * MIB,
-    )(place, table, extended, correction, near, far, blocks, others, begun, part)
-
-
-def assemble_body(scale, levels, index, quotient, first, second, gram, pencil):
-    rows = quotient.shape[0]
-    shift = levels[index[0]]
-    sums = (first[...] + second[...]) * scale
-    overlap = sums[: 2 * rows, rows:]
-    old, mixed = sums[2 * rows :, rows:], sums[2 * rows :, :rows]
-    left = jnp.concatenate([old, overlap[:rows].T], 0)
-    whole = jnp.concatenate([left, overlap], 1)
-    gram[...] = whole
-    projected = jnp.concatenate([jnp.concatenate([quotient[...], mixed], 0), sums[: 2 * rows, :rows]], 1)
-    pencil[...] = projected - shift * whole
+    keep[...] = out[row_half(place[0], keep)]
+    send[...] = out[row_half(1 - place[0], keep)]
+
+
+def row_half(index, part):
+    return pl.ds(pl.multiple_of(index * part.shape[0], 8), part.shape[0])
+
+
+def assemble_body(scale, place, shift, moments, first, second, gram, pencil, whole):
+    rows = moments.shape[0]
+    whole[row_half(place[0], first)] = first[...] * scale
+    whole[row_half(1 - place[0], first)] = second[...] * scale
+    top, bottom = whole[0 : 2 * rows], whole[2 * rows :]
+    overlap = top[:, rows:]
+    mixed = jnp.concatenate([bottom[:, :rows], bottom[:, rows:]], 0)
+    left = jnp.concatenate([moments[:, rows:], overlap[:rows].T], 0)
+    product = jnp.concatenate([left, overlap], 1)
+    gram[...] = product
+    projected = jnp.concatenate([jnp.concatenate([moments[:, :rows], mixed], 0), top[:, :rows]], 1)
+    pencil[...] = projected - shift[0:1] * product
 
 
 def swapped(operand):
@@ -377,10 +365,15 @@
     return [route for route in routes if route]
 
 
+def summed_up(parts):
+    while len(parts) > 1:
+        parts = [a + b for a, b in zip(parts[::2], parts[1::2])]
+    return parts[0]
+
+
 def shared_out(part, reach, radix):
     slabs = lax.axis_size("slab")
     split = radix // 2
-    core = lax.axis_index("vec")
     received = []
     for offset in range(split):
         route = []
@@ -389,10 +382,19 @@
                 route.append((2 * i, 2 * (i ^ (offset * reach))))
             route.append((2 * i + 1, 2 * (i ^ ((offset + split) * reach)) + 1))
         received.append(lax.ppermute(part, CHAIN, route))
-    received[0] = jnp.where(core == 0, part, received[0])
-    while len(received) > 1:
-        received = [a + b for a, b in zip(received[::2], received[1::2])]
-    return received[0]
+    received[0] = jnp.where(lax.axis_index("vec") == 0, part, received[0])
+    return summed_up(received)
+
+
+def slab_total(part):
+    slabs = lax.axis_size("slab")
+    reach = 1
+    while reach < slabs:
+        radix = min(4, slabs // reach)
+        routes = [[(i, i ^ (offset * reach)) for i in range(slabs)] for offset in range(1, radix)]
+        part = summed_up([part] + [lax.ppermute(part, "slab", route) for route in routes])
+        reach *= radix
+    return part
 
 
 def on_device(
@@ -419,24 +421,17 @@
     steps = [max(2**l // own_count, 1) for l in levels]
     place = jnp.stack([core] + [link // step % 2 for step in steps]).astype(jnp.int32)
 
+    weights = (level_lower, swapped(level_lower), level_upper, swapped(level_upper))
+    below, above = along(vectors, "slab", 1), along(vectors, "slab", -1)
     slab_ids = slab * slab_count + jnp.arange(slab_count, dtype=jnp.int32)[:, None]
     near = jnp.broadcast_to(jnp.arange(-1, 2, dtype=jnp.int32), (slab_count, 3))
     table = jnp.concatenate([near, far_source - slab_ids, slab_blocks, far_block], 1)
-    flat = vectors.reshape(slab_count * rows, half)
-    note = jnp.pad(table.astype(bf16), ((0, 16 - slab_count), (0, half - table.shape[1])))
-    above = along(vectors, "slab", -1)
-    lifted = along(jnp.concatenate([flat, note], 0), "slab", 1)
-    below = lifted[: slab_count * rows].reshape(vectors.shape)
-    lower_table = lifted[slab_count * rows :][:slab_count, : table.shape[1]].astype(jnp.int32)
-    tables = jnp.concatenate([lower_table, table], 0)
-
-    weights = (level_lower, swapped(level_lower), level_upper, swapped(level_upper))
     (held_blocks,) = load_whole(place, place, [blocks])
     extended = lax.all_gather(jnp.concatenate([below, vectors, above], 0), "vec", axis=2, tiled=True)
-    keep, send, quotient = image_halves(place, table, extended, vectors, in_vmem(held_blocks))
-    received, quotient = swapped(send), quotient + swapped(quotient)
+    keep, send, moments = image_halves(place, table, extended, vectors, in_vmem(held_blocks))
+    received, moments = swapped(send), moments + swapped(moments)
     image = jnp.where(core == 0, jnp.concatenate([keep, received], 2), jnp.concatenate([received, keep], 2))
-    image, quotient = lax.optimization_barrier((image, quotient))
+    image, moments = lax.optimization_barrier((image, moments))
 
     inner_route, outer_route = pair_routes(1)
     outer = lax.ppermute(lax.dynamic_slice_in_dim(image, (own_count - 1) * core, 1), CHAIN, outer_route)
@@ -444,36 +439,40 @@
     reach = 1
     while reach < slabs:
         radix = min(8, slabs // reach)
-        share = shared_out(quotient, reach, radix)
-        quotient = share + swapped(share)
+        share = shared_out(moments, reach, radix)
+        moments = share + swapped(share)
         reach *= radix
-    quotient = quotient / rows_total
-
-    buffers = [pltpu.VMEM((2, 2, own_count, width, half), bf16), pltpu.SemaphoreType.DMA((2, 2))]
-    held_weights = [in_hbm(x) for x in weights]
+    moments = moments / rows_total
+
+    matrices = in_vmem(load(functools.partial(load_body, 0), place, image, weights))
     vectors_1 = kernel_call(
         first_vectors_body,
         struct(image.shape),
-        [SMEM, ANY, VMEM] + [ANY] * 4,
-        buffers,
+        [SMEM] + [VMEM] * 2,
         flops=level_flops(image, 2),
-        size=8 * own_count * width * half,
-    )(place, image, extended, *held_weights)
+    )(place, extended, matrices)
+    both = kernel_call(
+        first_body,
+        struct((own_count, 2 * rows, width)),
+        [SMEM] + [VMEM] * 5,
+        flops=level_flops(image, 2),
+    )(place, image, inner, outer, vectors_1, matrices)
+    matrices = in_vmem(load(functools.partial(load_body, 1), place, both, weights))
+    outer, inner = lax.ppermute(both, CHAIN, outer_route), swapped(both)
     residual = kernel_call(
-        first_body,
+        second_body,
         struct(image.shape),
-        [SMEM] + [VMEM] * 5 + [ANY] * 4,
-        buffers,
-        flops=level_flops(image, 2),
-        size=8 * own_count * width * half,
-    )(place, image, inner, outer, vectors_1, quotient, *held_weights)
-
-    finals = (level_final, swapped(level_final))
-    others = swapped(blocks)
+        [SMEM] + [VMEM] * 5,
+        flops=level_flops(both, 2),
+    )(place, both, inner, outer, matrices, moments)
+
+    late_blocks, late_final, residual = lax.optimization_barrier((blocks, level_final, residual))
+    finals = (level_final, swapped(late_final))
+    others = swapped(late_blocks)
     part = struct((own_count, rows, half))
     ends = (struct(residual.shape), part, part)
     one_partner = chain == 2 * steps[-1]
-    for level, step in zip(levels[1:], steps[1:]):
+    for level, step in zip(levels[2:], steps[2:]):
         last = level == levels[-1]
         if last:
             held_blocks, others = load_whole(place, residual, [blocks, others])
@@ -481,6 +480,7 @@
             matrices = load(functools.partial(load_last_body, level), place, residual, weights + finals)
             (route,) = pair_routes(step)
             other = lax.ppermute(residual, CHAIN, route)
+            other, held_blocks, others = lax.optimization_barrier((other, held_blocks, others))
             correction, keep, send = kernel_call(
                 last_body,
                 ends,
@@ -490,12 +490,13 @@
             )(place, residual, other, in_vmem(matrices))
             break
         matrices = load(functools.partial(load_body, level), place, residual, weights)
-        if step == 1:
-            partners = [lax.ppermute(residual, CHAIN, outer_route), swapped(residual)][::-1]
-        else:
-            partners = [along(residual, CHAIN, step), along(residual, CHAIN, -step)]
+        partners = [along(residual, CHAIN, step), along(residual, CHAIN, -step)]
+        if level == levels[-2]:
+            matrices, note = lax.optimization_barrier((matrices, table))
+            lower_table = along(note, "slab", 1)
+            partners, lower_table = lax.optimization_barrier((partners, lower_table))
         residual = kernel_call(
-            second_body if step == 1 else level_body,
+            level_body,
             struct(residual.shape),
             [SMEM] + [VMEM] * 4,
             flops=level_flops(residual, 2),
@@ -511,23 +512,38 @@
     held_blocks, others = in_vmem(held_blocks), in_vmem(others)
 
     far, near = along(correction, CHAIN, 2), along(correction, CHAIN, 1)
-    part = pencil_parts(place, tables, extended, image, correction, near, far, held_blocks, others)
     received = swapped(send)
     result = jnp.where(core == 0, jnp.concatenate([keep, received], 0), jnp.concatenate([received, keep], 0))
-
-    part = part + swapped(part)
-    radix = min(4, slabs)
-    part = shared_out(part, 1, radix)
-    reach = radix
-    while reach < slabs:
-        part = part + lax.ppermute(part, "slab", [(i, i ^ reach) for i in range(slabs)])
-        reach *= 2
+    far, near, result = lax.optimization_barrier((far, near, result))
+    tables = jnp.concatenate([lower_table, table], 0)
+    flops = level_flops(image, 7)
+    sums = (5 * rows // 2, 2 * rows)
+    begun, part, shift = kernel_call(
+        own_pairs_body,
+        (struct(image.shape, f32), struct(sums, f32), struct((8, 2 * rows), f32)),
+        [SMEM] * 4 + [VMEM] * 5,
+        flops=flops,
+    )(place, tables, shift_levels, shift_index, extended, image, correction, held_blocks, others)
+    share = struct((sums[0] // 2, sums[1]), f32)
+    keep, send = kernel_call(
+        cross_pairs_body,
+        (share, share),
+        [SMEM] * 2 + [VMEM] * 8,
+        [
+            pltpu.VMEM((3 * own_count, rows, width), bf16),
+            pltpu.VMEM((3 * own_count, rows, width), f32),
+            pltpu.VMEM(sums, f32),
+        ],
+        flops=flops,
+    )(place, tables, extended, correction, near, far, held_blocks, others, begun, part)
+    share = slab_total(keep + swapped(send))
     square = struct((2 * rows, 2 * rows), f32)
     gram, pencil = kernel_call(
         functools.partial(assemble_body, 1.0 / rows_total),
         (square, square),
-        [SMEM, SMEM] + [VMEM] * 3,
-    )(shift_levels, shift_index, quotient, part, swapped(part))
+        [SMEM] + [VMEM] * 4,
+        [pltpu.VMEM(sums, f32)],
+    )(place, shift, moments, share, swapped(share))
     return (result, gram, pencil)
 
 

time: 126 us -> 127 us (level)
  waiting for transfers between devices: 28.5 us -> 19.6 us
  starting transfers between devices: 52.7 us -> 60.3 us
  blocking collectives: 4.73 us -> 7.08 us
  local copies, waits for them, and re-layouts: 1.12 us -> 3.05 us
  other arithmetic: 3.35 us -> 1.72 us
    ppermute x1, starting transfers between devices: 0.62 us -> 6.39 us  [on_device(): other = lax.ppermute(residual, CHAIN, route)]
    ppermute x6 -> x4, waiting for transfers between devices: 5.07 us -> 0.01 us  [shared_out(): received.append(lax.ppermute(part, CHAIN, route))]
    ppermute x1, waiting for transfers between devices: 3.91 us -> 0.01 us  [on_device(): other = lax.ppermute(residual, CHAIN, route)]
    ppermute x2 -> x5, waiting for transfers between devices: 4.51 us -> 8.26 us  [the longest x4 8.25 us: slab_total(): lax.ppermute(part, 'slab', route)]
    ppermute x8 -> x9, waiting for transfers between devices: 10.5 us -> 7.28 us  [along(): return lax.ppermute(operand, axis, route)]
    pallas_call x8, Pallas kernels: 15.7 us -> 13.1 us  [the longest x1 2.55 us: on_device(): kernel_call(own_pairs_body, (struct(image.shape, f32), struct(sums, f32),...]
    ppermute x2 -> x5, starting transfers between devices: 3.5 us -> 5.95 us  [the longest x4 5.29 us: slab_total(): lax.ppermute(part, 'slab', route)]
    pallas_call x4 -> x5, Pallas kernels: 8.38 us -> 10.7 us  [load(): pl.pallas_call(body, out_shape=pltpu.VMEM(shape, bf16), in_specs=[SMEM] +...]
  transfers between devices with their start and end apart: 30 -> 32, of which waited for: 13 -> 11; matrix products, arithmetic and copies ran while one was open for 3% -> 1% of each run, Pallas kernels for 23% -> 21%
where the time goes in v6:
time: 127 us
  starting transfers between devices  60.3 us (47%)
  Pallas kernels  33.2 us (26%)
  waiting for transfers between devices  19.6 us (15%)
  blocking collectives  7.08 us (6%)
  local copies, waits for them, and re-layouts  3.05 us (2%)
  between operations  1.77 us (1%)
  other arithmetic  1.72 us (1%)
    ppermute x9, starting transfers between devices, along(): return lax.ppermute(operand, axis, route)  24.8 us
    ppermute x12, starting transfers between devices, swapped(): return lax.ppermute(operand, 'vec', SWAP)  14.9 us
    pallas_call x5, Pallas kernels, load(): pl.pallas_call(body, out_shape=pltpu.VMEM(shape, bf16), in_specs=[SMEM] +...  10.7 us
    ppermute x4, waiting for transfers between devices, slab_total(): lax.ppermute(part, 'slab', route)  8.25 us
    ppermute x4, starting transfers between devices, shared_out(): received.append(lax.ppermute(part, CHAIN, route))  7.57 us
    ppermute x9, waiting for transfers between devices, along(): return lax.ppermute(operand, axis, route)  7.28 us
    all_gather x1, blocking collectives, on_device(): lax.all_gather(jnp.concatenate([below, vectors, above], 0), 'vec', axis=2...  7.08 us
    pallas_call x2, Pallas kernels, load_whole(): pl.pallas_call(load_whole_body, out_shape=[pltpu.VMEM(x.shape, x.dtype) f...  6.76 us
  transfers between devices with their start and end apart: 32, of which 11 were waited for; matrix products, arithmetic and copies ran while one was open for 1% of the time, Pallas kernels for 21%

profile of v6, /device:TPU:0, one launch (start us, length us, event | category | flops | bytes accessed | tf_op | source)
XLA Modules:
  0.0 126.6 jit_solution(10892004693073156794)
XLA Ops:
  1.2 4.8 %collective-permute-start = (bf16[4,64,256]{2,1,0:T(8,128)(2,1)}, bf16[4,64,256]{2,1,0:T(8,128)(2,1)S(1)}, u32[]{:S(2)}, u32[]{:S(2)}) collective-permute-start(bf16[4,64,256]{2,1,0:T(8,128)(2,1)} %vectors.1), channel_id=1, source_target_pairs={{0,2},{2,4},{4,6},{6,8},{8,10},{10,12},{12,14},{1,3},{3,5},{5,7},{... | collective-permute-start | bytes 393224 | tf_op jit(solution)/shard_map/ppermute | solution.py:356
  8.2 2.7 %shard_map.121.blocks = bf16[16,512,256]{2,1,0:T(8,128)(2,1)S(1)} custom-call(s32[6]{0:T(128)S(1)} %stack.24.place.token, s32[6]{0:T(128)S(1)} %stack.24.place.token, bf16[16,512,256]{2,1,0:T(8,128)(2,1)} %rest_0_.12), custom_call_target="tpu_custom_call" | custom-call | bytes 4194304 | tf_op jit(solution)/shard_map/pallas_call | solution.py:120
  11.1 2.3 %collective-permute-done.1 = bf16[4,64,256]{2,1,0:T(8,128)(2,1)S(1)} collective-permute-done((bf16[4,64,256]{2,1,0:T(8,128)(2,1)}, bf16[4,64,256]{2,1,0:T(8,128)(2,1)S(1)}, u32[]{:S(2)}, u32[]{:S(2)}) %collective-permute-start.1) | collective-permute-done | bytes 131104 | tf_op jit(solution)/shard_map/ppermute | solution.py:356
  13.4 7.1 %all_gather.3.extended = bf16[12,64,512]{2,1,0:T(8,128)(2,1)S(1)} all-gather(bf16[12,64,256]{2,1,0:T(8,128)(2,1)S(1)} %pad_maximum_fusion), channel_id=1, replica_groups=mesh['groups'=2,'slab'=8,'vec'=2] {'vec'}, dimensions={2}, use_global_device_ids=true | all-gather | bytes 1179648 | tf_op jit(solution)/shard_map/all_gather | solution.py:430
  20.5 2.2 %shard_map.122 = (bf16[2,64,256]{2,1,0:T(8,128)(2,1)S(1)}, bf16[2,64,256]{2,1,0:T(8,128)(2,1)S(1)}, f32[64,128]{1,0:T(8,128)S(1)}) custom-call(s32[6]{0:T(128)S(1)} %stack.24.place.token, s32[4,14]{1,0:T(4,128)S(1)} %pad_add_fusion.table, bf16[12,64,512]{2,1,0:T(8,128)(2,1)S(1)} %all_gather.3.extended, bf16[4,64,256]{2,1,0:T(8,128)(2,1)S(1)} %copy-done, ...), custom_call_target="tpu_custom_call" | custom-call | flops 469762048 | bytes 4194304 | tf_op jit(solution)/shard_map/pallas_call | solution.py:157
  26.0 4.2 %collective-permute-start.11 = (f32[64,128]{1,0:T(8,128)S(1)}, f32[64,128]{1,0:T(8,128)S(1)}, u32[]{:S(2)}, u32[]{:S(2)}) collective-permute-start(f32[64,128]{1,0:T(8,128)S(1)} %add.80), channel_id=1, source_target_pairs={{0,2},{1,11},{2,0},{3,9},{4,6},{5,15},{6,4},{7,13},{8,10},{9,3},{1... | collective-permute-start | bytes 98312 | tf_op jit(solution)/shard_map/ppermute | solution.py:384
  37.1 5.3 %collective-permute-start.8 = (bf16[2,128,512]{2,1,0:T(8,128)(2,1)S(1)}, bf16[2,128,512]{2,1,0:T(8,128)(2,1)S(1)}, u32[]{:S(2)}, u32[]{:S(2)}) collective-permute-start(bf16[2,128,512]{2,1,0:T(8,128)(2,1)S(1)} %shard_map.125.token.own), channel_id=1, source_target_pairs={{0,1},{1,0},{2,3},{3,2},{4,5},{5,4},{6,7},{7,6},{8,9},{9,8},{10,11... | collective-permute-start | bytes 786440 | tf_op jit(solution)/shard_map/ppermute | solution.py:350
  43.2 2.8 %collective-permute-start.14 = (f32[64,128]{1,0:T(8,128)S(1)}, f32[64,128]{1,0:T(8,128)S(1)}, u32[]{:S(2)}, u32[]{:S(2)}) collective-permute-start(f32[64,128]{1,0:T(8,128)S(1)} %add_add_fusion.1), channel_id=1, source_target_pairs={{0,1},{1,0},{2,3},{3,2},{4,5},{5,4},{6,7},{7,6},{8,9},{9,8},{10,11... | collective-permute-start | bytes 98312 | tf_op jit(solution)/shard_map/ppermute | solution.py:350
  46.9 2.4 %shard_map.126.weights = bf16[2,2,2,512,256]{4,3,2,1,0:T(8,128)(2,1)S(1)} custom-call(s32[6]{0:T(128)S(1)} %stack.24.place.token, bf16[2,128,512]{2,1,0:T(8,128)(2,1)S(1)} %shard_map.125.token.own, bf16[6,4,512,256]{3,2,1,0:T(8,128)(2,1)} %rest_0_.13, bf16[6,4,512,256]{3,2,1,0:T(8,128)(2,1)} %collective-permute-done.6.rest_1_, ...), custom_call_target="tpu_custom_call" | custom-call | bytes 4194304 | tf_op jit(solution)/shard_map/pallas_call | solution.py:102
  51.0 2.8 %collective-permute-start.21 = (bf16[16,512,256]{2,1,0:T(8,128)(2,1)S(1)}, bf16[16,512,256]{2,1,0:T(8,128)(2,1)S(1)}, u32[]{:S(2)}, u32[]{:S(2)}) collective-permute-start(bf16[16,512,256]{2,1,0:T(8,128)(2,1)S(1)} %copy-done.2), channel_id=1, source_target_pairs={{0,1},{1,0},{2,3},{3,2},{4,5},{5,4},{6,7},{7,6},{8,9},{9,8},{10,11... | collective-permute-start | bytes 12582920 | tf_op jit(solution)/shard_map/ppermute | solution.py:350
  53.9 4.7 %collective-permute-start.15 = (bf16[2,64,512]{2,1,0:T(8,128)(2,1)S(1)}, bf16[2,64,512]{2,1,0:T(8,128)(2,1)S(1)}, u32[]{:S(2)}, u32[]{:S(2)}) collective-permute-start(bf16[2,64,512]{2,1,0:T(8,128)(2,1)S(1)} %shard_map.127.token.own), channel_id=1, source_target_pairs={{0,2},{1,3},{2,4},{3,5},{4,6},{5,7},{6,8},{7,9},{8,10},{9,11},{10,... | collective-permute-start | bytes 393224 | tf_op jit(solution)/shard_map/ppermute | solution.py:356
  62.0 3.7 %collective-permute-done.16.above = bf16[2,64,512]{2,1,0:T(8,128)(2,1)S(1)} collective-permute-done((bf16[2,64,512]{2,1,0:T(8,128)(2,1)S(1)}, bf16[2,64,512]{2,1,0:T(8,128)(2,1)S(1)}, u32[]{:S(2)}, u32[]{:S(2)}) %collective-permute-start.16) | collective-permute-done | bytes 131104 | tf_op jit(solution)/shard_map/ppermute | solution.py:356
  66.7 2.8 %collective-permute-start.17 = (bf16[2,64,512]{2,1,0:T(8,128)(2,1)S(1)}, bf16[2,64,512]{2,1,0:T(8,128)(2,1)S(1)}, u32[]{:S(2)}, u32[]{:S(2)}) collective-permute-start(bf16[2,64,512]{2,1,0:T(8,128)(2,1)S(1)} %shard_map.129.token.own), channel_id=1, source_target_pairs={{0,4},{1,5},{2,6},{3,7},{4,8},{5,9},{6,10},{7,11},{8,12},{9,13},{1... | collective-permute-start | bytes 393224 | tf_op jit(solution)/shard_map/ppermute | solution.py:356
  70.8 2.1 %shard_map.130.weights = bf16[2,2,2,512,256]{4,3,2,1,0:T(8,128)(2,1)S(1)} custom-call(s32[6]{0:T(128)S(1)} %stack.24.place.token, bf16[2,64,512]{2,1,0:T(8,128)(2,1)S(1)} %shard_map.129.token.own, bf16[6,4,512,256]{3,2,1,0:T(8,128)(2,1)} %rest_0_.13, bf16[6,4,512,256]{3,2,1,0:T(8,128)(2,1)} %collective-permute-done.6.rest_1_, ...), custom_call_target="tpu_custom_call" | custom-call | bytes 4194304 | tf_op jit(solution)/shard_map/pallas_call | solution.py:102
  72.9 3.1 %collective-permute-start.19 = (s32[4,14]{1,0:T(4,128)S(1)}, s32[4,14]{1,0:T(4,128)S(1)}, u32[]{:S(2)}, u32[]{:S(2)}) collective-permute-start(s32[4,14]{1,0:T(4,128)S(1)} %pad_add_fusion.table), channel_id=1, source_target_pairs={{0,2},{2,4},{4,6},{6,8},{8,10},{10,12},{12,14},{1,3},{3,5},{5,7},{... | collective-permute-start | bytes 680 | tf_op jit(solution)/shard_map/ppermute | solution.py:356
  78.4 6.4 %collective-permute-start.20 = (bf16[2,64,512]{2,1,0:T(8,128)(2,1)S(1)}, bf16[2,64,512]{2,1,0:T(8,128)(2,1)S(1)}, u32[]{:S(2)}, u32[]{:S(2)}) collective-permute-start(bf16[2,64,512]{2,1,0:T(8,128)(2,1)S(1)} %shard_map.131.token.own), channel_id=1, source_target_pairs={{0,8},{1,9},{2,10},{3,11},{4,12},{5,13},{6,14},{7,15},{8,0},{9,1},... | collective-permute-start | bytes 393224 | tf_op jit(solution)/shard_map/ppermute | solution.py:482
  90.5 4.0 %shard_map.132 = (bf16[16,512,256]{2,1,0:T(8,128)(2,1)S(1)}, bf16[16,512,256]{2,1,0:T(8,128)(2,1)S(1)}) custom-call(s32[6]{0:T(128)S(1)} %stack.24.place.token, bf16[2,64,512]{2,1,0:T(8,128)(2,1)S(1)} %shard_map.131.token.own, bf16[16,512,256]{2,1,0:T(8,128)(2,1)} %rest_0_.12, bf16[16,512,256]{2,1,0:T(8,128)(2,1)} %copy-done.3), custom_call_target="tpu_custom_call" | custom-call | bytes 8388608 | tf_op jit(solution)/shard_map/pallas_call | solution.py:120
  95.8 3.3 %collective-permute-start.23 = (bf16[2,64,512]{2,1,0:T(8,128)(2,1)S(1)}, bf16[2,64,512]{2,1,0:T(8,128)(2,1)S(1)}, u32[]{:S(2)}, u32[]{:S(2)}) collective-permute-start(bf16[2,64,512]{2,1,0:T(8,128)(2,1)S(1)} %get-tuple-element.49.correction), channel_id=1, source_target_pairs={{0,2},{1,3},{2,4},{3,5},{4,6},{5,7},{6,8},{7,9},{8,10},{9,11},{10,... | collective-permute-start | bytes 393224 | tf_op jit(solution)/shard_map/ppermute | solution.py:356
  99.1 2.1 %collective-permute-start.24 = (bf16[2,64,512]{2,1,0:T(8,128)(2,1)S(1)}, bf16[2,64,512]{2,1,0:T(8,128)(2,1)S(1)}, u32[]{:S(2)}, u32[]{:S(2)}) collective-permute-start(bf16[2,64,512]{2,1,0:T(8,128)(2,1)S(1)} %get-tuple-element.49.correction), channel_id=1, source_target_pairs={{0,1},{1,2},{2,3},{3,4},{4,5},{5,6},{6,7},{7,8},{8,9},{9,10},{10,1... | collective-permute-start | bytes 393224 | tf_op jit(solution)/shard_map/ppermute | solution.py:356
  101.3 2.5 %shard_map.135 = (f32[2,64,512]{2,1,0:T(8,128)S(1)}, f32[160,128]{1,0:T(8,128)S(1)}, f32[8,128]{1,0:T(8,128)S(1)}) custom-call(s32[6]{0:T(128)S(1)} %stack.24.place.token, s32[8,14]{1,0:T(8,128)S(1)} %add_add_fusion.2.table, f32[8]{0:T(128)S(1)} %copy-done.1, s32[1]{0:T(128)S(6)} %copy.13.index, bf16[12,64,512]{2,1,0:T(8,128)(2,1)S(1)} %all_gather.3.extended, ...), custom_call_target="tpu_custom_call" | custom-call | flops 469762048 | tf_op jit(solution)/shard_map/pallas_call | solution.py:521
  104.5 2.5 %shard_map.136 = (f32[80,128]{1,0:T(8,128)S(1)}, f32[80,128]{1,0:T(8,128)S(1)}) custom-call(s32[6]{0:T(128)S(1)} %stack.24.place.token, s32[8,14]{1,0:T(8,128)S(1)} %add_add_fusion.2.table, bf16[12,64,512]{2,1,0:T(8,128)(2,1)S(1)} %all_gather.3.extended, bf16[2,64,512]{2,1,0:T(8,128)(2,1)S(1)} %get-tuple-element.49.correction, ...), custom_call_target="tpu_custom_call" | custom-call | flops 469762048 | tf_op jit(solution)/shard_map/pallas_call | solution.py:528
  107.0 2.5 %collective-permute-start.26 = (f32[80,128]{1,0:T(8,128)S(1)}, f32[80,128]{1,0:T(8,128)S(1)}, u32[]{:S(2)}, u32[]{:S(2)}) collective-permute-start(f32[80,128]{1,0:T(8,128)S(1)} %get-tuple-element.62), channel_id=1, source_target_pairs={{0,1},{1,0},{2,3},{3,2},{4,5},{5,4},{6,7},{7,6},{8,9},{9,8},{10,11... | collective-permute-start | bytes 122888 | tf_op jit(solution)/shard_map/ppermute | solution.py:350
  110.3 3.7 %collective-permute-start.27 = (f32[80,128]{1,0:T(8,128)S(1)}, f32[80,128]{1,0:T(8,128)S(1)}, u32[]{:S(2)}, u32[]{:S(2)}) collective-permute-start(f32[80,128]{1,0:T(8,128)S(1)} %add.87), channel_id=1, source_target_pairs={{0,2},{2,0},{4,6},{6,4},{8,10},{10,8},{12,14},{14,12},{1,3},{3,1},... | collective-permute-start | bytes 122888 | tf_op jit(solution)/shard_map/ppermute | solution.py:395
  119.0 4.9 %collective-permute-done.30 = f32[80,128]{1,0:T(8,128)S(1)} collective-permute-done((f32[80,128]{1,0:T(8,128)S(1)}, f32[80,128]{1,0:T(8,128)S(1)}, u32[]{:S(2)}, u32[]{:S(2)}) %collective-permute-start.30) | collective-permute-done | bytes 40992 | tf_op jit(solution)/shard_map/ppermute | solution.py:395
  (91 shorter events, 40.0 us)
Async XLA Ops:
  0.6 29.6 %collective-permute-start.6 = (bf16[6,4,512,256]{3,2,1,0:T(8,128)(2,1)}, bf16[6,4,512,256]{3,2,1,0:T(8,128)(2,1)}, u32[]{:S(2)}, u32[]{:S(2)}) collective-permute-start(bf16[6,4,512,256]{3,2,1,0:T(8,128)(2,1)} %rest_0_.13), channel_id=1, source_target_pairs={{0,1},{1,0},{2,3},{3,2},{4,5},{5,4},{6,7},{7,6},{8,9},{9,8},{10,11... | collective-permute-start | bytes 18874376 | tf_op jit(solution)/shard_map/ppermute | solution.py:350
  1.1 30.9 %collective-permute-start.7 = (bf16[6,4,512,256]{3,2,1,0:T(8,128)(2,1)}, bf16[6,4,512,256]{3,2,1,0:T(8,128)(2,1)}, u32[]{:S(2)}, u32[]{:S(2)}) collective-permute-start(bf16[6,4,512,256]{3,2,1,0:T(8,128)(2,1)} %rest_2_.9), channel_id=1, source_target_pairs={{0,1},{1,0},{2,3},{3,2},{4,5},{5,4},{6,7},{7,6},{8,9},{9,8},{10,11... | collective-permute-start | bytes 18874376 | tf_op jit(solution)/shard_map/ppermute | solution.py:350
  1.2 9.8 %collective-permute-start = (bf16[4,64,256]{2,1,0:T(8,128)(2,1)}, bf16[4,64,256]{2,1,0:T(8,128)(2,1)S(1)}, u32[]{:S(2)}, u32[]{:S(2)}) collective-permute-start(bf16[4,64,256]{2,1,0:T(8,128)(2,1)} %vectors.1), channel_id=1, source_target_pairs={{0,2},{2,4},{4,6},{6,8},{8,10},{10,12},{12,14},{1,3},{3,5},{5,7},{... | collective-permute-start | bytes 393224 | tf_op jit(solution)/shard_map/ppermute | solution.py:356
  6.1 7.3 %collective-permute-start.1 = (bf16[4,64,256]{2,1,0:T(8,128)(2,1)}, bf16[4,64,256]{2,1,0:T(8,128)(2,1)S(1)}, u32[]{:S(2)}, u32[]{:S(2)}) collective-permute-start(bf16[4,64,256]{2,1,0:T(8,128)(2,1)} %vectors.1), channel_id=1, source_target_pairs={{2,0},{4,2},{6,4},{8,6},{10,8},{12,10},{14,12},{3,1},{5,3},{7,5},{... | collective-permute-start | bytes 393224 | tf_op jit(solution)/shard_map/ppermute | solution.py:356
  24.7 11.4 %collective-permute-start.5 = (bf16[1,64,512]{2,1,0:T(8,128)(2,1)S(1)}, bf16[1,64,512]{2,1,0:T(8,128)(2,1)S(1)}, u32[]{:S(2)}, u32[]{:S(2)}) collective-permute-start(bf16[1,64,512]{2,1,0:T(8,128)(2,1)S(1)} %get-tuple-element.65), channel_id=1, source_target_pairs={{1,2},{3,4},{5,6},{7,8},{9,10},{11,12},{13,14},{2,1},{4,3},{6,5},{... | collective-permute-start | bytes 196616 | tf_op jit(solution)/shard_map/ppermute | solution.py:437
  25.3 17.1 %collective-permute-start.10 = (f32[64,128]{1,0:T(8,128)S(1)}, f32[64,128]{1,0:T(8,128)S(1)}, u32[]{:S(2)}, u32[]{:S(2)}) collective-permute-start(f32[64,128]{1,0:T(8,128)S(1)} %add.80), channel_id=1, source_target_pairs={{1,9},{3,11},{5,13},{7,15},{9,1},{11,3},{13,5},{15,7},{17,25},{19,... | collective-permute-start | bytes 98312 | tf_op jit(solution)/shard_map/ppermute | solution.py:384
  26.0 17.1 %collective-permute-start.11 = (f32[64,128]{1,0:T(8,128)S(1)}, f32[64,128]{1,0:T(8,128)S(1)}, u32[]{:S(2)}, u32[]{:S(2)}) collective-permute-start(f32[64,128]{1,0:T(8,128)S(1)} %add.80), channel_id=1, source_target_pairs={{0,2},{1,11},{2,0},{3,9},{4,6},{5,15},{6,4},{7,13},{8,10},{9,3},{1... | collective-permute-start | bytes 98312 | tf_op jit(solution)/shard_map/ppermute | solution.py:384
  30.2 12.9 %collective-permute-start.12 = (f32[64,128]{1,0:T(8,128)S(1)}, f32[64,128]{1,0:T(8,128)S(1)}, u32[]{:S(2)}, u32[]{:S(2)}) collective-permute-start(f32[64,128]{1,0:T(8,128)S(1)} %add.80), channel_id=1, source_target_pairs={{0,4},{1,13},{2,6},{3,15},{4,0},{5,9},{6,2},{7,11},{8,12},{9,5},{1... | collective-permute-start | bytes 98312 | tf_op jit(solution)/shard_map/ppermute | solution.py:384
  32.1 11.1 %collective-permute-start.13 = (f32[64,128]{1,0:T(8,128)S(1)}, f32[64,128]{1,0:T(8,128)S(1)}, u32[]{:S(2)}, u32[]{:S(2)}) collective-permute-start(f32[64,128]{1,0:T(8,128)S(1)} %add.80), channel_id=1, source_target_pairs={{0,6},{1,15},{2,4},{3,13},{4,2},{5,11},{6,0},{7,9},{8,14},{9,7},{1... | collective-permute-start | bytes 98312 | tf_op jit(solution)/shard_map/ppermute | solution.py:384
  37.1 12.1 %collective-permute-start.8 = (bf16[2,128,512]{2,1,0:T(8,128)(2,1)S(1)}, bf16[2,128,512]{2,1,0:T(8,128)(2,1)S(1)}, u32[]{:S(2)}, u32[]{:S(2)}) collective-permute-start(bf16[2,128,512]{2,1,0:T(8,128)(2,1)S(1)} %shard_map.125.token.own), channel_id=1, source_target_pairs={{0,1},{1,0},{2,3},{3,2},{4,5},{5,4},{6,7},{7,6},{8,9},{9,8},{10,11... | collective-permute-start | bytes 786440 | tf_op jit(solution)/shard_map/ppermute | solution.py:350
  42.4 6.8 %collective-permute-start.9 = (bf16[2,128,512]{2,1,0:T(8,128)(2,1)S(1)}, bf16[2,128,512]{2,1,0:T(8,128)(2,1)S(1)}, u32[]{:S(2)}, u32[]{:S(2)}) collective-permute-start(bf16[2,128,512]{2,1,0:T(8,128)(2,1)S(1)} %shard_map.125.token.own), channel_id=1, source_target_pairs={{1,2},{3,4},{5,6},{7,8},{9,10},{11,12},{13,14},{2,1},{4,3},{6,5},{... | collective-permute-start | bytes 786440 | tf_op jit(solution)/shard_map/ppermute | solution.py:461
  51.0 37.5 %collective-permute-start.21 = (bf16[16,512,256]{2,1,0:T(8,128)(2,1)S(1)}, bf16[16,512,256]{2,1,0:T(8,128)(2,1)S(1)}, u32[]{:S(2)}, u32[]{:S(2)}) collective-permute-start(bf16[16,512,256]{2,1,0:T(8,128)(2,1)S(1)} %copy-done.2), channel_id=1, source_target_pairs={{0,1},{1,0},{2,3},{3,2},{4,5},{5,4},{6,7},{7,6},{8,9},{9,8},{10,11... | collective-permute-start | bytes 12582920 | tf_op jit(solution)/shard_map/ppermute | solution.py:350
  53.8 31.6 %collective-permute-start.22 = (bf16[4,512,256]{2,1,0:T(8,128)(2,1)S(1)}, bf16[4,512,256]{2,1,0:T(8,128)(2,1)S(1)}, u32[]{:S(2)}, u32[]{:S(2)}) collective-permute-start(bf16[4,512,256]{2,1,0:T(8,128)(2,1)S(1)} %copy-done.4), channel_id=1, source_target_pairs={{0,1},{1,0},{2,3},{3,2},{4,5},{5,4},{6,7},{7,6},{8,9},{9,8},{10,11... | collective-permute-start | bytes 3145736 | tf_op jit(solution)/shard_map/ppermute | solution.py:350
  53.9 8.1 %collective-permute-start.15 = (bf16[2,64,512]{2,1,0:T(8,128)(2,1)S(1)}, bf16[2,64,512]{2,1,0:T(8,128)(2,1)S(1)}, u32[]{:S(2)}, u32[]{:S(2)}) collective-permute-start(bf16[2,64,512]{2,1,0:T(8,128)(2,1)S(1)} %shard_map.127.token.own), channel_id=1, source_target_pairs={{0,2},{1,3},{2,4},{3,5},{4,6},{5,7},{6,8},{7,9},{8,10},{9,11},{10,... | collective-permute-start | bytes 393224 | tf_op jit(solution)/shard_map/ppermute | solution.py:356
  58.6 7.1 %collective-permute-start.16 = (bf16[2,64,512]{2,1,0:T(8,128)(2,1)S(1)}, bf16[2,64,512]{2,1,0:T(8,128)(2,1)S(1)}, u32[]{:S(2)}, u32[]{:S(2)}) collective-permute-start(bf16[2,64,512]{2,1,0:T(8,128)(2,1)S(1)} %shard_map.127.token.own), channel_id=1, source_target_pairs={{2,0},{3,1},{4,2},{5,3},{6,4},{7,5},{8,6},{9,7},{10,8},{11,9},{12,... | collective-permute-start | bytes 393224 | tf_op jit(solution)/shard_map/ppermute | solution.py:356
  66.7 10.7 %collective-permute-start.17 = (bf16[2,64,512]{2,1,0:T(8,128)(2,1)S(1)}, bf16[2,64,512]{2,1,0:T(8,128)(2,1)S(1)}, u32[]{:S(2)}, u32[]{:S(2)}) collective-permute-start(bf16[2,64,512]{2,1,0:T(8,128)(2,1)S(1)} %shard_map.129.token.own), channel_id=1, source_target_pairs={{0,4},{1,5},{2,6},{3,7},{4,8},{5,9},{6,10},{7,11},{8,12},{9,13},{1... | collective-permute-start | bytes 393224 | tf_op jit(solution)/shard_map/ppermute | solution.py:356
  69.5 7.8 %collective-permute-start.18 = (bf16[2,64,512]{2,1,0:T(8,128)(2,1)S(1)}, bf16[2,64,512]{2,1,0:T(8,128)(2,1)S(1)}, u32[]{:S(2)}, u32[]{:S(2)}) collective-permute-start(bf16[2,64,512]{2,1,0:T(8,128)(2,1)S(1)} %shard_map.129.token.own), channel_id=1, source_target_pairs={{4,0},{5,1},{6,2},{7,3},{8,4},{9,5},{10,6},{11,7},{12,8},{13,9},{1... | collective-permute-start | bytes 393224 | tf_op jit(solution)/shard_map/ppermute | solution.py:356
  78.4 16.1 %collective-permute-start.20 = (bf16[2,64,512]{2,1,0:T(8,128)(2,1)S(1)}, bf16[2,64,512]{2,1,0:T(8,128)(2,1)S(1)}, u32[]{:S(2)}, u32[]{:S(2)}) collective-permute-start(bf16[2,64,512]{2,1,0:T(8,128)(2,1)S(1)} %shard_map.131.token.own), channel_id=1, source_target_pairs={{0,8},{1,9},{2,10},{3,11},{4,12},{5,13},{6,14},{7,15},{8,0},{9,1},... | collective-permute-start | bytes 393224 | tf_op jit(solution)/shard_map/ppermute | solution.py:482
  95.6 8.2 %collective-permute-start.25 = (bf16[2,64,256]{2,1,0:T(8,128)(2,1)S(1)}, bf16[2,64,256]{2,1,0:T(8,128)(2,1)S(1)}, u32[]{:S(2)}, u32[]{:S(2)}) collective-permute-start(bf16[2,64,256]{2,1,0:T(8,128)(2,1)S(1)} %get-tuple-element.51), channel_id=1, source_target_pairs={{0,1},{1,0},{2,3},{3,2},{4,5},{5,4},{6,7},{7,6},{8,9},{9,8},{10,11... | collective-permute-start | bytes 196616 | tf_op jit(solution)/shard_map/ppermute | solution.py:350
  95.8 8.7 %collective-permute-start.23 = (bf16[2,64,512]{2,1,0:T(8,128)(2,1)S(1)}, bf16[2,64,512]{2,1,0:T(8,128)(2,1)S(1)}, u32[]{:S(2)}, u32[]{:S(2)}) collective-permute-start(bf16[2,64,512]{2,1,0:T(8,128)(2,1)S(1)} %get-tuple-element.49.correction), channel_id=1, source_target_pairs={{0,2},{1,3},{2,4},{3,5},{4,6},{5,7},{6,8},{7,9},{8,10},{9,11},{10,... | collective-permute-start | bytes 393224 | tf_op jit(solution)/shard_map/ppermute | solution.py:356
  99.1 5.4 %collective-permute-start.24 = (bf16[2,64,512]{2,1,0:T(8,128)(2,1)S(1)}, bf16[2,64,512]{2,1,0:T(8,128)(2,1)S(1)}, u32[]{:S(2)}, u32[]{:S(2)}) collective-permute-start(bf16[2,64,512]{2,1,0:T(8,128)(2,1)S(1)} %get-tuple-element.49.correction), channel_id=1, source_target_pairs={{0,1},{1,2},{2,3},{3,4},{4,5},{5,6},{6,7},{7,8},{8,9},{9,10},{10,1... | collective-permute-start | bytes 393224 | tf_op jit(solution)/shard_map/ppermute | solution.py:356
  110.3 5.7 %collective-permute-start.27 = (f32[80,128]{1,0:T(8,128)S(1)}, f32[80,128]{1,0:T(8,128)S(1)}, u32[]{:S(2)}, u32[]{:S(2)}) collective-permute-start(f32[80,128]{1,0:T(8,128)S(1)} %add.87), channel_id=1, source_target_pairs={{0,2},{2,0},{4,6},{6,4},{8,10},{10,8},{12,14},{14,12},{1,3},{3,1},... | collective-permute-start | bytes 122888 | tf_op jit(solution)/shard_map/ppermute | solution.py:395
  114.0 4.9 %collective-permute-start.29 = (f32[80,128]{1,0:T(8,128)S(1)}, f32[80,128]{1,0:T(8,128)S(1)}, u32[]{:S(2)}, u32[]{:S(2)}) collective-permute-start(f32[80,128]{1,0:T(8,128)S(1)} %add.87), channel_id=1, source_target_pairs={{0,6},{2,4},{4,2},{6,0},{8,14},{10,12},{12,10},{14,8},{1,7},{3,5},... | collective-permute-start | bytes 122888 | tf_op jit(solution)/shard_map/ppermute | solution.py:395
  118.9 5.0 %collective-permute-start.30 = (f32[80,128]{1,0:T(8,128)S(1)}, f32[80,128]{1,0:T(8,128)S(1)}, u32[]{:S(2)}, u32[]{:S(2)}) collective-permute-start(f32[80,128]{1,0:T(8,128)S(1)} %add_add_fusion), channel_id=1, source_target_pairs={{0,8},{2,10},{4,12},{6,14},{8,0},{10,2},{12,4},{14,6},{1,9},{3,11}... | collective-permute-start | bytes 122888 | tf_op jit(solution)/shard_map/ppermute | solution.py:395
  (16 other events, 58.5 us)

commit v7 on v6

--- a/solution.py
+++ b/solution.py
@@ -52,17 +52,6 @@
     return pltpu.with_memory_space_constraint(operand, pltpu.HBM)
 
 
-def weight_copies(level, place, sources, weights, sem):
-    count = weights.shape[2]
-    slabs = pl.ds(place[0] * count, count)
-    copies = []
-    for side in range(2):
-        for part in range(2):
-            source = sources[2 * side + part].at[level, slabs]
-            copies.append(pltpu.make_async_copy(source, weights.at[side, part], sem.at[side, part]))
-    return copies
-
-
 def run(copies):
     for copy in copies:
         copy.start()
@@ -70,64 +59,103 @@
         copy.wait()
 
 
-def load_body(level, place, token, *rest):
-    *sources, weights, sem = rest
-    run(weight_copies(level, place, sources, weights, sem))
-
-
-def load_last_body(level, place, token, *rest):
-    *sources, final, final_other, weights, sem = rest
+def pack_body(levels, place, token, *rest):
+    *sources, sem = rest
+    outs = sources[len(sources) - (2 if levels[0] == 0 else 1) :]
+    lower, upper = sources[:2]
+    count = outs[0].shape[1]
+    copies = []
+    for out, core in zip(outs, (1 - place[0], place[0])):
+        slabs = pl.ds(core * count, count)
+        parts = [ref.at[level, slabs] for level in levels for ref in (lower, upper)]
+        if levels[0] != 0:
+            parts.append(sources[2].at[slabs])
+        for k, part in enumerate(parts):
+            copies.append(pltpu.make_async_copy(part, out.at[k], sem.at[len(copies)]))
+    run(copies)
+
+
+def pack(levels, place, token, lower, upper, final=None):
+    _, slabs, rows, half = lower.shape
+    count = 2 * len(levels) + (0 if final is None else 1)
+    shape = struct((count, slabs // 2, rows, half))
+    outs = [shape] if final is not None else [shape, shape]
+    operands = [in_hbm(x) for x in (lower, upper, final) if x is not None]
+    return pl.pallas_call(
+        functools.partial(pack_body, levels),
+        out_shape=outs,
+        in_specs=[SMEM] + [ANY] * (1 + len(operands)),
+        out_specs=[VMEM] * len(outs),
+        scratch_shapes=[pltpu.SemaphoreType.DMA((len(outs) * count,))],
+        compiler_params=pltpu.CompilerParams(vmem_limit_bytes=6 * MIB),
+        cost_estimate=pl.CostEstimate(
+            flops=0, bytes_accessed=2 * len(outs) * count * slabs * rows * half // 2, transcendentals=0
+        ),
+    )(place, token, *operands)
+
+
+def load_body(level, first, place, token, lower, upper, packed, weights, sem):
     count = weights.shape[2]
     slabs = pl.ds(place[0] * count, count)
-    above = place[1 + level] == 0
+    copies = []
+    for side, ref in enumerate((lower, upper)):
+        sources = (ref.at[level, slabs], packed.at[2 * (level - first) + side])
+        for part, source in enumerate(sources):
+            copies.append(pltpu.make_async_copy(source, weights.at[side, part], sem.at[side, part]))
+    run(copies)
+
+
+def load_last_body(level, first, place, token, lower, upper, packed, final, weights, sem):
+    count = weights.shape[2]
+    slabs = pl.ds(place[0] * count, count)
+    above = 1 - place[1 + level]
 
     def copy(source, side, part):
         return pltpu.make_async_copy(source, weights.at[side, part], sem.at[side, part])
 
-    for part in range(2):
-        pl.when(above)(lambda: copy(sources[2 + part].at[level, slabs], 0, part).start())
-        pl.when(jnp.logical_not(above))(lambda: copy(sources[part].at[level, slabs], 0, part).start())
-    finals = [copy(ref.at[slabs], 1, part) for part, ref in enumerate((final, final_other))]
-    for each in finals:
+    pl.when(above == 1)(lambda: copy(upper.at[level, slabs], 0, 0).start())
+    pl.when(above == 0)(lambda: copy(lower.at[level, slabs], 0, 0).start())
+    others = [
+        copy(packed.at[2 * (level - first) + above], 0, 1),
+        copy(final.at[slabs], 1, 0),
+        copy(packed.at[packed.shape[0] - 1], 1, 1),
+    ]
+    for each in others:
         each.start()
-    for part in range(2):
-        copy(sources[part].at[level, slabs], 0, part).wait()
-    for each in finals:
+    copy(lower.at[level, slabs], 0, 0).wait()
+    for each in others:
         each.wait()
 
 
-def load(body, place, token, sources):
-    _, slabs, rows, half = sources[0].shape
+def load(body, place, token, lower, upper, packed, *finals):
+    _, slabs, rows, half = lower.shape
     shape = (2, 2, slabs // 2, rows, half)
+    operands = [in_hbm(lower), in_hbm(upper), packed] + [in_hbm(x) for x in finals]
     return pl.pallas_call(
         body,
         out_shape=pltpu.VMEM(shape, bf16),
-        in_specs=[SMEM] + [ANY] * (1 + len(sources)),
+        in_specs=[SMEM] + [ANY] * (1 + len(operands)),
         out_specs=VMEM,
         scratch_shapes=[pltpu.SemaphoreType.DMA((2, 2))],
         compiler_params=pltpu.CompilerParams(vmem_limit_bytes=4 * MIB),
         cost_estimate=pl.CostEstimate(flops=0, bytes_accessed=8 * slabs * rows * half, transcendentals=0),
-    )(place, token, *[in_hbm(x) for x in sources])
-
-
-def load_whole_body(place, token, *rest):
-    count = len(rest) // 2
-    sources, targets, sem = rest[:count], rest[count:-1], rest[-1]
-    run([pltpu.make_async_copy(*pair, sem.at[k]) for k, pair in enumerate(zip(sources, targets))])
-
-
-def load_whole(place, token, arrays):
+    )(place, token, *operands)
+
+
+def load_whole_body(place, token, source, target, sem):
+    run([pltpu.make_async_copy(source, target, sem.at[0])])
+
+
+def load_whole(place, token, array):
     return pl.pallas_call(
         load_whole_body,
-        out_shape=[pltpu.VMEM(x.shape, x.dtype) for x in arrays],
-        in_specs=[SMEM] + [ANY] * (1 + len(arrays)),
-        out_specs=[VMEM] * len(arrays),
-        scratch_shapes=[pltpu.SemaphoreType.DMA((len(arrays),))],
-        compiler_params=pltpu.CompilerParams(vmem_limit_bytes=12 * MIB),
-        cost_estimate=pl.CostEstimate(
-            flops=0, bytes_accessed=sum(2 * x.size for x in arrays), transcendentals=0
-        ),
-    )(place, token, *[in_hbm(x) for x in arrays])
+        out_shape=pltpu.VMEM(array.shape, array.dtype),
+        in_specs=[SMEM, ANY, ANY],
+        out_specs=VMEM,
+        scratch_shapes=[pltpu.SemaphoreType.DMA((1,))],
+        compiler_params=pltpu.CompilerParams(vmem_limit_bytes=6 * MIB),
+        cost_estimate=pl.CostEstimate(flops=0, bytes_accessed=2 * array.size, transcendentals=0),
+    )(place, token, in_hbm(array))
 
 
 def image_body(place, table, extended, vectors, blocks, keep, send, moments, image):
@@ -168,28 +196,28 @@
     return columns(place[0], half), columns(1 - place[0], half)
 
 
-def first_vectors_body(place, extended, weights, out):
-    count, half = out.shape[0], weights.shape[-1]
+def first_vectors_body(place, extended, mine, packed, out):
+    count, half = out.shape[0], mine.shape[-1]
     first = extended.shape[0] // 3 + count * place[0]
-    for part, cols in enumerate(both_parts(place, half)):
+    for weights, cols in zip((mine, packed), both_parts(place, half)):
         for slab in range(count):
             own = first + slab
-            summed = dot(extended[own - 1], weights[0, part, slab])
-            summed = summed + dot(extended[own + 1], weights[1, part, slab])
+            summed = dot(extended[own - 1], weights[0, slab])
+            summed = summed + dot(extended[own + 1], weights[1, slab])
             out[slab, :, cols] = (extended[own, :, cols].astype(f32) - summed).astype(bf16)
 
 
-def first_body(place, image, inner, outer, vectors, weights, out):
+def first_body(place, image, inner, outer, vectors, mine, packed, out):
     count, rows, _ = image.shape
-    half = weights.shape[-1]
+    half = mine.shape[-1]
     odd = place[0] == 1
     below = [jnp.where(odd, inner[0], outer[0])] + [image[slab] for slab in range(count - 1)]
     above = [image[slab] for slab in range(1, count)] + [jnp.where(odd, outer[0], inner[0])]
     for slab in range(count):
         out[slab, rows : 2 * rows] = vectors[slab]
-    for part, cols in enumerate(both_parts(place, half)):
+    for weights, cols in zip((mine, packed), both_parts(place, half)):
         for slab in range(count):
-            summed = dot(below[slab], weights[0, part, slab]) + dot(above[slab], weights[1, part, slab])
+            summed = dot(below[slab], weights[0, slab]) + dot(above[slab], weights[1, slab])
             out[slab, 0:rows, cols] = (image[slab, :, cols].astype(f32) - summed).astype(bf16)
 
 
@@ -203,23 +231,31 @@
             out[slab, :, cols] = (own[slab, :, cols].astype(f32) - summed).astype(bf16)
 
 
-def second_body(place, own, inner, outer, weights, moments, out):
+def second_body(place, own, inner, outer, mine, packed, moments, note, out, lifted):
     count, rows, _ = out.shape
+    lifted[count * rows :] = note[...]
     high = moments[:, 0:rows].astype(bf16)
     low = (moments[:, 0:rows] - high.astype(f32)).astype(bf16)
     factors = (high.T, low.T)
-    for part, cols in enumerate(both_parts(place, weights.shape[-1])):
+    for weights, cols in zip((mine, packed), both_parts(place, mine.shape[-1])):
         for slab in range(count):
-            summed = dot(inner[slab], weights[1 - place[0], part, slab])
-            summed = summed + dot(outer[slab], weights[place[0], part, slab])
+            summed = dot(inner[slab], weights[2 + 1 - place[0], slab])
+            summed = summed + dot(outer[slab], weights[2 + place[0], slab])
             both = own[slab, :, cols].astype(f32) - summed
             image, vectors = both[:rows], both[rows:].astype(bf16)
             for factor in factors:
                 image = image - dot(factor, vectors)
             out[slab, :, cols] = image.astype(bf16)
+            lifted[slab * rows : (slab + 1) * rows, cols] = image.astype(bf16)
 
 
 def level_body(place, own, below, above, weights, out):
+    reduce_rows(place, own, (below, above), (0, 1), weights, out)
+
+
+def third_body(place, own, lifted, above, weights, out):
+    count, rows, _ = own.shape
+    below = [lifted[slab * rows : (slab + 1) * rows] for slab in range(count)]
     reduce_rows(place, own, (below, above), (0, 1), weights, out)
 
 
@@ -236,12 +272,12 @@
     product(place, rows, weights.at[1], whole, (keep, send))
 
 
-def final_body(place, own, final, final_other, whole, keep, send, weights, sem):
+def final_body(place, own, final, packed, whole, keep, send, weights, sem):
     count = own.shape[0]
-    slabs = pl.ds(place[0] * count, count)
+    sources = (final.at[pl.ds(place[0] * count, count)], packed.at[packed.shape[0] - 1])
     run([
-        pltpu.make_async_copy(ref.at[slabs], weights.at[part], sem.at[part])
-        for part, ref in enumerate((final, final_other))
+        pltpu.make_async_copy(source, weights.at[part], sem.at[part])
+        for part, source in enumerate(sources)
     ])
     product(place, own, weights, whole, (keep, send))
 
@@ -421,13 +457,16 @@
     steps = [max(2**l // own_count, 1) for l in levels]
     place = jnp.stack([core] + [link // step % 2 for step in steps]).astype(jnp.int32)
 
-    weights = (level_lower, swapped(level_lower), level_upper, swapped(level_upper))
     below, above = along(vectors, "slab", 1), along(vectors, "slab", -1)
     slab_ids = slab * slab_count + jnp.arange(slab_count, dtype=jnp.int32)[:, None]
     near = jnp.broadcast_to(jnp.arange(-1, 2, dtype=jnp.int32), (slab_count, 3))
     table = jnp.concatenate([near, far_source - slab_ids, slab_blocks, far_block], 1)
-    (held_blocks,) = load_whole(place, place, [blocks])
+    note = jnp.pad(table.astype(bf16), ((0, 16 - slab_count), (0, width - table.shape[1])))
+    held_blocks = load_whole(place, place, blocks)
+    theirs, mine = pack(levels[:2], place, held_blocks, level_lower, level_upper)
     extended = lax.all_gather(jnp.concatenate([below, vectors, above], 0), "vec", axis=2, tiled=True)
+    theirs, extended = lax.optimization_barrier((theirs, extended))
+    packed, mine = in_vmem(swapped(theirs)), in_vmem(mine)
     keep, send, moments = image_halves(place, table, extended, vectors, in_vmem(held_blocks))
     received, moments = swapped(send), moments + swapped(moments)
     image = jnp.where(core == 0, jnp.concatenate([keep, received], 2), jnp.concatenate([received, keep], 2))
@@ -437,50 +476,52 @@
     outer = lax.ppermute(lax.dynamic_slice_in_dim(image, (own_count - 1) * core, 1), CHAIN, outer_route)
     inner = swapped(lax.dynamic_slice_in_dim(image, (own_count - 1) * (1 - core), 1))
     reach = 1
-    while reach < slabs:
+    while True:
         radix = min(8, slabs // reach)
         share = shared_out(moments, reach, radix)
+        reach *= radix
+        if reach >= slabs:
+            break
         moments = share + swapped(share)
-        reach *= radix
-    moments = moments / rows_total
-
-    matrices = in_vmem(load(functools.partial(load_body, 0), place, image, weights))
+
     vectors_1 = kernel_call(
         first_vectors_body,
         struct(image.shape),
-        [SMEM] + [VMEM] * 2,
+        [SMEM] + [VMEM] * 3,
         flops=level_flops(image, 2),
-    )(place, extended, matrices)
+    )(place, extended, mine, packed)
     both = kernel_call(
         first_body,
         struct((own_count, 2 * rows, width)),
-        [SMEM] + [VMEM] * 5,
+        [SMEM] + [VMEM] * 6,
         flops=level_flops(image, 2),
-    )(place, image, inner, outer, vectors_1, matrices)
-    matrices = in_vmem(load(functools.partial(load_body, 1), place, both, weights))
+    )(place, image, inner, outer, vectors_1, mine, packed)
+    both, share = lax.optimization_barrier((both, share))
     outer, inner = lax.ppermute(both, CHAIN, outer_route), swapped(both)
-    residual = kernel_call(
+    moments = (share + swapped(share)) / rows_total
+    (theirs,) = pack(levels[2:], place, both, level_lower, level_upper, level_final)
+    theirs, inner, outer, moments = lax.optimization_barrier((theirs, inner, outer, moments))
+    residual, lifted = kernel_call(
         second_body,
-        struct(image.shape),
-        [SMEM] + [VMEM] * 5,
+        (struct(image.shape), struct((own_count * rows + 16, width))),
+        [SMEM] + [VMEM] * 7,
         flops=level_flops(both, 2),
-    )(place, both, inner, outer, matrices, moments)
-
-    late_blocks, late_final, residual = lax.optimization_barrier((blocks, level_final, residual))
-    finals = (level_final, swapped(late_final))
-    others = swapped(late_blocks)
+    )(place, both, inner, outer, mine, packed, moments, note)
+
+    packed = swapped(theirs)
     part = struct((own_count, rows, half))
     ends = (struct(residual.shape), part, part)
     one_partner = chain == 2 * steps[-1]
     for level, step in zip(levels[2:], steps[2:]):
         last = level == levels[-1]
         if last:
-            held_blocks, others = load_whole(place, residual, [blocks, others])
+            held_blocks = load_whole(place, residual, blocks)
         if last and one_partner:
-            matrices = load(functools.partial(load_last_body, level), place, residual, weights + finals)
+            body = functools.partial(load_last_body, level, 2)
+            matrices = load(body, place, residual, level_lower, level_upper, packed, level_final)
             (route,) = pair_routes(step)
             other = lax.ppermute(residual, CHAIN, route)
-            other, held_blocks, others = lax.optimization_barrier((other, held_blocks, others))
+            other, held_blocks = lax.optimization_barrier((other, held_blocks))
             correction, keep, send = kernel_call(
                 last_body,
                 ends,
@@ -489,18 +530,21 @@
                 flops=level_flops(residual, 2),
             )(place, residual, other, in_vmem(matrices))
             break
-        matrices = load(functools.partial(load_body, level), place, residual, weights)
-        partners = [along(residual, CHAIN, step), along(residual, CHAIN, -step)]
-        if level == levels[-2]:
-            matrices, note = lax.optimization_barrier((matrices, table))
-            lower_table = along(note, "slab", 1)
-            partners, lower_table = lax.optimization_barrier((partners, lower_table))
+        body = functools.partial(load_body, level, 2)
+        matrices = load(body, place, residual, level_lower, level_upper, packed)
+        below, above = along(residual if level > 2 else lifted, CHAIN, step), along(residual, CHAIN, -step)
+        if level == 2:
+            count = own_count * rows
+            lower_table = below[count : count + slab_count, : table.shape[1]].astype(jnp.int32)
         residual = kernel_call(
-            level_body,
+            level_body if level > 2 else third_body,
             struct(residual.shape),
             [SMEM] + [VMEM] * 4,
             flops=level_flops(residual, 2),
-        )(place, residual, *partners, in_vmem(matrices))
+        )(place, residual, below, above, in_vmem(matrices))
+        if level == 2:
+            late_blocks, residual = lax.optimization_barrier((blocks, residual))
+            others = swapped(late_blocks)
     if not one_partner:
         correction, keep, send = kernel_call(
             final_body,
@@ -508,13 +552,12 @@
             [SMEM, VMEM, ANY, ANY],
             [pltpu.VMEM((2, own_count, width, half), bf16), pltpu.SemaphoreType.DMA((2,))],
             flops=level_flops(residual, 1),
-        )(place, residual, *[in_hbm(x) for x in finals])
+        )(place, residual, in_hbm(level_final), packed)
     held_blocks, others = in_vmem(held_blocks), in_vmem(others)
 
     far, near = along(correction, CHAIN, 2), along(correction, CHAIN, 1)
     received = swapped(send)
     result = jnp.where(core == 0, jnp.concatenate([keep, received], 0), jnp.concatenate([received, keep], 0))
-    far, near, result = lax.optimization_barrier((far, near, result))
     tables = jnp.concatenate([lower_table, table], 0)
     flops = level_flops(image, 7)
     sums = (5 * rows // 2, 2 * rows)

time: 127 us -> 118 us (0.929)
  starting transfers between devices: 60.3 us -> 54.4 us
  blocking collectives: 7.08 us -> 2.37 us
  Pallas kernels: 33.2 us -> 37.9 us
  waiting for transfers between devices: 19.6 us -> 17.1 us
    pallas_call x6 -> x8, Pallas kernels: 11.5 us -> 20.1 us  [the longest x2 7.74 us: pack(): pl.pallas_call(functools.partial(pack_body, levels), out_shape=outs, in_s...]
    pallas_call x5 -> x3, Pallas kernels: 10.7 us -> 5.37 us  [load(): pl.pallas_call(body, out_shape=pltpu.VMEM(shape, bf16), in_specs=[SMEM] +...]
    all_gather x1, blocking collectives: 7.08 us -> 2.37 us  [on_device(): lax.all_gather(jnp.concatenate([below, vectors, above], 0), 'vec', axis=2...]
    ppermute x12 -> x11, starting transfers between devices: 14.9 us -> 11.1 us  [swapped(): return lax.ppermute(operand, 'vec', SWAP)]
    ppermute x4, starting transfers between devices: 5.29 us -> 8.04 us  [slab_total(): lax.ppermute(part, 'slab', route)]
    ppermute x1, starting transfers between devices: 6.39 us -> 3.72 us  [on_device(): other = lax.ppermute(residual, CHAIN, route)]
    ppermute x4, waiting for transfers between devices: 8.25 us -> 5.6 us  [slab_total(): lax.ppermute(part, 'slab', route)]
    ppermute x4, starting transfers between devices: 7.57 us -> 5.28 us  [shared_out(): received.append(lax.ppermute(part, CHAIN, route))]
  transfers between devices with their start and end apart: 32 -> 30, of which waited for: 11 -> 12; matrix products, arithmetic and copies ran while one was open for 1% -> 1% of each run, Pallas kernels for 21% -> 26%
where the time goes in v7:
time: 118 us; the launch traced here: 117 us
  starting transfers between devices  54.4 us (46%)
  Pallas kernels  37.9 us (32%)
  waiting for transfers between devices  17.1 us (14%)
  blocking collectives  2.37 us (2%)
  local copies, waits for them, and re-layouts  2.35 us (2%)
  between operations  1.83 us (2%)
    ppermute x8, starting transfers between devices, along(): return lax.ppermute(operand, axis, route)  25 us
    ppermute x11, starting transfers between devices, swapped(): return lax.ppermute(operand, 'vec', SWAP)  11.1 us
    ppermute x4, starting transfers between devices, slab_total(): lax.ppermute(part, 'slab', route)  8.04 us
    pallas_call x2, Pallas kernels, pack(): pl.pallas_call(functools.partial(pack_body, levels), out_shape=outs, in_s...  7.74 us
    ppermute x8, waiting for transfers between devices, along(): return lax.ppermute(operand, axis, route)  5.71 us
    ppermute x4, waiting for transfers between devices, slab_total(): lax.ppermute(part, 'slab', route)  5.6 us
    pallas_call x2, Pallas kernels, load_whole(): pl.pallas_call(load_whole_body, out_shape=pltpu.VMEM(array.shape, array.d...  5.47 us
    pallas_call x3, Pallas kernels, load(): pl.pallas_call(body, out_shape=pltpu.VMEM(shape, bf16), in_specs=[SMEM] +...  5.37 us
  transfers between devices with their start and end apart: 30, of which 12 were waited for; matrix products, arithmetic and copies ran while one was open for 1% of the time, Pallas kernels for 26%

profile of v7, /device:TPU:0, one launch (start us, length us, event | category | flops | bytes accessed | tf_op | source)
XLA Modules:
  0.0 117.0 jit_solution(2990114699667496069)
XLA Ops:
  1.9 5.5 %collective-permute-start = (bf16[4,64,256]{2,1,0:T(8,128)(2,1)}, bf16[4,64,256]{2,1,0:T(8,128)(2,1)S(1)}, u32[]{:S(2)}, u32[]{:S(2)}) collective-permute-start(bf16[4,64,256]{2,1,0:T(8,128)(2,1)} %vectors.1), channel_id=1, source_target_pairs={{0,2},{2,4},{4,6},{6,8},{8,10},{10,12},{12,14},{1,3},{3,5},{5,7},{... | collective-permute-start | bytes 393224 | tf_op jit(solution)/shard_map/ppermute | solution.py:392
  7.6 2.7 %shard_map.121.token.blocks = bf16[16,512,256]{2,1,0:T(8,128)(2,1)S(1)} custom-call(s32[6]{0:T(128)S(1)} %stack.24.place.token, s32[6]{0:T(128)S(1)} %stack.24.place.token, bf16[16,512,256]{2,1,0:T(8,128)(2,1)} %source.3), custom_call_target="tpu_custom_call" | custom-call | bytes 4194304 | tf_op jit(solution)/shard_map/pallas_call | solution.py:150
  10.4 5.1 %shard_map.122 = (bf16[4,2,512,256]{3,2,1,0:T(8,128)(2,1)}, bf16[4,2,512,256]{3,2,1,0:T(8,128)(2,1)S(1)}) custom-call(s32[6]{0:T(128)S(1)} %stack.24.place.token, bf16[16,512,256]{2,1,0:T(8,128)(2,1)S(1)} %shard_map.121.token.blocks, bf16[6,4,512,256]{3,2,1,0:T(8,128)(2,1)} %lower.5, bf16[6,4,512,256]{3,2,1,0:T(8,128)(2,1)} %upper.5), custom_call_target="tpu_custom_call" | custom-call | bytes 4194304 | tf_op jit(solution)/shard_map/pallas_call | solution.py:84
  15.6 2.4 %all_gather.3.extended = bf16[12,64,512]{2,1,0:T(8,128)(2,1)S(1)} all-gather(bf16[12,64,256]{2,1,0:T(8,128)(2,1)S(1)} %pad_maximum_fusion), channel_id=1, replica_groups=mesh['groups'=2,'slab'=8,'vec'=2] {'vec'}, dimensions={2}, use_global_device_ids=true | all-gather | bytes 1179648 | tf_op jit(solution)/shard_map/all_gather | solution.py:467
  18.3 2.2 %copy-done.1 = bf16[16,512,256]{2,1,0:T(8,128)(2,1)S(1)} copy-done((bf16[16,512,256]{2,1,0:T(8,128)(2,1)S(1)}, bf16[16,512,256]{2,1,0:T(8,128)(2,1)}, u32[]{:S(2)}) %copy-start.1) | copy-done | bytes 4194328
  20.5 2.2 %shard_map.123 = (bf16[2,64,256]{2,1,0:T(8,128)(2,1)S(1)}, bf16[2,64,256]{2,1,0:T(8,128)(2,1)S(1)}, f32[64,128]{1,0:T(8,128)S(1)}) custom-call(s32[6]{0:T(128)S(1)} %stack.24.place.token, s32[4,14]{1,0:T(4,128)S(1)} %get-tuple-element.66.table, bf16[12,64,512]{2,1,0:T(8,128)(2,1)S(1)} %all_gather.3.extended, bf16[4,64,256]{2,1,0:T(8,128)(2,1)S(1)} %copy-done.2, ...), custom_call_target="tpu_custom_call" | custom-call | flops 469762048 | bytes 4194304 | tf_op jit(solution)/shard_map/pallas_call | solution.py:185
  24.4 4.0 %collective-permute-start.10 = (f32[64,128]{1,0:T(8,128)S(1)}, f32[64,128]{1,0:T(8,128)S(1)}, u32[]{:S(2)}, u32[]{:S(2)}) collective-permute-start(f32[64,128]{1,0:T(8,128)S(1)} %add.82), channel_id=1, source_target_pairs={{0,6},{1,15},{2,4},{3,13},{4,2},{5,11},{6,0},{7,9},{8,14},{9,7},{1... | collective-permute-start | bytes 98312 | tf_op jit(solution)/shard_map/ppermute | solution.py:420
  32.5 3.3 %collective-permute-start.4 = (bf16[1,64,512]{2,1,0:T(8,128)(2,1)S(1)}, bf16[1,64,512]{2,1,0:T(8,128)(2,1)S(1)}, u32[]{:S(2)}, u32[]{:S(2)}) collective-permute-start(bf16[1,64,512]{2,1,0:T(8,128)(2,1)S(1)} %get-tuple-element.68), channel_id=1, source_target_pairs={{0,1},{1,0},{2,3},{3,2},{4,5},{5,4},{6,7},{7,6},{8,9},{9,8},{10,11... | collective-permute-start | bytes 196616 | tf_op jit(solution)/shard_map/ppermute | solution.py:386
  35.8 2.1 %shard_map.124.vectors = bf16[2,64,512]{2,1,0:T(8,128)(2,1)S(1)} custom-call(s32[6]{0:T(128)S(1)} %stack.24.place.token, bf16[12,64,512]{2,1,0:T(8,128)(2,1)S(1)} %all_gather.3.extended, bf16[4,2,512,256]{3,2,1,0:T(8,128)(2,1)S(1)} %get-tuple-element.40.mine, bf16[4,2,512,256]{3,2,1,0:T(8,128)(2,1)} %collective-permute-done.6.packed), custom_call_target="tpu_custom_call" | custom-call | flops 134217728 | tf_op jit(solution)/shard_map/pallas_call | solution.py:487
  37.9 2.1 %shard_map.125.token.own = bf16[2,128,512]{2,1,0:T(8,128)(2,1)S(1)} custom-call(s32[6]{0:T(128)S(1)} %stack.24.place.token, bf16[2,64,512]{2,1,0:T(8,128)(2,1)S(1)} %maximum_select_fusion.image, bf16[1,64,512]{2,1,0:T(8,128)(2,1)S(1)} %collective-permute-done.4.inner, bf16[1,64,512]{2,1,0:T(8,128)(2,1)S(1)} %collective-permute-done.5.outer, ...), custom_call_target="tpu_custom_call" | custom-call | flops 134217728 | tf_op jit(solution)/shard_map/pallas_call | solution.py:493
  40.6 3.7 %collective-permute-start.11 = (bf16[2,128,512]{2,1,0:T(8,128)(2,1)S(1)}, bf16[2,128,512]{2,1,0:T(8,128)(2,1)S(1)}, u32[]{:S(2)}, u32[]{:S(2)}) collective-permute-start(bf16[2,128,512]{2,1,0:T(8,128)(2,1)S(1)} %shard_map.125.token.own), channel_id=1, source_target_pairs={{0,1},{1,0},{2,3},{3,2},{4,5},{5,4},{6,7},{7,6},{8,9},{9,8},{10,11... | collective-permute-start | bytes 786440 | tf_op jit(solution)/shard_map/ppermute | solution.py:386
  44.5 2.6 %shard_map.126 = bf16[7,2,512,256]{3,2,1,0:T(8,128)(2,1)S(1)} custom-call(s32[6]{0:T(128)S(1)} %stack.24.place.token, bf16[2,128,512]{2,1,0:T(8,128)(2,1)S(1)} %shard_map.125.token.own, bf16[6,4,512,256]{3,2,1,0:T(8,128)(2,1)} %lower.5, bf16[6,4,512,256]{3,2,1,0:T(8,128)(2,1)} %upper.5, bf16[4,512,256]{2,1,0:T(8,128)(2,1)} %final.1), custom_call_target="tpu_custom_call" | custom-call | bytes 3670016 | tf_op jit(solution)/shard_map/pallas_call | solution.py:84
  49.1 2.8 %shard_map.127 = (bf16[2,64,512]{2,1,0:T(8,128)(2,1)S(1)}, bf16[144,512]{1,0:T(8,128)(2,1)S(1)}) custom-call(s32[6]{0:T(128)S(1)} %stack.24.place.token, bf16[2,128,512]{2,1,0:T(8,128)(2,1)S(1)} %shard_map.125.token.own, bf16[2,128,512]{2,1,0:T(8,128)(2,1)S(1)} %collective-permute-done.11.inner, bf16[2,128,512]{2,1,0:T(8,128)(2,1)S(1)} %collective-permute-done.12.outer, ...), custom_call_target="tpu_custom_call" | custom-call | flops 268435456 | tf_op jit(solution)/shard_map/pallas_call | solution.py:504
  51.9 6.0 %collective-permute-start.14 = (bf16[144,512]{1,0:T(8,128)(2,1)S(1)}, bf16[144,512]{1,0:T(8,128)(2,1)S(1)}, u32[]{:S(2)}, u32[]{:S(2)}) collective-permute-start(bf16[144,512]{1,0:T(8,128)(2,1)S(1)} %get-tuple-element.49), channel_id=1, source_target_pairs={{0,2},{1,3},{2,4},{3,5},{4,6},{5,7},{6,8},{7,9},{8,10},{9,11},{10,... | collective-permute-start | bytes 442376 | tf_op jit(solution)/shard_map/ppermute | solution.py:392
  61.3 4.8 %collective-permute-done.15.above = bf16[2,64,512]{2,1,0:T(8,128)(2,1)S(1)} collective-permute-done((bf16[2,64,512]{2,1,0:T(8,128)(2,1)S(1)}, bf16[2,64,512]{2,1,0:T(8,128)(2,1)S(1)}, u32[]{:S(2)}, u32[]{:S(2)}) %collective-permute-start.15) | collective-permute-done | bytes 131104 | tf_op jit(solution)/shard_map/ppermute | solution.py:392
  68.5 5.0 %collective-permute-start.17 = (bf16[2,64,512]{2,1,0:T(8,128)(2,1)S(1)}, bf16[2,64,512]{2,1,0:T(8,128)(2,1)S(1)}, u32[]{:S(2)}, u32[]{:S(2)}) collective-permute-start(bf16[2,64,512]{2,1,0:T(8,128)(2,1)S(1)} %shard_map.129.token.own), channel_id=1, source_target_pairs={{0,4},{1,5},{2,6},{3,7},{4,8},{5,9},{6,10},{7,11},{8,12},{9,13},{1... | collective-permute-start | bytes 393224 | tf_op jit(solution)/shard_map/ppermute | solution.py:392
  77.9 3.7 %collective-permute-start.19 = (bf16[2,64,512]{2,1,0:T(8,128)(2,1)S(1)}, bf16[2,64,512]{2,1,0:T(8,128)(2,1)S(1)}, u32[]{:S(2)}, u32[]{:S(2)}) collective-permute-start(bf16[2,64,512]{2,1,0:T(8,128)(2,1)S(1)} %shard_map.131.token.own), channel_id=1, source_target_pairs={{0,8},{1,9},{2,10},{3,11},{4,12},{5,13},{6,14},{7,15},{8,0},{9,1},... | collective-permute-start | bytes 393224 | tf_op jit(solution)/shard_map/ppermute | solution.py:523
  81.6 2.7 %shard_map.132.blocks = bf16[16,512,256]{2,1,0:T(8,128)(2,1)S(1)} custom-call(s32[6]{0:T(128)S(1)} %stack.24.place.token, bf16[2,64,512]{2,1,0:T(8,128)(2,1)S(1)} %shard_map.131.token.own, bf16[16,512,256]{2,1,0:T(8,128)(2,1)} %source.3), custom_call_target="tpu_custom_call" | custom-call | bytes 4194304 | tf_op jit(solution)/shard_map/pallas_call | solution.py:150
  88.6 3.0 %collective-permute-start.23 = (bf16[2,64,512]{2,1,0:T(8,128)(2,1)S(1)}, bf16[2,64,512]{2,1,0:T(8,128)(2,1)S(1)}, u32[]{:S(2)}, u32[]{:S(2)}) collective-permute-start(bf16[2,64,512]{2,1,0:T(8,128)(2,1)S(1)} %get-tuple-element.55.correction), channel_id=1, source_target_pairs={{0,2},{1,3},{2,4},{3,5},{4,6},{5,7},{6,8},{7,9},{8,10},{9,11},{10,... | collective-permute-start | bytes 393224 | tf_op jit(solution)/shard_map/ppermute | solution.py:392
  93.0 3.0 %shard_map.135 = (f32[2,64,512]{2,1,0:T(8,128)S(1)}, f32[160,128]{1,0:T(8,128)S(1)}, f32[8,128]{1,0:T(8,128)S(1)}) custom-call(s32[6]{0:T(128)S(1)} %stack.24.place.token, s32[8,14]{1,0:T(8,128)S(1)} %add_add_fusion.2.table, f32[8]{0:T(128)S(1)} %copy-done.3, s32[1]{0:T(128)S(6)} %copy.13.index, bf16[12,64,512]{2,1,0:T(8,128)(2,1)S(1)} %all_gather.3.extended, ...), custom_call_target="tpu_custom_call" | custom-call | flops 469762048 | tf_op jit(solution)/shard_map/pallas_call | solution.py:564
  96.0 2.5 %shard_map.136 = (f32[80,128]{1,0:T(8,128)S(1)}, f32[80,128]{1,0:T(8,128)S(1)}) custom-call(s32[6]{0:T(128)S(1)} %stack.24.place.token, s32[8,14]{1,0:T(8,128)S(1)} %add_add_fusion.2.table, bf16[12,64,512]{2,1,0:T(8,128)(2,1)S(1)} %all_gather.3.extended, bf16[2,64,512]{2,1,0:T(8,128)(2,1)S(1)} %get-tuple-element.55.correction, ...), custom_call_target="tpu_custom_call" | custom-call | flops 469762048 | tf_op jit(solution)/shard_map/pallas_call | solution.py:571
  100.6 3.6 %collective-permute-start.27 = (f32[80,128]{1,0:T(8,128)S(1)}, f32[80,128]{1,0:T(8,128)S(1)}, u32[]{:S(2)}, u32[]{:S(2)}) collective-permute-start(f32[80,128]{1,0:T(8,128)S(1)} %add.89), channel_id=1, source_target_pairs={{0,6},{2,4},{4,2},{6,0},{8,14},{10,12},{12,10},{14,8},{1,7},{3,5},... | collective-permute-start | bytes 122888 | tf_op jit(solution)/shard_map/ppermute | solution.py:431
  109.3 2.7 %collective-permute-start.28 = (f32[80,128]{1,0:T(8,128)S(1)}, f32[80,128]{1,0:T(8,128)S(1)}, u32[]{:S(2)}, u32[]{:S(2)}) collective-permute-start(f32[80,128]{1,0:T(8,128)S(1)} %add_add_fusion), channel_id=1, source_target_pairs={{0,8},{2,10},{4,12},{6,14},{8,0},{10,2},{12,4},{14,6},{1,9},{3,11}... | collective-permute-start | bytes 122888 | tf_op jit(solution)/shard_map/ppermute | solution.py:431
  112.0 2.3 %collective-permute-done.28 = f32[80,128]{1,0:T(8,128)S(1)} collective-permute-done((f32[80,128]{1,0:T(8,128)S(1)}, f32[80,128]{1,0:T(8,128)S(1)}, u32[]{:S(2)}, u32[]{:S(2)}) %collective-permute-start.28) | collective-permute-done | bytes 40992 | tf_op jit(solution)/shard_map/ppermute | solution.py:431
  (89 shorter events, 35.2 us)
Async XLA Ops:
  0.6 14.9 %collective-permute-start.1 = (bf16[4,64,256]{2,1,0:T(8,128)(2,1)}, bf16[4,64,256]{2,1,0:T(8,128)(2,1)S(1)}, u32[]{:S(2)}, u32[]{:S(2)}) collective-permute-start(bf16[4,64,256]{2,1,0:T(8,128)(2,1)} %vectors.1), channel_id=1, source_target_pairs={{2,0},{4,2},{6,4},{8,6},{10,8},{12,10},{14,12},{3,1},{5,3},{7,5},{... | collective-permute-start | bytes 393224 | tf_op jit(solution)/shard_map/ppermute | solution.py:392
  1.9 13.6 %collective-permute-start = (bf16[4,64,256]{2,1,0:T(8,128)(2,1)}, bf16[4,64,256]{2,1,0:T(8,128)(2,1)S(1)}, u32[]{:S(2)}, u32[]{:S(2)}) collective-permute-start(bf16[4,64,256]{2,1,0:T(8,128)(2,1)} %vectors.1), channel_id=1, source_target_pairs={{0,2},{2,4},{4,6},{6,8},{8,10},{10,12},{12,14},{1,3},{3,5},{5,7},{... | collective-permute-start | bytes 393224 | tf_op jit(solution)/shard_map/ppermute | solution.py:392
  18.0 17.7 %collective-permute-start.6 = (bf16[4,2,512,256]{3,2,1,0:T(8,128)(2,1)}, bf16[4,2,512,256]{3,2,1,0:T(8,128)(2,1)}, u32[]{:S(2)}, u32[]{:S(2)}) collective-permute-start(bf16[4,2,512,256]{3,2,1,0:T(8,128)(2,1)} %get-tuple-element.41), channel_id=1, source_target_pairs={{0,1},{1,0},{2,3},{3,2},{4,5},{5,4},{6,7},{7,6},{8,9},{9,8},{10,11... | collective-permute-start | bytes 6291464 | tf_op jit(solution)/shard_map/ppermute | solution.py:386
  24.4 6.2 %collective-permute-start.10 = (f32[64,128]{1,0:T(8,128)S(1)}, f32[64,128]{1,0:T(8,128)S(1)}, u32[]{:S(2)}, u32[]{:S(2)}) collective-permute-start(f32[64,128]{1,0:T(8,128)S(1)} %add.82), channel_id=1, source_target_pairs={{0,6},{1,15},{2,4},{3,13},{4,2},{5,11},{6,0},{7,9},{8,14},{9,7},{1... | collective-permute-start | bytes 98312 | tf_op jit(solution)/shard_map/ppermute | solution.py:420
  28.4 4.0 %collective-permute-start.9 = (f32[64,128]{1,0:T(8,128)S(1)}, f32[64,128]{1,0:T(8,128)S(1)}, u32[]{:S(2)}, u32[]{:S(2)}) collective-permute-start(f32[64,128]{1,0:T(8,128)S(1)} %add.82), channel_id=1, source_target_pairs={{0,4},{1,13},{2,6},{3,15},{4,0},{5,9},{6,2},{7,11},{8,12},{9,5},{1... | collective-permute-start | bytes 98312 | tf_op jit(solution)/shard_map/ppermute | solution.py:420
  28.9 6.9 %collective-permute-start.8 = (f32[64,128]{1,0:T(8,128)S(1)}, f32[64,128]{1,0:T(8,128)S(1)}, u32[]{:S(2)}, u32[]{:S(2)}) collective-permute-start(f32[64,128]{1,0:T(8,128)S(1)} %add.82), channel_id=1, source_target_pairs={{0,2},{1,11},{2,0},{3,9},{4,6},{5,15},{6,4},{7,13},{8,10},{9,3},{1... | collective-permute-start | bytes 98312 | tf_op jit(solution)/shard_map/ppermute | solution.py:420
  29.1 6.7 %collective-permute-start.7 = (f32[64,128]{1,0:T(8,128)S(1)}, f32[64,128]{1,0:T(8,128)S(1)}, u32[]{:S(2)}, u32[]{:S(2)}) collective-permute-start(f32[64,128]{1,0:T(8,128)S(1)} %add.82), channel_id=1, source_target_pairs={{1,9},{3,11},{5,13},{7,15},{9,1},{11,3},{13,5},{15,7},{17,25},{19,... | collective-permute-start | bytes 98312 | tf_op jit(solution)/shard_map/ppermute | solution.py:420
  30.7 7.2 %collective-permute-start.5 = (bf16[1,64,512]{2,1,0:T(8,128)(2,1)S(1)}, bf16[1,64,512]{2,1,0:T(8,128)(2,1)S(1)}, u32[]{:S(2)}, u32[]{:S(2)}) collective-permute-start(bf16[1,64,512]{2,1,0:T(8,128)(2,1)S(1)} %get-tuple-element.67), channel_id=1, source_target_pairs={{1,2},{3,4},{5,6},{7,8},{9,10},{11,12},{13,14},{2,1},{4,3},{6,5},{... | collective-permute-start | bytes 196616 | tf_op jit(solution)/shard_map/ppermute | solution.py:476
  32.5 5.4 %collective-permute-start.4 = (bf16[1,64,512]{2,1,0:T(8,128)(2,1)S(1)}, bf16[1,64,512]{2,1,0:T(8,128)(2,1)S(1)}, u32[]{:S(2)}, u32[]{:S(2)}) collective-permute-start(bf16[1,64,512]{2,1,0:T(8,128)(2,1)S(1)} %get-tuple-element.68), channel_id=1, source_target_pairs={{0,1},{1,0},{2,3},{3,2},{4,5},{5,4},{6,7},{7,6},{8,9},{9,8},{10,11... | collective-permute-start | bytes 196616 | tf_op jit(solution)/shard_map/ppermute | solution.py:386
  40.0 7.1 %collective-permute-start.12 = (bf16[2,128,512]{2,1,0:T(8,128)(2,1)S(1)}, bf16[2,128,512]{2,1,0:T(8,128)(2,1)S(1)}, u32[]{:S(2)}, u32[]{:S(2)}) collective-permute-start(bf16[2,128,512]{2,1,0:T(8,128)(2,1)S(1)} %shard_map.125.token.own), channel_id=1, source_target_pairs={{1,2},{3,4},{5,6},{7,8},{9,10},{11,12},{13,14},{2,1},{4,3},{6,5},{... | collective-permute-start | bytes 786440 | tf_op jit(solution)/shard_map/ppermute | solution.py:500
  40.6 6.5 %collective-permute-start.11 = (bf16[2,128,512]{2,1,0:T(8,128)(2,1)S(1)}, bf16[2,128,512]{2,1,0:T(8,128)(2,1)S(1)}, u32[]{:S(2)}, u32[]{:S(2)}) collective-permute-start(bf16[2,128,512]{2,1,0:T(8,128)(2,1)S(1)} %shard_map.125.token.own), channel_id=1, source_target_pairs={{0,1},{1,0},{2,3},{3,2},{4,5},{5,4},{6,7},{7,6},{8,9},{9,8},{10,11... | collective-permute-start | bytes 786440 | tf_op jit(solution)/shard_map/ppermute | solution.py:386
  47.1 12.4 %collective-permute-start.16 = (bf16[7,2,512,256]{3,2,1,0:T(8,128)(2,1)S(1)}, bf16[7,2,512,256]{3,2,1,0:T(8,128)(2,1)S(1)}, u32[]{:S(2)}, u32[]{:S(2)}) collective-permute-start(bf16[7,2,512,256]{3,2,1,0:T(8,128)(2,1)S(1)} %shard_map.126), channel_id=1, source_target_pairs={{0,1},{1,0},{2,3},{3,2},{4,5},{5,4},{6,7},{7,6},{8,9},{9,8},{10,11... | collective-permute-start | bytes 11010056 | tf_op jit(solution)/shard_map/ppermute | solution.py:386
  51.9 14.2 %collective-permute-start.14 = (bf16[144,512]{1,0:T(8,128)(2,1)S(1)}, bf16[144,512]{1,0:T(8,128)(2,1)S(1)}, u32[]{:S(2)}, u32[]{:S(2)}) collective-permute-start(bf16[144,512]{1,0:T(8,128)(2,1)S(1)} %get-tuple-element.49), channel_id=1, source_target_pairs={{0,2},{1,3},{2,4},{3,5},{4,6},{5,7},{6,8},{7,9},{8,10},{9,11},{10,... | collective-permute-start | bytes 442376 | tf_op jit(solution)/shard_map/ppermute | solution.py:392
  58.0 8.1 %collective-permute-start.15 = (bf16[2,64,512]{2,1,0:T(8,128)(2,1)S(1)}, bf16[2,64,512]{2,1,0:T(8,128)(2,1)S(1)}, u32[]{:S(2)}, u32[]{:S(2)}) collective-permute-start(bf16[2,64,512]{2,1,0:T(8,128)(2,1)S(1)} %get-tuple-element.48.token.own), channel_id=1, source_target_pairs={{2,0},{3,1},{4,2},{5,3},{6,4},{7,5},{8,6},{9,7},{10,8},{11,9},{12,... | collective-permute-start | bytes 393224 | tf_op jit(solution)/shard_map/ppermute | solution.py:392
  67.1 25.9 %collective-permute-start.21 = (bf16[16,512,256]{2,1,0:T(8,128)(2,1)S(1)}, bf16[16,512,256]{2,1,0:T(8,128)(2,1)S(1)}, u32[]{:S(2)}, u32[]{:S(2)}) collective-permute-start(bf16[16,512,256]{2,1,0:T(8,128)(2,1)S(1)} %copy-done.4), channel_id=1, source_target_pairs={{0,1},{1,0},{2,3},{3,2},{4,5},{5,4},{6,7},{7,6},{8,9},{9,8},{10,11... | collective-permute-start | bytes 12582920 | tf_op jit(solution)/shard_map/ppermute | solution.py:386
  67.2 8.7 %collective-permute-start.18 = (bf16[2,64,512]{2,1,0:T(8,128)(2,1)S(1)}, bf16[2,64,512]{2,1,0:T(8,128)(2,1)S(1)}, u32[]{:S(2)}, u32[]{:S(2)}) collective-permute-start(bf16[2,64,512]{2,1,0:T(8,128)(2,1)S(1)} %shard_map.129.token.own), channel_id=1, source_target_pairs={{4,0},{5,1},{6,2},{7,3},{8,4},{9,5},{10,6},{11,7},{12,8},{13,9},{1... | collective-permute-start | bytes 393224 | tf_op jit(solution)/shard_map/ppermute | solution.py:392
  68.5 8.3 %collective-permute-start.17 = (bf16[2,64,512]{2,1,0:T(8,128)(2,1)S(1)}, bf16[2,64,512]{2,1,0:T(8,128)(2,1)S(1)}, u32[]{:S(2)}, u32[]{:S(2)}) collective-permute-start(bf16[2,64,512]{2,1,0:T(8,128)(2,1)S(1)} %shard_map.129.token.own), channel_id=1, source_target_pairs={{0,4},{1,5},{2,6},{3,7},{4,8},{5,9},{6,10},{7,11},{8,12},{9,13},{1... | collective-permute-start | bytes 393224 | tf_op jit(solution)/shard_map/ppermute | solution.py:392
  77.9 9.6 %collective-permute-start.19 = (bf16[2,64,512]{2,1,0:T(8,128)(2,1)S(1)}, bf16[2,64,512]{2,1,0:T(8,128)(2,1)S(1)}, u32[]{:S(2)}, u32[]{:S(2)}) collective-permute-start(bf16[2,64,512]{2,1,0:T(8,128)(2,1)S(1)} %shard_map.131.token.own), channel_id=1, source_target_pairs={{0,8},{1,9},{2,10},{3,11},{4,12},{5,13},{6,14},{7,15},{8,0},{9,1},... | collective-permute-start | bytes 393224 | tf_op jit(solution)/shard_map/ppermute | solution.py:523
  88.6 7.4 %collective-permute-start.23 = (bf16[2,64,512]{2,1,0:T(8,128)(2,1)S(1)}, bf16[2,64,512]{2,1,0:T(8,128)(2,1)S(1)}, u32[]{:S(2)}, u32[]{:S(2)}) collective-permute-start(bf16[2,64,512]{2,1,0:T(8,128)(2,1)S(1)} %get-tuple-element.55.correction), channel_id=1, source_target_pairs={{0,2},{1,3},{2,4},{3,5},{4,6},{5,7},{6,8},{7,9},{8,10},{9,11},{10,... | collective-permute-start | bytes 393224 | tf_op jit(solution)/shard_map/ppermute | solution.py:392
  91.6 4.4 %collective-permute-start.22 = (bf16[2,64,512]{2,1,0:T(8,128)(2,1)S(1)}, bf16[2,64,512]{2,1,0:T(8,128)(2,1)S(1)}, u32[]{:S(2)}, u32[]{:S(2)}) collective-permute-start(bf16[2,64,512]{2,1,0:T(8,128)(2,1)S(1)} %get-tuple-element.55.correction), channel_id=1, source_target_pairs={{0,1},{1,2},{2,3},{3,4},{4,5},{5,6},{6,7},{7,8},{8,9},{9,10},{10,1... | collective-permute-start | bytes 393224 | tf_op jit(solution)/shard_map/ppermute | solution.py:392
  100.6 5.6 %collective-permute-start.27 = (f32[80,128]{1,0:T(8,128)S(1)}, f32[80,128]{1,0:T(8,128)S(1)}, u32[]{:S(2)}, u32[]{:S(2)}) collective-permute-start(f32[80,128]{1,0:T(8,128)S(1)} %add.89), channel_id=1, source_target_pairs={{0,6},{2,4},{4,2},{6,0},{8,14},{10,12},{12,10},{14,8},{1,7},{3,5},... | collective-permute-start | bytes 122888 | tf_op jit(solution)/shard_map/ppermute | solution.py:431
  104.2 4.0 %collective-permute-start.26 = (f32[80,128]{1,0:T(8,128)S(1)}, f32[80,128]{1,0:T(8,128)S(1)}, u32[]{:S(2)}, u32[]{:S(2)}) collective-permute-start(f32[80,128]{1,0:T(8,128)S(1)} %add.89), channel_id=1, source_target_pairs={{0,4},{2,6},{4,0},{6,2},{8,12},{10,14},{12,8},{14,10},{1,5},{3,7},... | collective-permute-start | bytes 122888 | tf_op jit(solution)/shard_map/ppermute | solution.py:431
  105.9 8.3 %collective-permute-start.20 = (bf16[2,64,256]{2,1,0:T(8,128)(2,1)S(1)}, bf16[2,64,256]{2,1,0:T(8,128)(2,1)S(1)}, u32[]{:S(2)}, u32[]{:S(2)}) collective-permute-start(bf16[2,64,256]{2,1,0:T(8,128)(2,1)S(1)} %get-tuple-element.54), channel_id=1, source_target_pairs={{0,1},{1,0},{2,3},{3,2},{4,5},{5,4},{6,7},{7,6},{8,9},{9,8},{10,11... | collective-permute-start | bytes 196616 | tf_op jit(solution)/shard_map/ppermute | solution.py:386
  109.3 5.0 %collective-permute-start.28 = (f32[80,128]{1,0:T(8,128)S(1)}, f32[80,128]{1,0:T(8,128)S(1)}, u32[]{:S(2)}, u32[]{:S(2)}) collective-permute-start(f32[80,128]{1,0:T(8,128)S(1)} %add_add_fusion), channel_id=1, source_target_pairs={{0,8},{2,10},{4,12},{6,14},{8,0},{10,2},{12,4},{14,6},{1,9},{3,11}... | collective-permute-start | bytes 122888 | tf_op jit(solution)/shard_map/ppermute | solution.py:431
  (14 other events, 66.8 us)

commit v8 on v7

--- a/solution.py
+++ b/solution.py
@@ -59,39 +59,28 @@
         copy.wait()
 
 
-def pack_body(levels, place, token, *rest):
-    *sources, sem = rest
-    outs = sources[len(sources) - (2 if levels[0] == 0 else 1) :]
-    lower, upper = sources[:2]
-    count = outs[0].shape[1]
-    copies = []
-    for out, core in zip(outs, (1 - place[0], place[0])):
-        slabs = pl.ds(core * count, count)
-        parts = [ref.at[level, slabs] for level in levels for ref in (lower, upper)]
-        if levels[0] != 0:
-            parts.append(sources[2].at[slabs])
-        for k, part in enumerate(parts):
-            copies.append(pltpu.make_async_copy(part, out.at[k], sem.at[len(copies)]))
-    run(copies)
-
-
-def pack(levels, place, token, lower, upper, final=None):
-    _, slabs, rows, half = lower.shape
-    count = 2 * len(levels) + (0 if final is None else 1)
-    shape = struct((count, slabs // 2, rows, half))
-    outs = [shape] if final is not None else [shape, shape]
-    operands = [in_hbm(x) for x in (lower, upper, final) if x is not None]
+def pack_body(levels, place, token, lower, upper, *rest):
+    *final, out, sem = rest
+    count = out.shape[1]
+    slabs = pl.ds((1 - place[0]) * count, count)
+    parts = [ref.at[level, slabs] for level in levels for ref in (lower, upper)]
+    parts += [ref.at[slabs] for ref in final]
+    run([pltpu.make_async_copy(part, out.at[k], sem.at[k]) for k, part in enumerate(parts)])
+
+
+def pack(levels, place, token, *operands):
+    _, slabs, rows, half = operands[0].shape
+    count = 2 * len(levels) + len(operands) - 2
+    out = struct((count, slabs // 2, rows, half))
     return pl.pallas_call(
         functools.partial(pack_body, levels),
-        out_shape=outs,
+        out_shape=out,
         in_specs=[SMEM] + [ANY] * (1 + len(operands)),
-        out_specs=[VMEM] * len(outs),
-        scratch_shapes=[pltpu.SemaphoreType.DMA((len(outs) * count,))],
+        out_specs=VMEM,
+        scratch_shapes=[pltpu.SemaphoreType.DMA((count,))],
         compiler_params=pltpu.CompilerParams(vmem_limit_bytes=6 * MIB),
-        cost_estimate=pl.CostEstimate(
-            flops=0, bytes_accessed=2 * len(outs) * count * slabs * rows * half // 2, transcendentals=0
-        ),
-    )(place, token, *operands)
+        cost_estimate=pl.CostEstimate(flops=0, bytes_accessed=2 * out.size, transcendentals=0),
+    )(place, token, *[in_hbm(x) for x in operands])
 
 
 def load_body(level, first, place, token, lower, upper, packed, weights, sem):
@@ -196,28 +185,28 @@
     return columns(place[0], half), columns(1 - place[0], half)
 
 
-def first_vectors_body(place, extended, mine, packed, out):
-    count, half = out.shape[0], mine.shape[-1]
+def first_vectors_body(place, extended, weights, out):
+    count, half = out.shape[0], weights.shape[-1]
     first = extended.shape[0] // 3 + count * place[0]
-    for weights, cols in zip((mine, packed), both_parts(place, half)):
+    for part, cols in enumerate(both_parts(place, half)):
         for slab in range(count):
             own = first + slab
-            summed = dot(extended[own - 1], weights[0, slab])
-            summed = summed + dot(extended[own + 1], weights[1, slab])
+            summed = dot(extended[own - 1], weights[0, part, slab])
+            summed = summed + dot(extended[own + 1], weights[1, part, slab])
             out[slab, :, cols] = (extended[own, :, cols].astype(f32) - summed).astype(bf16)
 
 
-def first_body(place, image, inner, outer, vectors, mine, packed, out):
+def first_body(place, image, inner, outer, vectors, weights, out):
     count, rows, _ = image.shape
-    half = mine.shape[-1]
+    half = weights.shape[-1]
     odd = place[0] == 1
     below = [jnp.where(odd, inner[0], outer[0])] + [image[slab] for slab in range(count - 1)]
     above = [image[slab] for slab in range(1, count)] + [jnp.where(odd, outer[0], inner[0])]
     for slab in range(count):
         out[slab, rows : 2 * rows] = vectors[slab]
-    for weights, cols in zip((mine, packed), both_parts(place, half)):
+    for part, cols in enumerate(both_parts(place, half)):
         for slab in range(count):
-            summed = dot(below[slab], weights[0, slab]) + dot(above[slab], weights[1, slab])
+            summed = dot(below[slab], weights[0, part, slab]) + dot(above[slab], weights[1, part, slab])
             out[slab, 0:rows, cols] = (image[slab, :, cols].astype(f32) - summed).astype(bf16)
 
 
@@ -231,16 +220,16 @@
             out[slab, :, cols] = (own[slab, :, cols].astype(f32) - summed).astype(bf16)
 
 
-def second_body(place, own, inner, outer, mine, packed, moments, note, out, lifted):
+def second_body(place, own, inner, outer, weights, moments, note, out, lifted):
     count, rows, _ = out.shape
     lifted[count * rows :] = note[...]
     high = moments[:, 0:rows].astype(bf16)
     low = (moments[:, 0:rows] - high.astype(f32)).astype(bf16)
     factors = (high.T, low.T)
-    for weights, cols in zip((mine, packed), both_parts(place, mine.shape[-1])):
+    for part, cols in enumerate(both_parts(place, weights.shape[-1])):
         for slab in range(count):
-            summed = dot(inner[slab], weights[2 + 1 - place[0], slab])
-            summed = summed + dot(outer[slab], weights[2 + place[0], slab])
+            summed = dot(inner[slab], weights[1 - place[0], part, slab])
+            summed = summed + dot(outer[slab], weights[place[0], part, slab])
             both = own[slab, :, cols].astype(f32) - summed
             image, vectors = both[:rows], both[rows:].astype(bf16)
             for factor in factors:
@@ -407,21 +396,6 @@
     return parts[0]
 
 
-def shared_out(part, reach, radix):
-    slabs = lax.axis_size("slab")
-    split = radix // 2
-    received = []
-    for offset in range(split):
-        route = []
-        for i in range(slabs):
-            if offset:
-                route.append((2 * i, 2 * (i ^ (offset * reach))))
-            route.append((2 * i + 1, 2 * (i ^ ((offset + split) * reach)) + 1))
-        received.append(lax.ppermute(part, CHAIN, route))
-    received[0] = jnp.where(lax.axis_index("vec") == 0, part, received[0])
-    return summed_up(received)
-
-
 def slab_total(part):
     slabs = lax.axis_size("slab")
     reach = 1
@@ -463,52 +437,49 @@
     table = jnp.concatenate([near, far_source - slab_ids, slab_blocks, far_block], 1)
     note = jnp.pad(table.astype(bf16), ((0, 16 - slab_count), (0, width - table.shape[1])))
     held_blocks = load_whole(place, place, blocks)
-    theirs, mine = pack(levels[:2], place, held_blocks, level_lower, level_upper)
+    theirs = pack(levels[:3], place, held_blocks, level_lower, level_upper)
     extended = lax.all_gather(jnp.concatenate([below, vectors, above], 0), "vec", axis=2, tiled=True)
     theirs, extended = lax.optimization_barrier((theirs, extended))
-    packed, mine = in_vmem(swapped(theirs)), in_vmem(mine)
     keep, send, moments = image_halves(place, table, extended, vectors, in_vmem(held_blocks))
     received, moments = swapped(send), moments + swapped(moments)
     image = jnp.where(core == 0, jnp.concatenate([keep, received], 2), jnp.concatenate([received, keep], 2))
-    image, moments = lax.optimization_barrier((image, moments))
+    image, moments, theirs = lax.optimization_barrier((image, moments, theirs))
+    packed = swapped(theirs)
 
     inner_route, outer_route = pair_routes(1)
     outer = lax.ppermute(lax.dynamic_slice_in_dim(image, (own_count - 1) * core, 1), CHAIN, outer_route)
     inner = swapped(lax.dynamic_slice_in_dim(image, (own_count - 1) * (1 - core), 1))
-    reach = 1
-    while True:
-        radix = min(8, slabs // reach)
-        share = shared_out(moments, reach, radix)
-        reach *= radix
-        if reach >= slabs:
-            break
-        moments = share + swapped(share)
-
+    flips = [[(i, i ^ 2**bit) for i in range(slabs)] for bit in range((slabs - 1).bit_length())]
+    received = lax.ppermute(moments, "slab", flips[0])
+    body = functools.partial(load_body, 0, 0)
+    matrices = in_vmem(load(body, place, image, level_lower, level_upper, packed))
     vectors_1 = kernel_call(
         first_vectors_body,
         struct(image.shape),
-        [SMEM] + [VMEM] * 3,
+        [SMEM] + [VMEM] * 2,
         flops=level_flops(image, 2),
-    )(place, extended, mine, packed)
+    )(place, extended, matrices)
     both = kernel_call(
         first_body,
         struct((own_count, 2 * rows, width)),
-        [SMEM] + [VMEM] * 6,
+        [SMEM] + [VMEM] * 5,
         flops=level_flops(image, 2),
-    )(place, image, inner, outer, vectors_1, mine, packed)
-    both, share = lax.optimization_barrier((both, share))
+    )(place, image, inner, outer, vectors_1, matrices)
+    both, received = lax.optimization_barrier((both, received))
     outer, inner = lax.ppermute(both, CHAIN, outer_route), swapped(both)
-    moments = (share + swapped(share)) / rows_total
-    (theirs,) = pack(levels[2:], place, both, level_lower, level_upper, level_final)
-    theirs, inner, outer, moments = lax.optimization_barrier((theirs, inner, outer, moments))
+    for flip in flips[1:]:
+        moments = moments + received
+        received = lax.ppermute(moments, "slab", flip)
+    moments = (moments + received) / rows_total
+    body = functools.partial(load_body, 1, 0)
+    matrices = in_vmem(load(body, place, both, level_lower, level_upper, packed))
     residual, lifted = kernel_call(
         second_body,
         (struct(image.shape), struct((own_count * rows + 16, width))),
-        [SMEM] + [VMEM] * 7,
+        [SMEM] + [VMEM] * 6,
         flops=level_flops(both, 2),
-    )(place, both, inner, outer, mine, packed, moments, note)
-
-    packed = swapped(theirs)
+    )(place, both, inner, outer, matrices, moments, note)
+
     part = struct((own_count, rows, half))
     ends = (struct(residual.shape), part, part)
     one_partner = chain == 2 * steps[-1]
@@ -517,7 +488,7 @@
         if last:
             held_blocks = load_whole(place, residual, blocks)
         if last and one_partner:
-            body = functools.partial(load_last_body, level, 2)
+            body = functools.partial(load_last_body, level, 3)
             matrices = load(body, place, residual, level_lower, level_upper, packed, level_final)
             (route,) = pair_routes(step)
             other = lax.ppermute(residual, CHAIN, route)
@@ -530,21 +501,24 @@
                 flops=level_flops(residual, 2),
             )(place, residual, other, in_vmem(matrices))
             break
-        body = functools.partial(load_body, level, 2)
+        body = functools.partial(load_body, level, 0 if level == 2 else 3)
         matrices = load(body, place, residual, level_lower, level_upper, packed)
         below, above = along(residual if level > 2 else lifted, CHAIN, step), along(residual, CHAIN, -step)
         if level == 2:
             count = own_count * rows
             lower_table = below[count : count + slab_count, : table.shape[1]].astype(jnp.int32)
+            theirs = pack(levels[3:], place, matrices, level_lower, level_upper, level_final)
+            theirs, below, above = lax.optimization_barrier((theirs, below, above))
+            packed = swapped(theirs)
+        if level == 3:
+            late_blocks, below, above = lax.optimization_barrier((blocks, below, above))
+            others = swapped(late_blocks)
         residual = kernel_call(
             level_body if level > 2 else third_body,
             struct(residual.shape),
             [SMEM] + [VMEM] * 4,
             flops=level_flops(residual, 2),
         )(place, residual, below, above, in_vmem(matrices))
-        if level == 2:
-            late_blocks, residual = lax.optimization_barrier((blocks, residual))
-            others = swapped(late_blocks)
     if not one_partner:
         correction, keep, send = kernel_call(
             final_body,

time: 118 us -> 124 us (1.051)
  waiting for transfers between devices: 17.1 us -> 35.9 us
  starting transfers between devices: 54.4 us -> 45.2 us
  Pallas kernels: 37.9 us -> 34.8 us
    ppermute x11 -> x10, waiting for transfers between devices: 2.49 us -> 12.6 us  [swapped(): return lax.ppermute(operand, 'vec', SWAP)]
    ppermute x11 -> x10, starting transfers between devices: 11.1 us -> 2.73 us  [swapped(): return lax.ppermute(operand, 'vec', SWAP)]
    ppermute x4 -> x3, starting transfers between devices: 5.28 us -> 10.7 us  [the longest x2 6.71 us: on_device(): received = lax.ppermute(moments, 'slab', flip)]
    pallas_call x3, Pallas kernels: 9.82 us -> 5.99 us  [the longest x2 4.97 us: pack(): pl.pallas_call(functools.partial(pack_body, levels), out_shape=out, in_sp...]
    pallas_call x3 -> x5, Pallas kernels: 5.37 us -> 8.95 us  [load(): pl.pallas_call(body, out_shape=pltpu.VMEM(shape, bf16), in_specs=[SMEM] +...]
    ppermute x8, starting transfers between devices: 25 us -> 21.9 us  [along(): return lax.ppermute(operand, axis, route)]
    ppermute x8, waiting for transfers between devices: 5.71 us -> 8.42 us  [along(): return lax.ppermute(operand, axis, route)]
    ppermute x4 -> x3, waiting for transfers between devices: 2.05 us -> 4.38 us  [the longest x2 4.38 us: on_device(): received = lax.ppermute(moments, 'slab', flip)]
  transfers between devices with their start and end apart: 30 -> 28, of which waited for: 12 -> 16; matrix products, arithmetic and copies ran while one was open for 1% -> 1% of each run, Pallas kernels for 26% -> 21%
where the time goes in v8:
time: 124 us; the launch traced here: 123 us
  starting transfers between devices  45.2 us (36%)
  waiting for transfers between devices  35.9 us (29%)
  Pallas kernels  34.8 us (28%)
  blocking collectives  2.37 us (2%)
  local copies, waits for them, and re-layouts  1.78 us (1%)
  other arithmetic  1.73 us (1%)
  between operations  1.71 us (1%)
    ppermute x8, starting transfers between devices, along(): return lax.ppermute(operand, axis, route)  21.9 us
    ppermute x10, waiting for transfers between devices, swapped(): return lax.ppermute(operand, 'vec', SWAP)  12.6 us
    pallas_call x5, Pallas kernels, load(): pl.pallas_call(body, out_shape=pltpu.VMEM(shape, bf16), in_specs=[SMEM] +...  8.95 us
    ppermute x8, waiting for transfers between devices, along(): return lax.ppermute(operand, axis, route)  8.42 us
    ppermute x4, waiting for transfers between devices, slab_total(): lax.ppermute(part, 'slab', route)  7.22 us
    ppermute x4, starting transfers between devices, slab_total(): lax.ppermute(part, 'slab', route)  6.95 us
    ppermute x2, starting transfers between devices, on_device(): received = lax.ppermute(moments, 'slab', flip)  6.71 us
    pallas_call x2, Pallas kernels, load_whole(): pl.pallas_call(load_whole_body, out_shape=pltpu.VMEM(array.shape, array.d...  5.47 us
  transfers between devices with their start and end apart: 28, of which 16 were waited for; matrix products, arithmetic and copies ran while one was open for 1% of the time, Pallas kernels for 21%

profile of v8, /device:TPU:0, one launch (start us, length us, event | category | flops | bytes accessed | tf_op | source)
XLA Modules:
  0.0 123.5 jit_solution(4139328449440752958)
XLA Ops:
  0.6 4.9 %collective-permute-start = (bf16[4,64,256]{2,1,0:T(8,128)(2,1)}, bf16[4,64,256]{2,1,0:T(8,128)(2,1)S(1)}, u32[]{:S(2)}, u32[]{:S(2)}) collective-permute-start(bf16[4,64,256]{2,1,0:T(8,128)(2,1)} %vectors.1), channel_id=1, source_target_pairs={{0,2},{2,4},{4,6},{6,8},{8,10},{10,12},{12,14},{1,3},{3,5},{5,7},{... | collective-permute-start | bytes 393224 | tf_op jit(solution)/shard_map/ppermute | solution.py:381
  7.6 2.7 %shard_map.121.token.blocks = bf16[16,512,256]{2,1,0:T(8,128)(2,1)S(1)} custom-call(s32[6]{0:T(128)S(1)} %stack.24.place.token, s32[6]{0:T(128)S(1)} %stack.24.place.token, bf16[16,512,256]{2,1,0:T(8,128)(2,1)} %source.3), custom_call_target="tpu_custom_call" | custom-call | bytes 4194304 | tf_op jit(solution)/shard_map/pallas_call | solution.py:139
  10.4 2.4 %shard_map.122 = bf16[6,2,512,256]{3,2,1,0:T(8,128)(2,1)S(1)} custom-call(s32[6]{0:T(128)S(1)} %stack.24.place.token, bf16[16,512,256]{2,1,0:T(8,128)(2,1)S(1)} %shard_map.121.token.blocks, bf16[6,4,512,256]{3,2,1,0:T(8,128)(2,1)} %lower.13, bf16[6,4,512,256]{3,2,1,0:T(8,128)(2,1)} %upper.13), custom_call_target="tpu_custom_call" | custom-call | bytes 3145728 | tf_op jit(solution)/shard_map/pallas_call | solution.py:75
  14.7 2.4 %all_gather.3.extended = bf16[12,64,512]{2,1,0:T(8,128)(2,1)S(1)} all-gather(bf16[12,64,256]{2,1,0:T(8,128)(2,1)S(1)} %pad_maximum_fusion), channel_id=1, replica_groups=mesh['groups'=2,'slab'=8,'vec'=2] {'vec'}, dimensions={2}, use_global_device_ids=true | all-gather | bytes 1179648 | tf_op jit(solution)/shard_map/all_gather | solution.py:441
  17.0 2.2 %shard_map.123 = (bf16[2,64,256]{2,1,0:T(8,128)(2,1)S(1)}, bf16[2,64,256]{2,1,0:T(8,128)(2,1)S(1)}, f32[64,128]{1,0:T(8,128)S(1)}) custom-call(s32[6]{0:T(128)S(1)} %stack.24.place.token, s32[4,14]{1,0:T(4,128)S(1)} %get-tuple-element.64.table, bf16[12,64,512]{2,1,0:T(8,128)(2,1)S(1)} %all_gather.3.extended, bf16[4,64,256]{2,1,0:T(8,128)(2,1)S(1)} %copy-done.3, ...), custom_call_target="tpu_custom_call" | custom-call | flops 469762048 | bytes 4194304 | tf_op jit(solution)/shard_map/pallas_call | solution.py:174
  22.2 4.0 %collective-permute-start.7 = (f32[64,128]{1,0:T(8,128)S(1)}, f32[64,128]{1,0:T(8,128)S(1)}, u32[]{:S(2)}, u32[]{:S(2)}) collective-permute-start(f32[64,128]{1,0:T(8,128)S(1)} %add.79), channel_id=1, source_target_pairs={{0,2},{2,0},{4,6},{6,4},{8,10},{10,8},{12,14},{14,12},{1,3},{3,1},... | collective-permute-start | bytes 98312 | tf_op jit(solution)/shard_map/ppermute | solution.py:453
  30.7 3.7 %collective-permute-start.10 = (f32[64,128]{1,0:T(8,128)S(1)}, f32[64,128]{1,0:T(8,128)S(1)}, u32[]{:S(2)}, u32[]{:S(2)}) collective-permute-start(f32[64,128]{1,0:T(8,128)S(1)} %add.82), channel_id=1, source_target_pairs={{0,4},{2,6},{4,0},{6,2},{8,12},{10,14},{12,8},{14,10},{1,5},{3,7},... | collective-permute-start | bytes 98312 | tf_op jit(solution)/shard_map/ppermute | solution.py:472
  36.3 3.0 %collective-permute-start.11 = (f32[64,128]{1,0:T(8,128)S(1)}, f32[64,128]{1,0:T(8,128)S(1)}, u32[]{:S(2)}, u32[]{:S(2)}) collective-permute-start(f32[64,128]{1,0:T(8,128)S(1)} %add.83), channel_id=1, source_target_pairs={{0,8},{2,10},{4,12},{6,14},{8,0},{10,2},{12,4},{14,6},{1,9},{3,11}... | collective-permute-start | bytes 98312 | tf_op jit(solution)/shard_map/ppermute | solution.py:472
  41.1 3.2 %collective-permute-done.11 = f32[64,128]{1,0:T(8,128)S(1)} collective-permute-done((f32[64,128]{1,0:T(8,128)S(1)}, f32[64,128]{1,0:T(8,128)S(1)}, u32[]{:S(2)}, u32[]{:S(2)}) %collective-permute-start.11) | collective-permute-done | bytes 32800 | tf_op jit(solution)/shard_map/ppermute | solution.py:472
  46.1 3.1 %collective-permute-start.12 = (bf16[144,512]{1,0:T(8,128)(2,1)S(1)}, bf16[144,512]{1,0:T(8,128)(2,1)S(1)}, u32[]{:S(2)}, u32[]{:S(2)}) collective-permute-start(bf16[144,512]{1,0:T(8,128)(2,1)S(1)} %get-tuple-element.44), channel_id=1, source_target_pairs={{0,2},{1,3},{2,4},{3,5},{4,6},{5,7},{6,8},{7,9},{8,10},{9,11},{10,... | collective-permute-start | bytes 442376 | tf_op jit(solution)/shard_map/ppermute | solution.py:381
  50.5 1.8 %shard_map.129.token.weights = bf16[2,2,2,512,256]{4,3,2,1,0:T(8,128)(2,1)S(1)} custom-call(s32[6]{0:T(128)S(1)} %stack.24.place.token, bf16[2,64,512]{2,1,0:T(8,128)(2,1)S(1)} %get-tuple-element.43.token.own, bf16[6,4,512,256]{3,2,1,0:T(8,128)(2,1)} %lower.13, bf16[6,4,512,256]{3,2,1,0:T(8,128)(2,1)} %upper.13, ...), custom_call_target="tpu_custom_call" | custom-call | bytes 4194304 | tf_op jit(solution)/shard_map/pallas_call | solution.py:123
  52.3 2.5 %shard_map.130 = bf16[5,2,512,256]{3,2,1,0:T(8,128)(2,1)S(1)} custom-call(s32[6]{0:T(128)S(1)} %stack.24.place.token, bf16[2,2,2,512,256]{4,3,2,1,0:T(8,128)(2,1)S(1)} %shard_map.129.token.weights, bf16[6,4,512,256]{3,2,1,0:T(8,128)(2,1)} %lower.13, bf16[6,4,512,256]{3,2,1,0:T(8,128)(2,1)} %upper.13, bf16[4,512,256]{2,1,0:T(8,128)(2,1)} %final.1), custom_call_target="tpu_custom_call" | custom-call | bytes 2621440 | tf_op jit(solution)/shard_map/pallas_call | solution.py:75
  57.2 4.5 %collective-permute-start.14 = (bf16[2,64,512]{2,1,0:T(8,128)(2,1)S(1)}, bf16[2,64,512]{2,1,0:T(8,128)(2,1)S(1)}, u32[]{:S(2)}, u32[]{:S(2)}) collective-permute-start(bf16[2,64,512]{2,1,0:T(8,128)(2,1)S(1)} %shard_map.131.token.own), channel_id=1, source_target_pairs={{0,4},{1,5},{2,6},{3,7},{4,8},{5,9},{6,10},{7,11},{8,12},{9,13},{1... | collective-permute-start | bytes 393224 | tf_op jit(solution)/shard_map/ppermute | solution.py:381
  64.7 4.9 %collective-permute-done.15.above = bf16[2,64,512]{2,1,0:T(8,128)(2,1)S(1)} collective-permute-done((bf16[2,64,512]{2,1,0:T(8,128)(2,1)S(1)}, bf16[2,64,512]{2,1,0:T(8,128)(2,1)S(1)}, u32[]{:S(2)}, u32[]{:S(2)}) %collective-permute-start.15) | collective-permute-done | bytes 131104 | tf_op jit(solution)/shard_map/ppermute | solution.py:381
  70.8 9.7 %collective-permute-done.16.packed = bf16[5,2,512,256]{3,2,1,0:T(8,128)(2,1)S(1)} collective-permute-done((bf16[5,2,512,256]{3,2,1,0:T(8,128)(2,1)S(1)}, bf16[5,2,512,256]{3,2,1,0:T(8,128)(2,1)S(1)}, u32[]{:S(2)}, u32[]{:S(2)}) %collective-permute-start.16) | collective-permute-done | bytes 2621472 | tf_op jit(solution)/shard_map/ppermute | solution.py:375
  84.9 2.7 %shard_map.134.blocks = bf16[16,512,256]{2,1,0:T(8,128)(2,1)S(1)} custom-call(s32[6]{0:T(128)S(1)} %stack.24.place.token, bf16[2,64,512]{2,1,0:T(8,128)(2,1)S(1)} %shard_map.133.token.own, bf16[16,512,256]{2,1,0:T(8,128)(2,1)} %source.3), custom_call_target="tpu_custom_call" | custom-call | bytes 4194304 | tf_op jit(solution)/shard_map/pallas_call | solution.py:139
  87.7 1.8 %shard_map.135.weights = bf16[2,2,2,512,256]{4,3,2,1,0:T(8,128)(2,1)S(1)} custom-call(s32[6]{0:T(128)S(1)} %stack.24.place.token, bf16[2,64,512]{2,1,0:T(8,128)(2,1)S(1)} %shard_map.133.token.own, bf16[6,4,512,256]{3,2,1,0:T(8,128)(2,1)} %lower.13, bf16[6,4,512,256]{3,2,1,0:T(8,128)(2,1)} %upper.13, ...), custom_call_target="tpu_custom_call" | custom-call | bytes 4194304 | tf_op jit(solution)/shard_map/pallas_call | solution.py:123
  89.5 3.2 %collective-permute-done.17.other = bf16[2,64,512]{2,1,0:T(8,128)(2,1)S(1)} collective-permute-done((bf16[2,64,512]{2,1,0:T(8,128)(2,1)S(1)}, bf16[2,64,512]{2,1,0:T(8,128)(2,1)S(1)}, u32[]{:S(2)}, u32[]{:S(2)}) %collective-permute-start.17) | collective-permute-done | bytes 131104 | tf_op jit(solution)/shard_map/ppermute | solution.py:494
  95.1 4.2 %collective-permute-start.21 = (bf16[2,64,512]{2,1,0:T(8,128)(2,1)S(1)}, bf16[2,64,512]{2,1,0:T(8,128)(2,1)S(1)}, u32[]{:S(2)}, u32[]{:S(2)}) collective-permute-start(bf16[2,64,512]{2,1,0:T(8,128)(2,1)S(1)} %get-tuple-element.53.correction), channel_id=1, source_target_pairs={{0,2},{1,3},{2,4},{3,5},{4,6},{5,7},{6,8},{7,9},{8,10},{9,11},{10,... | collective-permute-start | bytes 393224 | tf_op jit(solution)/shard_map/ppermute | solution.py:381
  99.5 2.3 %shard_map.137 = (f32[2,64,512]{2,1,0:T(8,128)S(1)}, f32[160,128]{1,0:T(8,128)S(1)}, f32[8,128]{1,0:T(8,128)S(1)}) custom-call(s32[6]{0:T(128)S(1)} %stack.24.place.token, s32[8,14]{1,0:T(8,128)S(1)} %add_add_fusion.1.table, f32[8]{0:T(128)S(1)} %copy-done.4, s32[1]{0:T(128)S(6)} %copy.13.index, bf16[12,64,512]{2,1,0:T(8,128)(2,1)S(1)} %copy-done.1, ...), custom_call_target="tpu_custom_call" | custom-call | flops 469762048 | tf_op jit(solution)/shard_map/pallas_call | solution.py:538
  102.3 2.5 %shard_map.138 = (f32[80,128]{1,0:T(8,128)S(1)}, f32[80,128]{1,0:T(8,128)S(1)}) custom-call(s32[6]{0:T(128)S(1)} %stack.24.place.token, s32[8,14]{1,0:T(8,128)S(1)} %add_add_fusion.1.table, bf16[12,64,512]{2,1,0:T(8,128)(2,1)S(1)} %copy-done.1, bf16[2,64,512]{2,1,0:T(8,128)(2,1)S(1)} %get-tuple-element.53.correction, ...), custom_call_target="tpu_custom_call" | custom-call | flops 469762048 | tf_op jit(solution)/shard_map/pallas_call | solution.py:545
  106.6 4.3 %collective-permute-start.23 = (f32[80,128]{1,0:T(8,128)S(1)}, f32[80,128]{1,0:T(8,128)S(1)}, u32[]{:S(2)}, u32[]{:S(2)}) collective-permute-start(f32[80,128]{1,0:T(8,128)S(1)} %add.85), channel_id=1, source_target_pairs={{0,2},{2,0},{4,6},{6,4},{8,10},{10,8},{12,14},{14,12},{1,3},{3,1},... | collective-permute-start | bytes 122888 | tf_op jit(solution)/shard_map/ppermute | solution.py:405
  112.8 2.0 %collective-permute-done.24 = f32[80,128]{1,0:T(8,128)S(1)} collective-permute-done((f32[80,128]{1,0:T(8,128)S(1)}, f32[80,128]{1,0:T(8,128)S(1)}, u32[]{:S(2)}, u32[]{:S(2)}) %collective-permute-start.24) | collective-permute-done | bytes 40992 | tf_op jit(solution)/shard_map/ppermute | solution.py:405
  116.9 3.9 %collective-permute-done.26 = f32[80,128]{1,0:T(8,128)S(1)} collective-permute-done((f32[80,128]{1,0:T(8,128)S(1)}, f32[80,128]{1,0:T(8,128)S(1)}, u32[]{:S(2)}, u32[]{:S(2)}) %collective-permute-start.26) | collective-permute-done | bytes 40992 | tf_op jit(solution)/shard_map/ppermute | solution.py:405
  (88 shorter events, 39.7 us)
Async XLA Ops:
  0.6 14.0 %collective-permute-start = (bf16[4,64,256]{2,1,0:T(8,128)(2,1)}, bf16[4,64,256]{2,1,0:T(8,128)(2,1)S(1)}, u32[]{:S(2)}, u32[]{:S(2)}) collective-permute-start(bf16[4,64,256]{2,1,0:T(8,128)(2,1)} %vectors.1), channel_id=1, source_target_pairs={{0,2},{2,4},{4,6},{6,8},{8,10},{10,12},{12,14},{1,3},{3,5},{5,7},{... | collective-permute-start | bytes 393224 | tf_op jit(solution)/shard_map/ppermute | solution.py:381
  5.5 9.1 %collective-permute-start.1 = (bf16[4,64,256]{2,1,0:T(8,128)(2,1)}, bf16[4,64,256]{2,1,0:T(8,128)(2,1)S(1)}, u32[]{:S(2)}, u32[]{:S(2)}) collective-permute-start(bf16[4,64,256]{2,1,0:T(8,128)(2,1)} %vectors.1), channel_id=1, source_target_pairs={{2,0},{4,2},{6,4},{8,6},{10,8},{12,10},{14,12},{3,1},{5,3},{7,5},{... | collective-permute-start | bytes 393224 | tf_op jit(solution)/shard_map/ppermute | solution.py:381
  20.8 6.0 %collective-permute-start.6 = (bf16[6,2,512,256]{3,2,1,0:T(8,128)(2,1)}, bf16[6,2,512,256]{3,2,1,0:T(8,128)(2,1)S(1)}, u32[]{:S(2)}, u32[]{:S(2)}) collective-permute-start(bf16[6,2,512,256]{3,2,1,0:T(8,128)(2,1)} %copy-done.2), channel_id=1, source_target_pairs={{0,1},{1,0},{2,3},{3,2},{4,5},{5,4},{6,7},{7,6},{8,9},{9,8},{10,11... | collective-permute-start | bytes 9437192 | tf_op jit(solution)/shard_map/ppermute | solution.py:375
  21.2 8.4 %collective-permute-start.4 = (bf16[1,64,512]{2,1,0:T(8,128)(2,1)S(1)}, bf16[1,64,512]{2,1,0:T(8,128)(2,1)S(1)}, u32[]{:S(2)}, u32[]{:S(2)}) collective-permute-start(bf16[1,64,512]{2,1,0:T(8,128)(2,1)S(1)} %get-tuple-element.66), channel_id=1, source_target_pairs={{0,1},{1,0},{2,3},{3,2},{4,5},{5,4},{6,7},{7,6},{8,9},{9,8},{10,11... | collective-permute-start | bytes 196616 | tf_op jit(solution)/shard_map/ppermute | solution.py:375
  21.4 8.2 %collective-permute-start.5 = (bf16[1,64,512]{2,1,0:T(8,128)(2,1)S(1)}, bf16[1,64,512]{2,1,0:T(8,128)(2,1)S(1)}, u32[]{:S(2)}, u32[]{:S(2)}) collective-permute-start(bf16[1,64,512]{2,1,0:T(8,128)(2,1)S(1)} %get-tuple-element.65), channel_id=1, source_target_pairs={{1,2},{3,4},{5,6},{7,8},{9,10},{11,12},{13,14},{2,1},{4,3},{6,5},{... | collective-permute-start | bytes 196616 | tf_op jit(solution)/shard_map/ppermute | solution.py:450
  22.2 8.5 %collective-permute-start.7 = (f32[64,128]{1,0:T(8,128)S(1)}, f32[64,128]{1,0:T(8,128)S(1)}, u32[]{:S(2)}, u32[]{:S(2)}) collective-permute-start(f32[64,128]{1,0:T(8,128)S(1)} %add.79), channel_id=1, source_target_pairs={{0,2},{2,0},{4,6},{6,4},{8,10},{10,8},{12,14},{14,12},{1,3},{3,1},... | collective-permute-start | bytes 98312 | tf_op jit(solution)/shard_map/ppermute | solution.py:453
  30.7 5.6 %collective-permute-start.10 = (f32[64,128]{1,0:T(8,128)S(1)}, f32[64,128]{1,0:T(8,128)S(1)}, u32[]{:S(2)}, u32[]{:S(2)}) collective-permute-start(f32[64,128]{1,0:T(8,128)S(1)} %add.82), channel_id=1, source_target_pairs={{0,4},{2,6},{4,0},{6,2},{8,12},{10,14},{12,8},{14,10},{1,5},{3,7},... | collective-permute-start | bytes 98312 | tf_op jit(solution)/shard_map/ppermute | solution.py:472
  34.4 10.0 %collective-permute-start.8 = (bf16[2,128,512]{2,1,0:T(8,128)(2,1)S(1)}, bf16[2,128,512]{2,1,0:T(8,128)(2,1)S(1)}, u32[]{:S(2)}, u32[]{:S(2)}) collective-permute-start(bf16[2,128,512]{2,1,0:T(8,128)(2,1)S(1)} %shard_map.126.token.own), channel_id=1, source_target_pairs={{0,1},{1,0},{2,3},{3,2},{4,5},{5,4},{6,7},{7,6},{8,9},{9,8},{10,11... | collective-permute-start | bytes 786440 | tf_op jit(solution)/shard_map/ppermute | solution.py:375
  34.5 9.9 %collective-permute-start.9 = (bf16[2,128,512]{2,1,0:T(8,128)(2,1)S(1)}, bf16[2,128,512]{2,1,0:T(8,128)(2,1)S(1)}, u32[]{:S(2)}, u32[]{:S(2)}) collective-permute-start(bf16[2,128,512]{2,1,0:T(8,128)(2,1)S(1)} %shard_map.126.token.own), channel_id=1, source_target_pairs={{1,2},{3,4},{5,6},{7,8},{9,10},{11,12},{13,14},{2,1},{4,3},{6,5},{... | collective-permute-start | bytes 786440 | tf_op jit(solution)/shard_map/ppermute | solution.py:469
  36.3 8.0 %collective-permute-start.11 = (f32[64,128]{1,0:T(8,128)S(1)}, f32[64,128]{1,0:T(8,128)S(1)}, u32[]{:S(2)}, u32[]{:S(2)}) collective-permute-start(f32[64,128]{1,0:T(8,128)S(1)} %add.83), channel_id=1, source_target_pairs={{0,8},{2,10},{4,12},{6,14},{8,0},{10,2},{12,4},{14,6},{1,9},{3,11}... | collective-permute-start | bytes 98312 | tf_op jit(solution)/shard_map/ppermute | solution.py:472
  46.1 10.1 %collective-permute-start.12 = (bf16[144,512]{1,0:T(8,128)(2,1)S(1)}, bf16[144,512]{1,0:T(8,128)(2,1)S(1)}, u32[]{:S(2)}, u32[]{:S(2)}) collective-permute-start(bf16[144,512]{1,0:T(8,128)(2,1)S(1)} %get-tuple-element.44), channel_id=1, source_target_pairs={{0,2},{1,3},{2,4},{3,5},{4,6},{5,7},{6,8},{7,9},{8,10},{9,11},{10,... | collective-permute-start | bytes 442376 | tf_op jit(solution)/shard_map/ppermute | solution.py:381
  49.2 7.0 %collective-permute-start.13 = (bf16[2,64,512]{2,1,0:T(8,128)(2,1)S(1)}, bf16[2,64,512]{2,1,0:T(8,128)(2,1)S(1)}, u32[]{:S(2)}, u32[]{:S(2)}) collective-permute-start(bf16[2,64,512]{2,1,0:T(8,128)(2,1)S(1)} %get-tuple-element.43.token.own), channel_id=1, source_target_pairs={{2,0},{3,1},{4,2},{5,3},{6,4},{7,5},{8,6},{9,7},{10,8},{11,9},{12,... | collective-permute-start | bytes 393224 | tf_op jit(solution)/shard_map/ppermute | solution.py:381
  57.2 7.5 %collective-permute-start.14 = (bf16[2,64,512]{2,1,0:T(8,128)(2,1)S(1)}, bf16[2,64,512]{2,1,0:T(8,128)(2,1)S(1)}, u32[]{:S(2)}, u32[]{:S(2)}) collective-permute-start(bf16[2,64,512]{2,1,0:T(8,128)(2,1)S(1)} %shard_map.131.token.own), channel_id=1, source_target_pairs={{0,4},{1,5},{2,6},{3,7},{4,8},{5,9},{6,10},{7,11},{8,12},{9,13},{1... | collective-permute-start | bytes 393224 | tf_op jit(solution)/shard_map/ppermute | solution.py:381
  61.7 7.9 %collective-permute-start.15 = (bf16[2,64,512]{2,1,0:T(8,128)(2,1)S(1)}, bf16[2,64,512]{2,1,0:T(8,128)(2,1)S(1)}, u32[]{:S(2)}, u32[]{:S(2)}) collective-permute-start(bf16[2,64,512]{2,1,0:T(8,128)(2,1)S(1)} %shard_map.131.token.own), channel_id=1, source_target_pairs={{4,0},{5,1},{6,2},{7,3},{8,4},{9,5},{10,6},{11,7},{12,8},{13,9},{1... | collective-permute-start | bytes 393224 | tf_op jit(solution)/shard_map/ppermute | solution.py:381
  69.7 29.8 %collective-permute-start.19 = (bf16[16,512,256]{2,1,0:T(8,128)(2,1)S(1)}, bf16[16,512,256]{2,1,0:T(8,128)(2,1)S(1)}, u32[]{:S(2)}, u32[]{:S(2)}) collective-permute-start(bf16[16,512,256]{2,1,0:T(8,128)(2,1)S(1)} %copy-done.5), channel_id=1, source_target_pairs={{0,1},{1,0},{2,3},{3,2},{4,5},{5,4},{6,7},{7,6},{8,9},{9,8},{10,11... | collective-permute-start | bytes 12582920 | tf_op jit(solution)/shard_map/ppermute | solution.py:375
  69.7 10.9 %collective-permute-start.16 = (bf16[5,2,512,256]{3,2,1,0:T(8,128)(2,1)S(1)}, bf16[5,2,512,256]{3,2,1,0:T(8,128)(2,1)S(1)}, u32[]{:S(2)}, u32[]{:S(2)}) collective-permute-start(bf16[5,2,512,256]{3,2,1,0:T(8,128)(2,1)S(1)} %shard_map.130), channel_id=1, source_target_pairs={{0,1},{1,0},{2,3},{3,2},{4,5},{5,4},{6,7},{7,6},{8,9},{9,8},{10,11... | collective-permute-start | bytes 7864328 | tf_op jit(solution)/shard_map/ppermute | solution.py:375
  83.4 9.3 %collective-permute-start.17 = (bf16[2,64,512]{2,1,0:T(8,128)(2,1)S(1)}, bf16[2,64,512]{2,1,0:T(8,128)(2,1)S(1)}, u32[]{:S(2)}, u32[]{:S(2)}) collective-permute-start(bf16[2,64,512]{2,1,0:T(8,128)(2,1)S(1)} %shard_map.133.token.own), channel_id=1, source_target_pairs={{0,8},{1,9},{2,10},{3,11},{4,12},{5,13},{6,14},{7,15},{8,0},{9,1},... | collective-permute-start | bytes 393224 | tf_op jit(solution)/shard_map/ppermute | solution.py:494
  93.8 8.0 %collective-permute-start.20 = (bf16[2,64,512]{2,1,0:T(8,128)(2,1)S(1)}, bf16[2,64,512]{2,1,0:T(8,128)(2,1)S(1)}, u32[]{:S(2)}, u32[]{:S(2)}) collective-permute-start(bf16[2,64,512]{2,1,0:T(8,128)(2,1)S(1)} %get-tuple-element.53.correction), channel_id=1, source_target_pairs={{0,1},{1,2},{2,3},{3,4},{4,5},{5,6},{6,7},{7,8},{8,9},{9,10},{10,1... | collective-permute-start | bytes 393224 | tf_op jit(solution)/shard_map/ppermute | solution.py:381
  95.1 7.1 %collective-permute-start.21 = (bf16[2,64,512]{2,1,0:T(8,128)(2,1)S(1)}, bf16[2,64,512]{2,1,0:T(8,128)(2,1)S(1)}, u32[]{:S(2)}, u32[]{:S(2)}) collective-permute-start(bf16[2,64,512]{2,1,0:T(8,128)(2,1)S(1)} %get-tuple-element.53.correction), channel_id=1, source_target_pairs={{0,2},{1,3},{2,4},{3,5},{4,6},{5,7},{6,8},{7,9},{8,10},{9,11},{10,... | collective-permute-start | bytes 393224 | tf_op jit(solution)/shard_map/ppermute | solution.py:381
  106.6 6.3 %collective-permute-start.23 = (f32[80,128]{1,0:T(8,128)S(1)}, f32[80,128]{1,0:T(8,128)S(1)}, u32[]{:S(2)}, u32[]{:S(2)}) collective-permute-start(f32[80,128]{1,0:T(8,128)S(1)} %add.85), channel_id=1, source_target_pairs={{0,2},{2,0},{4,6},{6,4},{8,10},{10,8},{12,14},{14,12},{1,3},{3,1},... | collective-permute-start | bytes 122888 | tf_op jit(solution)/shard_map/ppermute | solution.py:405
  110.9 4.0 %collective-permute-start.24 = (f32[80,128]{1,0:T(8,128)S(1)}, f32[80,128]{1,0:T(8,128)S(1)}, u32[]{:S(2)}, u32[]{:S(2)}) collective-permute-start(f32[80,128]{1,0:T(8,128)S(1)} %add.85), channel_id=1, source_target_pairs={{0,4},{2,6},{4,0},{6,2},{8,12},{10,14},{12,8},{14,10},{1,5},{3,7},... | collective-permute-start | bytes 122888 | tf_op jit(solution)/shard_map/ppermute | solution.py:405
  110.9 4.9 %collective-permute-start.25 = (f32[80,128]{1,0:T(8,128)S(1)}, f32[80,128]{1,0:T(8,128)S(1)}, u32[]{:S(2)}, u32[]{:S(2)}) collective-permute-start(f32[80,128]{1,0:T(8,128)S(1)} %add.85), channel_id=1, source_target_pairs={{0,6},{2,4},{4,2},{6,0},{8,14},{10,12},{12,10},{14,8},{1,7},{3,5},... | collective-permute-start | bytes 122888 | tf_op jit(solution)/shard_map/ppermute | solution.py:405
  112.4 8.4 %collective-permute-start.18 = (bf16[2,64,256]{2,1,0:T(8,128)(2,1)S(1)}, bf16[2,64,256]{2,1,0:T(8,128)(2,1)S(1)}, u32[]{:S(2)}, u32[]{:S(2)}) collective-permute-start(bf16[2,64,256]{2,1,0:T(8,128)(2,1)S(1)} %get-tuple-element.52), channel_id=1, source_target_pairs={{0,1},{1,0},{2,3},{3,2},{4,5},{5,4},{6,7},{7,6},{8,9},{9,8},{10,11... | collective-permute-start | bytes 196616 | tf_op jit(solution)/shard_map/ppermute | solution.py:375
  115.8 5.0 %collective-permute-start.26 = (f32[80,128]{1,0:T(8,128)S(1)}, f32[80,128]{1,0:T(8,128)S(1)}, u32[]{:S(2)}, u32[]{:S(2)}) collective-permute-start(f32[80,128]{1,0:T(8,128)S(1)} %add_add_fusion), channel_id=1, source_target_pairs={{0,8},{2,10},{4,12},{6,14},{8,0},{10,2},{12,4},{14,6},{1,9},{3,11}... | collective-permute-start | bytes 122888 | tf_op jit(solution)/shard_map/ppermute | solution.py:405
  (12 other events, 58.3 us)

commit v9 on v8

--- a/solution.py
+++ b/solution.py
@@ -60,26 +60,36 @@
 
 
 def pack_body(levels, place, token, lower, upper, *rest):
-    *final, out, sem = rest
+    *final, out, held, sem = rest
     count = out.shape[1]
     slabs = pl.ds((1 - place[0]) * count, count)
     parts = [ref.at[level, slabs] for level in levels for ref in (lower, upper)]
     parts += [ref.at[slabs] for ref in final]
-    run([pltpu.make_async_copy(part, out.at[k], sem.at[k]) for k, part in enumerate(parts)])
+    ins = [pltpu.make_async_copy(part, held.at[k], sem.at[0, k]) for k, part in enumerate(parts)]
+    outs = [pltpu.make_async_copy(held.at[k], out.at[k], sem.at[1, k]) for k in range(len(parts))]
+    for copy in ins:
+        copy.start()
+    for copy, following in zip(ins, outs):
+        copy.wait()
+        following.start()
+    for copy in outs:
+        copy.wait()
 
 
 def pack(levels, place, token, *operands):
     _, slabs, rows, half = operands[0].shape
     count = 2 * len(levels) + len(operands) - 2
-    out = struct((count, slabs // 2, rows, half))
+    shape = (count, slabs // 2, rows, half)
     return pl.pallas_call(
         functools.partial(pack_body, levels),
-        out_shape=out,
+        out_shape=pltpu.HBM(shape, bf16),
         in_specs=[SMEM] + [ANY] * (1 + len(operands)),
-        out_specs=VMEM,
-        scratch_shapes=[pltpu.SemaphoreType.DMA((count,))],
+        out_specs=ANY,
+        scratch_shapes=[pltpu.VMEM(shape, bf16), pltpu.SemaphoreType.DMA((2, count))],
         compiler_params=pltpu.CompilerParams(vmem_limit_bytes=6 * MIB),
-        cost_estimate=pl.CostEstimate(flops=0, bytes_accessed=2 * out.size, transcendentals=0),
+        cost_estimate=pl.CostEstimate(
+            flops=0, bytes_accessed=4 * count * (slabs // 2) * rows * half, transcendentals=0
+        ),
     )(place, token, *[in_hbm(x) for x in operands])
 
 
@@ -275,33 +285,36 @@
     return 2 * products * operand.size * operand.shape[-1]
 
 
-def add_pairs(table, row, entries, position, inside, window, blocks, others, place, summed, slot):
+def add_pairs(place, table, targets, inside, window, blocks, others, summed):
     half = blocks.shape[-1]
+    reach = table.shape[1] // 2
+    first = place[0] * 2
     mine, theirs = columns(place[0], half), columns(1 - place[0], half)
-    for entry in range(entries):
-        source = position + table[row, entry]
-
-        @pl.when(inside(source))
-        def _():
-            block = table[row, entries + entry]
-            vectors = window(source)
-            summed[slot, :, mine] += dot(vectors, blocks[block])
-            summed[slot, :, theirs] += dot(vectors, others[block])
+    for target in targets:
+
+        @pl.loop(0, reach)
+        def _(entry):
+            source = target + table[first + target, entry]
+
+            @pl.when(inside(source))
+            def _():
+                block = table[first + target, reach + entry]
+                vectors = window(source)
+                summed[target, :, mine] += dot(vectors, blocks[block])
+                summed[target, :, theirs] += dot(vectors, others[block])
 
 
 def own_pairs_body(place, table, levels, index, extended, image, correction, blocks, others, summed, out, shift):
     own, rows, _ = image.shape
-    reach = table.shape[1] // 2
     below = extended.shape[0] // 3
     first = place[0] * own
     shift[...] = jnp.full(shift.shape, levels[index[0]], f32)
     summed[...] = jnp.zeros(summed.shape, f32)
-    for slab in range(own):
-        add_pairs(
-            table, first + below + slab, reach, slab,
-            lambda source: jnp.logical_and(source >= 0, source < own),
-            lambda source: correction[source], blocks, others, place, summed, slab,
-        )
+    add_pairs(
+        place, table, range(below + own),
+        lambda source: jnp.logical_and(source >= below, source < below + own),
+        lambda source: correction[source - below], blocks, others, summed,
+    )
     overlap = jnp.zeros((2 * rows, rows), f32)
     mixed = jnp.zeros((rows, rows), f32)
     for slab in range(own):
@@ -318,35 +331,22 @@
     place, table, extended, correction, near, far, blocks, others, begun, part, keep, send, window, summed, out
 ):
     own, rows, _ = correction.shape
-    reach = table.shape[1] // 2
-    below = window.shape[0] - own
-    half = blocks.shape[-1]
+    below = window.shape[0]
     first = place[0] * own
-    mine, theirs = columns(place[0], half), columns(1 - place[0], half)
     window[0:own] = far[...]
     window[own : 2 * own] = near[...]
-    window[below : below + own] = correction[...]
-    summed[0:below] = jnp.zeros((below,) + summed.shape[1:], f32)
-    summed[below : below + own] = begun[...]
-
-    @pl.loop(0, (below + own) * reach)
-    def _(pair):
-        target = lax.div(pair, reach)
-        entry = pair - target * reach
-        source = target + table[first + target, entry]
-        inside = jnp.logical_and(source >= 0, source < below + own)
-
-        @pl.when(jnp.logical_and(inside, (target >= below) != (source >= below)))
-        def _():
-            block = table[first + target, reach + entry]
-            vectors = window[source]
-            summed[target, :, mine] += dot(vectors, blocks[block])
-            summed[target, :, theirs] += dot(vectors, others[block])
-
+    summed[below : below + own] = begun[below : below + own]
+    add_pairs(
+        place, table, range(below, below + own),
+        lambda source: jnp.logical_and(source >= 0, source < below),
+        lambda source: window[source], blocks, others, summed,
+    )
     pencil = jnp.zeros((2 * rows, rows), f32)
     for slab in range(below + own):
-        basis = jnp.concatenate([extended[first + slab], window[slab]], 0)
-        pencil = pencil + dot_t(basis, summed[slab].astype(bf16))
+        fixed = window[slab] if slab < below else correction[slab - below]
+        terms = begun[slab] if slab < below else summed[slab]
+        basis = jnp.concatenate([extended[first + slab], fixed], 0)
+        pencil = pencil + dot_t(basis, terms.astype(bf16))
     out[...] = part[...]
     out[0 : 2 * rows, 0:rows] = pencil
     keep[...] = out[row_half(place[0], keep)]
@@ -357,8 +357,11 @@
     return pl.ds(pl.multiple_of(index * part.shape[0], 8), part.shape[0])
 
 
-def assemble_body(scale, place, shift, moments, first, second, gram, pencil, whole):
+def assemble_body(scale, place, shift, moments, keep, received, first, second, gram, pencil, result, whole):
     rows = moments.shape[0]
+    own = keep.shape[0]
+    result[pl.ds(place[0] * own, own)] = keep[...]
+    result[pl.ds((1 - place[0]) * own, own)] = received[...]
     whole[row_half(place[0], first)] = first[...] * scale
     whole[row_half(1 - place[0], first)] = second[...] * scale
     top, bottom = whole[0 : 2 * rows], whole[2 * rows :]
@@ -473,6 +476,9 @@
     moments = (moments + received) / rows_total
     body = functools.partial(load_body, 1, 0)
     matrices = in_vmem(load(body, place, both, level_lower, level_upper, packed))
+    theirs = pack(levels[3:], place, matrices, level_lower, level_upper, level_final)
+    theirs, inner, outer, moments = lax.optimization_barrier((theirs, inner, outer, moments))
+    following = swapped(theirs)
     residual, lifted = kernel_call(
         second_body,
         (struct(image.shape), struct((own_count * rows + 16, width))),
@@ -507,11 +513,9 @@
         if level == 2:
             count = own_count * rows
             lower_table = below[count : count + slab_count, : table.shape[1]].astype(jnp.int32)
-            theirs = pack(levels[3:], place, matrices, level_lower, level_upper, level_final)
-            theirs, below, above = lax.optimization_barrier((theirs, below, above))
-            packed = swapped(theirs)
+            packed, below, above = lax.optimization_barrier((following, below, above))
         if level == 3:
-            late_blocks, below, above = lax.optimization_barrier((blocks, below, above))
+            late_blocks, below, above, matrices = lax.optimization_barrier((blocks, below, above, matrices))
             others = swapped(late_blocks)
         residual = kernel_call(
             level_body if level > 2 else third_body,
@@ -531,13 +535,13 @@
 
     far, near = along(correction, CHAIN, 2), along(correction, CHAIN, 1)
     received = swapped(send)
-    result = jnp.where(core == 0, jnp.concatenate([keep, received], 0), jnp.concatenate([received, keep], 0))
+    result_parts = (keep, received)
     tables = jnp.concatenate([lower_table, table], 0)
     flops = level_flops(image, 7)
     sums = (5 * rows // 2, 2 * rows)
     begun, part, shift = kernel_call(
         own_pairs_body,
-        (struct(image.shape, f32), struct(sums, f32), struct((8, 2 * rows), f32)),
+        (struct((3 * own_count, rows, width), f32), struct(sums, f32), struct((8, 2 * rows), f32)),
         [SMEM] * 4 + [VMEM] * 5,
         flops=flops,
     )(place, tables, shift_levels, shift_index, extended, image, correction, held_blocks, others)
@@ -547,7 +551,7 @@
         (share, share),
         [SMEM] * 2 + [VMEM] * 8,
         [
-            pltpu.VMEM((3 * own_count, rows, width), bf16),
+            pltpu.VMEM((2 * own_count, rows, width), bf16),
             pltpu.VMEM((3 * own_count, rows, width), f32),
             pltpu.VMEM(sums, f32),
         ],
@@ -555,12 +559,12 @@
     )(place, tables, extended, correction, near, far, held_blocks, others, begun, part)
     share = slab_total(keep + swapped(send))
     square = struct((2 * rows, 2 * rows), f32)
-    gram, pencil = kernel_call(
+    gram, pencil, result = kernel_call(
         functools.partial(assemble_body, 1.0 / rows_total),
-        (square, square),
-        [SMEM] + [VMEM] * 4,
+        (square, square, struct(vectors.shape)),
+        [SMEM] + [VMEM] * 6,
         [pltpu.VMEM(sums, f32)],
-    )(place, shift, moments, share, swapped(share))
+    )(place, shift, moments, *result_parts, share, swapped(share))
     return (result, gram, pencil)
 
 

time: 124 us -> 109 us (0.88)
  waiting for transfers between devices: 35.9 us -> 23.8 us
  starting transfers between devices: 45.2 us -> 42.4 us
  Pallas kernels: 34.8 us -> 36.6 us
  local copies, waits for them, and re-layouts: 1.78 us -> 0.14 us
    ppermute x10, waiting for transfers between devices: 12.6 us -> 3.63 us  [swapped(): return lax.ppermute(operand, 'vec', SWAP)]
    ppermute x2, waiting for transfers between devices: 4.38 us -> 1.49 us  [on_device(): received = lax.ppermute(moments, 'slab', flip)]
    pallas_call x3, Pallas kernels: 7.3 us -> 10.1 us  [the longest x2 6.49 us: pack(): pl.pallas_call(functools.partial(pack_body, levels), out_shape=pltpu.HBM(...]
    unnamed x16 -> x14, local copies, waits for them, and re-layouts: 1.68 us -> 0.04 us
    ppermute x4, starting transfers between devices: 6.95 us -> 5.56 us  [slab_total(): lax.ppermute(part, 'slab', route)]
    ppermute x10, starting transfers between devices: 2.73 us -> 1.44 us  [swapped(): return lax.ppermute(operand, 'vec', SWAP)]
  transfers between devices with their start and end apart: 28 -> 28, of which waited for: 16 -> 13; matrix products, arithmetic and copies ran while one was open for 1% -> 1% of each run, Pallas kernels for 21% -> 28%
where the time goes in v9:
time: 109 us; the launch traced here: 108 us
  starting transfers between devices  42.4 us (39%)
  Pallas kernels  36.6 us (34%)
  waiting for transfers between devices  23.8 us (22%)
  blocking collectives  2.37 us (2%)
  between operations  1.76 us (2%)
    ppermute x8, starting transfers between devices, along(): return lax.ppermute(operand, axis, route)  21.9 us
    pallas_call x5, Pallas kernels, load(): pl.pallas_call(body, out_shape=pltpu.VMEM(shape, bf16), in_specs=[SMEM] +...  8.95 us
    ppermute x8, waiting for transfers between devices, along(): return lax.ppermute(operand, axis, route)  8.36 us
    ppermute x4, waiting for transfers between devices, slab_total(): lax.ppermute(part, 'slab', route)  7.03 us
    pallas_call x2, Pallas kernels, pack(): pl.pallas_call(functools.partial(pack_body, levels), out_shape=pltpu.HBM(...  6.49 us
    ppermute x2, starting transfers between devices, on_device(): received = lax.ppermute(moments, 'slab', flip)  6.1 us
    ppermute x4, starting transfers between devices, slab_total(): lax.ppermute(part, 'slab', route)  5.56 us
    pallas_call x2, Pallas kernels, load_whole(): pl.pallas_call(load_whole_body, out_shape=pltpu.VMEM(array.shape, array.d...  5.47 us
  transfers between devices with their start and end apart: 28, of which 13 were waited for; matrix products, arithmetic and copies ran while one was open for 1% of the time, Pallas kernels for 28%

profile of v9, /device:TPU:0, one launch (start us, length us, event | category | flops | bytes accessed | tf_op | source)
XLA Modules:
  0.0 108.3 jit_solution(10067494816168825880)
XLA Ops:
  1.9 5.5 %collective-permute-start = (bf16[4,64,256]{2,1,0:T(8,128)(2,1)}, bf16[4,64,256]{2,1,0:T(8,128)(2,1)S(1)}, u32[]{:S(2)}, u32[]{:S(2)}) collective-permute-start(bf16[4,64,256]{2,1,0:T(8,128)(2,1)} %vectors.1), channel_id=1, source_target_pairs={{0,2},{2,4},{4,6},{6,8},{8,10},{10,12},{12,14},{1,3},{3,5},{5,7},{... | collective-permute-start | bytes 393224 | tf_op jit(solution)/shard_map/ppermute | solution.py:384
  8.3 2.7 %shard_map.121.token.blocks = bf16[16,512,256]{2,1,0:T(8,128)(2,1)S(1)} custom-call(s32[6]{0:T(128)S(1)} %stack.24.place.token, s32[6]{0:T(128)S(1)} %stack.24.place.token, bf16[16,512,256]{2,1,0:T(8,128)(2,1)} %source.3), custom_call_target="tpu_custom_call" | custom-call | bytes 4194304 | tf_op jit(solution)/shard_map/pallas_call | solution.py:149
  11.1 3.3 %shard_map.122 = bf16[6,2,512,256]{3,2,1,0:T(8,128)(2,1)} custom-call(s32[6]{0:T(128)S(1)} %stack.24.place.token, bf16[16,512,256]{2,1,0:T(8,128)(2,1)S(1)} %shard_map.121.token.blocks, bf16[6,4,512,256]{3,2,1,0:T(8,128)(2,1)} %lower.13, bf16[6,4,512,256]{3,2,1,0:T(8,128)(2,1)} %upper.13), custom_call_target="tpu_custom_call" | custom-call | bytes 6291456 | tf_op jit(solution)/shard_map/pallas_call | solution.py:83
  14.6 2.4 %all_gather.3.extended = bf16[12,64,512]{2,1,0:T(8,128)(2,1)S(1)} all-gather(bf16[12,64,256]{2,1,0:T(8,128)(2,1)S(1)} %pad_maximum_fusion), channel_id=1, replica_groups=mesh['groups'=2,'slab'=8,'vec'=2] {'vec'}, dimensions={2}, use_global_device_ids=true | all-gather | bytes 1179648 | tf_op jit(solution)/shard_map/all_gather | solution.py:444
  17.0 2.2 %shard_map.123 = (bf16[2,64,256]{2,1,0:T(8,128)(2,1)S(1)}, bf16[2,64,256]{2,1,0:T(8,128)(2,1)S(1)}, f32[64,128]{1,0:T(8,128)S(1)}) custom-call(s32[6]{0:T(128)S(1)} %stack.24.place.token, s32[4,14]{1,0:T(4,128)S(1)} %get-tuple-element.76.table, bf16[12,64,512]{2,1,0:T(8,128)(2,1)S(1)} %all_gather.3.extended, bf16[4,64,256]{2,1,0:T(8,128)(2,1)S(1)} %copy-done.2, ...), custom_call_target="tpu_custom_call" | custom-call | flops 469762048 | bytes 4194304 | tf_op jit(solution)/shard_map/pallas_call | solution.py:184
  22.1 4.2 %collective-permute-start.7 = (f32[64,128]{1,0:T(8,128)S(1)}, f32[64,128]{1,0:T(8,128)S(1)}, u32[]{:S(2)}, u32[]{:S(2)}) collective-permute-start(f32[64,128]{1,0:T(8,128)S(1)} %add.79), channel_id=1, source_target_pairs={{0,2},{2,0},{4,6},{6,4},{8,10},{10,8},{12,14},{14,12},{1,3},{3,1},... | collective-permute-start | bytes 98312 | tf_op jit(solution)/shard_map/ppermute | solution.py:456
  30.6 2.2 %collective-permute-start.10 = (f32[64,128]{1,0:T(8,128)S(1)}, f32[64,128]{1,0:T(8,128)S(1)}, u32[]{:S(2)}, u32[]{:S(2)}) collective-permute-start(f32[64,128]{1,0:T(8,128)S(1)} %add.82), channel_id=1, source_target_pairs={{0,4},{2,6},{4,0},{6,2},{8,12},{10,14},{12,8},{14,10},{1,5},{3,7},... | collective-permute-start | bytes 98312 | tf_op jit(solution)/shard_map/ppermute | solution.py:475
  34.7 3.9 %collective-permute-start.11 = (f32[64,128]{1,0:T(8,128)S(1)}, f32[64,128]{1,0:T(8,128)S(1)}, u32[]{:S(2)}, u32[]{:S(2)}) collective-permute-start(f32[64,128]{1,0:T(8,128)S(1)} %add.83), channel_id=1, source_target_pairs={{0,8},{2,10},{4,12},{6,14},{8,0},{10,2},{12,4},{14,6},{1,9},{3,11}... | collective-permute-start | bytes 98312 | tf_op jit(solution)/shard_map/ppermute | solution.py:475
  40.4 3.2 %shard_map.128 = bf16[5,2,512,256]{3,2,1,0:T(8,128)(2,1)} custom-call(s32[6]{0:T(128)S(1)} %stack.24.place.token, bf16[2,2,2,512,256]{4,3,2,1,0:T(8,128)(2,1)S(1)} %shard_map.127.token.weights, bf16[6,4,512,256]{3,2,1,0:T(8,128)(2,1)} %lower.13, bf16[6,4,512,256]{3,2,1,0:T(8,128)(2,1)} %upper.13, bf16[4,512,256]{2,1,0:T(8,128)(2,1)} %final.1), custom_call_target="tpu_custom_call" | custom-call | bytes 5242880 | tf_op jit(solution)/shard_map/pallas_call | solution.py:83
  45.8 3.6 %collective-permute-start.12 = (bf16[144,512]{1,0:T(8,128)(2,1)S(1)}, bf16[144,512]{1,0:T(8,128)(2,1)S(1)}, u32[]{:S(2)}, u32[]{:S(2)}) collective-permute-start(bf16[144,512]{1,0:T(8,128)(2,1)S(1)} %get-tuple-element.52), channel_id=1, source_target_pairs={{0,2},{1,3},{2,4},{3,5},{4,6},{5,7},{6,8},{7,9},{8,10},{9,11},{10,... | collective-permute-start | bytes 442376 | tf_op jit(solution)/shard_map/ppermute | solution.py:384
  50.7 1.8 %shard_map.130.weights = bf16[2,2,2,512,256]{4,3,2,1,0:T(8,128)(2,1)S(1)} custom-call(s32[6]{0:T(128)S(1)} %stack.24.place.token, bf16[2,64,512]{2,1,0:T(8,128)(2,1)S(1)} %get-tuple-element.53.token.own, bf16[6,4,512,256]{3,2,1,0:T(8,128)(2,1)} %lower.13, bf16[6,4,512,256]{3,2,1,0:T(8,128)(2,1)} %upper.13, ...), custom_call_target="tpu_custom_call" | custom-call | bytes 4194304 | tf_op jit(solution)/shard_map/pallas_call | solution.py:133
  52.5 4.4 %collective-permute-done.14.above = bf16[2,64,512]{2,1,0:T(8,128)(2,1)S(1)} collective-permute-done((bf16[2,64,512]{2,1,0:T(8,128)(2,1)S(1)}, bf16[2,64,512]{2,1,0:T(8,128)(2,1)S(1)}, u32[]{:S(2)}, u32[]{:S(2)}) %collective-permute-start.14) | collective-permute-done | bytes 131104 | tf_op jit(solution)/shard_map/ppermute | solution.py:384
  58.0 3.9 %collective-permute-start.15 = (bf16[2,64,512]{2,1,0:T(8,128)(2,1)S(1)}, bf16[2,64,512]{2,1,0:T(8,128)(2,1)S(1)}, u32[]{:S(2)}, u32[]{:S(2)}) collective-permute-start(bf16[2,64,512]{2,1,0:T(8,128)(2,1)S(1)} %shard_map.131.token.own), channel_id=1, source_target_pairs={{0,4},{1,5},{2,6},{3,7},{4,8},{5,9},{6,10},{7,11},{8,12},{9,13},{1... | collective-permute-start | bytes 393224 | tf_op jit(solution)/shard_map/ppermute | solution.py:384
  63.2 1.8 %shard_map.132.weights = bf16[2,2,2,512,256]{4,3,2,1,0:T(8,128)(2,1)S(1)} custom-call(s32[6]{0:T(128)S(1)} %stack.24.place.token, bf16[2,64,512]{2,1,0:T(8,128)(2,1)S(1)} %shard_map.131.token.own, bf16[6,4,512,256]{3,2,1,0:T(8,128)(2,1)} %lower.13, bf16[6,4,512,256]{3,2,1,0:T(8,128)(2,1)} %upper.13, bf16[5,2,512,256]{3,2,1,0:T(8,128)(2,1)S(1)} %collective-permute-done.13.packed), custom_call_target="tpu_custom_call" | custom-call | bytes 4194304 | tf_op jit(solution)/shard_map/pallas_call | solution.py:133
  65.0 3.9 %collective-permute-done.16.above = bf16[2,64,512]{2,1,0:T(8,128)(2,1)S(1)} collective-permute-done((bf16[2,64,512]{2,1,0:T(8,128)(2,1)S(1)}, bf16[2,64,512]{2,1,0:T(8,128)(2,1)S(1)}, u32[]{:S(2)}, u32[]{:S(2)}) %collective-permute-start.16) | collective-permute-done | bytes 131104 | tf_op jit(solution)/shard_map/ppermute | solution.py:384
  70.6 1.8 %collective-permute-start.17 = (bf16[2,64,512]{2,1,0:T(8,128)(2,1)S(1)}, bf16[2,64,512]{2,1,0:T(8,128)(2,1)S(1)}, u32[]{:S(2)}, u32[]{:S(2)}) collective-permute-start(bf16[2,64,512]{2,1,0:T(8,128)(2,1)S(1)} %shard_map.133.token.own), channel_id=1, source_target_pairs={{0,8},{1,9},{2,10},{3,11},{4,12},{5,13},{6,14},{7,15},{8,0},{9,1},... | collective-permute-start | bytes 393224 | tf_op jit(solution)/shard_map/ppermute | solution.py:500
  72.4 2.7 %shard_map.134.blocks = bf16[16,512,256]{2,1,0:T(8,128)(2,1)S(1)} custom-call(s32[6]{0:T(128)S(1)} %stack.24.place.token, bf16[2,64,512]{2,1,0:T(8,128)(2,1)S(1)} %shard_map.133.token.own, bf16[16,512,256]{2,1,0:T(8,128)(2,1)} %source.3), custom_call_target="tpu_custom_call" | custom-call | bytes 4194304 | tf_op jit(solution)/shard_map/pallas_call | solution.py:149
  75.1 1.8 %shard_map.135.weights = bf16[2,2,2,512,256]{4,3,2,1,0:T(8,128)(2,1)S(1)} custom-call(s32[6]{0:T(128)S(1)} %stack.24.place.token, bf16[2,64,512]{2,1,0:T(8,128)(2,1)S(1)} %shard_map.133.token.own, bf16[6,4,512,256]{3,2,1,0:T(8,128)(2,1)} %lower.13, bf16[6,4,512,256]{3,2,1,0:T(8,128)(2,1)} %upper.13, ...), custom_call_target="tpu_custom_call" | custom-call | bytes 4194304 | tf_op jit(solution)/shard_map/pallas_call | solution.py:133
  76.9 3.3 %collective-permute-done.17.other = bf16[2,64,512]{2,1,0:T(8,128)(2,1)S(1)} collective-permute-done((bf16[2,64,512]{2,1,0:T(8,128)(2,1)S(1)}, bf16[2,64,512]{2,1,0:T(8,128)(2,1)S(1)}, u32[]{:S(2)}, u32[]{:S(2)}) %collective-permute-start.17) | collective-permute-done | bytes 131104 | tf_op jit(solution)/shard_map/ppermute | solution.py:500
  83.0 3.4 %collective-permute-start.21 = (bf16[2,64,512]{2,1,0:T(8,128)(2,1)S(1)}, bf16[2,64,512]{2,1,0:T(8,128)(2,1)S(1)}, u32[]{:S(2)}, u32[]{:S(2)}) collective-permute-start(bf16[2,64,512]{2,1,0:T(8,128)(2,1)S(1)} %get-tuple-element.62.correction), channel_id=1, source_target_pairs={{0,2},{1,3},{2,4},{3,5},{4,6},{5,7},{6,8},{7,9},{8,10},{9,11},{10,... | collective-permute-start | bytes 393224 | tf_op jit(solution)/shard_map/ppermute | solution.py:384
  86.5 3.6 %shard_map.137 = (f32[6,64,512]{2,1,0:T(8,128)S(1)}, f32[160,128]{1,0:T(8,128)S(1)}, f32[8,128]{1,0:T(8,128)S(1)}) custom-call(s32[6]{0:T(128)S(1)} %stack.24.place.token, s32[8,14]{1,0:T(8,128)S(1)} %add_add_fusion.1.table, f32[8]{0:T(128)S(1)} %copy-done.3, s32[1]{0:T(128)S(6)} %copy.13.index, bf16[12,64,512]{2,1,0:T(8,128)(2,1)S(1)} %copy-done.1, ...), custom_call_target="tpu_custom_call" | custom-call | flops 469762048 | tf_op jit(solution)/shard_map/pallas_call | solution.py:542
  92.9 2.2 %collective-permute-start.24 = (f32[80,128]{1,0:T(8,128)S(1)}, f32[80,128]{1,0:T(8,128)S(1)}, u32[]{:S(2)}, u32[]{:S(2)}) collective-permute-start(f32[80,128]{1,0:T(8,128)S(1)} %add.85), channel_id=1, source_target_pairs={{0,4},{2,6},{4,0},{6,2},{8,12},{10,14},{12,8},{14,10},{1,5},{3,7},... | collective-permute-start | bytes 122888 | tf_op jit(solution)/shard_map/ppermute | solution.py:408
  97.1 2.9 %collective-permute-done.25 = f32[80,128]{1,0:T(8,128)S(1)} collective-permute-done((f32[80,128]{1,0:T(8,128)S(1)}, f32[80,128]{1,0:T(8,128)S(1)}, u32[]{:S(2)}, u32[]{:S(2)}) %collective-permute-start.25) | collective-permute-done | bytes 40992 | tf_op jit(solution)/shard_map/ppermute | solution.py:408
  102.3 3.2 %collective-permute-done.26 = f32[80,128]{1,0:T(8,128)S(1)} collective-permute-done((f32[80,128]{1,0:T(8,128)S(1)}, f32[80,128]{1,0:T(8,128)S(1)}, u32[]{:S(2)}, u32[]{:S(2)}) %collective-permute-start.26) | collective-permute-done | bytes 40992 | tf_op jit(solution)/shard_map/ppermute | solution.py:408
  (85 shorter events, 32.5 us)
Async XLA Ops:
  0.6 13.9 %collective-permute-start.1 = (bf16[4,64,256]{2,1,0:T(8,128)(2,1)}, bf16[4,64,256]{2,1,0:T(8,128)(2,1)S(1)}, u32[]{:S(2)}, u32[]{:S(2)}) collective-permute-start(bf16[4,64,256]{2,1,0:T(8,128)(2,1)} %vectors.1), channel_id=1, source_target_pairs={{2,0},{4,2},{6,4},{8,6},{10,8},{12,10},{14,12},{3,1},{5,3},{7,5},{... | collective-permute-start | bytes 393224 | tf_op jit(solution)/shard_map/ppermute | solution.py:384
  1.9 12.6 %collective-permute-start = (bf16[4,64,256]{2,1,0:T(8,128)(2,1)}, bf16[4,64,256]{2,1,0:T(8,128)(2,1)S(1)}, u32[]{:S(2)}, u32[]{:S(2)}) collective-permute-start(bf16[4,64,256]{2,1,0:T(8,128)(2,1)} %vectors.1), channel_id=1, source_target_pairs={{0,2},{2,4},{4,6},{6,8},{8,10},{10,12},{12,14},{1,3},{3,5},{5,7},{... | collective-permute-start | bytes 393224 | tf_op jit(solution)/shard_map/ppermute | solution.py:384
  20.7 6.0 %collective-permute-start.6 = (bf16[6,2,512,256]{3,2,1,0:T(8,128)(2,1)}, bf16[6,2,512,256]{3,2,1,0:T(8,128)(2,1)S(1)}, u32[]{:S(2)}, u32[]{:S(2)}) collective-permute-start(bf16[6,2,512,256]{3,2,1,0:T(8,128)(2,1)} %shard_map.122), channel_id=1, source_target_pairs={{0,1},{1,0},{2,3},{3,2},{4,5},{5,4},{6,7},{7,6},{8,9},{9,8},{10,11... | collective-permute-start | bytes 9437192 | tf_op jit(solution)/shard_map/ppermute | solution.py:378
  21.1 8.4 %collective-permute-start.4 = (bf16[1,64,512]{2,1,0:T(8,128)(2,1)S(1)}, bf16[1,64,512]{2,1,0:T(8,128)(2,1)S(1)}, u32[]{:S(2)}, u32[]{:S(2)}) collective-permute-start(bf16[1,64,512]{2,1,0:T(8,128)(2,1)S(1)} %get-tuple-element.78), channel_id=1, source_target_pairs={{0,1},{1,0},{2,3},{3,2},{4,5},{5,4},{6,7},{7,6},{8,9},{9,8},{10,11... | collective-permute-start | bytes 196616 | tf_op jit(solution)/shard_map/ppermute | solution.py:378
  21.4 8.2 %collective-permute-start.5 = (bf16[1,64,512]{2,1,0:T(8,128)(2,1)S(1)}, bf16[1,64,512]{2,1,0:T(8,128)(2,1)S(1)}, u32[]{:S(2)}, u32[]{:S(2)}) collective-permute-start(bf16[1,64,512]{2,1,0:T(8,128)(2,1)S(1)} %get-tuple-element.77), channel_id=1, source_target_pairs={{1,2},{3,4},{5,6},{7,8},{9,10},{11,12},{13,14},{2,1},{4,3},{6,5},{... | collective-permute-start | bytes 196616 | tf_op jit(solution)/shard_map/ppermute | solution.py:453
  22.1 8.5 %collective-permute-start.7 = (f32[64,128]{1,0:T(8,128)S(1)}, f32[64,128]{1,0:T(8,128)S(1)}, u32[]{:S(2)}, u32[]{:S(2)}) collective-permute-start(f32[64,128]{1,0:T(8,128)S(1)} %add.79), channel_id=1, source_target_pairs={{0,2},{2,0},{4,6},{6,4},{8,10},{10,8},{12,14},{14,12},{1,3},{3,1},... | collective-permute-start | bytes 98312 | tf_op jit(solution)/shard_map/ppermute | solution.py:456
  30.6 4.1 %collective-permute-start.10 = (f32[64,128]{1,0:T(8,128)S(1)}, f32[64,128]{1,0:T(8,128)S(1)}, u32[]{:S(2)}, u32[]{:S(2)}) collective-permute-start(f32[64,128]{1,0:T(8,128)S(1)} %add.82), channel_id=1, source_target_pairs={{0,4},{2,6},{4,0},{6,2},{8,12},{10,14},{12,8},{14,10},{1,5},{3,7},... | collective-permute-start | bytes 98312 | tf_op jit(solution)/shard_map/ppermute | solution.py:475
  32.8 11.1 %collective-permute-start.8 = (bf16[2,128,512]{2,1,0:T(8,128)(2,1)S(1)}, bf16[2,128,512]{2,1,0:T(8,128)(2,1)S(1)}, u32[]{:S(2)}, u32[]{:S(2)}) collective-permute-start(bf16[2,128,512]{2,1,0:T(8,128)(2,1)S(1)} %shard_map.126.token.own), channel_id=1, source_target_pairs={{0,1},{1,0},{2,3},{3,2},{4,5},{5,4},{6,7},{7,6},{8,9},{9,8},{10,11... | collective-permute-start | bytes 786440 | tf_op jit(solution)/shard_map/ppermute | solution.py:378
  32.9 11.1 %collective-permute-start.9 = (bf16[2,128,512]{2,1,0:T(8,128)(2,1)S(1)}, bf16[2,128,512]{2,1,0:T(8,128)(2,1)S(1)}, u32[]{:S(2)}, u32[]{:S(2)}) collective-permute-start(bf16[2,128,512]{2,1,0:T(8,128)(2,1)S(1)} %shard_map.126.token.own), channel_id=1, source_target_pairs={{1,2},{3,4},{5,6},{7,8},{9,10},{11,12},{13,14},{2,1},{4,3},{6,5},{... | collective-permute-start | bytes 786440 | tf_op jit(solution)/shard_map/ppermute | solution.py:472
  34.7 9.2 %collective-permute-start.11 = (f32[64,128]{1,0:T(8,128)S(1)}, f32[64,128]{1,0:T(8,128)S(1)}, u32[]{:S(2)}, u32[]{:S(2)}) collective-permute-start(f32[64,128]{1,0:T(8,128)S(1)} %add.83), channel_id=1, source_target_pairs={{0,8},{2,10},{4,12},{6,14},{8,0},{10,2},{12,4},{14,6},{1,9},{3,11}... | collective-permute-start | bytes 98312 | tf_op jit(solution)/shard_map/ppermute | solution.py:475
  44.0 13.0 %collective-permute-start.13 = (bf16[5,2,512,256]{3,2,1,0:T(8,128)(2,1)}, bf16[5,2,512,256]{3,2,1,0:T(8,128)(2,1)S(1)}, u32[]{:S(2)}, u32[]{:S(2)}) collective-permute-start(bf16[5,2,512,256]{3,2,1,0:T(8,128)(2,1)} %shard_map.128), channel_id=1, source_target_pairs={{0,1},{1,0},{2,3},{3,2},{4,5},{5,4},{6,7},{7,6},{8,9},{9,8},{10,11... | collective-permute-start | bytes 7864328 | tf_op jit(solution)/shard_map/ppermute | solution.py:378
  45.8 11.2 %collective-permute-start.12 = (bf16[144,512]{1,0:T(8,128)(2,1)S(1)}, bf16[144,512]{1,0:T(8,128)(2,1)S(1)}, u32[]{:S(2)}, u32[]{:S(2)}) collective-permute-start(bf16[144,512]{1,0:T(8,128)(2,1)S(1)} %get-tuple-element.52), channel_id=1, source_target_pairs={{0,2},{1,3},{2,4},{3,5},{4,6},{5,7},{6,8},{7,9},{8,10},{9,11},{10,... | collective-permute-start | bytes 442376 | tf_op jit(solution)/shard_map/ppermute | solution.py:384
  49.4 7.5 %collective-permute-start.14 = (bf16[2,64,512]{2,1,0:T(8,128)(2,1)S(1)}, bf16[2,64,512]{2,1,0:T(8,128)(2,1)S(1)}, u32[]{:S(2)}, u32[]{:S(2)}) collective-permute-start(bf16[2,64,512]{2,1,0:T(8,128)(2,1)S(1)} %get-tuple-element.53.token.own), channel_id=1, source_target_pairs={{2,0},{3,1},{4,2},{5,3},{6,4},{7,5},{8,6},{9,7},{10,8},{11,9},{12,... | collective-permute-start | bytes 393224 | tf_op jit(solution)/shard_map/ppermute | solution.py:384
  58.0 7.0 %collective-permute-start.15 = (bf16[2,64,512]{2,1,0:T(8,128)(2,1)S(1)}, bf16[2,64,512]{2,1,0:T(8,128)(2,1)S(1)}, u32[]{:S(2)}, u32[]{:S(2)}) collective-permute-start(bf16[2,64,512]{2,1,0:T(8,128)(2,1)S(1)} %shard_map.131.token.own), channel_id=1, source_target_pairs={{0,4},{1,5},{2,6},{3,7},{4,8},{5,9},{6,10},{7,11},{8,12},{9,13},{1... | collective-permute-start | bytes 393224 | tf_op jit(solution)/shard_map/ppermute | solution.py:384
  61.9 7.0 %collective-permute-start.16 = (bf16[2,64,512]{2,1,0:T(8,128)(2,1)S(1)}, bf16[2,64,512]{2,1,0:T(8,128)(2,1)S(1)}, u32[]{:S(2)}, u32[]{:S(2)}) collective-permute-start(bf16[2,64,512]{2,1,0:T(8,128)(2,1)S(1)} %shard_map.131.token.own), channel_id=1, source_target_pairs={{4,0},{5,1},{6,2},{7,3},{8,4},{9,5},{10,6},{11,7},{12,8},{13,9},{1... | collective-permute-start | bytes 393224 | tf_op jit(solution)/shard_map/ppermute | solution.py:384
  68.9 17.6 %collective-permute-start.18 = (bf16[16,512,256]{2,1,0:T(8,128)(2,1)S(1)}, bf16[16,512,256]{2,1,0:T(8,128)(2,1)S(1)}, u32[]{:S(2)}, u32[]{:S(2)}) collective-permute-start(bf16[16,512,256]{2,1,0:T(8,128)(2,1)S(1)} %copy-done.4), channel_id=1, source_target_pairs={{0,1},{1,0},{2,3},{3,2},{4,5},{5,4},{6,7},{7,6},{8,9},{9,8},{10,11... | collective-permute-start | bytes 12582920 | tf_op jit(solution)/shard_map/ppermute | solution.py:378
  70.6 9.7 %collective-permute-start.17 = (bf16[2,64,512]{2,1,0:T(8,128)(2,1)S(1)}, bf16[2,64,512]{2,1,0:T(8,128)(2,1)S(1)}, u32[]{:S(2)}, u32[]{:S(2)}) collective-permute-start(bf16[2,64,512]{2,1,0:T(8,128)(2,1)S(1)} %shard_map.133.token.own), channel_id=1, source_target_pairs={{0,8},{1,9},{2,10},{3,11},{4,12},{5,13},{6,14},{7,15},{8,0},{9,1},... | collective-permute-start | bytes 393224 | tf_op jit(solution)/shard_map/ppermute | solution.py:500
  81.4 8.7 %collective-permute-start.20 = (bf16[2,64,512]{2,1,0:T(8,128)(2,1)S(1)}, bf16[2,64,512]{2,1,0:T(8,128)(2,1)S(1)}, u32[]{:S(2)}, u32[]{:S(2)}) collective-permute-start(bf16[2,64,512]{2,1,0:T(8,128)(2,1)S(1)} %get-tuple-element.62.correction), channel_id=1, source_target_pairs={{0,1},{1,2},{2,3},{3,4},{4,5},{5,6},{6,7},{7,8},{8,9},{9,10},{10,1... | collective-permute-start | bytes 393224 | tf_op jit(solution)/shard_map/ppermute | solution.py:384
  83.0 7.1 %collective-permute-start.21 = (bf16[2,64,512]{2,1,0:T(8,128)(2,1)S(1)}, bf16[2,64,512]{2,1,0:T(8,128)(2,1)S(1)}, u32[]{:S(2)}, u32[]{:S(2)}) collective-permute-start(bf16[2,64,512]{2,1,0:T(8,128)(2,1)S(1)} %get-tuple-element.62.correction), channel_id=1, source_target_pairs={{0,2},{1,3},{2,4},{3,5},{4,6},{5,7},{6,8},{7,9},{8,10},{9,11},{10,... | collective-permute-start | bytes 393224 | tf_op jit(solution)/shard_map/ppermute | solution.py:384
  92.9 4.2 %collective-permute-start.24 = (f32[80,128]{1,0:T(8,128)S(1)}, f32[80,128]{1,0:T(8,128)S(1)}, u32[]{:S(2)}, u32[]{:S(2)}) collective-permute-start(f32[80,128]{1,0:T(8,128)S(1)} %add.85), channel_id=1, source_target_pairs={{0,4},{2,6},{4,0},{6,2},{8,12},{10,14},{12,8},{14,10},{1,5},{3,7},... | collective-permute-start | bytes 122888 | tf_op jit(solution)/shard_map/ppermute | solution.py:408
  95.1 4.9 %collective-permute-start.25 = (f32[80,128]{1,0:T(8,128)S(1)}, f32[80,128]{1,0:T(8,128)S(1)}, u32[]{:S(2)}, u32[]{:S(2)}) collective-permute-start(f32[80,128]{1,0:T(8,128)S(1)} %add.85), channel_id=1, source_target_pairs={{0,6},{2,4},{4,2},{6,0},{8,14},{10,12},{12,10},{14,8},{1,7},{3,5},... | collective-permute-start | bytes 122888 | tf_op jit(solution)/shard_map/ppermute | solution.py:408
  96.5 4.0 %collective-permute-start.23 = (f32[80,128]{1,0:T(8,128)S(1)}, f32[80,128]{1,0:T(8,128)S(1)}, u32[]{:S(2)}, u32[]{:S(2)}) collective-permute-start(f32[80,128]{1,0:T(8,128)S(1)} %add.85), channel_id=1, source_target_pairs={{0,2},{2,0},{4,6},{6,4},{8,10},{10,8},{12,14},{14,12},{1,3},{3,1},... | collective-permute-start | bytes 122888 | tf_op jit(solution)/shard_map/ppermute | solution.py:408
  100.5 5.0 %collective-permute-start.26 = (f32[80,128]{1,0:T(8,128)S(1)}, f32[80,128]{1,0:T(8,128)S(1)}, u32[]{:S(2)}, u32[]{:S(2)}) collective-permute-start(f32[80,128]{1,0:T(8,128)S(1)} %add_add_fusion), channel_id=1, source_target_pairs={{0,8},{2,10},{4,12},{6,14},{8,0},{10,2},{12,4},{14,6},{1,9},{3,11}... | collective-permute-start | bytes 122888 | tf_op jit(solution)/shard_map/ppermute | solution.py:408
  102.3 3.2 %collective-permute-start.19 = (bf16[2,64,256]{2,1,0:T(8,128)(2,1)S(1)}, bf16[2,64,256]{2,1,0:T(8,128)(2,1)S(1)}, u32[]{:S(2)}, u32[]{:S(2)}) collective-permute-start(bf16[2,64,256]{2,1,0:T(8,128)(2,1)S(1)} %get-tuple-element.67), channel_id=1, source_target_pairs={{0,1},{1,0},{2,3},{3,2},{4,5},{5,4},{6,7},{7,6},{8,9},{9,8},{10,11... | collective-permute-start | bytes 196616 | tf_op jit(solution)/shard_map/ppermute | solution.py:378
  (11 other events, 47.2 us)

commit v10 on v9

--- a/solution.py
+++ b/solution.py
@@ -59,41 +59,91 @@
         copy.wait()
 
 
-def pack_body(levels, place, token, lower, upper, *rest):
-    *final, out, held, sem = rest
-    count = out.shape[1]
-    slabs = pl.ds((1 - place[0]) * count, count)
-    parts = [ref.at[level, slabs] for level in levels for ref in (lower, upper)]
-    parts += [ref.at[slabs] for ref in final]
+def through(parts, held, outs, sem):
     ins = [pltpu.make_async_copy(part, held.at[k], sem.at[0, k]) for k, part in enumerate(parts)]
-    outs = [pltpu.make_async_copy(held.at[k], out.at[k], sem.at[1, k]) for k in range(len(parts))]
-    for copy in ins:
-        copy.start()
+    outs = [pltpu.make_async_copy(held.at[k], out, sem.at[1, k]) for k, out in enumerate(outs)]
+    return ins, outs
+
+
+def finish(ins, outs, others):
     for copy, following in zip(ins, outs):
         copy.wait()
         following.start()
-    for copy in outs:
+    for copy in others + outs:
         copy.wait()
 
 
-def pack(levels, place, token, *operands):
-    _, slabs, rows, half = operands[0].shape
-    count = 2 * len(levels) + len(operands) - 2
-    shape = (count, slabs // 2, rows, half)
+def prepare_body(place, lower, upper, blocks, held_blocks, first, second, held, sem, block_sem):
+    count = held.shape[1]
+    slabs = pl.ds((1 - place[0]) * count, count)
+    parts = [ref.at[level, slabs] for level in range(3) for ref in (lower, upper)]
+    outs = [first.at[k] for k in range(2)] + [second.at[k] for k in range(4)]
+    ins, outs = through(parts, held, outs, sem)
+    whole = pltpu.make_async_copy(blocks, held_blocks, block_sem.at[0])
+    for copy in ins + [whole]:
+        copy.start()
+    finish(ins, outs, [whole])
+
+
+def prepare(place, lower, upper, blocks):
+    _, slabs, rows, half = lower.shape
+    shape = (slabs // 2, rows, half)
+    size = 2 * slabs * rows * half
     return pl.pallas_call(
-        functools.partial(pack_body, levels),
-        out_shape=pltpu.HBM(shape, bf16),
-        in_specs=[SMEM] + [ANY] * (1 + len(operands)),
-        out_specs=ANY,
-        scratch_shapes=[pltpu.VMEM(shape, bf16), pltpu.SemaphoreType.DMA((2, count))],
-        compiler_params=pltpu.CompilerParams(vmem_limit_bytes=6 * MIB),
+        prepare_body,
+        out_shape=[
+            pltpu.VMEM(blocks.shape, bf16),
+            pltpu.HBM((2,) + shape, bf16),
+            pltpu.HBM((4,) + shape, bf16),
+        ],
+        in_specs=[SMEM] + [ANY] * 3,
+        out_specs=[VMEM, ANY, ANY],
+        scratch_shapes=[
+            pltpu.VMEM((6,) + shape, bf16),
+            pltpu.SemaphoreType.DMA((2, 6)),
+            pltpu.SemaphoreType.DMA((1,)),
+        ],
+        compiler_params=pltpu.CompilerParams(vmem_limit_bytes=10 * MIB),
         cost_estimate=pl.CostEstimate(
-            flops=0, bytes_accessed=4 * count * (slabs // 2) * rows * half, transcendentals=0
+            flops=0, bytes_accessed=2 * blocks.size + 6 * size, transcendentals=0
         ),
-    )(place, token, *[in_hbm(x) for x in operands])
-
-
-def load_body(level, first, place, token, lower, upper, packed, weights, sem):
+    )(place, *[in_hbm(x) for x in (lower, upper, blocks)])
+
+
+def load_and_pack_body(level, first, later, place, token, lower, upper, final, packed, weights, out, held, sem, pack_sem):
+    count = weights.shape[2]
+    slabs = pl.ds((1 - place[0]) * count, count)
+    parts = [ref.at[each, slabs] for each in later for ref in (lower, upper)] + [final.at[slabs]]
+    ins, outs = through(parts, held, [out.at[k] for k in range(len(parts))], pack_sem)
+    loads = level_copies(level, first, place, lower, upper, packed, weights, sem)
+    for copy in ins + loads:
+        copy.start()
+    finish(ins, outs, loads)
+
+
+def load_and_pack(level, first, later, place, token, lower, upper, final, packed):
+    _, slabs, rows, half = lower.shape
+    shape = (2, 2, slabs // 2, rows, half)
+    count = 2 * len(later) + 1
+    later_shape = (count,) + shape[2:]
+    return pl.pallas_call(
+        functools.partial(load_and_pack_body, level, first, later),
+        out_shape=[pltpu.VMEM(shape, bf16), pltpu.HBM(later_shape, bf16)],
+        in_specs=[SMEM] + [ANY] * 5,
+        out_specs=[VMEM, ANY],
+        scratch_shapes=[
+            pltpu.VMEM(later_shape, bf16),
+            pltpu.SemaphoreType.DMA((2, 2)),
+            pltpu.SemaphoreType.DMA((2, count)),
+        ],
+        compiler_params=pltpu.CompilerParams(vmem_limit_bytes=8 * MIB),
+        cost_estimate=pl.CostEstimate(
+            flops=0, bytes_accessed=(8 + 4 * count) * slabs * rows * half // 2, transcendentals=0
+        ),
+    )(place, token, *[in_hbm(x) for x in (lower, upper, final)], packed)
+
+
+def level_copies(level, first, place, lower, upper, packed, weights, sem):
     count = weights.shape[2]
     slabs = pl.ds(place[0] * count, count)
     copies = []
@@ -101,7 +151,11 @@
         sources = (ref.at[level, slabs], packed.at[2 * (level - first) + side])
         for part, source in enumerate(sources):
             copies.append(pltpu.make_async_copy(source, weights.at[side, part], sem.at[side, part]))
-    run(copies)
+    return copies
+
+
+def load_body(level, first, place, token, lower, upper, packed, weights, sem):
+    run(level_copies(level, first, place, lower, upper, packed, weights, sem))
 
 
 def load_last_body(level, first, place, token, lower, upper, packed, final, weights, sem):
@@ -439,10 +493,10 @@
     near = jnp.broadcast_to(jnp.arange(-1, 2, dtype=jnp.int32), (slab_count, 3))
     table = jnp.concatenate([near, far_source - slab_ids, slab_blocks, far_block], 1)
     note = jnp.pad(table.astype(bf16), ((0, 16 - slab_count), (0, width - table.shape[1])))
-    held_blocks = load_whole(place, place, blocks)
-    theirs = pack(levels[:3], place, held_blocks, level_lower, level_upper)
+    held_blocks, theirs_0, theirs = prepare(place, level_lower, level_upper, blocks)
     extended = lax.all_gather(jnp.concatenate([below, vectors, above], 0), "vec", axis=2, tiled=True)
-    theirs, extended = lax.optimization_barrier((theirs, extended))
+    theirs_0, extended = lax.optimization_barrier((theirs_0, extended))
+    packed_0 = swapped(theirs_0)
     keep, send, moments = image_halves(place, table, extended, vectors, in_vmem(held_blocks))
     received, moments = swapped(send), moments + swapped(moments)
     image = jnp.where(core == 0, jnp.concatenate([keep, received], 2), jnp.concatenate([received, keep], 2))
@@ -455,7 +509,7 @@
     flips = [[(i, i ^ 2**bit) for i in range(slabs)] for bit in range((slabs - 1).bit_length())]
     received = lax.ppermute(moments, "slab", flips[0])
     body = functools.partial(load_body, 0, 0)
-    matrices = in_vmem(load(body, place, image, level_lower, level_upper, packed))
+    matrices = in_vmem(load(body, place, keep, level_lower, level_upper, packed_0))
     vectors_1 = kernel_call(
         first_vectors_body,
         struct(image.shape),
@@ -468,15 +522,17 @@
         [SMEM] + [VMEM] * 5,
         flops=level_flops(image, 2),
     )(place, image, inner, outer, vectors_1, matrices)
-    both, received = lax.optimization_barrier((both, received))
+    both, received, late_blocks, packed = lax.optimization_barrier((both, received, blocks, packed))
+    others = swapped(late_blocks)
     outer, inner = lax.ppermute(both, CHAIN, outer_route), swapped(both)
     for flip in flips[1:]:
         moments = moments + received
         received = lax.ppermute(moments, "slab", flip)
     moments = (moments + received) / rows_total
-    body = functools.partial(load_body, 1, 0)
-    matrices = in_vmem(load(body, place, both, level_lower, level_upper, packed))
-    theirs = pack(levels[3:], place, matrices, level_lower, level_upper, level_final)
+    matrices, theirs = load_and_pack(
+        1, 1, levels[3:], place, both, level_lower, level_upper, level_final, packed
+    )
+    matrices = in_vmem(matrices)
     theirs, inner, outer, moments = lax.optimization_barrier((theirs, inner, outer, moments))
     following = swapped(theirs)
     residual, lifted = kernel_call(
@@ -507,7 +563,7 @@
                 flops=level_flops(residual, 2),
             )(place, residual, other, in_vmem(matrices))
             break
-        body = functools.partial(load_body, level, 0 if level == 2 else 3)
+        body = functools.partial(load_body, level, 1 if level == 2 else 3)
         matrices = load(body, place, residual, level_lower, level_upper, packed)
         below, above = along(residual if level > 2 else lifted, CHAIN, step), along(residual, CHAIN, -step)
         if level == 2:
@@ -515,8 +571,7 @@
             lower_table = below[count : count + slab_count, : table.shape[1]].astype(jnp.int32)
             packed, below, above = lax.optimization_barrier((following, below, above))
         if level == 3:
-            late_blocks, below, above, matrices = lax.optimization_barrier((blocks, below, above, matrices))
-            others = swapped(late_blocks)
+            below, above, matrices = lax.optimization_barrier((below, above, matrices))
         residual = kernel_call(
             level_body if level > 2 else third_body,
             struct(residual.shape),

time: 109 us -> 106 us (0.972)
  Pallas kernels: 36.6 us -> 33.6 us
    pallas_call x2 -> x1, Pallas kernels: 5.47 us -> 2.74 us  [load_whole(): pl.pallas_call(load_whole_body, out_shape=pltpu.VMEM(array.shape, array.d...]
    ppermute x10 -> x11, starting transfers between devices: 1.44 us -> 3.45 us  [swapped(): return lax.ppermute(operand, 'vec', SWAP)]
    ppermute x2, waiting for transfers between devices: 1.49 us -> 3.33 us  [on_device(): received = lax.ppermute(moments, 'slab', flip)]
    pallas_call x2, Pallas kernels: 6.49 us -> 8.14 us  [the longest x1 4.97 us: prepare(): pl.pallas_call(prepare_body, out_shape=[pltpu.VMEM(blocks.shape, bf16), p...]
    ppermute x1, waiting for transfers between devices: 3.32 us -> 1.8 us  [on_device(): other = lax.ppermute(residual, CHAIN, route)]
    pallas_call x5 -> x4, Pallas kernels: 8.95 us -> 7.47 us  [load(): pl.pallas_call(body, out_shape=pltpu.VMEM(shape, bf16), in_specs=[SMEM] +...]
    ppermute x10 -> x11, waiting for transfers between devices: 3.63 us -> 3.22 us  [swapped(): return lax.ppermute(operand, 'vec', SWAP)]
  transfers between devices with their start and end apart: 28 -> 29, of which waited for: 13 -> 14; matrix products, arithmetic and copies ran while one was open for 1% -> 1% of each run, Pallas kernels for 28% -> 27%
where the time goes in v10:
time: 106 us
  starting transfers between devices  43.1 us (41%)
  Pallas kernels  33.6 us (32%)
  waiting for transfers between devices  23.6 us (22%)
  blocking collectives  2.37 us (2%)
  between operations  1.69 us (2%)
    ppermute x8, starting transfers between devices, along(): return lax.ppermute(operand, axis, route)  20.9 us
    ppermute x8, waiting for transfers between devices, along(): return lax.ppermute(operand, axis, route)  7.84 us
    pallas_call x4, Pallas kernels, load(): pl.pallas_call(body, out_shape=pltpu.VMEM(shape, bf16), in_specs=[SMEM] +...  7.47 us
    ppermute x4, waiting for transfers between devices, slab_total(): lax.ppermute(part, 'slab', route)  7.39 us
    ppermute x2, starting transfers between devices, on_device(): received = lax.ppermute(moments, 'slab', flip)  6.05 us
    ppermute x4, starting transfers between devices, slab_total(): lax.ppermute(part, 'slab', route)  5.49 us
    pallas_call x1, Pallas kernels, prepare(): pl.pallas_call(prepare_body, out_shape=[pltpu.VMEM(blocks.shape, bf16), p...  4.97 us
    ppermute x1, starting transfers between devices, on_device(): received = lax.ppermute(moments, 'slab', flips[0])  4.23 us
  transfers between devices with their start and end apart: 29, of which 14 were waited for; matrix products, arithmetic and copies ran while one was open for 1% of the time, Pallas kernels for 27%

profile of v10, /device:TPU:0, one launch (start us, length us, event | category | flops | bytes accessed | tf_op | source)
XLA Modules:
  0.0 105.6 jit_solution(10706330204437846665)
XLA Ops:
  1.9 5.5 %collective-permute-start = (bf16[4,64,256]{2,1,0:T(8,128)(2,1)}, bf16[4,64,256]{2,1,0:T(8,128)(2,1)S(1)}, u32[]{:S(2)}, u32[]{:S(2)}) collective-permute-start(bf16[4,64,256]{2,1,0:T(8,128)(2,1)} %vectors.1), channel_id=1, source_target_pairs={{0,2},{2,4},{4,6},{6,8},{8,10},{10,12},{12,14},{1,3},{3,5},{5,7},{... | collective-permute-start | bytes 393224 | tf_op jit(solution)/shard_map/ppermute | solution.py:438
  8.3 5.0 %shard_map.121 = (bf16[16,512,256]{2,1,0:T(8,128)(2,1)S(1)}, bf16[2,2,512,256]{3,2,1,0:T(8,128)(2,1)}, bf16[4,2,512,256]{3,2,1,0:T(8,128)(2,1)}) custom-call(s32[6]{0:T(128)S(1)} %stack.24.place, bf16[6,4,512,256]{3,2,1,0:T(8,128)(2,1)} %lower.11, bf16[6,4,512,256]{3,2,1,0:T(8,128)(2,1)} %upper.11, bf16[16,512,256]{2,1,0:T(8,128)(2,1)} %source.1), custom_call_target="tpu_custom_call" | custom-call | bytes 10485760 | tf_op jit(solution)/shard_map/pallas_call | solution.py:92
  13.4 2.4 %all_gather.3.extended = bf16[12,64,512]{2,1,0:T(8,128)(2,1)S(1)} all-gather(bf16[12,64,256]{2,1,0:T(8,128)(2,1)S(1)} %pad_maximum_fusion), channel_id=1, replica_groups=mesh['groups'=2,'slab'=8,'vec'=2] {'vec'}, dimensions={2}, use_global_device_ids=true | all-gather | bytes 1179648 | tf_op jit(solution)/shard_map/all_gather | solution.py:497
  15.8 2.2 %shard_map.122 = (bf16[2,64,256]{2,1,0:T(8,128)(2,1)S(1)}, bf16[2,64,256]{2,1,0:T(8,128)(2,1)S(1)}, f32[64,128]{1,0:T(8,128)S(1)}) custom-call(s32[6]{0:T(128)S(1)} %stack.24.place, s32[4,14]{1,0:T(4,128)S(1)} %get-tuple-element.88.table, bf16[12,64,512]{2,1,0:T(8,128)(2,1)S(1)} %all_gather.3.extended, bf16[4,64,256]{2,1,0:T(8,128)(2,1)S(1)} %copy-done, ...), custom_call_target="tpu_custom_call" | custom-call | flops 469762048 | bytes 4194304 | tf_op jit(solution)/shard_map/pallas_call | solution.py:238
  21.2 4.2 %collective-permute-start.7 = (f32[64,128]{1,0:T(8,128)S(1)}, f32[64,128]{1,0:T(8,128)S(1)}, u32[]{:S(2)}, u32[]{:S(2)}) collective-permute-start(f32[64,128]{1,0:T(8,128)S(1)} %add.79), channel_id=1, source_target_pairs={{0,2},{2,0},{4,6},{6,4},{8,10},{10,8},{12,14},{14,12},{1,3},{3,1},... | collective-permute-start | bytes 98312 | tf_op jit(solution)/shard_map/ppermute | solution.py:510
  25.7 2.1 %shard_map.123.weights = bf16[2,2,2,512,256]{4,3,2,1,0:T(8,128)(2,1)S(1)} custom-call(s32[6]{0:T(128)S(1)} %stack.24.place, bf16[2,64,256]{2,1,0:T(8,128)(2,1)S(1)} %get-tuple-element.48.token, bf16[6,4,512,256]{3,2,1,0:T(8,128)(2,1)} %lower.11, bf16[6,4,512,256]{3,2,1,0:T(8,128)(2,1)} %upper.11, bf16[2,2,512,256]{3,2,1,0:T(8,128)(2,1)} %collective-permute-done.6.packed), custom_call_target="tpu_custom_call" | custom-call | bytes 4194304 | tf_op jit(solution)/shard_map/pallas_call | solution.py:187
  30.3 2.1 %collective-permute-start.11 = (f32[64,128]{1,0:T(8,128)S(1)}, f32[64,128]{1,0:T(8,128)S(1)}, u32[]{:S(2)}, u32[]{:S(2)}) collective-permute-start(f32[64,128]{1,0:T(8,128)S(1)} %add.82), channel_id=1, source_target_pairs={{0,4},{2,6},{4,0},{6,2},{8,12},{10,14},{12,8},{14,10},{1,5},{3,7},... | collective-permute-start | bytes 98312 | tf_op jit(solution)/shard_map/ppermute | solution.py:530
  34.3 3.9 %collective-permute-start.12 = (f32[64,128]{1,0:T(8,128)S(1)}, f32[64,128]{1,0:T(8,128)S(1)}, u32[]{:S(2)}, u32[]{:S(2)}) collective-permute-start(f32[64,128]{1,0:T(8,128)S(1)} %add.83), channel_id=1, source_target_pairs={{0,8},{2,10},{4,12},{6,14},{8,0},{10,2},{12,4},{14,6},{1,9},{3,11}... | collective-permute-start | bytes 98312 | tf_op jit(solution)/shard_map/ppermute | solution.py:530
  38.3 3.2 %shard_map.126 = (bf16[2,2,2,512,256]{4,3,2,1,0:T(8,128)(2,1)S(1)}, bf16[5,2,512,256]{3,2,1,0:T(8,128)(2,1)}) custom-call(s32[6]{0:T(128)S(1)} %stack.24.place, bf16[2,128,512]{2,1,0:T(8,128)(2,1)S(1)} %shard_map.125.token.own, bf16[6,4,512,256]{3,2,1,0:T(8,128)(2,1)} %lower.11, bf16[6,4,512,256]{3,2,1,0:T(8,128)(2,1)} %upper.11, ...), custom_call_target="tpu_custom_call" | custom-call | bytes 7340032 | tf_op jit(solution)/shard_map/pallas_call | solution.py:129
  41.5 2.1 %collective-permute-done.12 = f32[64,128]{1,0:T(8,128)S(1)} collective-permute-done((f32[64,128]{1,0:T(8,128)S(1)}, f32[64,128]{1,0:T(8,128)S(1)}, u32[]{:S(2)}, u32[]{:S(2)}) %collective-permute-start.12) | collective-permute-done | bytes 32800 | tf_op jit(solution)/shard_map/ppermute | solution.py:530
  45.4 3.5 %collective-permute-start.13 = (bf16[144,512]{1,0:T(8,128)(2,1)S(1)}, bf16[144,512]{1,0:T(8,128)(2,1)S(1)}, u32[]{:S(2)}, u32[]{:S(2)}) collective-permute-start(bf16[144,512]{1,0:T(8,128)(2,1)S(1)} %get-tuple-element.64), channel_id=1, source_target_pairs={{0,2},{1,3},{2,4},{3,5},{4,6},{5,7},{6,8},{7,9},{8,10},{9,11},{10,... | collective-permute-start | bytes 442376 | tf_op jit(solution)/shard_map/ppermute | solution.py:438
  50.3 1.8 %shard_map.128.weights = bf16[2,2,2,512,256]{4,3,2,1,0:T(8,128)(2,1)S(1)} custom-call(s32[6]{0:T(128)S(1)} %stack.24.place, bf16[2,64,512]{2,1,0:T(8,128)(2,1)S(1)} %get-tuple-element.65.token.own, bf16[6,4,512,256]{3,2,1,0:T(8,128)(2,1)} %lower.11, bf16[6,4,512,256]{3,2,1,0:T(8,128)(2,1)} %upper.11, bf16[4,2,512,256]{3,2,1,0:T(8,128)(2,1)S(1)} %collective-permute-done.8.packed), custom_call_target="tpu_custom_call" | custom-call | bytes 4194304 | tf_op jit(solution)/shard_map/pallas_call | solution.py:187
  52.1 4.4 %collective-permute-done.15.above = bf16[2,64,512]{2,1,0:T(8,128)(2,1)S(1)} collective-permute-done((bf16[2,64,512]{2,1,0:T(8,128)(2,1)S(1)}, bf16[2,64,512]{2,1,0:T(8,128)(2,1)S(1)}, u32[]{:S(2)}, u32[]{:S(2)}) %collective-permute-start.15) | collective-permute-done | bytes 131104 | tf_op jit(solution)/shard_map/ppermute | solution.py:438
  57.5 3.6 %collective-permute-start.16 = (bf16[2,64,512]{2,1,0:T(8,128)(2,1)S(1)}, bf16[2,64,512]{2,1,0:T(8,128)(2,1)S(1)}, u32[]{:S(2)}, u32[]{:S(2)}) collective-permute-start(bf16[2,64,512]{2,1,0:T(8,128)(2,1)S(1)} %shard_map.129.token.own), channel_id=1, source_target_pairs={{0,4},{1,5},{2,6},{3,7},{4,8},{5,9},{6,10},{7,11},{8,12},{9,13},{1... | collective-permute-start | bytes 393224 | tf_op jit(solution)/shard_map/ppermute | solution.py:438
  63.1 1.8 %shard_map.130.weights = bf16[2,2,2,512,256]{4,3,2,1,0:T(8,128)(2,1)S(1)} custom-call(s32[6]{0:T(128)S(1)} %stack.24.place, bf16[2,64,512]{2,1,0:T(8,128)(2,1)S(1)} %shard_map.129.token.own, bf16[6,4,512,256]{3,2,1,0:T(8,128)(2,1)} %lower.11, bf16[6,4,512,256]{3,2,1,0:T(8,128)(2,1)} %upper.11, bf16[5,2,512,256]{3,2,1,0:T(8,128)(2,1)S(1)} %collective-permute-done.14.packed), custom_call_target="tpu_custom_call" | custom-call | bytes 4194304 | tf_op jit(solution)/shard_map/pallas_call | solution.py:187
  64.9 3.3 %collective-permute-done.17.above = bf16[2,64,512]{2,1,0:T(8,128)(2,1)S(1)} collective-permute-done((bf16[2,64,512]{2,1,0:T(8,128)(2,1)S(1)}, bf16[2,64,512]{2,1,0:T(8,128)(2,1)S(1)}, u32[]{:S(2)}, u32[]{:S(2)}) %collective-permute-start.17) | collective-permute-done | bytes 131104 | tf_op jit(solution)/shard_map/ppermute | solution.py:438
  70.9 2.7 %shard_map.132.blocks = bf16[16,512,256]{2,1,0:T(8,128)(2,1)S(1)} custom-call(s32[6]{0:T(128)S(1)} %stack.24.place, bf16[2,64,512]{2,1,0:T(8,128)(2,1)S(1)} %shard_map.131.token.own, bf16[16,512,256]{2,1,0:T(8,128)(2,1)} %source.1), custom_call_target="tpu_custom_call" | custom-call | bytes 4194304 | tf_op jit(solution)/shard_map/pallas_call | solution.py:203
  73.6 1.8 %shard_map.133.weights = bf16[2,2,2,512,256]{4,3,2,1,0:T(8,128)(2,1)S(1)} custom-call(s32[6]{0:T(128)S(1)} %stack.24.place, bf16[2,64,512]{2,1,0:T(8,128)(2,1)S(1)} %shard_map.131.token.own, bf16[6,4,512,256]{3,2,1,0:T(8,128)(2,1)} %lower.11, bf16[6,4,512,256]{3,2,1,0:T(8,128)(2,1)} %upper.11, bf16[5,2,512,256]{3,2,1,0:T(8,128)(2,1)S(1)} %collective-permute-done.14.packed, ...), custom_call_target="tpu_custom_call" | custom-call | bytes 4194304 | tf_op jit(solution)/shard_map/pallas_call | solution.py:187
  75.4 1.8 %collective-permute-done.18.other = bf16[2,64,512]{2,1,0:T(8,128)(2,1)S(1)} collective-permute-done((bf16[2,64,512]{2,1,0:T(8,128)(2,1)S(1)}, bf16[2,64,512]{2,1,0:T(8,128)(2,1)S(1)}, u32[]{:S(2)}, u32[]{:S(2)}) %collective-permute-start.18) | collective-permute-done | bytes 131104 | tf_op jit(solution)/shard_map/ppermute | solution.py:556
  79.6 3.1 %collective-permute-start.22 = (bf16[2,64,512]{2,1,0:T(8,128)(2,1)S(1)}, bf16[2,64,512]{2,1,0:T(8,128)(2,1)S(1)}, u32[]{:S(2)}, u32[]{:S(2)}) collective-permute-start(bf16[2,64,512]{2,1,0:T(8,128)(2,1)S(1)} %get-tuple-element.74.correction), channel_id=1, source_target_pairs={{0,2},{1,3},{2,4},{3,5},{4,6},{5,7},{6,8},{7,9},{8,10},{9,11},{10,... | collective-permute-start | bytes 393224 | tf_op jit(solution)/shard_map/ppermute | solution.py:438
  82.9 3.2 %shard_map.135 = (f32[6,64,512]{2,1,0:T(8,128)S(1)}, f32[160,128]{1,0:T(8,128)S(1)}, f32[8,128]{1,0:T(8,128)S(1)}) custom-call(s32[6]{0:T(128)S(1)} %stack.24.place, s32[8,14]{1,0:T(8,128)S(1)} %add_add_fusion.1.table, f32[8]{0:T(128)S(1)} %copy-done.1, s32[1]{0:T(128)S(6)} %copy.13.index, bf16[12,64,512]{2,1,0:T(8,128)(2,1)S(1)} %all_gather.3.extended, ...), custom_call_target="tpu_custom_call" | custom-call | flops 469762048 | tf_op jit(solution)/shard_map/pallas_call | solution.py:597
  90.0 2.6 %collective-permute-start.25 = (f32[80,128]{1,0:T(8,128)S(1)}, f32[80,128]{1,0:T(8,128)S(1)}, u32[]{:S(2)}, u32[]{:S(2)}) collective-permute-start(f32[80,128]{1,0:T(8,128)S(1)} %add.85), channel_id=1, source_target_pairs={{0,4},{2,6},{4,0},{6,2},{8,12},{10,14},{12,8},{14,10},{1,5},{3,7},... | collective-permute-start | bytes 122888 | tf_op jit(solution)/shard_map/ppermute | solution.py:462
  94.5 2.9 %collective-permute-done.26 = f32[80,128]{1,0:T(8,128)S(1)} collective-permute-done((f32[80,128]{1,0:T(8,128)S(1)}, f32[80,128]{1,0:T(8,128)S(1)}, u32[]{:S(2)}, u32[]{:S(2)}) %collective-permute-start.26) | collective-permute-done | bytes 40992 | tf_op jit(solution)/shard_map/ppermute | solution.py:462
  99.3 3.6 %collective-permute-done.27 = f32[80,128]{1,0:T(8,128)S(1)} collective-permute-done((f32[80,128]{1,0:T(8,128)S(1)}, f32[80,128]{1,0:T(8,128)S(1)}, u32[]{:S(2)}, u32[]{:S(2)}) %collective-permute-start.27) | collective-permute-done | bytes 40992 | tf_op jit(solution)/shard_map/ppermute | solution.py:462
  (81 shorter events, 31.1 us)
Async XLA Ops:
  0.6 12.7 %collective-permute-start.1 = (bf16[4,64,256]{2,1,0:T(8,128)(2,1)}, bf16[4,64,256]{2,1,0:T(8,128)(2,1)S(1)}, u32[]{:S(2)}, u32[]{:S(2)}) collective-permute-start(bf16[4,64,256]{2,1,0:T(8,128)(2,1)} %vectors.1), channel_id=1, source_target_pairs={{2,0},{4,2},{6,4},{8,6},{10,8},{12,10},{14,12},{3,1},{5,3},{7,5},{... | collective-permute-start | bytes 393224 | tf_op jit(solution)/shard_map/ppermute | solution.py:438
  1.9 11.4 %collective-permute-start = (bf16[4,64,256]{2,1,0:T(8,128)(2,1)}, bf16[4,64,256]{2,1,0:T(8,128)(2,1)S(1)}, u32[]{:S(2)}, u32[]{:S(2)}) collective-permute-start(bf16[4,64,256]{2,1,0:T(8,128)(2,1)} %vectors.1), channel_id=1, source_target_pairs={{0,2},{2,4},{4,6},{6,8},{8,10},{10,12},{12,14},{1,3},{3,5},{5,7},{... | collective-permute-start | bytes 393224 | tf_op jit(solution)/shard_map/ppermute | solution.py:438
  19.5 10.4 %collective-permute-start.8 = (bf16[4,2,512,256]{3,2,1,0:T(8,128)(2,1)}, bf16[4,2,512,256]{3,2,1,0:T(8,128)(2,1)S(1)}, u32[]{:S(2)}, u32[]{:S(2)}) collective-permute-start(bf16[4,2,512,256]{3,2,1,0:T(8,128)(2,1)} %get-tuple-element.55), channel_id=1, source_target_pairs={{0,1},{1,0},{2,3},{3,2},{4,5},{5,4},{6,7},{7,6},{8,9},{9,8},{10,11... | collective-permute-start | bytes 6291464 | tf_op jit(solution)/shard_map/ppermute | solution.py:432
  19.9 5.7 %collective-permute-start.6 = (bf16[2,2,512,256]{3,2,1,0:T(8,128)(2,1)}, bf16[2,2,512,256]{3,2,1,0:T(8,128)(2,1)}, u32[]{:S(2)}, u32[]{:S(2)}) collective-permute-start(bf16[2,2,512,256]{3,2,1,0:T(8,128)(2,1)} %get-tuple-element.53), channel_id=1, source_target_pairs={{0,1},{1,0},{2,3},{3,2},{4,5},{5,4},{6,7},{7,6},{8,9},{9,8},{10,11... | collective-permute-start | bytes 3145736 | tf_op jit(solution)/shard_map/ppermute | solution.py:432
  20.1 8.7 %collective-permute-start.4 = (bf16[1,64,512]{2,1,0:T(8,128)(2,1)S(1)}, bf16[1,64,512]{2,1,0:T(8,128)(2,1)S(1)}, u32[]{:S(2)}, u32[]{:S(2)}) collective-permute-start(bf16[1,64,512]{2,1,0:T(8,128)(2,1)S(1)} %get-tuple-element.90), channel_id=1, source_target_pairs={{0,1},{1,0},{2,3},{3,2},{4,5},{5,4},{6,7},{7,6},{8,9},{9,8},{10,11... | collective-permute-start | bytes 196616 | tf_op jit(solution)/shard_map/ppermute | solution.py:432
  20.5 8.3 %collective-permute-start.5 = (bf16[1,64,512]{2,1,0:T(8,128)(2,1)S(1)}, bf16[1,64,512]{2,1,0:T(8,128)(2,1)S(1)}, u32[]{:S(2)}, u32[]{:S(2)}) collective-permute-start(bf16[1,64,512]{2,1,0:T(8,128)(2,1)S(1)} %get-tuple-element.89), channel_id=1, source_target_pairs={{1,2},{3,4},{5,6},{7,8},{9,10},{11,12},{13,14},{2,1},{4,3},{6,5},{... | collective-permute-start | bytes 196616 | tf_op jit(solution)/shard_map/ppermute | solution.py:507
  21.2 8.7 %collective-permute-start.7 = (f32[64,128]{1,0:T(8,128)S(1)}, f32[64,128]{1,0:T(8,128)S(1)}, u32[]{:S(2)}, u32[]{:S(2)}) collective-permute-start(f32[64,128]{1,0:T(8,128)S(1)} %add.79), channel_id=1, source_target_pairs={{0,2},{2,0},{4,6},{6,4},{8,10},{10,8},{12,14},{14,12},{1,3},{3,1},... | collective-permute-start | bytes 98312 | tf_op jit(solution)/shard_map/ppermute | solution.py:510
  30.0 52.9 %collective-permute-start.19 = (bf16[16,512,256]{2,1,0:T(8,128)(2,1)S(1)}, bf16[16,512,256]{2,1,0:T(8,128)(2,1)S(1)}, u32[]{:S(2)}, u32[]{:S(2)}) collective-permute-start(bf16[16,512,256]{2,1,0:T(8,128)(2,1)S(1)} %copy-done.2), channel_id=1, source_target_pairs={{0,1},{1,0},{2,3},{3,2},{4,5},{5,4},{6,7},{7,6},{8,9},{9,8},{10,11... | collective-permute-start | bytes 12582920 | tf_op jit(solution)/shard_map/ppermute | solution.py:432
  30.3 4.0 %collective-permute-start.11 = (f32[64,128]{1,0:T(8,128)S(1)}, f32[64,128]{1,0:T(8,128)S(1)}, u32[]{:S(2)}, u32[]{:S(2)}) collective-permute-start(f32[64,128]{1,0:T(8,128)S(1)} %add.82), channel_id=1, source_target_pairs={{0,4},{2,6},{4,0},{6,2},{8,12},{10,14},{12,8},{14,10},{1,5},{3,7},... | collective-permute-start | bytes 98312 | tf_op jit(solution)/shard_map/ppermute | solution.py:530
  32.4 11.2 %collective-permute-start.9 = (bf16[2,128,512]{2,1,0:T(8,128)(2,1)S(1)}, bf16[2,128,512]{2,1,0:T(8,128)(2,1)S(1)}, u32[]{:S(2)}, u32[]{:S(2)}) collective-permute-start(bf16[2,128,512]{2,1,0:T(8,128)(2,1)S(1)} %shard_map.125.token.own), channel_id=1, source_target_pairs={{0,1},{1,0},{2,3},{3,2},{4,5},{5,4},{6,7},{7,6},{8,9},{9,8},{10,11... | collective-permute-start | bytes 786440 | tf_op jit(solution)/shard_map/ppermute | solution.py:432
  32.4 11.2 %collective-permute-start.10 = (bf16[2,128,512]{2,1,0:T(8,128)(2,1)S(1)}, bf16[2,128,512]{2,1,0:T(8,128)(2,1)S(1)}, u32[]{:S(2)}, u32[]{:S(2)}) collective-permute-start(bf16[2,128,512]{2,1,0:T(8,128)(2,1)S(1)} %shard_map.125.token.own), channel_id=1, source_target_pairs={{1,2},{3,4},{5,6},{7,8},{9,10},{11,12},{13,14},{2,1},{4,3},{6,5},{... | collective-permute-start | bytes 786440 | tf_op jit(solution)/shard_map/ppermute | solution.py:527
  34.3 9.2 %collective-permute-start.12 = (f32[64,128]{1,0:T(8,128)S(1)}, f32[64,128]{1,0:T(8,128)S(1)}, u32[]{:S(2)}, u32[]{:S(2)}) collective-permute-start(f32[64,128]{1,0:T(8,128)S(1)} %add.83), channel_id=1, source_target_pairs={{0,8},{2,10},{4,12},{6,14},{8,0},{10,2},{12,4},{14,6},{1,9},{3,11}... | collective-permute-start | bytes 98312 | tf_op jit(solution)/shard_map/ppermute | solution.py:530
  43.6 12.9 %collective-permute-start.14 = (bf16[5,2,512,256]{3,2,1,0:T(8,128)(2,1)}, bf16[5,2,512,256]{3,2,1,0:T(8,128)(2,1)S(1)}, u32[]{:S(2)}, u32[]{:S(2)}) collective-permute-start(bf16[5,2,512,256]{3,2,1,0:T(8,128)(2,1)} %get-tuple-element.66), channel_id=1, source_target_pairs={{0,1},{1,0},{2,3},{3,2},{4,5},{5,4},{6,7},{7,6},{8,9},{9,8},{10,11... | collective-permute-start | bytes 7864328 | tf_op jit(solution)/shard_map/ppermute | solution.py:432
  45.4 11.1 %collective-permute-start.13 = (bf16[144,512]{1,0:T(8,128)(2,1)S(1)}, bf16[144,512]{1,0:T(8,128)(2,1)S(1)}, u32[]{:S(2)}, u32[]{:S(2)}) collective-permute-start(bf16[144,512]{1,0:T(8,128)(2,1)S(1)} %get-tuple-element.64), channel_id=1, source_target_pairs={{0,2},{1,3},{2,4},{3,5},{4,6},{5,7},{6,8},{7,9},{8,10},{9,11},{10,... | collective-permute-start | bytes 442376 | tf_op jit(solution)/shard_map/ppermute | solution.py:438
  49.0 7.5 %collective-permute-start.15 = (bf16[2,64,512]{2,1,0:T(8,128)(2,1)S(1)}, bf16[2,64,512]{2,1,0:T(8,128)(2,1)S(1)}, u32[]{:S(2)}, u32[]{:S(2)}) collective-permute-start(bf16[2,64,512]{2,1,0:T(8,128)(2,1)S(1)} %get-tuple-element.65.token.own), channel_id=1, source_target_pairs={{2,0},{3,1},{4,2},{5,3},{6,4},{7,5},{8,6},{9,7},{10,8},{11,9},{12,... | collective-permute-start | bytes 393224 | tf_op jit(solution)/shard_map/ppermute | solution.py:438
  57.5 7.3 %collective-permute-start.16 = (bf16[2,64,512]{2,1,0:T(8,128)(2,1)S(1)}, bf16[2,64,512]{2,1,0:T(8,128)(2,1)S(1)}, u32[]{:S(2)}, u32[]{:S(2)}) collective-permute-start(bf16[2,64,512]{2,1,0:T(8,128)(2,1)S(1)} %shard_map.129.token.own), channel_id=1, source_target_pairs={{0,4},{1,5},{2,6},{3,7},{4,8},{5,9},{6,10},{7,11},{8,12},{9,13},{1... | collective-permute-start | bytes 393224 | tf_op jit(solution)/shard_map/ppermute | solution.py:438
  61.1 7.0 %collective-permute-start.17 = (bf16[2,64,512]{2,1,0:T(8,128)(2,1)S(1)}, bf16[2,64,512]{2,1,0:T(8,128)(2,1)S(1)}, u32[]{:S(2)}, u32[]{:S(2)}) collective-permute-start(bf16[2,64,512]{2,1,0:T(8,128)(2,1)S(1)} %shard_map.129.token.own), channel_id=1, source_target_pairs={{4,0},{5,1},{6,2},{7,3},{8,4},{9,5},{10,6},{11,7},{12,8},{13,9},{1... | collective-permute-start | bytes 393224 | tf_op jit(solution)/shard_map/ppermute | solution.py:438
  69.2 8.0 %collective-permute-start.18 = (bf16[2,64,512]{2,1,0:T(8,128)(2,1)S(1)}, bf16[2,64,512]{2,1,0:T(8,128)(2,1)S(1)}, u32[]{:S(2)}, u32[]{:S(2)}) collective-permute-start(bf16[2,64,512]{2,1,0:T(8,128)(2,1)S(1)} %shard_map.131.token.own), channel_id=1, source_target_pairs={{0,8},{1,9},{2,10},{3,11},{4,12},{5,13},{6,14},{7,15},{8,0},{9,1},... | collective-permute-start | bytes 393224 | tf_op jit(solution)/shard_map/ppermute | solution.py:556
  78.3 7.7 %collective-permute-start.21 = (bf16[2,64,512]{2,1,0:T(8,128)(2,1)S(1)}, bf16[2,64,512]{2,1,0:T(8,128)(2,1)S(1)}, u32[]{:S(2)}, u32[]{:S(2)}) collective-permute-start(bf16[2,64,512]{2,1,0:T(8,128)(2,1)S(1)} %get-tuple-element.74.correction), channel_id=1, source_target_pairs={{0,1},{1,2},{2,3},{3,4},{4,5},{5,6},{6,7},{7,8},{8,9},{9,10},{10,1... | collective-permute-start | bytes 393224 | tf_op jit(solution)/shard_map/ppermute | solution.py:438
  79.6 6.5 %collective-permute-start.22 = (bf16[2,64,512]{2,1,0:T(8,128)(2,1)S(1)}, bf16[2,64,512]{2,1,0:T(8,128)(2,1)S(1)}, u32[]{:S(2)}, u32[]{:S(2)}) collective-permute-start(bf16[2,64,512]{2,1,0:T(8,128)(2,1)S(1)} %get-tuple-element.74.correction), channel_id=1, source_target_pairs={{0,2},{1,3},{2,4},{3,5},{4,6},{5,7},{6,8},{7,9},{8,10},{9,11},{10,... | collective-permute-start | bytes 393224 | tf_op jit(solution)/shard_map/ppermute | solution.py:438
  90.0 4.5 %collective-permute-start.25 = (f32[80,128]{1,0:T(8,128)S(1)}, f32[80,128]{1,0:T(8,128)S(1)}, u32[]{:S(2)}, u32[]{:S(2)}) collective-permute-start(f32[80,128]{1,0:T(8,128)S(1)} %add.85), channel_id=1, source_target_pairs={{0,4},{2,6},{4,0},{6,2},{8,12},{10,14},{12,8},{14,10},{1,5},{3,7},... | collective-permute-start | bytes 122888 | tf_op jit(solution)/shard_map/ppermute | solution.py:462
  92.5 4.9 %collective-permute-start.26 = (f32[80,128]{1,0:T(8,128)S(1)}, f32[80,128]{1,0:T(8,128)S(1)}, u32[]{:S(2)}, u32[]{:S(2)}) collective-permute-start(f32[80,128]{1,0:T(8,128)S(1)} %add.85), channel_id=1, source_target_pairs={{0,6},{2,4},{4,2},{6,0},{8,14},{10,12},{12,10},{14,8},{1,7},{3,5},... | collective-permute-start | bytes 122888 | tf_op jit(solution)/shard_map/ppermute | solution.py:462
  93.7 4.2 %collective-permute-start.24 = (f32[80,128]{1,0:T(8,128)S(1)}, f32[80,128]{1,0:T(8,128)S(1)}, u32[]{:S(2)}, u32[]{:S(2)}) collective-permute-start(f32[80,128]{1,0:T(8,128)S(1)} %add.85), channel_id=1, source_target_pairs={{0,2},{2,0},{4,6},{6,4},{8,10},{10,8},{12,14},{14,12},{1,3},{3,1},... | collective-permute-start | bytes 122888 | tf_op jit(solution)/shard_map/ppermute | solution.py:462
  97.9 5.0 %collective-permute-start.27 = (f32[80,128]{1,0:T(8,128)S(1)}, f32[80,128]{1,0:T(8,128)S(1)}, u32[]{:S(2)}, u32[]{:S(2)}) collective-permute-start(f32[80,128]{1,0:T(8,128)S(1)} %add_add_fusion), channel_id=1, source_target_pairs={{0,8},{2,10},{4,12},{6,14},{8,0},{10,2},{12,4},{14,6},{1,9},{3,11}... | collective-permute-start | bytes 122888 | tf_op jit(solution)/shard_map/ppermute | solution.py:462
  (10 other events, 36.4 us)

commit v11 on v10

--- a/solution.py
+++ b/solution.py
@@ -498,9 +498,13 @@
     theirs_0, extended = lax.optimization_barrier((theirs_0, extended))
     packed_0 = swapped(theirs_0)
     keep, send, moments = image_halves(place, table, extended, vectors, in_vmem(held_blocks))
+    send, moments, packed_0 = lax.optimization_barrier((send, moments, packed_0))
+    body = functools.partial(load_body, 0, 0)
+    matrices = load(body, place, keep, level_lower, level_upper, packed_0)
     received, moments = swapped(send), moments + swapped(moments)
     image = jnp.where(core == 0, jnp.concatenate([keep, received], 2), jnp.concatenate([received, keep], 2))
-    image, moments, theirs = lax.optimization_barrier((image, moments, theirs))
+    image, moments, theirs, matrices = lax.optimization_barrier((image, moments, theirs, matrices))
+    matrices = in_vmem(matrices)
     packed = swapped(theirs)
 
     inner_route, outer_route = pair_routes(1)
@@ -508,8 +512,6 @@
     inner = swapped(lax.dynamic_slice_in_dim(image, (own_count - 1) * (1 - core), 1))
     flips = [[(i, i ^ 2**bit) for i in range(slabs)] for bit in range((slabs - 1).bit_length())]
     received = lax.ppermute(moments, "slab", flips[0])
-    body = functools.partial(load_body, 0, 0)
-    matrices = in_vmem(load(body, place, keep, level_lower, level_upper, packed_0))
     vectors_1 = kernel_call(
         first_vectors_body,
         struct(image.shape),

time: 106 us -> 111 us (1.047)
  local copies, waits for them, and re-layouts: 0.2 us -> 6.44 us
  waiting for transfers between devices: 23.6 us -> 21.8 us
  Pallas kernels: 33.6 us -> 34.8 us
    unnamed x10 -> x20, local copies, waits for them, and re-layouts: 0.1 us -> 6.34 us
    ppermute x11, waiting for transfers between devices: 3.22 us -> 2.09 us  [swapped(): return lax.ppermute(operand, 'vec', SWAP)]
  transfers between devices with their start and end apart: 29 -> 29, of which waited for: 14 -> 12; matrix products, arithmetic and copies ran while one was open for 1% -> 0% of each run, Pallas kernels for 27% -> 29%
where the time goes in v11:
time: 111 us
  starting transfers between devices  43 us (39%)
  Pallas kernels  34.8 us (31%)
  waiting for transfers between devices  21.8 us (20%)
  local copies, waits for them, and re-layouts  6.44 us (6%)
  blocking collectives  2.37 us (2%)
  between operations  1.76 us (2%)
    ppermute x8, starting transfers between devices, along(): return lax.ppermute(operand, axis, route)  20.9 us
    ppermute x4, waiting for transfers between devices, slab_total(): lax.ppermute(part, 'slab', route)  7.62 us
    ppermute x8, waiting for transfers between devices, along(): return lax.ppermute(operand, axis, route)  7.48 us
    pallas_call x4, Pallas kernels, load(): pl.pallas_call(body, out_shape=pltpu.VMEM(shape, bf16), in_specs=[SMEM] +...  7.47 us
    unnamed x20, local copies, waits for them, and re-layouts  6.34 us
    ppermute x2, starting transfers between devices, on_device(): received = lax.ppermute(moments, 'slab', flip)  5.94 us
    ppermute x4, starting transfers between devices, slab_total(): lax.ppermute(part, 'slab', route)  5.72 us
    pallas_call x1, Pallas kernels, prepare(): pl.pallas_call(prepare_body, out_shape=[pltpu.VMEM(blocks.shape, bf16), p...  4.97 us
  transfers between devices with their start and end apart: 29, of which 12 were waited for; matrix products, arithmetic and copies ran while one was open for 0% of the time, Pallas kernels for 29%

profile of v11, /device:TPU:0, one launch (start us, length us, event | category | flops | bytes accessed | tf_op | source)
XLA Modules:
  0.0 110.6 jit_solution(16046435990745299295)
XLA Ops:
  1.9 5.5 %collective-permute-start = (bf16[4,64,256]{2,1,0:T(8,128)(2,1)}, bf16[4,64,256]{2,1,0:T(8,128)(2,1)S(1)}, u32[]{:S(2)}, u32[]{:S(2)}) collective-permute-start(bf16[4,64,256]{2,1,0:T(8,128)(2,1)} %vectors.1), channel_id=1, source_target_pairs={{0,2},{2,4},{4,6},{6,8},{8,10},{10,12},{12,14},{1,3},{3,5},{5,7},{... | collective-permute-start | bytes 393224 | tf_op jit(solution)/shard_map/ppermute | solution.py:438
  7.6 5.0 %shard_map.121 = (bf16[16,512,256]{2,1,0:T(8,128)(2,1)S(1)}, bf16[2,2,512,256]{3,2,1,0:T(8,128)(2,1)}, bf16[4,2,512,256]{3,2,1,0:T(8,128)(2,1)}) custom-call(s32[6]{0:T(128)S(1)} %stack.24.place, bf16[6,4,512,256]{3,2,1,0:T(8,128)(2,1)} %lower.11, bf16[6,4,512,256]{3,2,1,0:T(8,128)(2,1)} %upper.11, bf16[16,512,256]{2,1,0:T(8,128)(2,1)} %source.1), custom_call_target="tpu_custom_call" | custom-call | bytes 10485760 | tf_op jit(solution)/shard_map/pallas_call | solution.py:92
  12.6 1.9 %copy-done = bf16[16,512,256]{2,1,0:T(8,128)(2,1)} copy-done((bf16[16,512,256]{2,1,0:T(8,128)(2,1)}, bf16[16,512,256]{2,1,0:T(8,128)(2,1)S(1)}, u32[]{:S(2)}) %copy-start) | copy-done | bytes 4194328
  14.6 2.4 %all_gather.3.extended = bf16[12,64,512]{2,1,0:T(8,128)(2,1)S(1)} all-gather(bf16[12,64,256]{2,1,0:T(8,128)(2,1)S(1)} %pad_maximum_fusion), channel_id=1, replica_groups=mesh['groups'=2,'slab'=8,'vec'=2] {'vec'}, dimensions={2}, use_global_device_ids=true | all-gather | bytes 1179648 | tf_op jit(solution)/shard_map/all_gather | solution.py:497
  17.3 2.2 %copy-done.1 = bf16[16,512,256]{2,1,0:T(8,128)(2,1)S(1)} copy-done((bf16[16,512,256]{2,1,0:T(8,128)(2,1)S(1)}, bf16[16,512,256]{2,1,0:T(8,128)(2,1)}, u32[]{:S(2)}) %copy-start.1) | copy-done | bytes 4194328
  19.5 2.2 %shard_map.122 = (bf16[2,64,256]{2,1,0:T(8,128)(2,1)S(1)}, bf16[2,64,256]{2,1,0:T(8,128)(2,1)S(1)}, f32[64,128]{1,0:T(8,128)S(1)}) custom-call(s32[6]{0:T(128)S(1)} %stack.24.place, s32[4,14]{1,0:T(4,128)S(1)} %get-tuple-element.96.table, bf16[12,64,512]{2,1,0:T(8,128)(2,1)S(1)} %all_gather.3.extended, bf16[4,64,256]{2,1,0:T(8,128)(2,1)S(1)} %copy-done.4, ...), custom_call_target="tpu_custom_call" | custom-call | flops 469762048 | bytes 4194304 | tf_op jit(solution)/shard_map/pallas_call | solution.py:238
  27.7 4.4 %collective-permute-start.7 = (f32[64,128]{1,0:T(8,128)S(1)}, f32[64,128]{1,0:T(8,128)S(1)}, u32[]{:S(2)}, u32[]{:S(2)}) collective-permute-start(f32[64,128]{1,0:T(8,128)S(1)} %add.79), channel_id=1, source_target_pairs={{0,2},{2,0},{4,6},{6,4},{8,10},{10,8},{12,14},{14,12},{1,3},{3,1},... | collective-permute-start | bytes 98312 | tf_op jit(solution)/shard_map/ppermute | solution.py:514
  35.2 2.3 %collective-permute-start.11 = (f32[64,128]{1,0:T(8,128)S(1)}, f32[64,128]{1,0:T(8,128)S(1)}, u32[]{:S(2)}, u32[]{:S(2)}) collective-permute-start(f32[64,128]{1,0:T(8,128)S(1)} %add.82), channel_id=1, source_target_pairs={{0,4},{2,6},{4,0},{6,2},{8,12},{10,14},{12,8},{14,10},{1,5},{3,7},... | collective-permute-start | bytes 98312 | tf_op jit(solution)/shard_map/ppermute | solution.py:532
  39.5 3.6 %collective-permute-start.12 = (f32[64,128]{1,0:T(8,128)S(1)}, f32[64,128]{1,0:T(8,128)S(1)}, u32[]{:S(2)}, u32[]{:S(2)}) collective-permute-start(f32[64,128]{1,0:T(8,128)S(1)} %add.83), channel_id=1, source_target_pairs={{0,8},{2,10},{4,12},{6,14},{8,0},{10,2},{12,4},{14,6},{1,9},{3,11}... | collective-permute-start | bytes 98312 | tf_op jit(solution)/shard_map/ppermute | solution.py:532
  43.1 4.1 %shard_map.126 = (bf16[2,2,2,512,256]{4,3,2,1,0:T(8,128)(2,1)S(1)}, bf16[5,2,512,256]{3,2,1,0:T(8,128)(2,1)}) custom-call(s32[6]{0:T(128)S(1)} %stack.24.place, bf16[2,128,512]{2,1,0:T(8,128)(2,1)S(1)} %shard_map.125.token.own, bf16[6,4,512,256]{3,2,1,0:T(8,128)(2,1)} %lower.11, bf16[6,4,512,256]{3,2,1,0:T(8,128)(2,1)} %upper.11, ...), custom_call_target="tpu_custom_call" | custom-call | bytes 7340032 | tf_op jit(solution)/shard_map/pallas_call | solution.py:129
  50.3 3.5 %collective-permute-start.13 = (bf16[144,512]{1,0:T(8,128)(2,1)S(1)}, bf16[144,512]{1,0:T(8,128)(2,1)S(1)}, u32[]{:S(2)}, u32[]{:S(2)}) collective-permute-start(bf16[144,512]{1,0:T(8,128)(2,1)S(1)} %get-tuple-element.72), channel_id=1, source_target_pairs={{0,2},{1,3},{2,4},{3,5},{4,6},{5,7},{6,8},{7,9},{8,10},{9,11},{10,... | collective-permute-start | bytes 442376 | tf_op jit(solution)/shard_map/ppermute | solution.py:438
  55.1 2.1 %shard_map.128.weights = bf16[2,2,2,512,256]{4,3,2,1,0:T(8,128)(2,1)S(1)} custom-call(s32[6]{0:T(128)S(1)} %stack.24.place, bf16[2,64,512]{2,1,0:T(8,128)(2,1)S(1)} %get-tuple-element.73.token.own, bf16[6,4,512,256]{3,2,1,0:T(8,128)(2,1)} %lower.11, bf16[6,4,512,256]{3,2,1,0:T(8,128)(2,1)} %upper.11, bf16[4,2,512,256]{3,2,1,0:T(8,128)(2,1)} %collective-permute-done.8.packed), custom_call_target="tpu_custom_call" | custom-call | bytes 4194304 | tf_op jit(solution)/shard_map/pallas_call | solution.py:187
  57.2 4.1 %collective-permute-done.15.above = bf16[2,64,512]{2,1,0:T(8,128)(2,1)S(1)} collective-permute-done((bf16[2,64,512]{2,1,0:T(8,128)(2,1)S(1)}, bf16[2,64,512]{2,1,0:T(8,128)(2,1)S(1)}, u32[]{:S(2)}, u32[]{:S(2)}) %collective-permute-start.15) | collective-permute-done | bytes 131104 | tf_op jit(solution)/shard_map/ppermute | solution.py:438
  62.4 3.6 %collective-permute-start.16 = (bf16[2,64,512]{2,1,0:T(8,128)(2,1)S(1)}, bf16[2,64,512]{2,1,0:T(8,128)(2,1)S(1)}, u32[]{:S(2)}, u32[]{:S(2)}) collective-permute-start(bf16[2,64,512]{2,1,0:T(8,128)(2,1)S(1)} %shard_map.129.token.own), channel_id=1, source_target_pairs={{0,4},{1,5},{2,6},{3,7},{4,8},{5,9},{6,10},{7,11},{8,12},{9,13},{1... | collective-permute-start | bytes 393224 | tf_op jit(solution)/shard_map/ppermute | solution.py:438
  67.9 1.8 %shard_map.130.weights = bf16[2,2,2,512,256]{4,3,2,1,0:T(8,128)(2,1)S(1)} custom-call(s32[6]{0:T(128)S(1)} %stack.24.place, bf16[2,64,512]{2,1,0:T(8,128)(2,1)S(1)} %shard_map.129.token.own, bf16[6,4,512,256]{3,2,1,0:T(8,128)(2,1)} %lower.11, bf16[6,4,512,256]{3,2,1,0:T(8,128)(2,1)} %upper.11, bf16[5,2,512,256]{3,2,1,0:T(8,128)(2,1)S(1)} %collective-permute-done.14.packed), custom_call_target="tpu_custom_call" | custom-call | bytes 4194304 | tf_op jit(solution)/shard_map/pallas_call | solution.py:187
  69.7 3.3 %collective-permute-done.17.above = bf16[2,64,512]{2,1,0:T(8,128)(2,1)S(1)} collective-permute-done((bf16[2,64,512]{2,1,0:T(8,128)(2,1)S(1)}, bf16[2,64,512]{2,1,0:T(8,128)(2,1)S(1)}, u32[]{:S(2)}, u32[]{:S(2)}) %collective-permute-start.17) | collective-permute-done | bytes 131104 | tf_op jit(solution)/shard_map/ppermute | solution.py:438
  75.8 2.7 %shard_map.132.blocks = bf16[16,512,256]{2,1,0:T(8,128)(2,1)S(1)} custom-call(s32[6]{0:T(128)S(1)} %stack.24.place, bf16[2,64,512]{2,1,0:T(8,128)(2,1)S(1)} %shard_map.131.token.own, bf16[16,512,256]{2,1,0:T(8,128)(2,1)} %source.1), custom_call_target="tpu_custom_call" | custom-call | bytes 4194304 | tf_op jit(solution)/shard_map/pallas_call | solution.py:203
  78.5 1.8 %shard_map.133.weights = bf16[2,2,2,512,256]{4,3,2,1,0:T(8,128)(2,1)S(1)} custom-call(s32[6]{0:T(128)S(1)} %stack.24.place, bf16[2,64,512]{2,1,0:T(8,128)(2,1)S(1)} %shard_map.131.token.own, bf16[6,4,512,256]{3,2,1,0:T(8,128)(2,1)} %lower.11, bf16[6,4,512,256]{3,2,1,0:T(8,128)(2,1)} %upper.11, bf16[5,2,512,256]{3,2,1,0:T(8,128)(2,1)S(1)} %collective-permute-done.14.packed, ...), custom_call_target="tpu_custom_call" | custom-call | bytes 4194304 | tf_op jit(solution)/shard_map/pallas_call | solution.py:187
  80.3 1.9 %collective-permute-done.18.other = bf16[2,64,512]{2,1,0:T(8,128)(2,1)S(1)} collective-permute-done((bf16[2,64,512]{2,1,0:T(8,128)(2,1)S(1)}, bf16[2,64,512]{2,1,0:T(8,128)(2,1)S(1)}, u32[]{:S(2)}, u32[]{:S(2)}) %collective-permute-start.18) | collective-permute-done | bytes 131104 | tf_op jit(solution)/shard_map/ppermute | solution.py:558
  84.6 3.2 %collective-permute-start.22 = (bf16[2,64,512]{2,1,0:T(8,128)(2,1)S(1)}, bf16[2,64,512]{2,1,0:T(8,128)(2,1)S(1)}, u32[]{:S(2)}, u32[]{:S(2)}) collective-permute-start(bf16[2,64,512]{2,1,0:T(8,128)(2,1)S(1)} %get-tuple-element.82.correction), channel_id=1, source_target_pairs={{0,2},{1,3},{2,4},{3,5},{4,6},{5,7},{6,8},{7,9},{8,10},{9,11},{10,... | collective-permute-start | bytes 393224 | tf_op jit(solution)/shard_map/ppermute | solution.py:438
  87.8 3.4 %shard_map.135 = (f32[6,64,512]{2,1,0:T(8,128)S(1)}, f32[160,128]{1,0:T(8,128)S(1)}, f32[8,128]{1,0:T(8,128)S(1)}) custom-call(s32[6]{0:T(128)S(1)} %stack.24.place, s32[8,14]{1,0:T(8,128)S(1)} %add_add_fusion.1.table, f32[8]{0:T(128)S(1)} %copy-done.5, s32[1]{0:T(128)S(6)} %copy.13.index, bf16[12,64,512]{2,1,0:T(8,128)(2,1)S(1)} %all_gather.3.extended, ...), custom_call_target="tpu_custom_call" | custom-call | flops 469762048 | tf_op jit(solution)/shard_map/pallas_call | solution.py:599
  94.4 2.9 %collective-permute-start.25 = (f32[80,128]{1,0:T(8,128)S(1)}, f32[80,128]{1,0:T(8,128)S(1)}, u32[]{:S(2)}, u32[]{:S(2)}) collective-permute-start(f32[80,128]{1,0:T(8,128)S(1)} %add.85), channel_id=1, source_target_pairs={{0,4},{2,6},{4,0},{6,2},{8,12},{10,14},{12,8},{14,10},{1,5},{3,7},... | collective-permute-start | bytes 122888 | tf_op jit(solution)/shard_map/ppermute | solution.py:462
  99.3 2.9 %collective-permute-done.26 = f32[80,128]{1,0:T(8,128)S(1)} collective-permute-done((f32[80,128]{1,0:T(8,128)S(1)}, f32[80,128]{1,0:T(8,128)S(1)}, u32[]{:S(2)}, u32[]{:S(2)}) %collective-permute-start.26) | collective-permute-done | bytes 40992 | tf_op jit(solution)/shard_map/ppermute | solution.py:462
  104.2 3.6 %collective-permute-done.27 = f32[80,128]{1,0:T(8,128)S(1)} collective-permute-done((f32[80,128]{1,0:T(8,128)S(1)}, f32[80,128]{1,0:T(8,128)S(1)}, u32[]{:S(2)}, u32[]{:S(2)}) %collective-permute-start.27) | collective-permute-done | bytes 40992 | tf_op jit(solution)/shard_map/ppermute | solution.py:462
  (91 shorter events, 34.4 us)
Async XLA Ops:
  0.6 13.9 %collective-permute-start.1 = (bf16[4,64,256]{2,1,0:T(8,128)(2,1)}, bf16[4,64,256]{2,1,0:T(8,128)(2,1)S(1)}, u32[]{:S(2)}, u32[]{:S(2)}) collective-permute-start(bf16[4,64,256]{2,1,0:T(8,128)(2,1)} %vectors.1), channel_id=1, source_target_pairs={{2,0},{4,2},{6,4},{8,6},{10,8},{12,10},{14,12},{3,1},{5,3},{7,5},{... | collective-permute-start | bytes 393224 | tf_op jit(solution)/shard_map/ppermute | solution.py:438
  1.9 12.6 %collective-permute-start = (bf16[4,64,256]{2,1,0:T(8,128)(2,1)}, bf16[4,64,256]{2,1,0:T(8,128)(2,1)S(1)}, u32[]{:S(2)}, u32[]{:S(2)}) collective-permute-start(bf16[4,64,256]{2,1,0:T(8,128)(2,1)} %vectors.1), channel_id=1, source_target_pairs={{0,2},{2,4},{4,6},{6,8},{8,10},{10,12},{12,14},{1,3},{3,5},{5,7},{... | collective-permute-start | bytes 393224 | tf_op jit(solution)/shard_map/ppermute | solution.py:438
  17.0 4.7 %collective-permute-start.2 = (bf16[2,2,512,256]{3,2,1,0:T(8,128)(2,1)}, bf16[2,2,512,256]{3,2,1,0:T(8,128)(2,1)S(1)}, u32[]{:S(2)}, u32[]{:S(2)}) collective-permute-start(bf16[2,2,512,256]{3,2,1,0:T(8,128)(2,1)} %get-tuple-element.55), channel_id=1, source_target_pairs={{0,1},{1,0},{2,3},{3,2},{4,5},{5,4},{6,7},{7,6},{8,9},{9,8},{10,11... | collective-permute-start | bytes 3145736 | tf_op jit(solution)/shard_map/ppermute | solution.py:432
  26.3 8.3 %collective-permute-start.8 = (bf16[4,2,512,256]{3,2,1,0:T(8,128)(2,1)}, bf16[4,2,512,256]{3,2,1,0:T(8,128)(2,1)}, u32[]{:S(2)}, u32[]{:S(2)}) collective-permute-start(bf16[4,2,512,256]{3,2,1,0:T(8,128)(2,1)} %get-tuple-element.63), channel_id=1, source_target_pairs={{0,1},{1,0},{2,3},{3,2},{4,5},{5,4},{6,7},{7,6},{8,9},{9,8},{10,11... | collective-permute-start | bytes 6291464 | tf_op jit(solution)/shard_map/ppermute | solution.py:432
  26.7 6.4 %collective-permute-start.5 = (bf16[1,64,512]{2,1,0:T(8,128)(2,1)S(1)}, bf16[1,64,512]{2,1,0:T(8,128)(2,1)S(1)}, u32[]{:S(2)}, u32[]{:S(2)}) collective-permute-start(bf16[1,64,512]{2,1,0:T(8,128)(2,1)S(1)} %get-tuple-element.98), channel_id=1, source_target_pairs={{0,1},{1,0},{2,3},{3,2},{4,5},{5,4},{6,7},{7,6},{8,9},{9,8},{10,11... | collective-permute-start | bytes 196616 | tf_op jit(solution)/shard_map/ppermute | solution.py:432
  26.9 6.2 %collective-permute-start.6 = (bf16[1,64,512]{2,1,0:T(8,128)(2,1)S(1)}, bf16[1,64,512]{2,1,0:T(8,128)(2,1)S(1)}, u32[]{:S(2)}, u32[]{:S(2)}) collective-permute-start(bf16[1,64,512]{2,1,0:T(8,128)(2,1)S(1)} %get-tuple-element.97), channel_id=1, source_target_pairs={{1,2},{3,4},{5,6},{7,8},{9,10},{11,12},{13,14},{2,1},{4,3},{6,5},{... | collective-permute-start | bytes 196616 | tf_op jit(solution)/shard_map/ppermute | solution.py:511
  27.7 6.9 %collective-permute-start.7 = (f32[64,128]{1,0:T(8,128)S(1)}, f32[64,128]{1,0:T(8,128)S(1)}, u32[]{:S(2)}, u32[]{:S(2)}) collective-permute-start(f32[64,128]{1,0:T(8,128)S(1)} %add.79), channel_id=1, source_target_pairs={{0,2},{2,0},{4,6},{6,4},{8,10},{10,8},{12,14},{14,12},{1,3},{3,1},... | collective-permute-start | bytes 98312 | tf_op jit(solution)/shard_map/ppermute | solution.py:514
  34.6 53.2 %collective-permute-start.19 = (bf16[16,512,256]{2,1,0:T(8,128)(2,1)S(1)}, bf16[16,512,256]{2,1,0:T(8,128)(2,1)S(1)}, u32[]{:S(2)}, u32[]{:S(2)}) collective-permute-start(bf16[16,512,256]{2,1,0:T(8,128)(2,1)S(1)} %copy-done.6), channel_id=1, source_target_pairs={{0,1},{1,0},{2,3},{3,2},{4,5},{5,4},{6,7},{7,6},{8,9},{9,8},{10,11... | collective-permute-start | bytes 12582920 | tf_op jit(solution)/shard_map/ppermute | solution.py:432
  35.2 4.3 %collective-permute-start.11 = (f32[64,128]{1,0:T(8,128)S(1)}, f32[64,128]{1,0:T(8,128)S(1)}, u32[]{:S(2)}, u32[]{:S(2)}) collective-permute-start(f32[64,128]{1,0:T(8,128)S(1)} %add.82), channel_id=1, source_target_pairs={{0,4},{2,6},{4,0},{6,2},{8,12},{10,14},{12,8},{14,10},{1,5},{3,7},... | collective-permute-start | bytes 98312 | tf_op jit(solution)/shard_map/ppermute | solution.py:532
  37.5 10.9 %collective-permute-start.9 = (bf16[2,128,512]{2,1,0:T(8,128)(2,1)S(1)}, bf16[2,128,512]{2,1,0:T(8,128)(2,1)S(1)}, u32[]{:S(2)}, u32[]{:S(2)}) collective-permute-start(bf16[2,128,512]{2,1,0:T(8,128)(2,1)S(1)} %shard_map.125.token.own), channel_id=1, source_target_pairs={{0,1},{1,0},{2,3},{3,2},{4,5},{5,4},{6,7},{7,6},{8,9},{9,8},{10,11... | collective-permute-start | bytes 786440 | tf_op jit(solution)/shard_map/ppermute | solution.py:432
  37.7 10.7 %collective-permute-start.10 = (bf16[2,128,512]{2,1,0:T(8,128)(2,1)S(1)}, bf16[2,128,512]{2,1,0:T(8,128)(2,1)S(1)}, u32[]{:S(2)}, u32[]{:S(2)}) collective-permute-start(bf16[2,128,512]{2,1,0:T(8,128)(2,1)S(1)} %shard_map.125.token.own), channel_id=1, source_target_pairs={{1,2},{3,4},{5,6},{7,8},{9,10},{11,12},{13,14},{2,1},{4,3},{6,5},{... | collective-permute-start | bytes 786440 | tf_op jit(solution)/shard_map/ppermute | solution.py:529
  39.5 8.9 %collective-permute-start.12 = (f32[64,128]{1,0:T(8,128)S(1)}, f32[64,128]{1,0:T(8,128)S(1)}, u32[]{:S(2)}, u32[]{:S(2)}) collective-permute-start(f32[64,128]{1,0:T(8,128)S(1)} %add.83), channel_id=1, source_target_pairs={{0,8},{2,10},{4,12},{6,14},{8,0},{10,2},{12,4},{14,6},{1,9},{3,11}... | collective-permute-start | bytes 98312 | tf_op jit(solution)/shard_map/ppermute | solution.py:532
  48.4 12.9 %collective-permute-start.14 = (bf16[5,2,512,256]{3,2,1,0:T(8,128)(2,1)}, bf16[5,2,512,256]{3,2,1,0:T(8,128)(2,1)S(1)}, u32[]{:S(2)}, u32[]{:S(2)}) collective-permute-start(bf16[5,2,512,256]{3,2,1,0:T(8,128)(2,1)} %get-tuple-element.74), channel_id=1, source_target_pairs={{0,1},{1,0},{2,3},{3,2},{4,5},{5,4},{6,7},{7,6},{8,9},{9,8},{10,11... | collective-permute-start | bytes 7864328 | tf_op jit(solution)/shard_map/ppermute | solution.py:432
  50.3 11.1 %collective-permute-start.13 = (bf16[144,512]{1,0:T(8,128)(2,1)S(1)}, bf16[144,512]{1,0:T(8,128)(2,1)S(1)}, u32[]{:S(2)}, u32[]{:S(2)}) collective-permute-start(bf16[144,512]{1,0:T(8,128)(2,1)S(1)} %get-tuple-element.72), channel_id=1, source_target_pairs={{0,2},{1,3},{2,4},{3,5},{4,6},{5,7},{6,8},{7,9},{8,10},{9,11},{10,... | collective-permute-start | bytes 442376 | tf_op jit(solution)/shard_map/ppermute | solution.py:438
  53.8 7.5 %collective-permute-start.15 = (bf16[2,64,512]{2,1,0:T(8,128)(2,1)S(1)}, bf16[2,64,512]{2,1,0:T(8,128)(2,1)S(1)}, u32[]{:S(2)}, u32[]{:S(2)}) collective-permute-start(bf16[2,64,512]{2,1,0:T(8,128)(2,1)S(1)} %get-tuple-element.73.token.own), channel_id=1, source_target_pairs={{2,0},{3,1},{4,2},{5,3},{6,4},{7,5},{8,6},{9,7},{10,8},{11,9},{12,... | collective-permute-start | bytes 393224 | tf_op jit(solution)/shard_map/ppermute | solution.py:438
  62.4 7.3 %collective-permute-start.16 = (bf16[2,64,512]{2,1,0:T(8,128)(2,1)S(1)}, bf16[2,64,512]{2,1,0:T(8,128)(2,1)S(1)}, u32[]{:S(2)}, u32[]{:S(2)}) collective-permute-start(bf16[2,64,512]{2,1,0:T(8,128)(2,1)S(1)} %shard_map.129.token.own), channel_id=1, source_target_pairs={{0,4},{1,5},{2,6},{3,7},{4,8},{5,9},{6,10},{7,11},{8,12},{9,13},{1... | collective-permute-start | bytes 393224 | tf_op jit(solution)/shard_map/ppermute | solution.py:438
  66.0 7.1 %collective-permute-start.17 = (bf16[2,64,512]{2,1,0:T(8,128)(2,1)S(1)}, bf16[2,64,512]{2,1,0:T(8,128)(2,1)S(1)}, u32[]{:S(2)}, u32[]{:S(2)}) collective-permute-start(bf16[2,64,512]{2,1,0:T(8,128)(2,1)S(1)} %shard_map.129.token.own), channel_id=1, source_target_pairs={{4,0},{5,1},{6,2},{7,3},{8,4},{9,5},{10,6},{11,7},{12,8},{13,9},{1... | collective-permute-start | bytes 393224 | tf_op jit(solution)/shard_map/ppermute | solution.py:438
  74.1 8.1 %collective-permute-start.18 = (bf16[2,64,512]{2,1,0:T(8,128)(2,1)S(1)}, bf16[2,64,512]{2,1,0:T(8,128)(2,1)S(1)}, u32[]{:S(2)}, u32[]{:S(2)}) collective-permute-start(bf16[2,64,512]{2,1,0:T(8,128)(2,1)S(1)} %shard_map.131.token.own), channel_id=1, source_target_pairs={{0,8},{1,9},{2,10},{3,11},{4,12},{5,13},{6,14},{7,15},{8,0},{9,1},... | collective-permute-start | bytes 393224 | tf_op jit(solution)/shard_map/ppermute | solution.py:558
  83.3 8.0 %collective-permute-start.21 = (bf16[2,64,512]{2,1,0:T(8,128)(2,1)S(1)}, bf16[2,64,512]{2,1,0:T(8,128)(2,1)S(1)}, u32[]{:S(2)}, u32[]{:S(2)}) collective-permute-start(bf16[2,64,512]{2,1,0:T(8,128)(2,1)S(1)} %get-tuple-element.82.correction), channel_id=1, source_target_pairs={{0,1},{1,2},{2,3},{3,4},{4,5},{5,6},{6,7},{7,8},{8,9},{9,10},{10,1... | collective-permute-start | bytes 393224 | tf_op jit(solution)/shard_map/ppermute | solution.py:438
  84.6 6.7 %collective-permute-start.22 = (bf16[2,64,512]{2,1,0:T(8,128)(2,1)S(1)}, bf16[2,64,512]{2,1,0:T(8,128)(2,1)S(1)}, u32[]{:S(2)}, u32[]{:S(2)}) collective-permute-start(bf16[2,64,512]{2,1,0:T(8,128)(2,1)S(1)} %get-tuple-element.82.correction), channel_id=1, source_target_pairs={{0,2},{1,3},{2,4},{3,5},{4,6},{5,7},{6,8},{7,9},{8,10},{9,11},{10,... | collective-permute-start | bytes 393224 | tf_op jit(solution)/shard_map/ppermute | solution.py:438
  94.4 4.8 %collective-permute-start.25 = (f32[80,128]{1,0:T(8,128)S(1)}, f32[80,128]{1,0:T(8,128)S(1)}, u32[]{:S(2)}, u32[]{:S(2)}) collective-permute-start(f32[80,128]{1,0:T(8,128)S(1)} %add.85), channel_id=1, source_target_pairs={{0,4},{2,6},{4,0},{6,2},{8,12},{10,14},{12,8},{14,10},{1,5},{3,7},... | collective-permute-start | bytes 122888 | tf_op jit(solution)/shard_map/ppermute | solution.py:462
  97.3 4.9 %collective-permute-start.26 = (f32[80,128]{1,0:T(8,128)S(1)}, f32[80,128]{1,0:T(8,128)S(1)}, u32[]{:S(2)}, u32[]{:S(2)}) collective-permute-start(f32[80,128]{1,0:T(8,128)S(1)} %add.85), channel_id=1, source_target_pairs={{0,6},{2,4},{4,2},{6,0},{8,14},{10,12},{12,10},{14,8},{1,7},{3,5},... | collective-permute-start | bytes 122888 | tf_op jit(solution)/shard_map/ppermute | solution.py:462
  98.8 4.0 %collective-permute-start.24 = (f32[80,128]{1,0:T(8,128)S(1)}, f32[80,128]{1,0:T(8,128)S(1)}, u32[]{:S(2)}, u32[]{:S(2)}) collective-permute-start(f32[80,128]{1,0:T(8,128)S(1)} %add.85), channel_id=1, source_target_pairs={{0,2},{2,0},{4,6},{6,4},{8,10},{10,8},{12,14},{14,12},{1,3},{3,1},... | collective-permute-start | bytes 122888 | tf_op jit(solution)/shard_map/ppermute | solution.py:462
  102.8 5.0 %collective-permute-start.27 = (f32[80,128]{1,0:T(8,128)S(1)}, f32[80,128]{1,0:T(8,128)S(1)}, u32[]{:S(2)}, u32[]{:S(2)}) collective-permute-start(f32[80,128]{1,0:T(8,128)S(1)} %add_add_fusion), channel_id=1, source_target_pairs={{0,8},{2,10},{4,12},{6,14},{8,0},{10,2},{12,4},{14,6},{1,9},{3,11}... | collective-permute-start | bytes 122888 | tf_op jit(solution)/shard_map/ppermute | solution.py:462
  (15 other events, 72.3 us)

commit v12 on v10

--- a/solution.py
+++ b/solution.py
@@ -500,7 +500,8 @@
     keep, send, moments = image_halves(place, table, extended, vectors, in_vmem(held_blocks))
     received, moments = swapped(send), moments + swapped(moments)
     image = jnp.where(core == 0, jnp.concatenate([keep, received], 2), jnp.concatenate([received, keep], 2))
-    image, moments, theirs = lax.optimization_barrier((image, moments, theirs))
+    image, moments = lax.optimization_barrier((image, moments))
+    theirs, packed_0 = lax.optimization_barrier((theirs, packed_0))
     packed = swapped(theirs)
 
     inner_route, outer_route = pair_routes(1)

time: 106 us -> 113 us (1.066)
  local copies, waits for them, and re-layouts: 0.2 us -> 6.57 us
  waiting for transfers between devices: 23.6 us -> 26.3 us
  starting transfers between devices: 43.1 us -> 41.7 us
    unnamed x10 -> x20, local copies, waits for them, and re-layouts: 0.1 us -> 6.45 us
    ppermute x11, waiting for transfers between devices: 3.22 us -> 5.89 us  [swapped(): return lax.ppermute(operand, 'vec', SWAP)]
    ppermute x2, starting transfers between devices: 6.05 us -> 4.16 us  [on_device(): received = lax.ppermute(moments, 'slab', flip)]
  transfers between devices with their start and end apart: 29 -> 29, of which waited for: 14 -> 13; matrix products, arithmetic and copies ran while one was open for 1% -> 0% of each run, Pallas kernels for 27% -> 27%
where the time goes in v12:
time: 113 us; the launch traced here: 112 us
  starting transfers between devices  41.7 us (37%)
  Pallas kernels  33.4 us (30%)
  waiting for transfers between devices  26.3 us (23%)
  local copies, waits for them, and re-layouts  6.57 us (6%)
  blocking collectives  2.37 us (2%)
  between operations  1.76 us (2%)
    ppermute x8, starting transfers between devices, along(): return lax.ppermute(operand, axis, route)  21.9 us
    ppermute x8, waiting for transfers between devices, along(): return lax.ppermute(operand, axis, route)  7.71 us
    ppermute x4, waiting for transfers between devices, slab_total(): lax.ppermute(part, 'slab', route)  7.33 us
    pallas_call x4, Pallas kernels, load(): pl.pallas_call(body, out_shape=pltpu.VMEM(shape, bf16), in_specs=[SMEM] +...  7.16 us
    unnamed x20, local copies, waits for them, and re-layouts  6.45 us
    ppermute x4, starting transfers between devices, slab_total(): lax.ppermute(part, 'slab', route)  6.44 us
    ppermute x11, waiting for transfers between devices, swapped(): return lax.ppermute(operand, 'vec', SWAP)  5.89 us
    pallas_call x1, Pallas kernels, prepare(): pl.pallas_call(prepare_body, out_shape=[pltpu.VMEM(blocks.shape, bf16), p...  4.97 us
  transfers between devices with their start and end apart: 29, of which 13 were waited for; matrix products, arithmetic and copies ran while one was open for 0% of the time, Pallas kernels for 27%

profile of v12, /device:TPU:0, one launch (start us, length us, event | category | flops | bytes accessed | tf_op | source)
XLA Modules:
  0.0 112.4 jit_solution(1582202714204071872)
XLA Ops:
  1.9 5.5 %collective-permute-start = (bf16[4,64,256]{2,1,0:T(8,128)(2,1)}, bf16[4,64,256]{2,1,0:T(8,128)(2,1)S(1)}, u32[]{:S(2)}, u32[]{:S(2)}) collective-permute-start(bf16[4,64,256]{2,1,0:T(8,128)(2,1)} %vectors.1), channel_id=1, source_target_pairs={{0,2},{2,4},{4,6},{6,8},{8,10},{10,12},{12,14},{1,3},{3,5},{5,7},{... | collective-permute-start | bytes 393224 | tf_op jit(solution)/shard_map/ppermute | solution.py:438
  7.6 5.0 %shard_map.121 = (bf16[16,512,256]{2,1,0:T(8,128)(2,1)S(1)}, bf16[2,2,512,256]{3,2,1,0:T(8,128)(2,1)}, bf16[4,2,512,256]{3,2,1,0:T(8,128)(2,1)}) custom-call(s32[6]{0:T(128)S(1)} %stack.24.place, bf16[6,4,512,256]{3,2,1,0:T(8,128)(2,1)} %lower.11, bf16[6,4,512,256]{3,2,1,0:T(8,128)(2,1)} %upper.11, bf16[16,512,256]{2,1,0:T(8,128)(2,1)} %source.1), custom_call_target="tpu_custom_call" | custom-call | bytes 10485760 | tf_op jit(solution)/shard_map/pallas_call | solution.py:92
  12.6 2.0 %copy-done = bf16[16,512,256]{2,1,0:T(8,128)(2,1)} copy-done((bf16[16,512,256]{2,1,0:T(8,128)(2,1)}, bf16[16,512,256]{2,1,0:T(8,128)(2,1)S(1)}, u32[]{:S(2)}) %copy-start) | copy-done | bytes 4194328
  14.6 2.4 %all_gather.3.extended = bf16[12,64,512]{2,1,0:T(8,128)(2,1)S(1)} all-gather(bf16[12,64,256]{2,1,0:T(8,128)(2,1)S(1)} %pad_maximum_fusion), channel_id=1, replica_groups=mesh['groups'=2,'slab'=8,'vec'=2] {'vec'}, dimensions={2}, use_global_device_ids=true | all-gather | bytes 1179648 | tf_op jit(solution)/shard_map/all_gather | solution.py:497
  17.1 2.7 %collective-permute-done.6.packed = bf16[2,2,512,256]{3,2,1,0:T(8,128)(2,1)S(1)} collective-permute-done((bf16[2,2,512,256]{3,2,1,0:T(8,128)(2,1)}, bf16[2,2,512,256]{3,2,1,0:T(8,128)(2,1)S(1)}, u32[]{:S(2)}, u32[]{:S(2)}) %collective-permute-start.6) | collective-permute-done | bytes 1048608 | tf_op jit(solution)/shard_map/ppermute | solution.py:432
  21.1 2.2 %copy-done.1 = bf16[16,512,256]{2,1,0:T(8,128)(2,1)S(1)} copy-done((bf16[16,512,256]{2,1,0:T(8,128)(2,1)S(1)}, bf16[16,512,256]{2,1,0:T(8,128)(2,1)}, u32[]{:S(2)}) %copy-start.1) | copy-done | bytes 4194328
  23.3 2.2 %shard_map.122 = (bf16[2,64,256]{2,1,0:T(8,128)(2,1)S(1)}, bf16[2,64,256]{2,1,0:T(8,128)(2,1)S(1)}, f32[64,128]{1,0:T(8,128)S(1)}) custom-call(s32[6]{0:T(128)S(1)} %stack.24.place, s32[4,14]{1,0:T(4,128)S(1)} %get-tuple-element.90.table, bf16[12,64,512]{2,1,0:T(8,128)(2,1)S(1)} %all_gather.3.extended, bf16[4,64,256]{2,1,0:T(8,128)(2,1)S(1)} %copy-done.4, ...), custom_call_target="tpu_custom_call" | custom-call | flops 469762048 | bytes 4194304 | tf_op jit(solution)/shard_map/pallas_call | solution.py:238
  28.2 4.2 %collective-permute-start.7 = (f32[64,128]{1,0:T(8,128)S(1)}, f32[64,128]{1,0:T(8,128)S(1)}, u32[]{:S(2)}, u32[]{:S(2)}) collective-permute-start(f32[64,128]{1,0:T(8,128)S(1)} %add.79), channel_id=1, source_target_pairs={{0,2},{2,0},{4,6},{6,4},{8,10},{10,8},{12,14},{14,12},{1,3},{3,1},... | collective-permute-start | bytes 98312 | tf_op jit(solution)/shard_map/ppermute | solution.py:511
  42.0 2.6 %collective-permute-start.12 = (f32[64,128]{1,0:T(8,128)S(1)}, f32[64,128]{1,0:T(8,128)S(1)}, u32[]{:S(2)}, u32[]{:S(2)}) collective-permute-start(f32[64,128]{1,0:T(8,128)S(1)} %add.83), channel_id=1, source_target_pairs={{0,8},{2,10},{4,12},{6,14},{8,0},{10,2},{12,4},{14,6},{1,9},{3,11}... | collective-permute-start | bytes 98312 | tf_op jit(solution)/shard_map/ppermute | solution.py:531
  44.6 3.2 %shard_map.126 = (bf16[2,2,2,512,256]{4,3,2,1,0:T(8,128)(2,1)S(1)}, bf16[5,2,512,256]{3,2,1,0:T(8,128)(2,1)}) custom-call(s32[6]{0:T(128)S(1)} %stack.24.place, bf16[2,128,512]{2,1,0:T(8,128)(2,1)S(1)} %shard_map.125.token.own, bf16[6,4,512,256]{3,2,1,0:T(8,128)(2,1)} %lower.11, bf16[6,4,512,256]{3,2,1,0:T(8,128)(2,1)} %upper.11, ...), custom_call_target="tpu_custom_call" | custom-call | bytes 7340032 | tf_op jit(solution)/shard_map/pallas_call | solution.py:129
  47.8 2.0 %collective-permute-done.12 = f32[64,128]{1,0:T(8,128)S(1)} collective-permute-done((f32[64,128]{1,0:T(8,128)S(1)}, f32[64,128]{1,0:T(8,128)S(1)}, u32[]{:S(2)}, u32[]{:S(2)}) %collective-permute-start.12) | collective-permute-done | bytes 32800 | tf_op jit(solution)/shard_map/ppermute | solution.py:531
  51.7 3.8 %collective-permute-start.13 = (bf16[144,512]{1,0:T(8,128)(2,1)S(1)}, bf16[144,512]{1,0:T(8,128)(2,1)S(1)}, u32[]{:S(2)}, u32[]{:S(2)}) collective-permute-start(bf16[144,512]{1,0:T(8,128)(2,1)S(1)} %get-tuple-element.66), channel_id=1, source_target_pairs={{0,2},{1,3},{2,4},{3,5},{4,6},{5,7},{6,8},{7,9},{8,10},{9,11},{10,... | collective-permute-start | bytes 442376 | tf_op jit(solution)/shard_map/ppermute | solution.py:438
  56.8 1.8 %shard_map.128.weights = bf16[2,2,2,512,256]{4,3,2,1,0:T(8,128)(2,1)S(1)} custom-call(s32[6]{0:T(128)S(1)} %stack.24.place, bf16[2,64,512]{2,1,0:T(8,128)(2,1)S(1)} %get-tuple-element.67.token.own, bf16[6,4,512,256]{3,2,1,0:T(8,128)(2,1)} %lower.11, bf16[6,4,512,256]{3,2,1,0:T(8,128)(2,1)} %upper.11, bf16[4,2,512,256]{3,2,1,0:T(8,128)(2,1)S(1)} %collective-permute-done.8.packed), custom_call_target="tpu_custom_call" | custom-call | bytes 4194304 | tf_op jit(solution)/shard_map/pallas_call | solution.py:187
  58.6 4.4 %collective-permute-done.15.above = bf16[2,64,512]{2,1,0:T(8,128)(2,1)S(1)} collective-permute-done((bf16[2,64,512]{2,1,0:T(8,128)(2,1)S(1)}, bf16[2,64,512]{2,1,0:T(8,128)(2,1)S(1)}, u32[]{:S(2)}, u32[]{:S(2)}) %collective-permute-start.15) | collective-permute-done | bytes 131104 | tf_op jit(solution)/shard_map/ppermute | solution.py:438
  64.0 4.6 %collective-permute-start.16 = (bf16[2,64,512]{2,1,0:T(8,128)(2,1)S(1)}, bf16[2,64,512]{2,1,0:T(8,128)(2,1)S(1)}, u32[]{:S(2)}, u32[]{:S(2)}) collective-permute-start(bf16[2,64,512]{2,1,0:T(8,128)(2,1)S(1)} %shard_map.129.token.own), channel_id=1, source_target_pairs={{0,4},{1,5},{2,6},{3,7},{4,8},{5,9},{6,10},{7,11},{8,12},{9,13},{1... | collective-permute-start | bytes 393224 | tf_op jit(solution)/shard_map/ppermute | solution.py:438
  70.5 1.8 %shard_map.130.weights = bf16[2,2,2,512,256]{4,3,2,1,0:T(8,128)(2,1)S(1)} custom-call(s32[6]{0:T(128)S(1)} %stack.24.place, bf16[2,64,512]{2,1,0:T(8,128)(2,1)S(1)} %shard_map.129.token.own, bf16[6,4,512,256]{3,2,1,0:T(8,128)(2,1)} %lower.11, bf16[6,4,512,256]{3,2,1,0:T(8,128)(2,1)} %upper.11, bf16[5,2,512,256]{3,2,1,0:T(8,128)(2,1)S(1)} %collective-permute-done.14.packed), custom_call_target="tpu_custom_call" | custom-call | bytes 4194304 | tf_op jit(solution)/shard_map/pallas_call | solution.py:187
  72.3 3.3 %collective-permute-done.17.above = bf16[2,64,512]{2,1,0:T(8,128)(2,1)S(1)} collective-permute-done((bf16[2,64,512]{2,1,0:T(8,128)(2,1)S(1)}, bf16[2,64,512]{2,1,0:T(8,128)(2,1)S(1)}, u32[]{:S(2)}, u32[]{:S(2)}) %collective-permute-start.17) | collective-permute-done | bytes 131104 | tf_op jit(solution)/shard_map/ppermute | solution.py:438
  77.9 2.7 %shard_map.132.blocks = bf16[16,512,256]{2,1,0:T(8,128)(2,1)S(1)} custom-call(s32[6]{0:T(128)S(1)} %stack.24.place, bf16[2,64,512]{2,1,0:T(8,128)(2,1)S(1)} %shard_map.131.token.own, bf16[16,512,256]{2,1,0:T(8,128)(2,1)} %source.1), custom_call_target="tpu_custom_call" | custom-call | bytes 4194304 | tf_op jit(solution)/shard_map/pallas_call | solution.py:203
  80.7 1.8 %shard_map.133.weights = bf16[2,2,2,512,256]{4,3,2,1,0:T(8,128)(2,1)S(1)} custom-call(s32[6]{0:T(128)S(1)} %stack.24.place, bf16[2,64,512]{2,1,0:T(8,128)(2,1)S(1)} %shard_map.131.token.own, bf16[6,4,512,256]{3,2,1,0:T(8,128)(2,1)} %lower.11, bf16[6,4,512,256]{3,2,1,0:T(8,128)(2,1)} %upper.11, bf16[5,2,512,256]{3,2,1,0:T(8,128)(2,1)S(1)} %collective-permute-done.14.packed, ...), custom_call_target="tpu_custom_call" | custom-call | bytes 4194304 | tf_op jit(solution)/shard_map/pallas_call | solution.py:187
  86.6 2.9 %collective-permute-start.22 = (bf16[2,64,512]{2,1,0:T(8,128)(2,1)S(1)}, bf16[2,64,512]{2,1,0:T(8,128)(2,1)S(1)}, u32[]{:S(2)}, u32[]{:S(2)}) collective-permute-start(bf16[2,64,512]{2,1,0:T(8,128)(2,1)S(1)} %get-tuple-element.76.correction), channel_id=1, source_target_pairs={{0,2},{1,3},{2,4},{3,5},{4,6},{5,7},{6,8},{7,9},{8,10},{9,11},{10,... | collective-permute-start | bytes 393224 | tf_op jit(solution)/shard_map/ppermute | solution.py:438
  89.6 3.2 %shard_map.135 = (f32[6,64,512]{2,1,0:T(8,128)S(1)}, f32[160,128]{1,0:T(8,128)S(1)}, f32[8,128]{1,0:T(8,128)S(1)}) custom-call(s32[6]{0:T(128)S(1)} %stack.24.place, s32[8,14]{1,0:T(8,128)S(1)} %add_add_fusion.1.table, f32[8]{0:T(128)S(1)} %copy-done.5, s32[1]{0:T(128)S(6)} %copy.13.index, bf16[12,64,512]{2,1,0:T(8,128)(2,1)S(1)} %all_gather.3.extended, ...), custom_call_target="tpu_custom_call" | custom-call | flops 469762048 | tf_op jit(solution)/shard_map/pallas_call | solution.py:598
  95.9 3.2 %collective-permute-start.25 = (f32[80,128]{1,0:T(8,128)S(1)}, f32[80,128]{1,0:T(8,128)S(1)}, u32[]{:S(2)}, u32[]{:S(2)}) collective-permute-start(f32[80,128]{1,0:T(8,128)S(1)} %add.85), channel_id=1, source_target_pairs={{0,4},{2,6},{4,0},{6,2},{8,12},{10,14},{12,8},{14,10},{1,5},{3,7},... | collective-permute-start | bytes 122888 | tf_op jit(solution)/shard_map/ppermute | solution.py:462
  101.1 2.9 %collective-permute-done.26 = f32[80,128]{1,0:T(8,128)S(1)} collective-permute-done((f32[80,128]{1,0:T(8,128)S(1)}, f32[80,128]{1,0:T(8,128)S(1)}, u32[]{:S(2)}, u32[]{:S(2)}) %collective-permute-start.26) | collective-permute-done | bytes 40992 | tf_op jit(solution)/shard_map/ppermute | solution.py:462
  106.4 3.3 %collective-permute-done.27 = f32[80,128]{1,0:T(8,128)S(1)} collective-permute-done((f32[80,128]{1,0:T(8,128)S(1)}, f32[80,128]{1,0:T(8,128)S(1)}, u32[]{:S(2)}, u32[]{:S(2)}) %collective-permute-start.27) | collective-permute-done | bytes 40992 | tf_op jit(solution)/shard_map/ppermute | solution.py:462
  (91 shorter events, 37.0 us)
Async XLA Ops:
  0.6 13.9 %collective-permute-start.1 = (bf16[4,64,256]{2,1,0:T(8,128)(2,1)}, bf16[4,64,256]{2,1,0:T(8,128)(2,1)S(1)}, u32[]{:S(2)}, u32[]{:S(2)}) collective-permute-start(bf16[4,64,256]{2,1,0:T(8,128)(2,1)} %vectors.1), channel_id=1, source_target_pairs={{2,0},{4,2},{6,4},{8,6},{10,8},{12,10},{14,12},{3,1},{5,3},{7,5},{... | collective-permute-start | bytes 393224 | tf_op jit(solution)/shard_map/ppermute | solution.py:438
  1.9 12.6 %collective-permute-start = (bf16[4,64,256]{2,1,0:T(8,128)(2,1)}, bf16[4,64,256]{2,1,0:T(8,128)(2,1)S(1)}, u32[]{:S(2)}, u32[]{:S(2)}) collective-permute-start(bf16[4,64,256]{2,1,0:T(8,128)(2,1)} %vectors.1), channel_id=1, source_target_pairs={{0,2},{2,4},{4,6},{6,8},{8,10},{10,12},{12,14},{1,3},{3,5},{5,7},{... | collective-permute-start | bytes 393224 | tf_op jit(solution)/shard_map/ppermute | solution.py:438
  20.8 16.7 %collective-permute-start.8 = (bf16[4,2,512,256]{3,2,1,0:T(8,128)(2,1)}, bf16[4,2,512,256]{3,2,1,0:T(8,128)(2,1)S(1)}, u32[]{:S(2)}, u32[]{:S(2)}) collective-permute-start(bf16[4,2,512,256]{3,2,1,0:T(8,128)(2,1)} %get-tuple-element.57), channel_id=1, source_target_pairs={{0,1},{1,0},{2,3},{3,2},{4,5},{5,4},{6,7},{7,6},{8,9},{9,8},{10,11... | collective-permute-start | bytes 6291464 | tf_op jit(solution)/shard_map/ppermute | solution.py:432
  27.3 9.2 %collective-permute-start.4 = (bf16[1,64,512]{2,1,0:T(8,128)(2,1)S(1)}, bf16[1,64,512]{2,1,0:T(8,128)(2,1)S(1)}, u32[]{:S(2)}, u32[]{:S(2)}) collective-permute-start(bf16[1,64,512]{2,1,0:T(8,128)(2,1)S(1)} %get-tuple-element.92), channel_id=1, source_target_pairs={{0,1},{1,0},{2,3},{3,2},{4,5},{5,4},{6,7},{7,6},{8,9},{9,8},{10,11... | collective-permute-start | bytes 196616 | tf_op jit(solution)/shard_map/ppermute | solution.py:432
  27.5 9.0 %collective-permute-start.5 = (bf16[1,64,512]{2,1,0:T(8,128)(2,1)S(1)}, bf16[1,64,512]{2,1,0:T(8,128)(2,1)S(1)}, u32[]{:S(2)}, u32[]{:S(2)}) collective-permute-start(bf16[1,64,512]{2,1,0:T(8,128)(2,1)S(1)} %get-tuple-element.91), channel_id=1, source_target_pairs={{1,2},{3,4},{5,6},{7,8},{9,10},{11,12},{13,14},{2,1},{4,3},{6,5},{... | collective-permute-start | bytes 196616 | tf_op jit(solution)/shard_map/ppermute | solution.py:508
  28.2 9.4 %collective-permute-start.7 = (f32[64,128]{1,0:T(8,128)S(1)}, f32[64,128]{1,0:T(8,128)S(1)}, u32[]{:S(2)}, u32[]{:S(2)}) collective-permute-start(f32[64,128]{1,0:T(8,128)S(1)} %add.79), channel_id=1, source_target_pairs={{0,2},{2,0},{4,6},{6,4},{8,10},{10,8},{12,14},{14,12},{1,3},{3,1},... | collective-permute-start | bytes 98312 | tf_op jit(solution)/shard_map/ppermute | solution.py:511
  37.6 52.0 %collective-permute-start.19 = (bf16[16,512,256]{2,1,0:T(8,128)(2,1)S(1)}, bf16[16,512,256]{2,1,0:T(8,128)(2,1)S(1)}, u32[]{:S(2)}, u32[]{:S(2)}) collective-permute-start(bf16[16,512,256]{2,1,0:T(8,128)(2,1)S(1)} %copy-done.6), channel_id=1, source_target_pairs={{0,1},{1,0},{2,3},{3,2},{4,5},{5,4},{6,7},{7,6},{8,9},{9,8},{10,11... | collective-permute-start | bytes 12582920 | tf_op jit(solution)/shard_map/ppermute | solution.py:432
  38.1 3.9 %collective-permute-start.11 = (f32[64,128]{1,0:T(8,128)S(1)}, f32[64,128]{1,0:T(8,128)S(1)}, u32[]{:S(2)}, u32[]{:S(2)}) collective-permute-start(f32[64,128]{1,0:T(8,128)S(1)} %add.82), channel_id=1, source_target_pairs={{0,4},{2,6},{4,0},{6,2},{8,12},{10,14},{12,8},{14,10},{1,5},{3,7},... | collective-permute-start | bytes 98312 | tf_op jit(solution)/shard_map/ppermute | solution.py:531
  39.7 10.1 %collective-permute-start.9 = (bf16[2,128,512]{2,1,0:T(8,128)(2,1)S(1)}, bf16[2,128,512]{2,1,0:T(8,128)(2,1)S(1)}, u32[]{:S(2)}, u32[]{:S(2)}) collective-permute-start(bf16[2,128,512]{2,1,0:T(8,128)(2,1)S(1)} %shard_map.125.token.own), channel_id=1, source_target_pairs={{0,1},{1,0},{2,3},{3,2},{4,5},{5,4},{6,7},{7,6},{8,9},{9,8},{10,11... | collective-permute-start | bytes 786440 | tf_op jit(solution)/shard_map/ppermute | solution.py:432
  39.7 10.1 %collective-permute-start.10 = (bf16[2,128,512]{2,1,0:T(8,128)(2,1)S(1)}, bf16[2,128,512]{2,1,0:T(8,128)(2,1)S(1)}, u32[]{:S(2)}, u32[]{:S(2)}) collective-permute-start(bf16[2,128,512]{2,1,0:T(8,128)(2,1)S(1)} %shard_map.125.token.own), channel_id=1, source_target_pairs={{1,2},{3,4},{5,6},{7,8},{9,10},{11,12},{13,14},{2,1},{4,3},{6,5},{... | collective-permute-start | bytes 786440 | tf_op jit(solution)/shard_map/ppermute | solution.py:528
  42.0 7.8 %collective-permute-start.12 = (f32[64,128]{1,0:T(8,128)S(1)}, f32[64,128]{1,0:T(8,128)S(1)}, u32[]{:S(2)}, u32[]{:S(2)}) collective-permute-start(f32[64,128]{1,0:T(8,128)S(1)} %add.83), channel_id=1, source_target_pairs={{0,8},{2,10},{4,12},{6,14},{8,0},{10,2},{12,4},{14,6},{1,9},{3,11}... | collective-permute-start | bytes 98312 | tf_op jit(solution)/shard_map/ppermute | solution.py:531
  49.8 13.2 %collective-permute-start.14 = (bf16[5,2,512,256]{3,2,1,0:T(8,128)(2,1)}, bf16[5,2,512,256]{3,2,1,0:T(8,128)(2,1)S(1)}, u32[]{:S(2)}, u32[]{:S(2)}) collective-permute-start(bf16[5,2,512,256]{3,2,1,0:T(8,128)(2,1)} %get-tuple-element.68), channel_id=1, source_target_pairs={{0,1},{1,0},{2,3},{3,2},{4,5},{5,4},{6,7},{7,6},{8,9},{9,8},{10,11... | collective-permute-start | bytes 7864328 | tf_op jit(solution)/shard_map/ppermute | solution.py:432
  51.7 11.3 %collective-permute-start.13 = (bf16[144,512]{1,0:T(8,128)(2,1)S(1)}, bf16[144,512]{1,0:T(8,128)(2,1)S(1)}, u32[]{:S(2)}, u32[]{:S(2)}) collective-permute-start(bf16[144,512]{1,0:T(8,128)(2,1)S(1)} %get-tuple-element.66), channel_id=1, source_target_pairs={{0,2},{1,3},{2,4},{3,5},{4,6},{5,7},{6,8},{7,9},{8,10},{9,11},{10,... | collective-permute-start | bytes 442376 | tf_op jit(solution)/shard_map/ppermute | solution.py:438
  55.5 7.5 %collective-permute-start.15 = (bf16[2,64,512]{2,1,0:T(8,128)(2,1)S(1)}, bf16[2,64,512]{2,1,0:T(8,128)(2,1)S(1)}, u32[]{:S(2)}, u32[]{:S(2)}) collective-permute-start(bf16[2,64,512]{2,1,0:T(8,128)(2,1)S(1)} %get-tuple-element.67.token.own), channel_id=1, source_target_pairs={{2,0},{3,1},{4,2},{5,3},{6,4},{7,5},{8,6},{9,7},{10,8},{11,9},{12,... | collective-permute-start | bytes 393224 | tf_op jit(solution)/shard_map/ppermute | solution.py:438
  64.0 8.3 %collective-permute-start.16 = (bf16[2,64,512]{2,1,0:T(8,128)(2,1)S(1)}, bf16[2,64,512]{2,1,0:T(8,128)(2,1)S(1)}, u32[]{:S(2)}, u32[]{:S(2)}) collective-permute-start(bf16[2,64,512]{2,1,0:T(8,128)(2,1)S(1)} %shard_map.129.token.own), channel_id=1, source_target_pairs={{0,4},{1,5},{2,6},{3,7},{4,8},{5,9},{6,10},{7,11},{8,12},{9,13},{1... | collective-permute-start | bytes 393224 | tf_op jit(solution)/shard_map/ppermute | solution.py:438
  68.6 7.0 %collective-permute-start.17 = (bf16[2,64,512]{2,1,0:T(8,128)(2,1)S(1)}, bf16[2,64,512]{2,1,0:T(8,128)(2,1)S(1)}, u32[]{:S(2)}, u32[]{:S(2)}) collective-permute-start(bf16[2,64,512]{2,1,0:T(8,128)(2,1)S(1)} %shard_map.129.token.own), channel_id=1, source_target_pairs={{4,0},{5,1},{6,2},{7,3},{8,4},{9,5},{10,6},{11,7},{12,8},{13,9},{1... | collective-permute-start | bytes 393224 | tf_op jit(solution)/shard_map/ppermute | solution.py:438
  76.7 7.5 %collective-permute-start.18 = (bf16[2,64,512]{2,1,0:T(8,128)(2,1)S(1)}, bf16[2,64,512]{2,1,0:T(8,128)(2,1)S(1)}, u32[]{:S(2)}, u32[]{:S(2)}) collective-permute-start(bf16[2,64,512]{2,1,0:T(8,128)(2,1)S(1)} %shard_map.131.token.own), channel_id=1, source_target_pairs={{0,8},{1,9},{2,10},{3,11},{4,12},{5,13},{6,14},{7,15},{8,0},{9,1},... | collective-permute-start | bytes 393224 | tf_op jit(solution)/shard_map/ppermute | solution.py:557
  85.3 7.5 %collective-permute-start.21 = (bf16[2,64,512]{2,1,0:T(8,128)(2,1)S(1)}, bf16[2,64,512]{2,1,0:T(8,128)(2,1)S(1)}, u32[]{:S(2)}, u32[]{:S(2)}) collective-permute-start(bf16[2,64,512]{2,1,0:T(8,128)(2,1)S(1)} %get-tuple-element.76.correction), channel_id=1, source_target_pairs={{0,1},{1,2},{2,3},{3,4},{4,5},{5,6},{6,7},{7,8},{8,9},{9,10},{10,1... | collective-permute-start | bytes 393224 | tf_op jit(solution)/shard_map/ppermute | solution.py:438
  86.6 6.2 %collective-permute-start.22 = (bf16[2,64,512]{2,1,0:T(8,128)(2,1)S(1)}, bf16[2,64,512]{2,1,0:T(8,128)(2,1)S(1)}, u32[]{:S(2)}, u32[]{:S(2)}) collective-permute-start(bf16[2,64,512]{2,1,0:T(8,128)(2,1)S(1)} %get-tuple-element.76.correction), channel_id=1, source_target_pairs={{0,2},{1,3},{2,4},{3,5},{4,6},{5,7},{6,8},{7,9},{8,10},{9,11},{10,... | collective-permute-start | bytes 393224 | tf_op jit(solution)/shard_map/ppermute | solution.py:438
  95.9 5.2 %collective-permute-start.25 = (f32[80,128]{1,0:T(8,128)S(1)}, f32[80,128]{1,0:T(8,128)S(1)}, u32[]{:S(2)}, u32[]{:S(2)}) collective-permute-start(f32[80,128]{1,0:T(8,128)S(1)} %add.85), channel_id=1, source_target_pairs={{0,4},{2,6},{4,0},{6,2},{8,12},{10,14},{12,8},{14,10},{1,5},{3,7},... | collective-permute-start | bytes 122888 | tf_op jit(solution)/shard_map/ppermute | solution.py:462
  99.1 4.9 %collective-permute-start.26 = (f32[80,128]{1,0:T(8,128)S(1)}, f32[80,128]{1,0:T(8,128)S(1)}, u32[]{:S(2)}, u32[]{:S(2)}) collective-permute-start(f32[80,128]{1,0:T(8,128)S(1)} %add.85), channel_id=1, source_target_pairs={{0,6},{2,4},{4,2},{6,0},{8,14},{10,12},{12,10},{14,8},{1,7},{3,5},... | collective-permute-start | bytes 122888 | tf_op jit(solution)/shard_map/ppermute | solution.py:462
  100.7 4.0 %collective-permute-start.24 = (f32[80,128]{1,0:T(8,128)S(1)}, f32[80,128]{1,0:T(8,128)S(1)}, u32[]{:S(2)}, u32[]{:S(2)}) collective-permute-start(f32[80,128]{1,0:T(8,128)S(1)} %add.85), channel_id=1, source_target_pairs={{0,2},{2,0},{4,6},{6,4},{8,10},{10,8},{12,14},{14,12},{1,3},{3,1},... | collective-permute-start | bytes 122888 | tf_op jit(solution)/shard_map/ppermute | solution.py:462
  104.7 5.0 %collective-permute-start.27 = (f32[80,128]{1,0:T(8,128)S(1)}, f32[80,128]{1,0:T(8,128)S(1)}, u32[]{:S(2)}, u32[]{:S(2)}) collective-permute-start(f32[80,128]{1,0:T(8,128)S(1)} %add_add_fusion), channel_id=1, source_target_pairs={{0,8},{2,10},{4,12},{6,14},{8,0},{10,2},{12,4},{14,6},{1,9},{3,11}... | collective-permute-start | bytes 122888 | tf_op jit(solution)/shard_map/ppermute | solution.py:462
  106.3 3.4 %collective-permute-start.20 = (bf16[2,64,256]{2,1,0:T(8,128)(2,1)S(1)}, bf16[2,64,256]{2,1,0:T(8,128)(2,1)S(1)}, u32[]{:S(2)}, u32[]{:S(2)}) collective-permute-start(bf16[2,64,256]{2,1,0:T(8,128)(2,1)S(1)} %get-tuple-element.81), channel_id=1, source_target_pairs={{0,1},{1,0},{2,3},{3,2},{4,5},{5,4},{6,7},{7,6},{8,9},{9,8},{10,11... | collective-permute-start | bytes 196616 | tf_op jit(solution)/shard_map/ppermute | solution.py:432
  (15 other events, 73.4 us)

commit v13 on v10

--- a/solution.py
+++ b/solution.py
@@ -457,7 +457,7 @@
     slabs = lax.axis_size("slab")
     reach = 1
     while reach < slabs:
-        radix = min(4, slabs // reach)
+        radix = min(8, slabs // reach)
         routes = [[(i, i ^ (offset * reach)) for i in range(slabs)] for offset in range(1, radix)]
         part = summed_up([part] + [lax.ppermute(part, "slab", route) for route in routes])
         reach *= radix

time: 106 us -> 109 us (1.028)
  starting transfers between devices: 43.1 us -> 49.4 us
  waiting for transfers between devices: 23.6 us -> 20.1 us
    ppermute x4 -> x7, starting transfers between devices: 5.49 us -> 12 us  [slab_total(): lax.ppermute(part, 'slab', route)]
    ppermute x4 -> x7, waiting for transfers between devices: 7.39 us -> 3.92 us  [slab_total(): lax.ppermute(part, 'slab', route)]
  transfers between devices with their start and end apart: 29 -> 32, of which waited for: 14 -> 13; matrix products, arithmetic and copies ran while one was open for 1% -> 1% of each run, Pallas kernels for 27% -> 26%
where the time goes in v13:
time: 109 us; the launch traced here: 108 us
  starting transfers between devices  49.4 us (45%)
  Pallas kernels  33.7 us (31%)
  waiting for transfers between devices  20.1 us (18%)
  blocking collectives  2.37 us (2%)
  between operations  1.7 us (2%)
    ppermute x8, starting transfers between devices, along(): return lax.ppermute(operand, axis, route)  20.9 us
    ppermute x7, starting transfers between devices, slab_total(): lax.ppermute(part, 'slab', route)  12 us
    ppermute x8, waiting for transfers between devices, along(): return lax.ppermute(operand, axis, route)  7.83 us
    pallas_call x4, Pallas kernels, load(): pl.pallas_call(body, out_shape=pltpu.VMEM(shape, bf16), in_specs=[SMEM] +...  7.47 us
    ppermute x2, starting transfers between devices, on_device(): received = lax.ppermute(moments, 'slab', flip)  6.05 us
    pallas_call x1, Pallas kernels, prepare(): pl.pallas_call(prepare_body, out_shape=[pltpu.VMEM(blocks.shape, bf16), p...  4.97 us
    ppermute x1, starting transfers between devices, on_device(): received = lax.ppermute(moments, 'slab', flips[0])  4.23 us
    ppermute x7, waiting for transfers between devices, slab_total(): lax.ppermute(part, 'slab', route)  3.92 us
  transfers between devices with their start and end apart: 32, of which 13 were waited for; matrix products, arithmetic and copies ran while one was open for 1% of the time, Pallas kernels for 26%

profile of v13, /device:TPU:0, one launch (start us, length us, event | category | flops | bytes accessed | tf_op | source)
XLA Modules:
  0.0 108.5 jit_solution(12802637312991239870)
XLA Ops:
  1.9 5.5 %collective-permute-start = (bf16[4,64,256]{2,1,0:T(8,128)(2,1)}, bf16[4,64,256]{2,1,0:T(8,128)(2,1)S(1)}, u32[]{:S(2)}, u32[]{:S(2)}) collective-permute-start(bf16[4,64,256]{2,1,0:T(8,128)(2,1)} %vectors.1), channel_id=1, source_target_pairs={{0,2},{2,4},{4,6},{6,8},{8,10},{10,12},{12,14},{1,3},{3,5},{5,7},{... | collective-permute-start | bytes 393224 | tf_op jit(solution)/shard_map/ppermute | solution.py:438
  8.3 5.0 %shard_map.121 = (bf16[16,512,256]{2,1,0:T(8,128)(2,1)S(1)}, bf16[2,2,512,256]{3,2,1,0:T(8,128)(2,1)}, bf16[4,2,512,256]{3,2,1,0:T(8,128)(2,1)}) custom-call(s32[6]{0:T(128)S(1)} %stack.24.place, bf16[6,4,512,256]{3,2,1,0:T(8,128)(2,1)} %lower.11, bf16[6,4,512,256]{3,2,1,0:T(8,128)(2,1)} %upper.11, bf16[16,512,256]{2,1,0:T(8,128)(2,1)} %source.1), custom_call_target="tpu_custom_call" | custom-call | bytes 10485760 | tf_op jit(solution)/shard_map/pallas_call | solution.py:92
  13.4 2.4 %all_gather.3.extended = bf16[12,64,512]{2,1,0:T(8,128)(2,1)S(1)} all-gather(bf16[12,64,256]{2,1,0:T(8,128)(2,1)S(1)} %pad_maximum_fusion), channel_id=1, replica_groups=mesh['groups'=2,'slab'=8,'vec'=2] {'vec'}, dimensions={2}, use_global_device_ids=true | all-gather | bytes 1179648 | tf_op jit(solution)/shard_map/all_gather | solution.py:497
  15.8 2.2 %shard_map.122 = (bf16[2,64,256]{2,1,0:T(8,128)(2,1)S(1)}, bf16[2,64,256]{2,1,0:T(8,128)(2,1)S(1)}, f32[64,128]{1,0:T(8,128)S(1)}) custom-call(s32[6]{0:T(128)S(1)} %stack.24.place, s32[4,14]{1,0:T(4,128)S(1)} %get-tuple-element.88.table, bf16[12,64,512]{2,1,0:T(8,128)(2,1)S(1)} %all_gather.3.extended, bf16[4,64,256]{2,1,0:T(8,128)(2,1)S(1)} %copy-done, ...), custom_call_target="tpu_custom_call" | custom-call | flops 469762048 | bytes 4194304 | tf_op jit(solution)/shard_map/pallas_call | solution.py:238
  21.2 4.2 %collective-permute-start.7 = (f32[64,128]{1,0:T(8,128)S(1)}, f32[64,128]{1,0:T(8,128)S(1)}, u32[]{:S(2)}, u32[]{:S(2)}) collective-permute-start(f32[64,128]{1,0:T(8,128)S(1)} %add.88), channel_id=1, source_target_pairs={{0,2},{2,0},{4,6},{6,4},{8,10},{10,8},{12,14},{14,12},{1,3},{3,1},... | collective-permute-start | bytes 98312 | tf_op jit(solution)/shard_map/ppermute | solution.py:510
  25.7 2.1 %shard_map.123.weights = bf16[2,2,2,512,256]{4,3,2,1,0:T(8,128)(2,1)S(1)} custom-call(s32[6]{0:T(128)S(1)} %stack.24.place, bf16[2,64,256]{2,1,0:T(8,128)(2,1)S(1)} %get-tuple-element.48.token, bf16[6,4,512,256]{3,2,1,0:T(8,128)(2,1)} %lower.11, bf16[6,4,512,256]{3,2,1,0:T(8,128)(2,1)} %upper.11, bf16[2,2,512,256]{3,2,1,0:T(8,128)(2,1)} %collective-permute-done.6.packed), custom_call_target="tpu_custom_call" | custom-call | bytes 4194304 | tf_op jit(solution)/shard_map/pallas_call | solution.py:187
  30.3 2.1 %collective-permute-start.11 = (f32[64,128]{1,0:T(8,128)S(1)}, f32[64,128]{1,0:T(8,128)S(1)}, u32[]{:S(2)}, u32[]{:S(2)}) collective-permute-start(f32[64,128]{1,0:T(8,128)S(1)} %add.91), channel_id=1, source_target_pairs={{0,4},{2,6},{4,0},{6,2},{8,12},{10,14},{12,8},{14,10},{1,5},{3,7},... | collective-permute-start | bytes 98312 | tf_op jit(solution)/shard_map/ppermute | solution.py:530
  34.3 3.9 %collective-permute-start.12 = (f32[64,128]{1,0:T(8,128)S(1)}, f32[64,128]{1,0:T(8,128)S(1)}, u32[]{:S(2)}, u32[]{:S(2)}) collective-permute-start(f32[64,128]{1,0:T(8,128)S(1)} %add.92), channel_id=1, source_target_pairs={{0,8},{2,10},{4,12},{6,14},{8,0},{10,2},{12,4},{14,6},{1,9},{3,11}... | collective-permute-start | bytes 98312 | tf_op jit(solution)/shard_map/ppermute | solution.py:530
  38.3 3.2 %shard_map.126 = (bf16[2,2,2,512,256]{4,3,2,1,0:T(8,128)(2,1)S(1)}, bf16[5,2,512,256]{3,2,1,0:T(8,128)(2,1)}) custom-call(s32[6]{0:T(128)S(1)} %stack.24.place, bf16[2,128,512]{2,1,0:T(8,128)(2,1)S(1)} %shard_map.125.token.own, bf16[6,4,512,256]{3,2,1,0:T(8,128)(2,1)} %lower.11, bf16[6,4,512,256]{3,2,1,0:T(8,128)(2,1)} %upper.11, ...), custom_call_target="tpu_custom_call" | custom-call | bytes 7340032 | tf_op jit(solution)/shard_map/pallas_call | solution.py:129
  41.5 2.1 %collective-permute-done.12 = f32[64,128]{1,0:T(8,128)S(1)} collective-permute-done((f32[64,128]{1,0:T(8,128)S(1)}, f32[64,128]{1,0:T(8,128)S(1)}, u32[]{:S(2)}, u32[]{:S(2)}) %collective-permute-start.12) | collective-permute-done | bytes 32800 | tf_op jit(solution)/shard_map/ppermute | solution.py:530
  45.4 3.5 %collective-permute-start.13 = (bf16[144,512]{1,0:T(8,128)(2,1)S(1)}, bf16[144,512]{1,0:T(8,128)(2,1)S(1)}, u32[]{:S(2)}, u32[]{:S(2)}) collective-permute-start(bf16[144,512]{1,0:T(8,128)(2,1)S(1)} %get-tuple-element.64), channel_id=1, source_target_pairs={{0,2},{1,3},{2,4},{3,5},{4,6},{5,7},{6,8},{7,9},{8,10},{9,11},{10,... | collective-permute-start | bytes 442376 | tf_op jit(solution)/shard_map/ppermute | solution.py:438
  50.3 1.8 %shard_map.128.weights = bf16[2,2,2,512,256]{4,3,2,1,0:T(8,128)(2,1)S(1)} custom-call(s32[6]{0:T(128)S(1)} %stack.24.place, bf16[2,64,512]{2,1,0:T(8,128)(2,1)S(1)} %get-tuple-element.65.token.own, bf16[6,4,512,256]{3,2,1,0:T(8,128)(2,1)} %lower.11, bf16[6,4,512,256]{3,2,1,0:T(8,128)(2,1)} %upper.11, bf16[4,2,512,256]{3,2,1,0:T(8,128)(2,1)S(1)} %collective-permute-done.8.packed), custom_call_target="tpu_custom_call" | custom-call | bytes 4194304 | tf_op jit(solution)/shard_map/pallas_call | solution.py:187
  52.1 4.4 %collective-permute-done.15.above = bf16[2,64,512]{2,1,0:T(8,128)(2,1)S(1)} collective-permute-done((bf16[2,64,512]{2,1,0:T(8,128)(2,1)S(1)}, bf16[2,64,512]{2,1,0:T(8,128)(2,1)S(1)}, u32[]{:S(2)}, u32[]{:S(2)}) %collective-permute-start.15) | collective-permute-done | bytes 131104 | tf_op jit(solution)/shard_map/ppermute | solution.py:438
  57.5 3.6 %collective-permute-start.16 = (bf16[2,64,512]{2,1,0:T(8,128)(2,1)S(1)}, bf16[2,64,512]{2,1,0:T(8,128)(2,1)S(1)}, u32[]{:S(2)}, u32[]{:S(2)}) collective-permute-start(bf16[2,64,512]{2,1,0:T(8,128)(2,1)S(1)} %shard_map.129.token.own), channel_id=1, source_target_pairs={{0,4},{1,5},{2,6},{3,7},{4,8},{5,9},{6,10},{7,11},{8,12},{9,13},{1... | collective-permute-start | bytes 393224 | tf_op jit(solution)/shard_map/ppermute | solution.py:438
  64.9 3.3 %collective-permute-done.17.above = bf16[2,64,512]{2,1,0:T(8,128)(2,1)S(1)} collective-permute-done((bf16[2,64,512]{2,1,0:T(8,128)(2,1)S(1)}, bf16[2,64,512]{2,1,0:T(8,128)(2,1)S(1)}, u32[]{:S(2)}, u32[]{:S(2)}) %collective-permute-start.17) | collective-permute-done | bytes 131104 | tf_op jit(solution)/shard_map/ppermute | solution.py:438
  70.9 2.7 %shard_map.132.blocks = bf16[16,512,256]{2,1,0:T(8,128)(2,1)S(1)} custom-call(s32[6]{0:T(128)S(1)} %stack.24.place, bf16[2,64,512]{2,1,0:T(8,128)(2,1)S(1)} %shard_map.131.token.own, bf16[16,512,256]{2,1,0:T(8,128)(2,1)} %source.1), custom_call_target="tpu_custom_call" | custom-call | bytes 4194304 | tf_op jit(solution)/shard_map/pallas_call | solution.py:203
  73.6 1.8 %shard_map.133.weights = bf16[2,2,2,512,256]{4,3,2,1,0:T(8,128)(2,1)S(1)} custom-call(s32[6]{0:T(128)S(1)} %stack.24.place, bf16[2,64,512]{2,1,0:T(8,128)(2,1)S(1)} %shard_map.131.token.own, bf16[6,4,512,256]{3,2,1,0:T(8,128)(2,1)} %lower.11, bf16[6,4,512,256]{3,2,1,0:T(8,128)(2,1)} %upper.11, bf16[5,2,512,256]{3,2,1,0:T(8,128)(2,1)S(1)} %collective-permute-done.14.packed, ...), custom_call_target="tpu_custom_call" | custom-call | bytes 4194304 | tf_op jit(solution)/shard_map/pallas_call | solution.py:187
  75.4 1.8 %collective-permute-done.18.other = bf16[2,64,512]{2,1,0:T(8,128)(2,1)S(1)} collective-permute-done((bf16[2,64,512]{2,1,0:T(8,128)(2,1)S(1)}, bf16[2,64,512]{2,1,0:T(8,128)(2,1)S(1)}, u32[]{:S(2)}, u32[]{:S(2)}) %collective-permute-start.18) | collective-permute-done | bytes 131104 | tf_op jit(solution)/shard_map/ppermute | solution.py:556
  79.6 3.1 %collective-permute-start.22 = (bf16[2,64,512]{2,1,0:T(8,128)(2,1)S(1)}, bf16[2,64,512]{2,1,0:T(8,128)(2,1)S(1)}, u32[]{:S(2)}, u32[]{:S(2)}) collective-permute-start(bf16[2,64,512]{2,1,0:T(8,128)(2,1)S(1)} %get-tuple-element.74.correction), channel_id=1, source_target_pairs={{0,2},{1,3},{2,4},{3,5},{4,6},{5,7},{6,8},{7,9},{8,10},{9,11},{10,... | collective-permute-start | bytes 393224 | tf_op jit(solution)/shard_map/ppermute | solution.py:438
  82.9 3.2 %shard_map.135 = (f32[6,64,512]{2,1,0:T(8,128)S(1)}, f32[160,128]{1,0:T(8,128)S(1)}, f32[8,128]{1,0:T(8,128)S(1)}) custom-call(s32[6]{0:T(128)S(1)} %stack.24.place, s32[8,14]{1,0:T(8,128)S(1)} %add_add_fusion.1.table, f32[8]{0:T(128)S(1)} %copy-done.1, s32[1]{0:T(128)S(6)} %copy.13.index, bf16[12,64,512]{2,1,0:T(8,128)(2,1)S(1)} %all_gather.3.extended, ...), custom_call_target="tpu_custom_call" | custom-call | flops 469762048 | tf_op jit(solution)/shard_map/pallas_call | solution.py:597
  89.6 4.2 %collective-permute-start.29 = (f32[80,128]{1,0:T(8,128)S(1)}, f32[80,128]{1,0:T(8,128)S(1)}, u32[]{:S(2)}, u32[]{:S(2)}) collective-permute-start(f32[80,128]{1,0:T(8,128)S(1)} %add.94), channel_id=1, source_target_pairs={{0,12},{2,14},{4,8},{6,10},{8,4},{10,6},{12,0},{14,2},{1,13},{3,15... | collective-permute-start | bytes 122888 | tf_op jit(solution)/shard_map/ppermute | solution.py:462
  93.7 2.0 %collective-permute-start.30 = (f32[80,128]{1,0:T(8,128)S(1)}, f32[80,128]{1,0:T(8,128)S(1)}, u32[]{:S(2)}, u32[]{:S(2)}) collective-permute-start(f32[80,128]{1,0:T(8,128)S(1)} %add.94), channel_id=1, source_target_pairs={{0,14},{2,12},{4,10},{6,8},{8,6},{10,4},{12,2},{14,0},{1,15},{3,13... | collective-permute-start | bytes 122888 | tf_op jit(solution)/shard_map/ppermute | solution.py:462
  95.7 1.9 %collective-permute-start.28 = (f32[80,128]{1,0:T(8,128)S(1)}, f32[80,128]{1,0:T(8,128)S(1)}, u32[]{:S(2)}, u32[]{:S(2)}) collective-permute-start(f32[80,128]{1,0:T(8,128)S(1)} %add.94), channel_id=1, source_target_pairs={{0,10},{2,8},{4,14},{6,12},{8,2},{10,0},{12,6},{14,4},{1,11},{3,9}... | collective-permute-start | bytes 122888 | tf_op jit(solution)/shard_map/ppermute | solution.py:462
  99.0 2.6 %collective-permute-start.26 = (f32[80,128]{1,0:T(8,128)S(1)}, f32[80,128]{1,0:T(8,128)S(1)}, u32[]{:S(2)}, u32[]{:S(2)}) collective-permute-start(f32[80,128]{1,0:T(8,128)S(1)} %add.94), channel_id=1, source_target_pairs={{0,6},{2,4},{4,2},{6,0},{8,14},{10,12},{12,10},{14,8},{1,7},{3,5},... | collective-permute-start | bytes 122888 | tf_op jit(solution)/shard_map/ppermute | solution.py:462
  (86 shorter events, 34.2 us)
Async XLA Ops:
  0.6 12.7 %collective-permute-start.1 = (bf16[4,64,256]{2,1,0:T(8,128)(2,1)}, bf16[4,64,256]{2,1,0:T(8,128)(2,1)S(1)}, u32[]{:S(2)}, u32[]{:S(2)}) collective-permute-start(bf16[4,64,256]{2,1,0:T(8,128)(2,1)} %vectors.1), channel_id=1, source_target_pairs={{2,0},{4,2},{6,4},{8,6},{10,8},{12,10},{14,12},{3,1},{5,3},{7,5},{... | collective-permute-start | bytes 393224 | tf_op jit(solution)/shard_map/ppermute | solution.py:438
  1.9 11.4 %collective-permute-start = (bf16[4,64,256]{2,1,0:T(8,128)(2,1)}, bf16[4,64,256]{2,1,0:T(8,128)(2,1)S(1)}, u32[]{:S(2)}, u32[]{:S(2)}) collective-permute-start(bf16[4,64,256]{2,1,0:T(8,128)(2,1)} %vectors.1), channel_id=1, source_target_pairs={{0,2},{2,4},{4,6},{6,8},{8,10},{10,12},{12,14},{1,3},{3,5},{5,7},{... | collective-permute-start | bytes 393224 | tf_op jit(solution)/shard_map/ppermute | solution.py:438
  19.5 10.4 %collective-permute-start.8 = (bf16[4,2,512,256]{3,2,1,0:T(8,128)(2,1)}, bf16[4,2,512,256]{3,2,1,0:T(8,128)(2,1)S(1)}, u32[]{:S(2)}, u32[]{:S(2)}) collective-permute-start(bf16[4,2,512,256]{3,2,1,0:T(8,128)(2,1)} %get-tuple-element.55), channel_id=1, source_target_pairs={{0,1},{1,0},{2,3},{3,2},{4,5},{5,4},{6,7},{7,6},{8,9},{9,8},{10,11... | collective-permute-start | bytes 6291464 | tf_op jit(solution)/shard_map/ppermute | solution.py:432
  19.9 5.7 %collective-permute-start.6 = (bf16[2,2,512,256]{3,2,1,0:T(8,128)(2,1)}, bf16[2,2,512,256]{3,2,1,0:T(8,128)(2,1)}, u32[]{:S(2)}, u32[]{:S(2)}) collective-permute-start(bf16[2,2,512,256]{3,2,1,0:T(8,128)(2,1)} %get-tuple-element.53), channel_id=1, source_target_pairs={{0,1},{1,0},{2,3},{3,2},{4,5},{5,4},{6,7},{7,6},{8,9},{9,8},{10,11... | collective-permute-start | bytes 3145736 | tf_op jit(solution)/shard_map/ppermute | solution.py:432
  20.1 8.7 %collective-permute-start.4 = (bf16[1,64,512]{2,1,0:T(8,128)(2,1)S(1)}, bf16[1,64,512]{2,1,0:T(8,128)(2,1)S(1)}, u32[]{:S(2)}, u32[]{:S(2)}) collective-permute-start(bf16[1,64,512]{2,1,0:T(8,128)(2,1)S(1)} %get-tuple-element.90), channel_id=1, source_target_pairs={{0,1},{1,0},{2,3},{3,2},{4,5},{5,4},{6,7},{7,6},{8,9},{9,8},{10,11... | collective-permute-start | bytes 196616 | tf_op jit(solution)/shard_map/ppermute | solution.py:432
  20.5 8.3 %collective-permute-start.5 = (bf16[1,64,512]{2,1,0:T(8,128)(2,1)S(1)}, bf16[1,64,512]{2,1,0:T(8,128)(2,1)S(1)}, u32[]{:S(2)}, u32[]{:S(2)}) collective-permute-start(bf16[1,64,512]{2,1,0:T(8,128)(2,1)S(1)} %get-tuple-element.89), channel_id=1, source_target_pairs={{1,2},{3,4},{5,6},{7,8},{9,10},{11,12},{13,14},{2,1},{4,3},{6,5},{... | collective-permute-start | bytes 196616 | tf_op jit(solution)/shard_map/ppermute | solution.py:507
  21.2 8.7 %collective-permute-start.7 = (f32[64,128]{1,0:T(8,128)S(1)}, f32[64,128]{1,0:T(8,128)S(1)}, u32[]{:S(2)}, u32[]{:S(2)}) collective-permute-start(f32[64,128]{1,0:T(8,128)S(1)} %add.88), channel_id=1, source_target_pairs={{0,2},{2,0},{4,6},{6,4},{8,10},{10,8},{12,14},{14,12},{1,3},{3,1},... | collective-permute-start | bytes 98312 | tf_op jit(solution)/shard_map/ppermute | solution.py:510
  30.0 52.9 %collective-permute-start.19 = (bf16[16,512,256]{2,1,0:T(8,128)(2,1)S(1)}, bf16[16,512,256]{2,1,0:T(8,128)(2,1)S(1)}, u32[]{:S(2)}, u32[]{:S(2)}) collective-permute-start(bf16[16,512,256]{2,1,0:T(8,128)(2,1)S(1)} %copy-done.2), channel_id=1, source_target_pairs={{0,1},{1,0},{2,3},{3,2},{4,5},{5,4},{6,7},{7,6},{8,9},{9,8},{10,11... | collective-permute-start | bytes 12582920 | tf_op jit(solution)/shard_map/ppermute | solution.py:432
  32.4 11.2 %collective-permute-start.9 = (bf16[2,128,512]{2,1,0:T(8,128)(2,1)S(1)}, bf16[2,128,512]{2,1,0:T(8,128)(2,1)S(1)}, u32[]{:S(2)}, u32[]{:S(2)}) collective-permute-start(bf16[2,128,512]{2,1,0:T(8,128)(2,1)S(1)} %shard_map.125.token.own), channel_id=1, source_target_pairs={{0,1},{1,0},{2,3},{3,2},{4,5},{5,4},{6,7},{7,6},{8,9},{9,8},{10,11... | collective-permute-start | bytes 786440 | tf_op jit(solution)/shard_map/ppermute | solution.py:432
  32.4 11.2 %collective-permute-start.10 = (bf16[2,128,512]{2,1,0:T(8,128)(2,1)S(1)}, bf16[2,128,512]{2,1,0:T(8,128)(2,1)S(1)}, u32[]{:S(2)}, u32[]{:S(2)}) collective-permute-start(bf16[2,128,512]{2,1,0:T(8,128)(2,1)S(1)} %shard_map.125.token.own), channel_id=1, source_target_pairs={{1,2},{3,4},{5,6},{7,8},{9,10},{11,12},{13,14},{2,1},{4,3},{6,5},{... | collective-permute-start | bytes 786440 | tf_op jit(solution)/shard_map/ppermute | solution.py:527
  34.3 9.2 %collective-permute-start.12 = (f32[64,128]{1,0:T(8,128)S(1)}, f32[64,128]{1,0:T(8,128)S(1)}, u32[]{:S(2)}, u32[]{:S(2)}) collective-permute-start(f32[64,128]{1,0:T(8,128)S(1)} %add.92), channel_id=1, source_target_pairs={{0,8},{2,10},{4,12},{6,14},{8,0},{10,2},{12,4},{14,6},{1,9},{3,11}... | collective-permute-start | bytes 98312 | tf_op jit(solution)/shard_map/ppermute | solution.py:530
  43.6 12.9 %collective-permute-start.14 = (bf16[5,2,512,256]{3,2,1,0:T(8,128)(2,1)}, bf16[5,2,512,256]{3,2,1,0:T(8,128)(2,1)S(1)}, u32[]{:S(2)}, u32[]{:S(2)}) collective-permute-start(bf16[5,2,512,256]{3,2,1,0:T(8,128)(2,1)} %get-tuple-element.66), channel_id=1, source_target_pairs={{0,1},{1,0},{2,3},{3,2},{4,5},{5,4},{6,7},{7,6},{8,9},{9,8},{10,11... | collective-permute-start | bytes 7864328 | tf_op jit(solution)/shard_map/ppermute | solution.py:432
  45.4 11.1 %collective-permute-start.13 = (bf16[144,512]{1,0:T(8,128)(2,1)S(1)}, bf16[144,512]{1,0:T(8,128)(2,1)S(1)}, u32[]{:S(2)}, u32[]{:S(2)}) collective-permute-start(bf16[144,512]{1,0:T(8,128)(2,1)S(1)} %get-tuple-element.64), channel_id=1, source_target_pairs={{0,2},{1,3},{2,4},{3,5},{4,6},{5,7},{6,8},{7,9},{8,10},{9,11},{10,... | collective-permute-start | bytes 442376 | tf_op jit(solution)/shard_map/ppermute | solution.py:438
  49.0 7.5 %collective-permute-start.15 = (bf16[2,64,512]{2,1,0:T(8,128)(2,1)S(1)}, bf16[2,64,512]{2,1,0:T(8,128)(2,1)S(1)}, u32[]{:S(2)}, u32[]{:S(2)}) collective-permute-start(bf16[2,64,512]{2,1,0:T(8,128)(2,1)S(1)} %get-tuple-element.65.token.own), channel_id=1, source_target_pairs={{2,0},{3,1},{4,2},{5,3},{6,4},{7,5},{8,6},{9,7},{10,8},{11,9},{12,... | collective-permute-start | bytes 393224 | tf_op jit(solution)/shard_map/ppermute | solution.py:438
  57.5 7.3 %collective-permute-start.16 = (bf16[2,64,512]{2,1,0:T(8,128)(2,1)S(1)}, bf16[2,64,512]{2,1,0:T(8,128)(2,1)S(1)}, u32[]{:S(2)}, u32[]{:S(2)}) collective-permute-start(bf16[2,64,512]{2,1,0:T(8,128)(2,1)S(1)} %shard_map.129.token.own), channel_id=1, source_target_pairs={{0,4},{1,5},{2,6},{3,7},{4,8},{5,9},{6,10},{7,11},{8,12},{9,13},{1... | collective-permute-start | bytes 393224 | tf_op jit(solution)/shard_map/ppermute | solution.py:438
  61.1 7.0 %collective-permute-start.17 = (bf16[2,64,512]{2,1,0:T(8,128)(2,1)S(1)}, bf16[2,64,512]{2,1,0:T(8,128)(2,1)S(1)}, u32[]{:S(2)}, u32[]{:S(2)}) collective-permute-start(bf16[2,64,512]{2,1,0:T(8,128)(2,1)S(1)} %shard_map.129.token.own), channel_id=1, source_target_pairs={{4,0},{5,1},{6,2},{7,3},{8,4},{9,5},{10,6},{11,7},{12,8},{13,9},{1... | collective-permute-start | bytes 393224 | tf_op jit(solution)/shard_map/ppermute | solution.py:438
  69.2 8.0 %collective-permute-start.18 = (bf16[2,64,512]{2,1,0:T(8,128)(2,1)S(1)}, bf16[2,64,512]{2,1,0:T(8,128)(2,1)S(1)}, u32[]{:S(2)}, u32[]{:S(2)}) collective-permute-start(bf16[2,64,512]{2,1,0:T(8,128)(2,1)S(1)} %shard_map.131.token.own), channel_id=1, source_target_pairs={{0,8},{1,9},{2,10},{3,11},{4,12},{5,13},{6,14},{7,15},{8,0},{9,1},... | collective-permute-start | bytes 393224 | tf_op jit(solution)/shard_map/ppermute | solution.py:556
  78.3 7.7 %collective-permute-start.21 = (bf16[2,64,512]{2,1,0:T(8,128)(2,1)S(1)}, bf16[2,64,512]{2,1,0:T(8,128)(2,1)S(1)}, u32[]{:S(2)}, u32[]{:S(2)}) collective-permute-start(bf16[2,64,512]{2,1,0:T(8,128)(2,1)S(1)} %get-tuple-element.74.correction), channel_id=1, source_target_pairs={{0,1},{1,2},{2,3},{3,4},{4,5},{5,6},{6,7},{7,8},{8,9},{9,10},{10,1... | collective-permute-start | bytes 393224 | tf_op jit(solution)/shard_map/ppermute | solution.py:438
  79.6 6.5 %collective-permute-start.22 = (bf16[2,64,512]{2,1,0:T(8,128)(2,1)S(1)}, bf16[2,64,512]{2,1,0:T(8,128)(2,1)S(1)}, u32[]{:S(2)}, u32[]{:S(2)}) collective-permute-start(bf16[2,64,512]{2,1,0:T(8,128)(2,1)S(1)} %get-tuple-element.74.correction), channel_id=1, source_target_pairs={{0,2},{1,3},{2,4},{3,5},{4,6},{5,7},{6,8},{7,9},{8,10},{9,11},{10,... | collective-permute-start | bytes 393224 | tf_op jit(solution)/shard_map/ppermute | solution.py:438
  89.6 9.5 %collective-permute-start.29 = (f32[80,128]{1,0:T(8,128)S(1)}, f32[80,128]{1,0:T(8,128)S(1)}, u32[]{:S(2)}, u32[]{:S(2)}) collective-permute-start(f32[80,128]{1,0:T(8,128)S(1)} %add.94), channel_id=1, source_target_pairs={{0,12},{2,14},{4,8},{6,10},{8,4},{10,6},{12,0},{14,2},{1,13},{3,15... | collective-permute-start | bytes 122888 | tf_op jit(solution)/shard_map/ppermute | solution.py:462
  93.7 7.9 %collective-permute-start.30 = (f32[80,128]{1,0:T(8,128)S(1)}, f32[80,128]{1,0:T(8,128)S(1)}, u32[]{:S(2)}, u32[]{:S(2)}) collective-permute-start(f32[80,128]{1,0:T(8,128)S(1)} %add.94), channel_id=1, source_target_pairs={{0,14},{2,12},{4,10},{6,8},{8,6},{10,4},{12,2},{14,0},{1,15},{3,13... | collective-permute-start | bytes 122888 | tf_op jit(solution)/shard_map/ppermute | solution.py:462
  95.7 5.9 %collective-permute-start.27 = (f32[80,128]{1,0:T(8,128)S(1)}, f32[80,128]{1,0:T(8,128)S(1)}, u32[]{:S(2)}, u32[]{:S(2)}) collective-permute-start(f32[80,128]{1,0:T(8,128)S(1)} %add.94), channel_id=1, source_target_pairs={{0,8},{2,10},{4,12},{6,14},{8,0},{10,2},{12,4},{14,6},{1,9},{3,11}... | collective-permute-start | bytes 122888 | tf_op jit(solution)/shard_map/ppermute | solution.py:462
  95.7 7.2 %collective-permute-start.28 = (f32[80,128]{1,0:T(8,128)S(1)}, f32[80,128]{1,0:T(8,128)S(1)}, u32[]{:S(2)}, u32[]{:S(2)}) collective-permute-start(f32[80,128]{1,0:T(8,128)S(1)} %add.94), channel_id=1, source_target_pairs={{0,10},{2,8},{4,14},{6,12},{8,2},{10,0},{12,6},{14,4},{1,11},{3,9}... | collective-permute-start | bytes 122888 | tf_op jit(solution)/shard_map/ppermute | solution.py:462
  97.6 5.4 %collective-permute-start.25 = (f32[80,128]{1,0:T(8,128)S(1)}, f32[80,128]{1,0:T(8,128)S(1)}, u32[]{:S(2)}, u32[]{:S(2)}) collective-permute-start(f32[80,128]{1,0:T(8,128)S(1)} %add.94), channel_id=1, source_target_pairs={{0,4},{2,6},{4,0},{6,2},{8,12},{10,14},{12,8},{14,10},{1,5},{3,7},... | collective-permute-start | bytes 122888 | tf_op jit(solution)/shard_map/ppermute | solution.py:462
  (13 other events, 49.6 us)

commit v14 on v13

--- a/solution.py
+++ b/solution.py
@@ -457,7 +457,7 @@
     slabs = lax.axis_size("slab")
     reach = 1
     while reach < slabs:
-        radix = min(8, slabs // reach)
+        radix = min(2, slabs // reach)
         routes = [[(i, i ^ (offset * reach)) for i in range(slabs)] for offset in range(1, radix)]
         part = summed_up([part] + [lax.ppermute(part, "slab", route) for route in routes])
         reach *= radix

time: 109 us -> 107 us (0.982)
  starting transfers between devices: 49.4 us -> 43.7 us
  waiting for transfers between devices: 20.1 us -> 23.2 us
    ppermute x7 -> x3, starting transfers between devices: 12 us -> 6.86 us  [slab_total(): lax.ppermute(part, 'slab', route)]
    ppermute x7 -> x3, waiting for transfers between devices: 3.92 us -> 7.15 us  [slab_total(): lax.ppermute(part, 'slab', route)]
  transfers between devices with their start and end apart: 32 -> 28, of which waited for: 13 -> 12; matrix products, arithmetic and copies ran while one was open for 1% -> 1% of each run, Pallas kernels for 26% -> 27%
where the time goes in v14:
time: 107 us; the launch traced here: 106 us
  starting transfers between devices  43.7 us (41%)
  Pallas kernels  33.9 us (32%)
  waiting for transfers between devices  23.2 us (22%)
  blocking collectives  2.37 us (2%)
  between operations  1.69 us (2%)
    ppermute x8, starting transfers between devices, along(): return lax.ppermute(operand, axis, route)  20.9 us
    ppermute x8, waiting for transfers between devices, along(): return lax.ppermute(operand, axis, route)  7.71 us
    pallas_call x4, Pallas kernels, load(): pl.pallas_call(body, out_shape=pltpu.VMEM(shape, bf16), in_specs=[SMEM] +...  7.47 us
    ppermute x3, waiting for transfers between devices, slab_total(): lax.ppermute(part, 'slab', route)  7.15 us
    ppermute x3, starting transfers between devices, slab_total(): lax.ppermute(part, 'slab', route)  6.86 us
    ppermute x2, starting transfers between devices, on_device(): received = lax.ppermute(moments, 'slab', flip)  6.05 us
    pallas_call x1, Pallas kernels, prepare(): pl.pallas_call(prepare_body, out_shape=[pltpu.VMEM(blocks.shape, bf16), p...  4.97 us
    ppermute x1, starting transfers between devices, on_device(): received = lax.ppermute(moments, 'slab', flips[0])  4.23 us
  transfers between devices with their start and end apart: 28, of which 12 were waited for; matrix products, arithmetic and copies ran while one was open for 1% of the time, Pallas kernels for 27%

profile of v14, /device:TPU:0, one launch (start us, length us, event | category | flops | bytes accessed | tf_op | source)
XLA Modules:
  0.0 106.1 jit_solution(2144411627014763055)
XLA Ops:
  1.9 5.5 %collective-permute-start = (bf16[4,64,256]{2,1,0:T(8,128)(2,1)}, bf16[4,64,256]{2,1,0:T(8,128)(2,1)S(1)}, u32[]{:S(2)}, u32[]{:S(2)}) collective-permute-start(bf16[4,64,256]{2,1,0:T(8,128)(2,1)} %vectors.1), channel_id=1, source_target_pairs={{0,2},{2,4},{4,6},{6,8},{8,10},{10,12},{12,14},{1,3},{3,5},{5,7},{... | collective-permute-start | bytes 393224 | tf_op jit(solution)/shard_map/ppermute | solution.py:438
  8.3 5.0 %shard_map.121 = (bf16[16,512,256]{2,1,0:T(8,128)(2,1)S(1)}, bf16[2,2,512,256]{3,2,1,0:T(8,128)(2,1)}, bf16[4,2,512,256]{3,2,1,0:T(8,128)(2,1)}) custom-call(s32[6]{0:T(128)S(1)} %stack.24.place, bf16[6,4,512,256]{3,2,1,0:T(8,128)(2,1)} %lower.11, bf16[6,4,512,256]{3,2,1,0:T(8,128)(2,1)} %upper.11, bf16[16,512,256]{2,1,0:T(8,128)(2,1)} %source.1), custom_call_target="tpu_custom_call" | custom-call | bytes 10485760 | tf_op jit(solution)/shard_map/pallas_call | solution.py:92
  13.4 2.4 %all_gather.3.extended = bf16[12,64,512]{2,1,0:T(8,128)(2,1)S(1)} all-gather(bf16[12,64,256]{2,1,0:T(8,128)(2,1)S(1)} %pad_maximum_fusion), channel_id=1, replica_groups=mesh['groups'=2,'slab'=8,'vec'=2] {'vec'}, dimensions={2}, use_global_device_ids=true | all-gather | bytes 1179648 | tf_op jit(solution)/shard_map/all_gather | solution.py:497
  15.8 2.2 %shard_map.122 = (bf16[2,64,256]{2,1,0:T(8,128)(2,1)S(1)}, bf16[2,64,256]{2,1,0:T(8,128)(2,1)S(1)}, f32[64,128]{1,0:T(8,128)S(1)}) custom-call(s32[6]{0:T(128)S(1)} %stack.24.place, s32[4,14]{1,0:T(4,128)S(1)} %get-tuple-element.88.table, bf16[12,64,512]{2,1,0:T(8,128)(2,1)S(1)} %all_gather.3.extended, bf16[4,64,256]{2,1,0:T(8,128)(2,1)S(1)} %copy-done, ...), custom_call_target="tpu_custom_call" | custom-call | flops 469762048 | bytes 4194304 | tf_op jit(solution)/shard_map/pallas_call | solution.py:238
  21.2 4.2 %collective-permute-start.7 = (f32[64,128]{1,0:T(8,128)S(1)}, f32[64,128]{1,0:T(8,128)S(1)}, u32[]{:S(2)}, u32[]{:S(2)}) collective-permute-start(f32[64,128]{1,0:T(8,128)S(1)} %add.76), channel_id=1, source_target_pairs={{0,2},{2,0},{4,6},{6,4},{8,10},{10,8},{12,14},{14,12},{1,3},{3,1},... | collective-permute-start | bytes 98312 | tf_op jit(solution)/shard_map/ppermute | solution.py:510
  25.7 2.1 %shard_map.123.weights = bf16[2,2,2,512,256]{4,3,2,1,0:T(8,128)(2,1)S(1)} custom-call(s32[6]{0:T(128)S(1)} %stack.24.place, bf16[2,64,256]{2,1,0:T(8,128)(2,1)S(1)} %get-tuple-element.48.token, bf16[6,4,512,256]{3,2,1,0:T(8,128)(2,1)} %lower.11, bf16[6,4,512,256]{3,2,1,0:T(8,128)(2,1)} %upper.11, bf16[2,2,512,256]{3,2,1,0:T(8,128)(2,1)} %collective-permute-done.6.packed), custom_call_target="tpu_custom_call" | custom-call | bytes 4194304 | tf_op jit(solution)/shard_map/pallas_call | solution.py:187
  30.3 2.1 %collective-permute-start.11 = (f32[64,128]{1,0:T(8,128)S(1)}, f32[64,128]{1,0:T(8,128)S(1)}, u32[]{:S(2)}, u32[]{:S(2)}) collective-permute-start(f32[64,128]{1,0:T(8,128)S(1)} %add.79), channel_id=1, source_target_pairs={{0,4},{2,6},{4,0},{6,2},{8,12},{10,14},{12,8},{14,10},{1,5},{3,7},... | collective-permute-start | bytes 98312 | tf_op jit(solution)/shard_map/ppermute | solution.py:530
  34.3 3.9 %collective-permute-start.12 = (f32[64,128]{1,0:T(8,128)S(1)}, f32[64,128]{1,0:T(8,128)S(1)}, u32[]{:S(2)}, u32[]{:S(2)}) collective-permute-start(f32[64,128]{1,0:T(8,128)S(1)} %add.80), channel_id=1, source_target_pairs={{0,8},{2,10},{4,12},{6,14},{8,0},{10,2},{12,4},{14,6},{1,9},{3,11}... | collective-permute-start | bytes 98312 | tf_op jit(solution)/shard_map/ppermute | solution.py:530
  38.3 3.2 %shard_map.126 = (bf16[2,2,2,512,256]{4,3,2,1,0:T(8,128)(2,1)S(1)}, bf16[5,2,512,256]{3,2,1,0:T(8,128)(2,1)}) custom-call(s32[6]{0:T(128)S(1)} %stack.24.place, bf16[2,128,512]{2,1,0:T(8,128)(2,1)S(1)} %shard_map.125.token.own, bf16[6,4,512,256]{3,2,1,0:T(8,128)(2,1)} %lower.11, bf16[6,4,512,256]{3,2,1,0:T(8,128)(2,1)} %upper.11, ...), custom_call_target="tpu_custom_call" | custom-call | bytes 7340032 | tf_op jit(solution)/shard_map/pallas_call | solution.py:129
  41.5 2.1 %collective-permute-done.12 = f32[64,128]{1,0:T(8,128)S(1)} collective-permute-done((f32[64,128]{1,0:T(8,128)S(1)}, f32[64,128]{1,0:T(8,128)S(1)}, u32[]{:S(2)}, u32[]{:S(2)}) %collective-permute-start.12) | collective-permute-done | bytes 32800 | tf_op jit(solution)/shard_map/ppermute | solution.py:530
  45.4 3.5 %collective-permute-start.13 = (bf16[144,512]{1,0:T(8,128)(2,1)S(1)}, bf16[144,512]{1,0:T(8,128)(2,1)S(1)}, u32[]{:S(2)}, u32[]{:S(2)}) collective-permute-start(bf16[144,512]{1,0:T(8,128)(2,1)S(1)} %get-tuple-element.64), channel_id=1, source_target_pairs={{0,2},{1,3},{2,4},{3,5},{4,6},{5,7},{6,8},{7,9},{8,10},{9,11},{10,... | collective-permute-start | bytes 442376 | tf_op jit(solution)/shard_map/ppermute | solution.py:438
  52.1 4.4 %collective-permute-done.15.above = bf16[2,64,512]{2,1,0:T(8,128)(2,1)S(1)} collective-permute-done((bf16[2,64,512]{2,1,0:T(8,128)(2,1)S(1)}, bf16[2,64,512]{2,1,0:T(8,128)(2,1)S(1)}, u32[]{:S(2)}, u32[]{:S(2)}) %collective-permute-start.15) | collective-permute-done | bytes 131104 | tf_op jit(solution)/shard_map/ppermute | solution.py:438
  57.5 3.6 %collective-permute-start.16 = (bf16[2,64,512]{2,1,0:T(8,128)(2,1)S(1)}, bf16[2,64,512]{2,1,0:T(8,128)(2,1)S(1)}, u32[]{:S(2)}, u32[]{:S(2)}) collective-permute-start(bf16[2,64,512]{2,1,0:T(8,128)(2,1)S(1)} %shard_map.129.token.own), channel_id=1, source_target_pairs={{0,4},{1,5},{2,6},{3,7},{4,8},{5,9},{6,10},{7,11},{8,12},{9,13},{1... | collective-permute-start | bytes 393224 | tf_op jit(solution)/shard_map/ppermute | solution.py:438
  64.9 3.3 %collective-permute-done.17.above = bf16[2,64,512]{2,1,0:T(8,128)(2,1)S(1)} collective-permute-done((bf16[2,64,512]{2,1,0:T(8,128)(2,1)S(1)}, bf16[2,64,512]{2,1,0:T(8,128)(2,1)S(1)}, u32[]{:S(2)}, u32[]{:S(2)}) %collective-permute-start.17) | collective-permute-done | bytes 131104 | tf_op jit(solution)/shard_map/ppermute | solution.py:438
  70.9 2.7 %shard_map.132.blocks = bf16[16,512,256]{2,1,0:T(8,128)(2,1)S(1)} custom-call(s32[6]{0:T(128)S(1)} %stack.24.place, bf16[2,64,512]{2,1,0:T(8,128)(2,1)S(1)} %shard_map.131.token.own, bf16[16,512,256]{2,1,0:T(8,128)(2,1)} %source.1), custom_call_target="tpu_custom_call" | custom-call | bytes 4194304 | tf_op jit(solution)/shard_map/pallas_call | solution.py:203
  75.4 1.8 %collective-permute-done.18.other = bf16[2,64,512]{2,1,0:T(8,128)(2,1)S(1)} collective-permute-done((bf16[2,64,512]{2,1,0:T(8,128)(2,1)S(1)}, bf16[2,64,512]{2,1,0:T(8,128)(2,1)S(1)}, u32[]{:S(2)}, u32[]{:S(2)}) %collective-permute-start.18) | collective-permute-done | bytes 131104 | tf_op jit(solution)/shard_map/ppermute | solution.py:556
  79.6 3.1 %collective-permute-start.22 = (bf16[2,64,512]{2,1,0:T(8,128)(2,1)S(1)}, bf16[2,64,512]{2,1,0:T(8,128)(2,1)S(1)}, u32[]{:S(2)}, u32[]{:S(2)}) collective-permute-start(bf16[2,64,512]{2,1,0:T(8,128)(2,1)S(1)} %get-tuple-element.74.correction), channel_id=1, source_target_pairs={{0,2},{1,3},{2,4},{3,5},{4,6},{5,7},{6,8},{7,9},{8,10},{9,11},{10,... | collective-permute-start | bytes 393224 | tf_op jit(solution)/shard_map/ppermute | solution.py:438
  82.9 3.4 %shard_map.135 = (f32[6,64,512]{2,1,0:T(8,128)S(1)}, f32[160,128]{1,0:T(8,128)S(1)}, f32[8,128]{1,0:T(8,128)S(1)}) custom-call(s32[6]{0:T(128)S(1)} %stack.24.place, s32[8,14]{1,0:T(8,128)S(1)} %add_add_fusion.table, f32[8]{0:T(128)S(1)} %copy-done.1, s32[1]{0:T(128)S(6)} %copy.13.index, bf16[12,64,512]{2,1,0:T(8,128)(2,1)S(1)} %all_gather.3.extended, ...), custom_call_target="tpu_custom_call" | custom-call | flops 469762048 | tf_op jit(solution)/shard_map/pallas_call | solution.py:597
  89.3 3.1 %collective-permute-start.24 = (f32[80,128]{1,0:T(8,128)S(1)}, f32[80,128]{1,0:T(8,128)S(1)}, u32[]{:S(2)}, u32[]{:S(2)}) collective-permute-start(f32[80,128]{1,0:T(8,128)S(1)} %add.82), channel_id=1, source_target_pairs={{0,2},{2,0},{4,6},{6,4},{8,10},{10,8},{12,14},{14,12},{1,3},{3,1},... | collective-permute-start | bytes 122888 | tf_op jit(solution)/shard_map/ppermute | solution.py:462
  92.5 2.0 %collective-permute-done.24 = f32[80,128]{1,0:T(8,128)S(1)} collective-permute-done((f32[80,128]{1,0:T(8,128)S(1)}, f32[80,128]{1,0:T(8,128)S(1)}, u32[]{:S(2)}, u32[]{:S(2)}) %collective-permute-start.24) | collective-permute-done | bytes 40992 | tf_op jit(solution)/shard_map/ppermute | solution.py:462
  94.5 1.9 %collective-permute-start.25 = (f32[80,128]{1,0:T(8,128)S(1)}, f32[80,128]{1,0:T(8,128)S(1)}, u32[]{:S(2)}, u32[]{:S(2)}) collective-permute-start(f32[80,128]{1,0:T(8,128)S(1)} %add.83), channel_id=1, source_target_pairs={{0,4},{2,6},{4,0},{6,2},{8,12},{10,14},{12,8},{14,10},{1,5},{3,7},... | collective-permute-start | bytes 122888 | tf_op jit(solution)/shard_map/ppermute | solution.py:462
  96.3 2.1 %collective-permute-done.25 = f32[80,128]{1,0:T(8,128)S(1)} collective-permute-done((f32[80,128]{1,0:T(8,128)S(1)}, f32[80,128]{1,0:T(8,128)S(1)}, u32[]{:S(2)}, u32[]{:S(2)}) %collective-permute-start.25) | collective-permute-done | bytes 40992 | tf_op jit(solution)/shard_map/ppermute | solution.py:462
  98.5 1.9 %collective-permute-start.26 = (f32[80,128]{1,0:T(8,128)S(1)}, f32[80,128]{1,0:T(8,128)S(1)}, u32[]{:S(2)}, u32[]{:S(2)}) collective-permute-start(f32[80,128]{1,0:T(8,128)S(1)} %add.84), channel_id=1, source_target_pairs={{0,8},{2,10},{4,12},{6,14},{8,0},{10,2},{12,4},{14,6},{1,9},{3,11}... | collective-permute-start | bytes 122888 | tf_op jit(solution)/shard_map/ppermute | solution.py:462
  100.3 3.0 %collective-permute-done.26 = f32[80,128]{1,0:T(8,128)S(1)} collective-permute-done((f32[80,128]{1,0:T(8,128)S(1)}, f32[80,128]{1,0:T(8,128)S(1)}, u32[]{:S(2)}, u32[]{:S(2)}) %collective-permute-start.26) | collective-permute-done | bytes 40992 | tf_op jit(solution)/shard_map/ppermute | solution.py:462
  (80 shorter events, 31.9 us)
Async XLA Ops:
  0.6 12.7 %collective-permute-start.1 = (bf16[4,64,256]{2,1,0:T(8,128)(2,1)}, bf16[4,64,256]{2,1,0:T(8,128)(2,1)S(1)}, u32[]{:S(2)}, u32[]{:S(2)}) collective-permute-start(bf16[4,64,256]{2,1,0:T(8,128)(2,1)} %vectors.1), channel_id=1, source_target_pairs={{2,0},{4,2},{6,4},{8,6},{10,8},{12,10},{14,12},{3,1},{5,3},{7,5},{... | collective-permute-start | bytes 393224 | tf_op jit(solution)/shard_map/ppermute | solution.py:438
  1.9 11.4 %collective-permute-start = (bf16[4,64,256]{2,1,0:T(8,128)(2,1)}, bf16[4,64,256]{2,1,0:T(8,128)(2,1)S(1)}, u32[]{:S(2)}, u32[]{:S(2)}) collective-permute-start(bf16[4,64,256]{2,1,0:T(8,128)(2,1)} %vectors.1), channel_id=1, source_target_pairs={{0,2},{2,4},{4,6},{6,8},{8,10},{10,12},{12,14},{1,3},{3,5},{5,7},{... | collective-permute-start | bytes 393224 | tf_op jit(solution)/shard_map/ppermute | solution.py:438
  19.5 10.4 %collective-permute-start.8 = (bf16[4,2,512,256]{3,2,1,0:T(8,128)(2,1)}, bf16[4,2,512,256]{3,2,1,0:T(8,128)(2,1)S(1)}, u32[]{:S(2)}, u32[]{:S(2)}) collective-permute-start(bf16[4,2,512,256]{3,2,1,0:T(8,128)(2,1)} %get-tuple-element.55), channel_id=1, source_target_pairs={{0,1},{1,0},{2,3},{3,2},{4,5},{5,4},{6,7},{7,6},{8,9},{9,8},{10,11... | collective-permute-start | bytes 6291464 | tf_op jit(solution)/shard_map/ppermute | solution.py:432
  19.9 5.7 %collective-permute-start.6 = (bf16[2,2,512,256]{3,2,1,0:T(8,128)(2,1)}, bf16[2,2,512,256]{3,2,1,0:T(8,128)(2,1)}, u32[]{:S(2)}, u32[]{:S(2)}) collective-permute-start(bf16[2,2,512,256]{3,2,1,0:T(8,128)(2,1)} %get-tuple-element.53), channel_id=1, source_target_pairs={{0,1},{1,0},{2,3},{3,2},{4,5},{5,4},{6,7},{7,6},{8,9},{9,8},{10,11... | collective-permute-start | bytes 3145736 | tf_op jit(solution)/shard_map/ppermute | solution.py:432
  20.1 8.7 %collective-permute-start.4 = (bf16[1,64,512]{2,1,0:T(8,128)(2,1)S(1)}, bf16[1,64,512]{2,1,0:T(8,128)(2,1)S(1)}, u32[]{:S(2)}, u32[]{:S(2)}) collective-permute-start(bf16[1,64,512]{2,1,0:T(8,128)(2,1)S(1)} %get-tuple-element.90), channel_id=1, source_target_pairs={{0,1},{1,0},{2,3},{3,2},{4,5},{5,4},{6,7},{7,6},{8,9},{9,8},{10,11... | collective-permute-start | bytes 196616 | tf_op jit(solution)/shard_map/ppermute | solution.py:432
  20.5 8.3 %collective-permute-start.5 = (bf16[1,64,512]{2,1,0:T(8,128)(2,1)S(1)}, bf16[1,64,512]{2,1,0:T(8,128)(2,1)S(1)}, u32[]{:S(2)}, u32[]{:S(2)}) collective-permute-start(bf16[1,64,512]{2,1,0:T(8,128)(2,1)S(1)} %get-tuple-element.89), channel_id=1, source_target_pairs={{1,2},{3,4},{5,6},{7,8},{9,10},{11,12},{13,14},{2,1},{4,3},{6,5},{... | collective-permute-start | bytes 196616 | tf_op jit(solution)/shard_map/ppermute | solution.py:507
  21.2 8.7 %collective-permute-start.7 = (f32[64,128]{1,0:T(8,128)S(1)}, f32[64,128]{1,0:T(8,128)S(1)}, u32[]{:S(2)}, u32[]{:S(2)}) collective-permute-start(f32[64,128]{1,0:T(8,128)S(1)} %add.76), channel_id=1, source_target_pairs={{0,2},{2,0},{4,6},{6,4},{8,10},{10,8},{12,14},{14,12},{1,3},{3,1},... | collective-permute-start | bytes 98312 | tf_op jit(solution)/shard_map/ppermute | solution.py:510
  30.0 52.9 %collective-permute-start.19 = (bf16[16,512,256]{2,1,0:T(8,128)(2,1)S(1)}, bf16[16,512,256]{2,1,0:T(8,128)(2,1)S(1)}, u32[]{:S(2)}, u32[]{:S(2)}) collective-permute-start(bf16[16,512,256]{2,1,0:T(8,128)(2,1)S(1)} %copy-done.2), channel_id=1, source_target_pairs={{0,1},{1,0},{2,3},{3,2},{4,5},{5,4},{6,7},{7,6},{8,9},{9,8},{10,11... | collective-permute-start | bytes 12582920 | tf_op jit(solution)/shard_map/ppermute | solution.py:432
  30.3 4.0 %collective-permute-start.11 = (f32[64,128]{1,0:T(8,128)S(1)}, f32[64,128]{1,0:T(8,128)S(1)}, u32[]{:S(2)}, u32[]{:S(2)}) collective-permute-start(f32[64,128]{1,0:T(8,128)S(1)} %add.79), channel_id=1, source_target_pairs={{0,4},{2,6},{4,0},{6,2},{8,12},{10,14},{12,8},{14,10},{1,5},{3,7},... | collective-permute-start | bytes 98312 | tf_op jit(solution)/shard_map/ppermute | solution.py:530
  32.4 11.2 %collective-permute-start.9 = (bf16[2,128,512]{2,1,0:T(8,128)(2,1)S(1)}, bf16[2,128,512]{2,1,0:T(8,128)(2,1)S(1)}, u32[]{:S(2)}, u32[]{:S(2)}) collective-permute-start(bf16[2,128,512]{2,1,0:T(8,128)(2,1)S(1)} %shard_map.125.token.own), channel_id=1, source_target_pairs={{0,1},{1,0},{2,3},{3,2},{4,5},{5,4},{6,7},{7,6},{8,9},{9,8},{10,11... | collective-permute-start | bytes 786440 | tf_op jit(solution)/shard_map/ppermute | solution.py:432
  32.4 11.2 %collective-permute-start.10 = (bf16[2,128,512]{2,1,0:T(8,128)(2,1)S(1)}, bf16[2,128,512]{2,1,0:T(8,128)(2,1)S(1)}, u32[]{:S(2)}, u32[]{:S(2)}) collective-permute-start(bf16[2,128,512]{2,1,0:T(8,128)(2,1)S(1)} %shard_map.125.token.own), channel_id=1, source_target_pairs={{1,2},{3,4},{5,6},{7,8},{9,10},{11,12},{13,14},{2,1},{4,3},{6,5},{... | collective-permute-start | bytes 786440 | tf_op jit(solution)/shard_map/ppermute | solution.py:527
  34.3 9.2 %collective-permute-start.12 = (f32[64,128]{1,0:T(8,128)S(1)}, f32[64,128]{1,0:T(8,128)S(1)}, u32[]{:S(2)}, u32[]{:S(2)}) collective-permute-start(f32[64,128]{1,0:T(8,128)S(1)} %add.80), channel_id=1, source_target_pairs={{0,8},{2,10},{4,12},{6,14},{8,0},{10,2},{12,4},{14,6},{1,9},{3,11}... | collective-permute-start | bytes 98312 | tf_op jit(solution)/shard_map/ppermute | solution.py:530
  43.6 12.9 %collective-permute-start.14 = (bf16[5,2,512,256]{3,2,1,0:T(8,128)(2,1)}, bf16[5,2,512,256]{3,2,1,0:T(8,128)(2,1)S(1)}, u32[]{:S(2)}, u32[]{:S(2)}) collective-permute-start(bf16[5,2,512,256]{3,2,1,0:T(8,128)(2,1)} %get-tuple-element.66), channel_id=1, source_target_pairs={{0,1},{1,0},{2,3},{3,2},{4,5},{5,4},{6,7},{7,6},{8,9},{9,8},{10,11... | collective-permute-start | bytes 7864328 | tf_op jit(solution)/shard_map/ppermute | solution.py:432
  45.4 11.1 %collective-permute-start.13 = (bf16[144,512]{1,0:T(8,128)(2,1)S(1)}, bf16[144,512]{1,0:T(8,128)(2,1)S(1)}, u32[]{:S(2)}, u32[]{:S(2)}) collective-permute-start(bf16[144,512]{1,0:T(8,128)(2,1)S(1)} %get-tuple-element.64), channel_id=1, source_target_pairs={{0,2},{1,3},{2,4},{3,5},{4,6},{5,7},{6,8},{7,9},{8,10},{9,11},{10,... | collective-permute-start | bytes 442376 | tf_op jit(solution)/shard_map/ppermute | solution.py:438
  49.0 7.5 %collective-permute-start.15 = (bf16[2,64,512]{2,1,0:T(8,128)(2,1)S(1)}, bf16[2,64,512]{2,1,0:T(8,128)(2,1)S(1)}, u32[]{:S(2)}, u32[]{:S(2)}) collective-permute-start(bf16[2,64,512]{2,1,0:T(8,128)(2,1)S(1)} %get-tuple-element.65.token.own), channel_id=1, source_target_pairs={{2,0},{3,1},{4,2},{5,3},{6,4},{7,5},{8,6},{9,7},{10,8},{11,9},{12,... | collective-permute-start | bytes 393224 | tf_op jit(solution)/shard_map/ppermute | solution.py:438
  57.5 7.3 %collective-permute-start.16 = (bf16[2,64,512]{2,1,0:T(8,128)(2,1)S(1)}, bf16[2,64,512]{2,1,0:T(8,128)(2,1)S(1)}, u32[]{:S(2)}, u32[]{:S(2)}) collective-permute-start(bf16[2,64,512]{2,1,0:T(8,128)(2,1)S(1)} %shard_map.129.token.own), channel_id=1, source_target_pairs={{0,4},{1,5},{2,6},{3,7},{4,8},{5,9},{6,10},{7,11},{8,12},{9,13},{1... | collective-permute-start | bytes 393224 | tf_op jit(solution)/shard_map/ppermute | solution.py:438
  61.1 7.0 %collective-permute-start.17 = (bf16[2,64,512]{2,1,0:T(8,128)(2,1)S(1)}, bf16[2,64,512]{2,1,0:T(8,128)(2,1)S(1)}, u32[]{:S(2)}, u32[]{:S(2)}) collective-permute-start(bf16[2,64,512]{2,1,0:T(8,128)(2,1)S(1)} %shard_map.129.token.own), channel_id=1, source_target_pairs={{4,0},{5,1},{6,2},{7,3},{8,4},{9,5},{10,6},{11,7},{12,8},{13,9},{1... | collective-permute-start | bytes 393224 | tf_op jit(solution)/shard_map/ppermute | solution.py:438
  69.2 8.0 %collective-permute-start.18 = (bf16[2,64,512]{2,1,0:T(8,128)(2,1)S(1)}, bf16[2,64,512]{2,1,0:T(8,128)(2,1)S(1)}, u32[]{:S(2)}, u32[]{:S(2)}) collective-permute-start(bf16[2,64,512]{2,1,0:T(8,128)(2,1)S(1)} %shard_map.131.token.own), channel_id=1, source_target_pairs={{0,8},{1,9},{2,10},{3,11},{4,12},{5,13},{6,14},{7,15},{8,0},{9,1},... | collective-permute-start | bytes 393224 | tf_op jit(solution)/shard_map/ppermute | solution.py:556
  78.3 7.9 %collective-permute-start.21 = (bf16[2,64,512]{2,1,0:T(8,128)(2,1)S(1)}, bf16[2,64,512]{2,1,0:T(8,128)(2,1)S(1)}, u32[]{:S(2)}, u32[]{:S(2)}) collective-permute-start(bf16[2,64,512]{2,1,0:T(8,128)(2,1)S(1)} %get-tuple-element.74.correction), channel_id=1, source_target_pairs={{0,1},{1,2},{2,3},{3,4},{4,5},{5,6},{6,7},{7,8},{8,9},{9,10},{10,1... | collective-permute-start | bytes 393224 | tf_op jit(solution)/shard_map/ppermute | solution.py:438
  79.6 6.6 %collective-permute-start.22 = (bf16[2,64,512]{2,1,0:T(8,128)(2,1)S(1)}, bf16[2,64,512]{2,1,0:T(8,128)(2,1)S(1)}, u32[]{:S(2)}, u32[]{:S(2)}) collective-permute-start(bf16[2,64,512]{2,1,0:T(8,128)(2,1)S(1)} %get-tuple-element.74.correction), channel_id=1, source_target_pairs={{0,2},{1,3},{2,4},{3,5},{4,6},{5,7},{6,8},{7,9},{8,10},{9,11},{10,... | collective-permute-start | bytes 393224 | tf_op jit(solution)/shard_map/ppermute | solution.py:438
  89.3 5.1 %collective-permute-start.24 = (f32[80,128]{1,0:T(8,128)S(1)}, f32[80,128]{1,0:T(8,128)S(1)}, u32[]{:S(2)}, u32[]{:S(2)}) collective-permute-start(f32[80,128]{1,0:T(8,128)S(1)} %add.82), channel_id=1, source_target_pairs={{0,2},{2,0},{4,6},{6,4},{8,10},{10,8},{12,14},{14,12},{1,3},{3,1},... | collective-permute-start | bytes 122888 | tf_op jit(solution)/shard_map/ppermute | solution.py:462
  94.5 4.0 %collective-permute-start.25 = (f32[80,128]{1,0:T(8,128)S(1)}, f32[80,128]{1,0:T(8,128)S(1)}, u32[]{:S(2)}, u32[]{:S(2)}) collective-permute-start(f32[80,128]{1,0:T(8,128)S(1)} %add.83), channel_id=1, source_target_pairs={{0,4},{2,6},{4,0},{6,2},{8,12},{10,14},{12,8},{14,10},{1,5},{3,7},... | collective-permute-start | bytes 122888 | tf_op jit(solution)/shard_map/ppermute | solution.py:462
  98.5 4.9 %collective-permute-start.26 = (f32[80,128]{1,0:T(8,128)S(1)}, f32[80,128]{1,0:T(8,128)S(1)}, u32[]{:S(2)}, u32[]{:S(2)}) collective-permute-start(f32[80,128]{1,0:T(8,128)S(1)} %add.84), channel_id=1, source_target_pairs={{0,8},{2,10},{4,12},{6,14},{8,0},{10,2},{12,4},{14,6},{1,9},{3,11}... | collective-permute-start | bytes 122888 | tf_op jit(solution)/shard_map/ppermute | solution.py:462
  100.3 3.1 %collective-permute-start.20 = (bf16[2,64,256]{2,1,0:T(8,128)(2,1)S(1)}, bf16[2,64,256]{2,1,0:T(8,128)(2,1)S(1)}, u32[]{:S(2)}, u32[]{:S(2)}) collective-permute-start(bf16[2,64,256]{2,1,0:T(8,128)(2,1)S(1)} %get-tuple-element.79), channel_id=1, source_target_pairs={{0,1},{1,0},{2,3},{3,2},{4,5},{5,4},{6,7},{7,6},{8,9},{9,8},{10,11... | collective-permute-start | bytes 196616 | tf_op jit(solution)/shard_map/ppermute | solution.py:432
  (9 other events, 32.0 us)
